TPU v7x, 512 devices: a whole 4x4x16 slice. The times are simulated.
512 devices in a mesh: slab: 64 (over x, z), pen: 8 (over y, core).
Axes of the slice: x: 4, y: 4, z: 16, core: 2. Of those that a mesh axis runs over, the one named last changes fastest.
Arguments:
- pressure_rhs: float32 [256, 256, 256], P('slab', 'pen'), may hold values from -120 to 120
- permeability: float32 [256, 256, 256], P('slab', 'pen'), may hold values from 0.2 to 5
- accumulation: float32 [256, 256, 256], P('slab', 'pen'), may hold values from 1 to 8
- coarse_perm: float32 [128, 128, 128], P('slab', 'pen'), may hold values from 0.2 to 5
- coarse_accum: float32 [128, 128, 128], P('slab', 'pen'), may hold values from 1 to 8
- run_lengths: int32 [32], replicated, may hold values from 1 to 4, 64 in all
Outputs:
- updated_pressure: float32 [256, 256, 256], P('slab', 'pen')
Inputs may be any that keep to these rules, and one draw needn't show every extreme that they name: `run_lengths`: runs are laid end to end over the blocks 0 to 63 in order and sum to 64; some run has exactly 4 blocks.
All inputs are finite; a program needn't handle non-finite values.
Results may differ from a plain program's by a relative error of at most 0.00002.
Values sent between devices are 32-bit elements; how exact they have to be, the bound alone decides.
No kernel may reach another device: no remote copies, remote signals or barrier semaphores. Data moves between devices by JAX's collectives and lax.ppermute only.
A program may use at most 64 MiB of HBM per device.

v0:
```python
import jax
import jax.numpy as jnp
from jax import lax
from jax.sharding import PartitionSpec as P

POST = 2
COARSE_SWEEPS = 6
MOST = 4


OMEGA = 0.7


def with_halo(block, sides, width):
    for axis, dim in sides:
        count = lax.axis_size(axis)
        forward = [(i, i + 1) for i in range(count - 1)]
        backward = [(target, source) for source, target in forward]
        low = lax.ppermute(
            lax.slice_in_dim(block, block.shape[dim] - width, None, axis=dim), axis, forward
        )
        high = lax.ppermute(lax.slice_in_dim(block, 0, width, axis=dim), axis, backward)
        block = jnp.concatenate([low, block, high], axis=dim)
    return block


def shifted(x, axis, by):
    devices = lax.axis_size(axis)
    pairs = [(i, i + by) for i in range(devices) if 0 <= i + by < devices]
    return lax.ppermute(x, axis, pairs)


def neighbours(extended, lower_mask, upper_mask):
    plane_count = extended.shape[0] - 2
    row_count = extended.shape[1] - 2
    col_count = extended.shape[2] - 2
    layers = []
    for off_z in (-1, 0, 1):
        summed = jnp.zeros((plane_count, row_count, col_count), jnp.float32)
        for off_y in (-1, 0, 1):
            for off_x in (-1, 0, 1):
                distance = abs(off_z) + abs(off_y) + abs(off_x)
                if distance == 0:
                    continue
                weight = 0.5 ** (distance - 1)
                summed = (
                    summed
                    + weight
                    * extended[
                        1 + off_z : 1 + off_z + plane_count,
                        1 + off_y : 1 + off_y + row_count,
                        1 + off_x : 1 + off_x + col_count,
                    ]
                )
        layers.append(summed)
    return lower_mask * layers[0] + layers[1] + upper_mask * layers[2]


def fine_extend(field):
    widened = with_halo(field, (("slab", 0), ("pen", 1)), 1)
    return jnp.pad(widened, ((0, 0), (0, 0), (1, 1)))


def coarse_extend(field):
    widened = with_halo(field, (("slab", 0), ("pen", 1)), 1)
    return jnp.pad(widened, ((0, 0), (0, 0), (1, 1)))


def owner_extend(field):
    widened = with_halo(field, (("pen", 1),), 1)
    return jnp.pad(widened, ((1, 1), (0, 0), (1, 1)))


def operate(pressure, trans, diag, extend, lower_mask, upper_mask):
    return diag * pressure - trans * neighbours(extend(trans * pressure), lower_mask, upper_mask)


def on_device(pressure_rhs, permeability, accumulation, coarse_perm, coarse_accum, run_lengths):
    trans = jnp.sqrt(permeability)
    diag = trans * neighbours(fine_extend(trans), 1.0, 1.0) + accumulation
    pressure = OMEGA * pressure_rhs / diag
    pressure = (
        pressure
        + OMEGA * (pressure_rhs - operate(pressure, trans, diag, fine_extend, 1.0, 1.0)) / diag
    )
    residual = pressure_rhs - operate(pressure, trans, diag, fine_extend, 1.0, 1.0)
    half_depth = residual.shape[0] // 2
    half_rows = residual.shape[1] // 2
    half_cols = residual.shape[2] // 2
    coarse_res = residual.reshape(half_depth, 2, half_rows, 2, half_cols, 2).sum(axis=(1, 3, 5))
    coarse_trans = jnp.sqrt(coarse_perm)
    coarse_diag = coarse_trans * neighbours(coarse_extend(coarse_trans), 1.0, 1.0) + coarse_accum
    slab_index = lax.axis_index("slab")
    ends = jnp.cumsum(run_lengths)
    starts = ends - run_lengths
    run_id = jnp.sum((starts <= slab_index).astype(jnp.int32)) - 1
    chosen = jnp.arange(run_lengths.shape[0], dtype=jnp.int32) == run_id
    run_start = jnp.sum(jnp.where(chosen, starts, 0))
    offset = slab_index - run_start
    owned = jnp.sum(jnp.where(starts == slab_index, run_lengths, 0))
    bundle = jnp.stack([coarse_res, coarse_trans, coarse_diag])
    gathered = [bundle]
    for slot_index in range(1, MOST):
        gathered.append(shifted(bundle, "slab", -slot_index))
    domain = jnp.concatenate(gathered, axis=1)
    domain_res = domain[0]
    domain_trans = domain[1]
    domain_diag = domain[2]
    valid = (jnp.arange(MOST * half_depth, dtype=jnp.int32) < owned * half_depth)[:, None, None]
    safe_diag = jnp.where(valid, domain_diag, 1.0)
    estimate = jnp.where(valid, OMEGA * domain_res / safe_diag, 0.0)
    for sweep_step in range(COARSE_SWEEPS - 1):
        image = operate(estimate, domain_trans, domain_diag, owner_extend, 1.0, 1.0)
        estimate = jnp.where(valid, estimate + OMEGA * (domain_res - image) / safe_diag, 0.0)
    correction = estimate[:half_depth]
    for slot_index in range(1, MOST):
        outgoing = estimate[slot_index * half_depth : (slot_index + 1) * half_depth]
        arrived = shifted(outgoing, "slab", slot_index)
        correction = jnp.where(offset == slot_index, arrived, correction)
    prolonged = jnp.broadcast_to(
        correction[:, None, :, None, :, None], (half_depth, 2, half_rows, 2, half_cols, 2)
    ).reshape(residual.shape)
    pressure = pressure + prolonged
    for sweep_step in range(POST):
        pressure = (
            pressure
            + OMEGA * (pressure_rhs - operate(pressure, trans, diag, fine_extend, 1.0, 1.0)) / diag
        )
    return pressure


def solution(mesh):
    return jax.shard_map(
        on_device,
        mesh=mesh,
        in_specs=(
            P("slab", "pen", None),
            P("slab", "pen", None),
            P("slab", "pen", None),
            P("slab", "pen", None),
            P("slab", "pen", None),
            P(),
        ),
        out_specs=P("slab", "pen", None),
        check_vma=False,
    )
```

profile of v0, /device:TPU:15, one launch (start us, length us, event | category | flops | bytes accessed | tf_op | source)
XLA Modules:
  0.0 206.0 jit_solution(7219043243757187361)
XLA Ops:
  0.0 1.0 sqrt.6
  1.0 3.5 %collective-permute-start = (f32[1,32,256]{2,1,0:T(8,128)S(1)}, f32[1,32,256]{2,1,0:T(8,128)S(1)}, u32[]{:S(2)}, u32[]{:S(2)}) collective-permute-start(f32[1,32,256]{2,1,0:T(8,128)S(1)} %get-tuple-element.53), channel_id=1, source_target_pairs={{0,8},{8,16},{16,24},{24,32},{32,40},{40,48},{48,56},{56,64},{64,7... | collective-permute-start | bytes 98312 | tf_op jit(solution)/shard_map/ppermute | solution.py:19
  4.6 9.8 %collective-permute-start.1 = (f32[1,32,256]{2,1,0:T(8,128)S(1)}, f32[1,32,256]{2,1,0:T(8,128)S(1)}, u32[]{:S(2)}, u32[]{:S(2)}) collective-permute-start(f32[1,32,256]{2,1,0:T(8,128)S(1)} %get-tuple-element.54), channel_id=1, source_target_pairs={{8,0},{16,8},{24,16},{32,24},{40,32},{48,40},{56,48},{64,56},{72,6... | collective-permute-start | bytes 98312 | tf_op jit(solution)/shard_map/ppermute | solution.py:22
  15.1 1.9 collective-permute-start.12
  17.0 5.5 %collective-permute-start.13 = (f32[1,16,128]{2,1,0:T(8,128)S(1)}, f32[1,16,128]{2,1,0:T(8,128)S(1)}, u32[]{:S(2)}, u32[]{:S(2)}) collective-permute-start(f32[1,16,128]{2,1,0:T(8,128)S(1)} %get-tuple-element.75), channel_id=1, source_target_pairs={{8,0},{16,8},{24,16},{32,24},{40,32},{48,40},{56,48},{64,56},{72,6... | collective-permute-start | bytes 24584 | tf_op jit(solution)/shard_map/ppermute | solution.py:22
  23.4 1.3 fusion.305
  25.4 4.6 %collective-permute-start.2 = (f32[6,1,256]{2,1,0:T(1,128)S(1)}, f32[6,1,256]{2,1,0:T(1,128)S(1)}, u32[]{:S(2)}, u32[]{:S(2)}) collective-permute-start(f32[6,1,256]{2,1,0:T(1,128)S(1)} %get-tuple-element.43), channel_id=1, source_target_pairs={{0,1},{1,2},{2,3},{3,4},{4,5},{5,6},{6,7},{8,9},{9,10},{10,11},{11... | collective-permute-start | bytes 18440 | tf_op jit(solution)/shard_map/ppermute | solution.py:19
  30.0 1.9 collective-permute-start.3
  31.9 1.3 fusion.306
  33.8 1.2 collective-permute-done.3
  35.2 1.5 fusion.132
  36.7 1.9 collective-permute-start.4
  38.6 5.5 %collective-permute-start.5 = (f32[1,32,256]{2,1,0:T(8,128)S(1)}, f32[1,32,256]{2,1,0:T(8,128)S(1)}, u32[]{:S(2)}, u32[]{:S(2)}) collective-permute-start(f32[1,32,256]{2,1,0:T(8,128)S(1)} %get-tuple-element.52), channel_id=1, source_target_pairs={{8,0},{16,8},{24,16},{32,24},{40,32},{48,40},{56,48},{64,56},{72,6... | collective-permute-start | bytes 98312 | tf_op jit(solution)/shard_map/ppermute | solution.py:22
  44.1 3.1 %collective-permute-start.14 = (f32[4,1,128]{2,1,0:T(1,128)S(1)}, f32[4,1,128]{2,1,0:T(1,128)S(1)}, u32[]{:S(2)}, u32[]{:S(2)}) collective-permute-start(f32[4,1,128]{2,1,0:T(1,128)S(1)} %get-tuple-element.70), channel_id=1, source_target_pairs={{0,1},{1,2},{2,3},{3,4},{4,5},{5,6},{6,7},{8,9},{9,10},{10,11},{11... | collective-permute-start | bytes 6152 | tf_op jit(solution)/shard_map/ppermute | solution.py:19
  47.2 1.9 collective-permute-start.15
  49.2 3.6 %collective-permute-start.6 = (f32[6,1,256]{2,1,0:T(1,128)S(1)}, f32[6,1,256]{2,1,0:T(1,128)S(1)}, u32[]{:S(2)}, u32[]{:S(2)}) collective-permute-start(f32[6,1,256]{2,1,0:T(1,128)S(1)} %get-tuple-element.39), channel_id=1, source_target_pairs={{0,1},{1,2},{2,3},{3,4},{4,5},{5,6},{6,7},{8,9},{9,10},{10,11},{11... | collective-permute-start | bytes 18440 | tf_op jit(solution)/shard_map/ppermute | solution.py:19
  52.8 1.9 collective-permute-start.7
  54.8 3.0 %collective-permute-done.7 = f32[6,1,256]{2,1,0:T(1,128)S(1)} collective-permute-done((f32[6,1,256]{2,1,0:T(1,128)S(1)}, f32[6,1,256]{2,1,0:T(1,128)S(1)}, u32[]{:S(2)}, u32[]{:S(2)}) %collective-permute-start.7) | collective-permute-done | bytes 6176 | tf_op jit(solution)/shard_map/ppermute | solution.py:22
  58.0 1.4 sqrt_multiply_fusion.2
  59.5 1.9 collective-permute-start.8
  61.4 5.5 %collective-permute-start.9 = (f32[1,32,256]{2,1,0:T(8,128)S(1)}, f32[1,32,256]{2,1,0:T(8,128)S(1)}, u32[]{:S(2)}, u32[]{:S(2)}) collective-permute-start(f32[1,32,256]{2,1,0:T(8,128)S(1)} %get-tuple-element.50), channel_id=1, source_target_pairs={{8,0},{16,8},{24,16},{32,24},{40,32},{48,40},{56,48},{64,56},{72,6... | collective-permute-start | bytes 98312 | tf_op jit(solution)/shard_map/ppermute | solution.py:22
  67.9 3.2 %collective-permute-start.10 = (f32[6,1,256]{2,1,0:T(1,128)S(1)}, f32[6,1,256]{2,1,0:T(1,128)S(1)}, u32[]{:S(2)}, u32[]{:S(2)}) collective-permute-start(f32[6,1,256]{2,1,0:T(1,128)S(1)} %get-tuple-element.35), channel_id=1, source_target_pairs={{0,1},{1,2},{2,3},{3,4},{4,5},{5,6},{6,7},{8,9},{9,10},{10,11},{11... | collective-permute-start | bytes 18440 | tf_op jit(solution)/shard_map/ppermute | solution.py:19
  71.0 1.9 collective-permute-start.11
  73.1 2.9 %collective-permute-done.11 = f32[6,1,256]{2,1,0:T(1,128)S(1)} collective-permute-done((f32[6,1,256]{2,1,0:T(1,128)S(1)}, f32[6,1,256]{2,1,0:T(1,128)S(1)}, u32[]{:S(2)}, u32[]{:S(2)}) %collective-permute-start.11) | collective-permute-done | bytes 6176 | tf_op jit(solution)/shard_map/ppermute | solution.py:22
  76.7 9.8 %reshape.39 = f32[2,2,16,2,128,2]{5,4,3,2,1,0:T(8,128)} reshape(f32[4,32,256]{2,1,0:T(8,128)S(1)} %fusion.62) | data formatting | bytes 262144 | tf_op jit(solution)/shard_map/reshape | solution.py:90
  86.5 4.0 %reduce_sum.39 = f32[2,16,128]{2,1,0:T(8,128)S(1)} reduce(f32[2,2,16,2,128,2]{5,4,3,2,1,0:T(8,128)} %reshape.39, f32[]{:T(128)} %constant.13.clone.1), dimensions={1,3,5}, to_apply=%region_4.5 | reduce | flops 28672 | bytes 147460 | tf_op jit(solution)/shard_map/reduce_sum | solution.py:90
  90.5 6.2 %collective-permute-start.16 = (f32[3,2,16,128]{3,2,1,0:T(8,128)S(1)}, f32[3,2,16,128]{3,2,1,0:T(8,128)S(1)}, u32[]{:S(2)}, u32[]{:S(2)}) collective-permute-start(f32[3,2,16,128]{3,2,1,0:T(8,128)S(1)} %pad_maximum_fusion.27), channel_id=1, source_target_pairs={{8,0},{16,8},{24,16},{32,24},{40,32},{48,40},{56,48},{64,56},{72,6... | collective-permute-start | bytes 147464 | tf_op jit(solution)/shard_map/ppermute | solution.py:30
  96.7 1.9 collective-permute-start.17
  98.6 2.6 %collective-permute-start.18 = (f32[3,2,16,128]{3,2,1,0:T(8,128)S(1)}, f32[3,2,16,128]{3,2,1,0:T(8,128)S(1)}, u32[]{:S(2)}, u32[]{:S(2)}) collective-permute-start(f32[3,2,16,128]{3,2,1,0:T(8,128)S(1)} %pad_maximum_fusion.27), channel_id=1, source_target_pairs={{24,0},{32,8},{40,16},{48,24},{56,32},{64,40},{72,48},{80,56},{88,... | collective-permute-start | bytes 147464 | tf_op jit(solution)/shard_map/ppermute | solution.py:30
  101.3 1.2 collective-permute-done.17
  102.4 2.8 %collective-permute-done.18 = f32[3,2,16,128]{3,2,1,0:T(8,128)S(1)} collective-permute-done((f32[3,2,16,128]{3,2,1,0:T(8,128)S(1)}, f32[3,2,16,128]{3,2,1,0:T(8,128)S(1)}, u32[]{:S(2)}, u32[]{:S(2)}) %collective-permute-start.18) | collective-permute-done | bytes 49184 | tf_op jit(solution)/shard_map/ppermute | solution.py:30
  105.4 4.0 %collective-permute-start.19 = (f32[8,1,128]{2,1,0:T(1,128)S(1)}, f32[8,1,128]{2,1,0:T(1,128)S(1)}, u32[]{:S(2)}, u32[]{:S(2)}) collective-permute-start(f32[8,1,128]{2,1,0:T(1,128)S(1)} %get-tuple-element.66), channel_id=1, source_target_pairs={{0,1},{1,2},{2,3},{3,4},{4,5},{5,6},{6,7},{8,9},{9,10},{10,11},{11... | collective-permute-start | bytes 12296 | tf_op jit(solution)/shard_map/ppermute | solution.py:19
  109.4 1.9 collective-permute-start.20
  111.3 3.0 %collective-permute-done.20 = f32[8,1,128]{2,1,0:T(1,128)S(1)} collective-permute-done((f32[8,1,128]{2,1,0:T(1,128)S(1)}, f32[8,1,128]{2,1,0:T(1,128)S(1)}, u32[]{:S(2)}, u32[]{:S(2)}) %collective-permute-start.20) | collective-permute-done | bytes 4128 | tf_op jit(solution)/shard_map/ppermute | solution.py:22
  114.8 1.9 collective-permute-start.21
  116.8 2.4 %collective-permute-start.22 = (f32[8,1,128]{2,1,0:T(1,128)S(1)}, f32[8,1,128]{2,1,0:T(1,128)S(1)}, u32[]{:S(2)}, u32[]{:S(2)}) collective-permute-start(f32[8,1,128]{2,1,0:T(1,128)S(1)} %get-tuple-element.65), channel_id=1, source_target_pairs={{1,0},{2,1},{3,2},{4,3},{5,4},{6,5},{7,6},{9,8},{10,9},{11,10},{12... | collective-permute-start | bytes 12296 | tf_op jit(solution)/shard_map/ppermute | solution.py:22
  119.2 2.5 %collective-permute-done.22 = f32[8,1,128]{2,1,0:T(1,128)S(1)} collective-permute-done((f32[8,1,128]{2,1,0:T(1,128)S(1)}, f32[8,1,128]{2,1,0:T(1,128)S(1)}, u32[]{:S(2)}, u32[]{:S(2)}) %collective-permute-start.22) | collective-permute-done | bytes 4128 | tf_op jit(solution)/shard_map/ppermute | solution.py:22
  122.2 1.9 collective-permute-start.23
  124.2 2.4 %collective-permute-start.24 = (f32[8,1,128]{2,1,0:T(1,128)S(1)}, f32[8,1,128]{2,1,0:T(1,128)S(1)}, u32[]{:S(2)}, u32[]{:S(2)}) collective-permute-start(f32[8,1,128]{2,1,0:T(1,128)S(1)} %get-tuple-element.63), channel_id=1, source_target_pairs={{1,0},{2,1},{3,2},{4,3},{5,4},{6,5},{7,6},{9,8},{10,9},{11,10},{12... | collective-permute-start | bytes 12296 | tf_op jit(solution)/shard_map/ppermute | solution.py:22
  126.6 2.5 %collective-permute-done.24 = f32[8,1,128]{2,1,0:T(1,128)S(1)} collective-permute-done((f32[8,1,128]{2,1,0:T(1,128)S(1)}, f32[8,1,128]{2,1,0:T(1,128)S(1)}, u32[]{:S(2)}, u32[]{:S(2)}) %collective-permute-start.24) | collective-permute-done | bytes 4128 | tf_op jit(solution)/shard_map/ppermute | solution.py:22
  129.6 1.9 collective-permute-start.25
  131.6 2.4 %collective-permute-start.26 = (f32[8,1,128]{2,1,0:T(1,128)S(1)}, f32[8,1,128]{2,1,0:T(1,128)S(1)}, u32[]{:S(2)}, u32[]{:S(2)}) collective-permute-start(f32[8,1,128]{2,1,0:T(1,128)S(1)} %get-tuple-element.61), channel_id=1, source_target_pairs={{1,0},{2,1},{3,2},{4,3},{5,4},{6,5},{7,6},{9,8},{10,9},{11,10},{12... | collective-permute-start | bytes 12296 | tf_op jit(solution)/shard_map/ppermute | solution.py:22
  134.0 2.5 %collective-permute-done.26 = f32[8,1,128]{2,1,0:T(1,128)S(1)} collective-permute-done((f32[8,1,128]{2,1,0:T(1,128)S(1)}, f32[8,1,128]{2,1,0:T(1,128)S(1)}, u32[]{:S(2)}, u32[]{:S(2)}) %collective-permute-start.26) | collective-permute-done | bytes 4128 | tf_op jit(solution)/shard_map/ppermute | solution.py:22
  137.0 1.9 collective-permute-start.27
  139.0 2.4 %collective-permute-start.28 = (f32[8,1,128]{2,1,0:T(1,128)S(1)}, f32[8,1,128]{2,1,0:T(1,128)S(1)}, u32[]{:S(2)}, u32[]{:S(2)}) collective-permute-start(f32[8,1,128]{2,1,0:T(1,128)S(1)} %get-tuple-element.59), channel_id=1, source_target_pairs={{1,0},{2,1},{3,2},{4,3},{5,4},{6,5},{7,6},{9,8},{10,9},{11,10},{12... | collective-permute-start | bytes 12296 | tf_op jit(solution)/shard_map/ppermute | solution.py:22
  141.4 2.5 %collective-permute-done.28 = f32[8,1,128]{2,1,0:T(1,128)S(1)} collective-permute-done((f32[8,1,128]{2,1,0:T(1,128)S(1)}, f32[8,1,128]{2,1,0:T(1,128)S(1)}, u32[]{:S(2)}, u32[]{:S(2)}) %collective-permute-start.28) | collective-permute-done | bytes 4128 | tf_op jit(solution)/shard_map/ppermute | solution.py:22
  144.5 3.2 %collective-permute-start.29 = (f32[2,16,128]{2,1,0:T(8,128)S(1)}, f32[2,16,128]{2,1,0:T(8,128)S(1)}, u32[]{:S(2)}, u32[]{:S(2)}) collective-permute-start(f32[2,16,128]{2,1,0:T(8,128)S(1)} %get-tuple-element.57), channel_id=1, source_target_pairs={{0,24},{8,32},{16,40},{24,48},{32,56},{40,64},{48,72},{56,80},{64,... | collective-permute-start | bytes 49160 | tf_op jit(solution)/shard_map/ppermute | solution.py:30
  147.7 4.0 %collective-permute-start.30 = (f32[2,16,128]{2,1,0:T(8,128)S(1)}, f32[2,16,128]{2,1,0:T(8,128)S(1)}, u32[]{:S(2)}, u32[]{:S(2)}) collective-permute-start(f32[2,16,128]{2,1,0:T(8,128)S(1)} %get-tuple-element.56), channel_id=1, source_target_pairs={{0,16},{8,24},{16,32},{24,40},{32,48},{40,56},{48,64},{56,72},{64,... | collective-permute-start | bytes 49160 | tf_op jit(solution)/shard_map/ppermute | solution.py:30
  151.7 2.6 %collective-permute-start.31 = (f32[2,16,128]{2,1,0:T(8,128)S(1)}, f32[2,16,128]{2,1,0:T(8,128)S(1)}, u32[]{:S(2)}, u32[]{:S(2)}) collective-permute-start(f32[2,16,128]{2,1,0:T(8,128)S(1)} %get-tuple-element.55), channel_id=1, source_target_pairs={{0,8},{8,16},{16,24},{24,32},{32,40},{40,48},{48,56},{56,64},{64,7... | collective-permute-start | bytes 49160 | tf_op jit(solution)/shard_map/ppermute | solution.py:30
  155.0 2.1 collective-permute-done.30
  157.0 1.2 collective-permute-done.31
  158.3 3.9 %broadcast_in_dim.54 = f32[2,2,16,2,128,2]{5,4,3,2,1,0:T(8,128)} broadcast(f32[2,16,128]{2,1,0:T(8,128)S(1)} %fusion.280), dimensions={0,2,4} | broadcast | bytes 147456 | tf_op jit(solution)/shard_map/broadcast_in_dim | solution.py:120
  162.2 6.9 %reshape.40 = f32[4,32,256]{2,1,0:T(8,128)S(1)} reshape(f32[2,2,16,2,128,2]{5,4,3,2,1,0:T(8,128)} %broadcast_in_dim.54) | data formatting | bytes 262144 | tf_op jit(solution)/shard_map/reshape | solution.py:122
  169.2 1.9 collective-permute-start.32
  171.1 5.5 %collective-permute-start.33 = (f32[1,32,256]{2,1,0:T(8,128)S(1)}, f32[1,32,256]{2,1,0:T(8,128)S(1)}, u32[]{:S(2)}, u32[]{:S(2)}) collective-permute-start(f32[1,32,256]{2,1,0:T(8,128)S(1)} %get-tuple-element.48), channel_id=1, source_target_pairs={{8,0},{16,8},{24,16},{32,24},{40,32},{48,40},{56,48},{64,56},{72,6... | collective-permute-start | bytes 98312 | tf_op jit(solution)/shard_map/ppermute | solution.py:22
  177.6 4.5 %collective-permute-start.34 = (f32[6,1,256]{2,1,0:T(1,128)S(1)}, f32[6,1,256]{2,1,0:T(1,128)S(1)}, u32[]{:S(2)}, u32[]{:S(2)}) collective-permute-start(f32[6,1,256]{2,1,0:T(1,128)S(1)} %get-tuple-element.31), channel_id=1, source_target_pairs={{0,1},{1,2},{2,3},{3,4},{4,5},{5,6},{6,7},{8,9},{9,10},{10,11},{11... | collective-permute-start | bytes 18440 | tf_op jit(solution)/shard_map/ppermute | solution.py:19
  182.1 1.9 collective-permute-start.35
  184.1 3.0 %collective-permute-done.35 = f32[6,1,256]{2,1,0:T(1,128)S(1)} collective-permute-done((f32[6,1,256]{2,1,0:T(1,128)S(1)}, f32[6,1,256]{2,1,0:T(1,128)S(1)}, u32[]{:S(2)}, u32[]{:S(2)}) %collective-permute-start.35) | collective-permute-done | bytes 6176 | tf_op jit(solution)/shard_map/ppermute | solution.py:22
  187.8 1.9 collective-permute-start.36
  189.7 6.1 %collective-permute-start.37 = (f32[1,32,256]{2,1,0:T(8,128)S(1)}, f32[1,32,256]{2,1,0:T(8,128)S(1)}, u32[]{:S(2)}, u32[]{:S(2)}) collective-permute-start(f32[1,32,256]{2,1,0:T(8,128)S(1)} %get-tuple-element.46), channel_id=1, source_target_pairs={{8,0},{16,8},{24,16},{32,24},{40,32},{48,40},{56,48},{64,56},{72,6... | collective-permute-start | bytes 98312 | tf_op jit(solution)/shard_map/ppermute | solution.py:22
  196.8 3.0 %collective-permute-start.38 = (f32[6,1,256]{2,1,0:T(1,128)S(1)}, f32[6,1,256]{2,1,0:T(1,128)S(1)}, u32[]{:S(2)}, u32[]{:S(2)}) collective-permute-start(f32[6,1,256]{2,1,0:T(1,128)S(1)} %get-tuple-element.27), channel_id=1, source_target_pairs={{0,1},{1,2},{2,3},{3,4},{4,5},{5,6},{6,7},{8,9},{9,10},{10,11},{11... | collective-permute-start | bytes 18440 | tf_op jit(solution)/shard_map/ppermute | solution.py:19
  199.8 1.9 collective-permute-start.39
  201.7 3.0 %collective-permute-done.39 = f32[6,1,256]{2,1,0:T(1,128)S(1)} collective-permute-done((f32[6,1,256]{2,1,0:T(1,128)S(1)}, f32[6,1,256]{2,1,0:T(1,128)S(1)}, u32[]{:S(2)}, u32[]{:S(2)}) %collective-permute-start.39) | collective-permute-done | bytes 6176 | tf_op jit(solution)/shard_map/ppermute | solution.py:22
  204.9 1.1 fusion.11
  (85 shorter events, 9.6 us)
Async XLA Ops:
  0.0 76.2 %copy-start = (f32[4,32,256]{2,1,0:T(8,128)S(1)}, f32[4,32,256]{2,1,0:T(8,128)}, u32[]{:S(2)}) copy-start(f32[4,32,256]{2,1,0:T(8,128)} %param.7) | copy-start | bytes 393220
  0.0 76.3 %copy-start.1 = (f32[4,32,256]{2,1,0:T(8,128)S(1)}, f32[4,32,256]{2,1,0:T(8,128)}, u32[]{:S(2)}) copy-start(f32[4,32,256]{2,1,0:T(8,128)} %param.6) | copy-start | bytes 393220
  0.0 73.0 %copy-start.2 = (f32[2,16,128]{2,1,0:T(8,128)S(1)}, f32[2,16,128]{2,1,0:T(8,128)}, u32[]{:S(2)}) copy-start(f32[2,16,128]{2,1,0:T(8,128)} %param.10) | copy-start | bytes 49156
  1.0 24.3 %collective-permute-start = (f32[1,32,256]{2,1,0:T(8,128)S(1)}, f32[1,32,256]{2,1,0:T(8,128)S(1)}, u32[]{:S(2)}, u32[]{:S(2)}) collective-permute-start(f32[1,32,256]{2,1,0:T(8,128)S(1)} %get-tuple-element.53), channel_id=1, source_target_pairs={{0,8},{8,16},{16,24},{24,32},{32,40},{40,48},{48,56},{56,64},{64,7... | collective-permute-start | bytes 98312 | tf_op jit(solution)/shard_map/ppermute | solution.py:19
  4.6 20.8 %collective-permute-start.1 = (f32[1,32,256]{2,1,0:T(8,128)S(1)}, f32[1,32,256]{2,1,0:T(8,128)S(1)}, u32[]{:S(2)}, u32[]{:S(2)}) collective-permute-start(f32[1,32,256]{2,1,0:T(8,128)S(1)} %get-tuple-element.54), channel_id=1, source_target_pairs={{8,0},{16,8},{24,16},{32,24},{40,32},{48,40},{56,48},{64,56},{72,6... | collective-permute-start | bytes 98312 | tf_op jit(solution)/shard_map/ppermute | solution.py:22
  15.1 29.0 %collective-permute-start.12 = (f32[1,16,128]{2,1,0:T(8,128)S(1)}, f32[1,16,128]{2,1,0:T(8,128)S(1)}, u32[]{:S(2)}, u32[]{:S(2)}) collective-permute-start(f32[1,16,128]{2,1,0:T(8,128)S(1)} %get-tuple-element.74), channel_id=1, source_target_pairs={{0,8},{8,16},{16,24},{24,32},{32,40},{40,48},{48,56},{56,64},{64,7... | collective-permute-start | bytes 24584 | tf_op jit(solution)/shard_map/ppermute | solution.py:19
  17.0 27.1 %collective-permute-start.13 = (f32[1,16,128]{2,1,0:T(8,128)S(1)}, f32[1,16,128]{2,1,0:T(8,128)S(1)}, u32[]{:S(2)}, u32[]{:S(2)}) collective-permute-start(f32[1,16,128]{2,1,0:T(8,128)S(1)} %get-tuple-element.75), channel_id=1, source_target_pairs={{8,0},{16,8},{24,16},{32,24},{40,32},{48,40},{56,48},{64,56},{72,6... | collective-permute-start | bytes 24584 | tf_op jit(solution)/shard_map/ppermute | solution.py:22
  25.4 8.4 %collective-permute-start.2 = (f32[6,1,256]{2,1,0:T(1,128)S(1)}, f32[6,1,256]{2,1,0:T(1,128)S(1)}, u32[]{:S(2)}, u32[]{:S(2)}) collective-permute-start(f32[6,1,256]{2,1,0:T(1,128)S(1)} %get-tuple-element.43), channel_id=1, source_target_pairs={{0,1},{1,2},{2,3},{3,4},{4,5},{5,6},{6,7},{8,9},{9,10},{10,11},{11... | collective-permute-start | bytes 18440 | tf_op jit(solution)/shard_map/ppermute | solution.py:19
  30.0 4.9 %collective-permute-start.3 = (f32[6,1,256]{2,1,0:T(1,128)S(1)}, f32[6,1,256]{2,1,0:T(1,128)S(1)}, u32[]{:S(2)}, u32[]{:S(2)}) collective-permute-start(f32[6,1,256]{2,1,0:T(1,128)S(1)} %get-tuple-element.44), channel_id=1, source_target_pairs={{1,0},{2,1},{3,2},{4,3},{5,4},{6,5},{7,6},{9,8},{10,9},{11,10},{12... | collective-permute-start | bytes 18440 | tf_op jit(solution)/shard_map/ppermute | solution.py:22
  36.7 12.4 %collective-permute-start.4 = (f32[1,32,256]{2,1,0:T(8,128)S(1)}, f32[1,32,256]{2,1,0:T(8,128)S(1)}, u32[]{:S(2)}, u32[]{:S(2)}) collective-permute-start(f32[1,32,256]{2,1,0:T(8,128)S(1)} %get-tuple-element.51), channel_id=1, source_target_pairs={{0,8},{8,16},{16,24},{24,32},{32,40},{40,48},{48,56},{56,64},{64,7... | collective-permute-start | bytes 98312 | tf_op jit(solution)/shard_map/ppermute | solution.py:19
  38.6 10.5 %collective-permute-start.5 = (f32[1,32,256]{2,1,0:T(8,128)S(1)}, f32[1,32,256]{2,1,0:T(8,128)S(1)}, u32[]{:S(2)}, u32[]{:S(2)}) collective-permute-start(f32[1,32,256]{2,1,0:T(8,128)S(1)} %get-tuple-element.52), channel_id=1, source_target_pairs={{8,0},{16,8},{24,16},{32,24},{40,32},{48,40},{56,48},{64,56},{72,6... | collective-permute-start | bytes 98312 | tf_op jit(solution)/shard_map/ppermute | solution.py:22
  44.1 10.6 %collective-permute-start.14 = (f32[4,1,128]{2,1,0:T(1,128)S(1)}, f32[4,1,128]{2,1,0:T(1,128)S(1)}, u32[]{:S(2)}, u32[]{:S(2)}) collective-permute-start(f32[4,1,128]{2,1,0:T(1,128)S(1)} %get-tuple-element.70), channel_id=1, source_target_pairs={{0,1},{1,2},{2,3},{3,4},{4,5},{5,6},{6,7},{8,9},{9,10},{10,11},{11... | collective-permute-start | bytes 6152 | tf_op jit(solution)/shard_map/ppermute | solution.py:19
  47.2 7.6 %collective-permute-start.15 = (f32[4,1,128]{2,1,0:T(1,128)S(1)}, f32[4,1,128]{2,1,0:T(1,128)S(1)}, u32[]{:S(2)}, u32[]{:S(2)}) collective-permute-start(f32[4,1,128]{2,1,0:T(1,128)S(1)} %get-tuple-element.71), channel_id=1, source_target_pairs={{1,0},{2,1},{3,2},{4,3},{5,4},{6,5},{7,6},{9,8},{10,9},{11,10},{12... | collective-permute-start | bytes 6152 | tf_op jit(solution)/shard_map/ppermute | solution.py:22
  49.2 5.6 %collective-permute-start.6 = (f32[6,1,256]{2,1,0:T(1,128)S(1)}, f32[6,1,256]{2,1,0:T(1,128)S(1)}, u32[]{:S(2)}, u32[]{:S(2)}) collective-permute-start(f32[6,1,256]{2,1,0:T(1,128)S(1)} %get-tuple-element.39), channel_id=1, source_target_pairs={{0,1},{1,2},{2,3},{3,4},{4,5},{5,6},{6,7},{8,9},{9,10},{10,11},{11... | collective-permute-start | bytes 18440 | tf_op jit(solution)/shard_map/ppermute | solution.py:19
  52.8 4.9 %collective-permute-start.7 = (f32[6,1,256]{2,1,0:T(1,128)S(1)}, f32[6,1,256]{2,1,0:T(1,128)S(1)}, u32[]{:S(2)}, u32[]{:S(2)}) collective-permute-start(f32[6,1,256]{2,1,0:T(1,128)S(1)} %get-tuple-element.40), channel_id=1, source_target_pairs={{1,0},{2,1},{3,2},{4,3},{5,4},{6,5},{7,6},{9,8},{10,9},{11,10},{12... | collective-permute-start | bytes 18440 | tf_op jit(solution)/shard_map/ppermute | solution.py:22
  59.5 7.5 %collective-permute-start.8 = (f32[1,32,256]{2,1,0:T(8,128)S(1)}, f32[1,32,256]{2,1,0:T(8,128)S(1)}, u32[]{:S(2)}, u32[]{:S(2)}) collective-permute-start(f32[1,32,256]{2,1,0:T(8,128)S(1)} %get-tuple-element.49), channel_id=1, source_target_pairs={{0,8},{8,16},{16,24},{24,32},{32,40},{40,48},{48,56},{56,64},{64,7... | collective-permute-start | bytes 98312 | tf_op jit(solution)/shard_map/ppermute | solution.py:19
  61.4 6.5 %collective-permute-start.9 = (f32[1,32,256]{2,1,0:T(8,128)S(1)}, f32[1,32,256]{2,1,0:T(8,128)S(1)}, u32[]{:S(2)}, u32[]{:S(2)}) collective-permute-start(f32[1,32,256]{2,1,0:T(8,128)S(1)} %get-tuple-element.50), channel_id=1, source_target_pairs={{8,0},{16,8},{24,16},{32,24},{40,32},{48,40},{56,48},{64,56},{72,6... | collective-permute-start | bytes 98312 | tf_op jit(solution)/shard_map/ppermute | solution.py:22
  67.9 5.2 %collective-permute-start.10 = (f32[6,1,256]{2,1,0:T(1,128)S(1)}, f32[6,1,256]{2,1,0:T(1,128)S(1)}, u32[]{:S(2)}, u32[]{:S(2)}) collective-permute-start(f32[6,1,256]{2,1,0:T(1,128)S(1)} %get-tuple-element.35), channel_id=1, source_target_pairs={{0,1},{1,2},{2,3},{3,4},{4,5},{5,6},{6,7},{8,9},{9,10},{10,11},{11... | collective-permute-start | bytes 18440 | tf_op jit(solution)/shard_map/ppermute | solution.py:19
  71.0 4.9 %collective-permute-start.11 = (f32[6,1,256]{2,1,0:T(1,128)S(1)}, f32[6,1,256]{2,1,0:T(1,128)S(1)}, u32[]{:S(2)}, u32[]{:S(2)}) collective-permute-start(f32[6,1,256]{2,1,0:T(1,128)S(1)} %get-tuple-element.36), channel_id=1, source_target_pairs={{1,0},{2,1},{3,2},{4,3},{5,4},{6,5},{7,6},{9,8},{10,9},{11,10},{12... | collective-permute-start | bytes 18440 | tf_op jit(solution)/shard_map/ppermute | solution.py:22
  90.5 10.8 %collective-permute-start.16 = (f32[3,2,16,128]{3,2,1,0:T(8,128)S(1)}, f32[3,2,16,128]{3,2,1,0:T(8,128)S(1)}, u32[]{:S(2)}, u32[]{:S(2)}) collective-permute-start(f32[3,2,16,128]{3,2,1,0:T(8,128)S(1)} %pad_maximum_fusion.27), channel_id=1, source_target_pairs={{8,0},{16,8},{24,16},{32,24},{40,32},{48,40},{56,48},{64,56},{72,6... | collective-permute-start | bytes 147464 | tf_op jit(solution)/shard_map/ppermute | solution.py:30
  96.7 5.7 %collective-permute-start.17 = (f32[3,2,16,128]{3,2,1,0:T(8,128)S(1)}, f32[3,2,16,128]{3,2,1,0:T(8,128)S(1)}, u32[]{:S(2)}, u32[]{:S(2)}) collective-permute-start(f32[3,2,16,128]{3,2,1,0:T(8,128)S(1)} %pad_maximum_fusion.27), channel_id=1, source_target_pairs={{16,0},{24,8},{32,16},{40,24},{48,32},{56,40},{64,48},{72,56},{80,... | collective-permute-start | bytes 147464 | tf_op jit(solution)/shard_map/ppermute | solution.py:30
  98.6 6.6 %collective-permute-start.18 = (f32[3,2,16,128]{3,2,1,0:T(8,128)S(1)}, f32[3,2,16,128]{3,2,1,0:T(8,128)S(1)}, u32[]{:S(2)}, u32[]{:S(2)}) collective-permute-start(f32[3,2,16,128]{3,2,1,0:T(8,128)S(1)} %pad_maximum_fusion.27), channel_id=1, source_target_pairs={{24,0},{32,8},{40,16},{48,24},{56,32},{64,40},{72,48},{80,56},{88,... | collective-permute-start | bytes 147464 | tf_op jit(solution)/shard_map/ppermute | solution.py:30
  105.4 5.9 %collective-permute-start.19 = (f32[8,1,128]{2,1,0:T(1,128)S(1)}, f32[8,1,128]{2,1,0:T(1,128)S(1)}, u32[]{:S(2)}, u32[]{:S(2)}) collective-permute-start(f32[8,1,128]{2,1,0:T(1,128)S(1)} %get-tuple-element.66), channel_id=1, source_target_pairs={{0,1},{1,2},{2,3},{3,4},{4,5},{5,6},{6,7},{8,9},{9,10},{10,11},{11... | collective-permute-start | bytes 12296 | tf_op jit(solution)/shard_map/ppermute | solution.py:19
  109.4 4.9 %collective-permute-start.20 = (f32[8,1,128]{2,1,0:T(1,128)S(1)}, f32[8,1,128]{2,1,0:T(1,128)S(1)}, u32[]{:S(2)}, u32[]{:S(2)}) collective-permute-start(f32[8,1,128]{2,1,0:T(1,128)S(1)} %get-tuple-element.67), channel_id=1, source_target_pairs={{1,0},{2,1},{3,2},{4,3},{5,4},{6,5},{7,6},{9,8},{10,9},{11,10},{12... | collective-permute-start | bytes 12296 | tf_op jit(solution)/shard_map/ppermute | solution.py:22
  114.8 4.3 %collective-permute-start.21 = (f32[8,1,128]{2,1,0:T(1,128)S(1)}, f32[8,1,128]{2,1,0:T(1,128)S(1)}, u32[]{:S(2)}, u32[]{:S(2)}) collective-permute-start(f32[8,1,128]{2,1,0:T(1,128)S(1)} %get-tuple-element.64), channel_id=1, source_target_pairs={{0,1},{1,2},{2,3},{3,4},{4,5},{5,6},{6,7},{8,9},{9,10},{10,11},{11... | collective-permute-start | bytes 12296 | tf_op jit(solution)/shard_map/ppermute | solution.py:19
  116.8 4.9 %collective-permute-start.22 = (f32[8,1,128]{2,1,0:T(1,128)S(1)}, f32[8,1,128]{2,1,0:T(1,128)S(1)}, u32[]{:S(2)}, u32[]{:S(2)}) collective-permute-start(f32[8,1,128]{2,1,0:T(1,128)S(1)} %get-tuple-element.65), channel_id=1, source_target_pairs={{1,0},{2,1},{3,2},{4,3},{5,4},{6,5},{7,6},{9,8},{10,9},{11,10},{12... | collective-permute-start | bytes 12296 | tf_op jit(solution)/shard_map/ppermute | solution.py:22
  122.2 4.3 %collective-permute-start.23 = (f32[8,1,128]{2,1,0:T(1,128)S(1)}, f32[8,1,128]{2,1,0:T(1,128)S(1)}, u32[]{:S(2)}, u32[]{:S(2)}) collective-permute-start(f32[8,1,128]{2,1,0:T(1,128)S(1)} %get-tuple-element.62), channel_id=1, source_target_pairs={{0,1},{1,2},{2,3},{3,4},{4,5},{5,6},{6,7},{8,9},{9,10},{10,11},{11... | collective-permute-start | bytes 12296 | tf_op jit(solution)/shard_map/ppermute | solution.py:19
  124.2 4.9 %collective-permute-start.24 = (f32[8,1,128]{2,1,0:T(1,128)S(1)}, f32[8,1,128]{2,1,0:T(1,128)S(1)}, u32[]{:S(2)}, u32[]{:S(2)}) collective-permute-start(f32[8,1,128]{2,1,0:T(1,128)S(1)} %get-tuple-element.63), channel_id=1, source_target_pairs={{1,0},{2,1},{3,2},{4,3},{5,4},{6,5},{7,6},{9,8},{10,9},{11,10},{12... | collective-permute-start | bytes 12296 | tf_op jit(solution)/shard_map/ppermute | solution.py:22
  129.6 4.3 %collective-permute-start.25 = (f32[8,1,128]{2,1,0:T(1,128)S(1)}, f32[8,1,128]{2,1,0:T(1,128)S(1)}, u32[]{:S(2)}, u32[]{:S(2)}) collective-permute-start(f32[8,1,128]{2,1,0:T(1,128)S(1)} %get-tuple-element.60), channel_id=1, source_target_pairs={{0,1},{1,2},{2,3},{3,4},{4,5},{5,6},{6,7},{8,9},{9,10},{10,11},{11... | collective-permute-start | bytes 12296 | tf_op jit(solution)/shard_map/ppermute | solution.py:19
  131.6 4.9 %collective-permute-start.26 = (f32[8,1,128]{2,1,0:T(1,128)S(1)}, f32[8,1,128]{2,1,0:T(1,128)S(1)}, u32[]{:S(2)}, u32[]{:S(2)}) collective-permute-start(f32[8,1,128]{2,1,0:T(1,128)S(1)} %get-tuple-element.61), channel_id=1, source_target_pairs={{1,0},{2,1},{3,2},{4,3},{5,4},{6,5},{7,6},{9,8},{10,9},{11,10},{12... | collective-permute-start | bytes 12296 | tf_op jit(solution)/shard_map/ppermute | solution.py:22
  137.0 4.3 %collective-permute-start.27 = (f32[8,1,128]{2,1,0:T(1,128)S(1)}, f32[8,1,128]{2,1,0:T(1,128)S(1)}, u32[]{:S(2)}, u32[]{:S(2)}) collective-permute-start(f32[8,1,128]{2,1,0:T(1,128)S(1)} %get-tuple-element.58), channel_id=1, source_target_pairs={{0,1},{1,2},{2,3},{3,4},{4,5},{5,6},{6,7},{8,9},{9,10},{10,11},{11... | collective-permute-start | bytes 12296 | tf_op jit(solution)/shard_map/ppermute | solution.py:19
  139.0 4.9 %collective-permute-start.28 = (f32[8,1,128]{2,1,0:T(1,128)S(1)}, f32[8,1,128]{2,1,0:T(1,128)S(1)}, u32[]{:S(2)}, u32[]{:S(2)}) collective-permute-start(f32[8,1,128]{2,1,0:T(1,128)S(1)} %get-tuple-element.59), channel_id=1, source_target_pairs={{1,0},{2,1},{3,2},{4,3},{5,4},{6,5},{7,6},{9,8},{10,9},{11,10},{12... | collective-permute-start | bytes 12296 | tf_op jit(solution)/shard_map/ppermute | solution.py:22
  144.5 10.5 %collective-permute-start.29 = (f32[2,16,128]{2,1,0:T(8,128)S(1)}, f32[2,16,128]{2,1,0:T(8,128)S(1)}, u32[]{:S(2)}, u32[]{:S(2)}) collective-permute-start(f32[2,16,128]{2,1,0:T(8,128)S(1)} %get-tuple-element.57), channel_id=1, source_target_pairs={{0,24},{8,32},{16,40},{24,48},{32,56},{40,64},{48,72},{56,80},{64,... | collective-permute-start | bytes 49160 | tf_op jit(solution)/shard_map/ppermute | solution.py:30
  147.7 9.3 %collective-permute-start.30 = (f32[2,16,128]{2,1,0:T(8,128)S(1)}, f32[2,16,128]{2,1,0:T(8,128)S(1)}, u32[]{:S(2)}, u32[]{:S(2)}) collective-permute-start(f32[2,16,128]{2,1,0:T(8,128)S(1)} %get-tuple-element.56), channel_id=1, source_target_pairs={{0,16},{8,24},{16,32},{24,40},{32,48},{40,56},{48,64},{56,72},{64,... | collective-permute-start | bytes 49160 | tf_op jit(solution)/shard_map/ppermute | solution.py:30
  151.7 6.6 %collective-permute-start.31 = (f32[2,16,128]{2,1,0:T(8,128)S(1)}, f32[2,16,128]{2,1,0:T(8,128)S(1)}, u32[]{:S(2)}, u32[]{:S(2)}) collective-permute-start(f32[2,16,128]{2,1,0:T(8,128)S(1)} %get-tuple-element.55), channel_id=1, source_target_pairs={{0,8},{8,16},{16,24},{24,32},{32,40},{40,48},{48,56},{56,64},{64,7... | collective-permute-start | bytes 49160 | tf_op jit(solution)/shard_map/ppermute | solution.py:30
  169.2 7.4 %collective-permute-start.32 = (f32[1,32,256]{2,1,0:T(8,128)S(1)}, f32[1,32,256]{2,1,0:T(8,128)S(1)}, u32[]{:S(2)}, u32[]{:S(2)}) collective-permute-start(f32[1,32,256]{2,1,0:T(8,128)S(1)} %get-tuple-element.47), channel_id=1, source_target_pairs={{0,8},{8,16},{16,24},{24,32},{32,40},{40,48},{48,56},{56,64},{64,7... | collective-permute-start | bytes 98312 | tf_op jit(solution)/shard_map/ppermute | solution.py:19
  171.1 6.5 %collective-permute-start.33 = (f32[1,32,256]{2,1,0:T(8,128)S(1)}, f32[1,32,256]{2,1,0:T(8,128)S(1)}, u32[]{:S(2)}, u32[]{:S(2)}) collective-permute-start(f32[1,32,256]{2,1,0:T(8,128)S(1)} %get-tuple-element.48), channel_id=1, source_target_pairs={{8,0},{16,8},{24,16},{32,24},{40,32},{48,40},{56,48},{64,56},{72,6... | collective-permute-start | bytes 98312 | tf_op jit(solution)/shard_map/ppermute | solution.py:22
  177.6 6.5 %collective-permute-start.34 = (f32[6,1,256]{2,1,0:T(1,128)S(1)}, f32[6,1,256]{2,1,0:T(1,128)S(1)}, u32[]{:S(2)}, u32[]{:S(2)}) collective-permute-start(f32[6,1,256]{2,1,0:T(1,128)S(1)} %get-tuple-element.31), channel_id=1, source_target_pairs={{0,1},{1,2},{2,3},{3,4},{4,5},{5,6},{6,7},{8,9},{9,10},{10,11},{11... | collective-permute-start | bytes 18440 | tf_op jit(solution)/shard_map/ppermute | solution.py:19
  182.1 4.9 %collective-permute-start.35 = (f32[6,1,256]{2,1,0:T(1,128)S(1)}, f32[6,1,256]{2,1,0:T(1,128)S(1)}, u32[]{:S(2)}, u32[]{:S(2)}) collective-permute-start(f32[6,1,256]{2,1,0:T(1,128)S(1)} %get-tuple-element.32), channel_id=1, source_target_pairs={{1,0},{2,1},{3,2},{4,3},{5,4},{6,5},{7,6},{9,8},{10,9},{11,10},{12... | collective-permute-start | bytes 18440 | tf_op jit(solution)/shard_map/ppermute | solution.py:22
  187.8 8.0 %collective-permute-start.36 = (f32[1,32,256]{2,1,0:T(8,128)S(1)}, f32[1,32,256]{2,1,0:T(8,128)S(1)}, u32[]{:S(2)}, u32[]{:S(2)}) collective-permute-start(f32[1,32,256]{2,1,0:T(8,128)S(1)} %get-tuple-element.45), channel_id=1, source_target_pairs={{0,8},{8,16},{16,24},{24,32},{32,40},{40,48},{48,56},{56,64},{64,7... | collective-permute-start | bytes 98312 | tf_op jit(solution)/shard_map/ppermute | solution.py:19
  189.7 7.1 %collective-permute-start.37 = (f32[1,32,256]{2,1,0:T(8,128)S(1)}, f32[1,32,256]{2,1,0:T(8,128)S(1)}, u32[]{:S(2)}, u32[]{:S(2)}) collective-permute-start(f32[1,32,256]{2,1,0:T(8,128)S(1)} %get-tuple-element.46), channel_id=1, source_target_pairs={{8,0},{16,8},{24,16},{32,24},{40,32},{48,40},{56,48},{64,56},{72,6... | collective-permute-start | bytes 98312 | tf_op jit(solution)/shard_map/ppermute | solution.py:22
  196.8 4.9 %collective-permute-start.38 = (f32[6,1,256]{2,1,0:T(1,128)S(1)}, f32[6,1,256]{2,1,0:T(1,128)S(1)}, u32[]{:S(2)}, u32[]{:S(2)}) collective-permute-start(f32[6,1,256]{2,1,0:T(1,128)S(1)} %get-tuple-element.27), channel_id=1, source_target_pairs={{0,1},{1,2},{2,3},{3,4},{4,5},{5,6},{6,7},{8,9},{9,10},{10,11},{11... | collective-permute-start | bytes 18440 | tf_op jit(solution)/shard_map/ppermute | solution.py:19
  199.8 4.9 %collective-permute-start.39 = (f32[6,1,256]{2,1,0:T(1,128)S(1)}, f32[6,1,256]{2,1,0:T(1,128)S(1)}, u32[]{:S(2)}, u32[]{:S(2)}) collective-permute-start(f32[6,1,256]{2,1,0:T(1,128)S(1)} %get-tuple-element.28), channel_id=1, source_target_pairs={{1,0},{2,1},{3,2},{4,3},{5,4},{6,5},{7,6},{9,8},{10,9},{11,10},{12... | collective-permute-start | bytes 18440 | tf_op jit(solution)/shard_map/ppermute | solution.py:22
where the time goes:
time: 207 us; the launch traced here: 206 us
  starting transfers between devices  128 us (62%)
  waiting for transfers between devices  36.4 us (18%)
  local copies, waits for them, and re-layouts  23.2 us (11%)
  other arithmetic  15.7 us (8%)
  between operations  2.75 us (1%)
    ppermute x17, starting transfers between devices, with_halo(): lax.ppermute(lax.slice_in_dim(block, 0, width, axis=dim), axis, backward)  60.7 us
    ppermute x17, starting transfers between devices, with_halo(): lax.ppermute(lax.slice_in_dim(block, block.shape[dim] - width, None, axis...  46.8 us
    ppermute x17, waiting for transfers between devices, with_halo(): lax.ppermute(lax.slice_in_dim(block, 0, width, axis=dim), axis, backward)  29 us
    ppermute x6, starting transfers between devices, shifted(): return lax.ppermute(x, axis, pairs)  20.5 us
    reshape x1, local copies, waits for them, and re-layouts, on_device(): residual.reshape(half_depth, 2, half_rows, 2, half_cols, 2)  9.76 us
    ppermute x6, waiting for transfers between devices, shifted(): return lax.ppermute(x, axis, pairs)  7.32 us
    reshape x1, local copies, waits for them, and re-layouts, on_device(): prolonged = jnp.broadcast_to(correction[:, None, :, None, :, None], (half...  6.93 us
    mul x9, other arithmetic, operate(): trans * pressure  4.83 us
  transfers between devices with their start and end apart: 40, of which 17 were waited for; matrix products, arithmetic and copies ran while one was open for 3% of the time, Pallas kernels for 0%

commit v1 on v0

v1 whole, which is shorter than its diff:
```python
import jax
import jax.numpy as jnp
from jax import lax
from jax.experimental import pallas as pl
from jax.experimental.pallas import tpu as pltpu
from jax.sharding import PartitionSpec as P

OMEGA = 0.7
KEEP = 1.0 - OMEGA
COARSE_SWEEPS = 6

FR = 40
ROWS = 32
COLS = 256
CR = 32
CROWS = 16
CCOLS = 128


def shifted(x, axis, by):
    devices = lax.axis_size(axis)
    pairs = [(i, i + by) for i in range(devices) if 0 <= i + by < devices]
    return lax.ppermute(x, axis, pairs)


def rotated(x, axis, by):
    devices = lax.axis_size(axis)
    return lax.ppermute(x, axis, [(i, (i + by) % devices) for i in range(devices)])


def smooth_xy(v):
    rows, cols = v.shape
    col = lax.broadcasted_iota(jnp.int32, v.shape, 1)
    left = jnp.where(col == 0, 0.0, pltpu.roll(v, 1, 1))
    right = jnp.where(col == cols - 1, 0.0, pltpu.roll(v, cols - 1, 1))
    h = v + 0.5 * (left + right)
    return h + 0.5 * (pltpu.roll(h, 1, 0) + pltpu.roll(h, rows - 1, 0))


def to_wide(x):
    return jnp.concatenate([x[0:8], x[8:16]], axis=1)


def from_wide(x):
    return jnp.concatenate([x[:, 0:CCOLS], x[:, CCOLS:COLS]], axis=0)


Z1_RHS = 96
Z1_ACC = 160
Z1_CO = 224
Z1_ROWS = 232


def pack_z1(rhs, perm, acc, cperm, up, down):
    for out, first3, first2, coarse in ((up, 1, 2, 1), (down, 0, 0, 0)):
        for k in range(3):
            out[32 * k : 32 * k + 32, :] = perm[first3 + k]
        for k in range(2):
            out[Z1_RHS + 32 * k : Z1_RHS + 32 * k + 32, :] = rhs[first2 + k]
            out[Z1_ACC + 32 * k : Z1_ACC + 32 * k + 32, :] = acc[first2 + k]
        out[Z1_CO : Z1_CO + 8, :] = to_wide(cperm[coarse])


def fine_rows(own, lo, hi, base, depth, z, first, count):
    if z < 0:
        at = base + 32 * (z + depth)
        return lo[at + first : at + first + count, :]
    if z > 3:
        at = base + 32 * (z - 4)
        return hi[at + first : at + first + count, :]
    return own[z, first : first + count, :]


def coarse_plane(cperm, lo, hi, c):
    if c < 0:
        return from_wide(lo[Z1_CO : Z1_CO + 8, :])
    if c > 1:
        return from_wide(hi[Z1_CO : Z1_CO + 8, :])
    return cperm[c]


Y1_RHS = 30
Y1_ACC = 46
Y1_CO = 62
Y1_ROWS = 64


def pack_y1(rhs, perm, acc, cperm, lo, hi, up, down):
    for out, top in ((up, True), (down, False)):
        r3 = ROWS - 3 if top else 0
        r2 = ROWS - 2 if top else 0
        for k in range(10):
            out[3 * k : 3 * k + 3, :] = fine_rows(perm, lo, hi, 0, 3, k - 3, r3, 3)
        for k in range(8):
            at = Y1_RHS + 2 * k
            out[at : at + 2, :] = fine_rows(rhs, lo, hi, Z1_RHS, 2, k - 2, r2, 2)
            at = Y1_ACC + 2 * k
            out[at : at + 2, :] = fine_rows(acc, lo, hi, Z1_ACC, 2, k - 2, r2, 2)
        rc = CROWS - 1 if top else 0
        for k in range(4):
            plane = coarse_plane(cperm, lo, hi, k - 1)
            at = Y1_CO + k // 2
            lane = CCOLS * (k % 2)
            out[at : at + 1, lane : lane + CCOLS] = plane[rc : rc + 1, :]


def pre_kernel(
    masks, rhs, perm, acc, cperm, cacc, lo, hi, ylo, yhi,
    t_out, a_out, b_out, u_out, ct_out, ab_out, zup, zdn,
    ts, rs, cs, xs, us, ds, fs,
):
    mlo = masks[0]
    mhi = masks[1]
    zeros = jnp.zeros((FR, COLS), jnp.float32)
    for k in range(10):
        z = k - 3
        ts[k] = zeros
        ts[k, 4:36, :] = jnp.sqrt(fine_rows(perm, lo, hi, 0, 3, z, 0, ROWS))
        ts[k, 1:4, :] = jnp.sqrt(ylo[3 * k : 3 * k + 3, :] * mlo)
        ts[k, 36:39, :] = jnp.sqrt(yhi[3 * k : 3 * k + 3, :] * mhi)
    for k in range(8):
        z = k - 2
        for ref, own, base, ybase in ((rs, rhs, Z1_RHS, Y1_RHS), (cs, acc, Z1_ACC, Y1_ACC)):
            ref[k] = zeros
            ref[k, 4:36, :] = fine_rows(own, lo, hi, base, 2, z, 0, ROWS)
            ref[k, 2:4, :] = ylo[ybase + 2 * k : ybase + 2 * k + 2, :] * mlo
            ref[k, 36:38, :] = yhi[ybase + 2 * k : ybase + 2 * k + 2, :] * mhi
    for k in range(10):
        xs[k] = smooth_xy(ts[k])
    for k in range(8):
        t = ts[k + 1]
        w = 2.0 * (xs[k + 1] + 0.5 * (xs[k] + xs[k + 2]) - t)
        d = t * w + cs[k]
        d = jnp.where(d > 0.0, d, 1.0)
        q = OMEGA * t / d
        if 2 <= k < 6:
            ds[k - 2] = d
        t_out[k] = t
        rs_k = rs[k]
        us[k] = q * rs_k
        cs[k] = q * t
    for k in range(8):
        xs[k] = smooth_xy(us[k])
    for k in range(6):
        a = us[k + 1]
        b = cs[k + 1]
        w = 2.0 * (xs[k + 1] + 0.5 * (xs[k] + xs[k + 2]) - a)
        a_out[k] = a
        b_out[k] = b
        u_out[k] = (1.0 + KEEP) * a + b * w
    for k in range(6):
        xs[k] = smooth_xy(u_out[k])
    sums = []
    for k in range(4):
        u = u_out[k + 1]
        t = ts[k + 3]
        w = 2.0 * (xs[k + 1] + 0.5 * (xs[k] + xs[k + 2]) - u)
        r = rs[k + 2] + t * w - ds[k] * (u / t)
        sums.append(r)
    pairs = []
    for k in range(2):
        both = sums[2 * k] + sums[2 * k + 1]
        halves = []
        for half in range(2):
            at = 2 * k + half
            fs[at] = both[:, CCOLS * half : CCOLS * half + CCOLS]
            halves.append(fs[at, pl.ds(4, CROWS, 2), :] + fs[at, pl.ds(5, CROWS, 2), :])
        pairs.append(jnp.concatenate(halves, axis=1))
    stacked = jnp.concatenate(pairs, axis=0)
    src = lax.broadcasted_iota(jnp.int32, (COLS, CCOLS), 0)
    dst = lax.broadcasted_iota(jnp.int32, (COLS, CCOLS), 1)
    fold = jnp.where(src // 2 == dst, 1.0, 0.0)
    res = jnp.dot(
        stacked, fold, precision=lax.Precision.HIGHEST, preferred_element_type=jnp.float32
    )
    for k in range(4):
        ct_out[k] = jnp.zeros((CR, CCOLS), jnp.float32)
        ct_out[k, 8:24, :] = jnp.sqrt(coarse_plane(cperm, lo, hi, k - 1))
        at = Y1_CO + k // 2
        lane = CCOLS * (k % 2)
        ct_out[k, 7:8, :] = jnp.sqrt(ylo[at : at + 1, lane : lane + CCOLS] * mlo)
        ct_out[k, 24:25, :] = jnp.sqrt(yhi[at : at + 1, lane : lane + CCOLS] * mhi)
    cx = [smooth_xy(ct_out[k]) for k in range(4)]
    for k in range(2):
        t = ct_out[k + 1]
        w = 2.0 * (cx[k + 1] + 0.5 * (cx[k] + cx[k + 2]) - t)
        t = t[8:24]
        d = t * w[8:24] + cacc[k]
        q = OMEGA * t / d
        a = q * res[CROWS * k : CROWS * k + CROWS]
        b = q * t
        for out in (ab_out, zup, zdn):
            out[k] = a
            out[2 + k] = b
    for out, plane in ((zup, 3), (zdn, 2)):
        for k in range(4):
            row = 4 + 16 * (k // 2)
            lane = CCOLS * (k % 2)
            out[4 + k] = u_out[plane, row : row + 16, lane : lane + CCOLS]


Y2_B = 112
Y2_U = 208
Y2_ROWS = 240


def coarse_a(ab, r3lo, r3hi, r4lo, r4hi, c):
    if c < -4:
        return r4lo.at[c + 10]
    if c < -2:
        return r4lo.at[c + 4]
    if c < 0:
        return r3lo.at[c + 2]
    if c < 2:
        return ab.at[c]
    if c < 4:
        return r3hi.at[c - 2]
    if c < 6:
        return r4hi.at[c - 4]
    return r4hi.at[c - 2]


def coarse_b(ab, r3lo, r3hi, r4lo, r4hi, c):
    if c == -5:
        return r4lo.at[6]
    if c < -2:
        return r4lo.at[c + 6]
    if c < 0:
        return r3lo.at[c + 4]
    if c < 2:
        return ab.at[c + 2]
    if c < 4:
        return r3hi.at[c]
    if c < 6:
        return r4hi.at[c - 2]
    return r4hi.at[6]


def pack_y2(ab, u, r3lo, r3hi, r4lo, r4hi, up, down):
    for out, top in ((up, True), (down, False)):
        first = 8 if top else 0
        for k in range(14):
            plane = coarse_a(ab, r3lo, r3hi, r4lo, r4hi, k - 6)
            out[8 * k : 8 * k + 8, :] = plane[first : first + 8, :]
        for k in range(12):
            plane = coarse_b(ab, r3lo, r3hi, r4lo, r4hi, k - 5)
            out[Y2_B + 8 * k : Y2_B + 8 * k + 8, :] = plane[first : first + 8, :]
        for k in range(8):
            at = Y2_U + 4 * k
            for half in range(2):
                if 0 < k < 7:
                    row = 34 if top else 4
                    rows = u[k - 1, row : row + 2, CCOLS * half : CCOLS * half + CCOLS]
                else:
                    edge = r3lo if k == 0 else r3hi
                    if top:
                        rows = edge[6 + half, 14:16, :]
                    else:
                        rows = edge[4 + half, 0:2, :]
                out[at + 2 * half : at + 2 * half + 2, :] = rows


def post_kernel(
    masks, t_in, a_in, b_in, u_in, ct, ab, r3lo, r3hi, r4lo, r4hi, ylo, yhi,
    out, uf, cf, xs,
):
    mlo = masks[0]
    mhi = masks[1]
    a = []
    for k in range(14):
        own = coarse_a(ab, r3lo, r3hi, r4lo, r4hi, k - 6)[...]
        lo = ylo[8 * k : 8 * k + 8, :] * mlo
        hi = yhi[8 * k : 8 * k + 8, :] * mhi
        a.append(jnp.concatenate([lo, own, hi], axis=0))
    b = [None]
    for k in range(12):
        own = coarse_b(ab, r3lo, r3hi, r4lo, r4hi, k - 5)[...]
        lo = ylo[Y2_B + 8 * k : Y2_B + 8 * k + 8, :] * mlo
        hi = yhi[Y2_B + 8 * k : Y2_B + 8 * k + 8, :] * mhi
        b.append(jnp.concatenate([lo, own, hi], axis=0))
    link = [0.5] * 13
    for j in range(6):
        link[2 * j + 1] = 0.5 * masks[2 + j]
    u = list(a)
    for sweep in range(1, COARSE_SWEEPS):
        first, last = sweep, 13 - sweep
        smooth = {k: smooth_xy(u[k]) for k in range(first - 1, last + 2)}
        fresh = list(u)
        for k in range(first, last + 1):
            w = 2.0 * (
                smooth[k] + link[k - 1] * smooth[k - 1] + link[k] * smooth[k + 1] - u[k]
            )
            fresh[k] = KEEP * u[k] + a[k] + b[k] * w
        u = fresh
    corr = []
    for k in range(4):
        t = ct[k]
        inside = t > 0.0
        corr.append(jnp.where(inside, u[5 + k] / jnp.where(inside, t, 1.0), 0.0))
    stacked = jnp.concatenate(corr, axis=0)
    dst = lax.broadcasted_iota(jnp.int32, (CCOLS, COLS), 1)
    src = lax.broadcasted_iota(jnp.int32, (CCOLS, COLS), 0)
    spread = jnp.where(dst // 2 == src, 1.0, 0.0)
    wide = jnp.dot(
        stacked, spread, precision=lax.Precision.HIGHEST, preferred_element_type=jnp.float32
    )
    for k in range(4):
        for half in range(2):
            rows = wide[CR * k + 6 : CR * k + 26, CCOLS * half : CCOLS * half + CCOLS]
            cf[2 * k + half, pl.ds(0, 20, 2), :] = rows
            cf[2 * k + half, pl.ds(1, 20, 2), :] = rows
    zeros = jnp.zeros((FR, COLS), jnp.float32)
    for k in range(8):
        if 0 < k < 7:
            uf[k] = u_in[k - 1]
        else:
            uf[k] = zeros
            edge = r3lo if k == 0 else r3hi
            for j in range(4):
                row = 4 + 16 * (j // 2)
                lane = CCOLS * (j % 2)
                uf[k, row : row + 16, lane : lane + CCOLS] = edge[4 + j]
        at = Y2_U + 4 * k
        for half in range(2):
            lane = CCOLS * half
            uf[k, 2:4, lane : lane + CCOLS] = ylo[at + 2 * half : at + 2 * half + 2, :] * mlo
            uf[k, 36:38, lane : lane + CCOLS] = yhi[at + 2 * half : at + 2 * half + 2, :] * mhi
        both = 2 * (k // 2)
        uf[k] = uf[k] + t_in[k] * jnp.concatenate([cf[both], cf[both + 1]], axis=1)
    for k in range(8):
        xs[k] = smooth_xy(uf[k])
    for k in range(6):
        v = uf[k + 1]
        w = 2.0 * (xs[k + 1] + 0.5 * (xs[k] + xs[k + 2]) - v)
        uf[k + 1] = KEEP * v + a_in[k] + b_in[k] * w
    for k in range(6):
        xs[k] = smooth_xy(uf[k + 1])
    for k in range(4):
        v = uf[k + 2]
        w = 2.0 * (xs[k + 1] + 0.5 * (xs[k] + xs[k + 2]) - v)
        new = KEEP * v + a_in[k + 1] + b_in[k + 1] * w
        uf[k + 2] = new / t_in[k + 2]
        out[k] = uf[k + 2, 4:36, :]


VM = pl.BlockSpec(memory_space=pltpu.VMEM)
SM = pl.BlockSpec(memory_space=pltpu.SMEM)


def f32(*shape):
    return jax.ShapeDtypeStruct(shape, jnp.float32)


def call(kernel, specs, outs, scratch=()):
    return pl.pallas_call(
        kernel,
        in_specs=specs,
        out_specs=jax.tree.map(lambda _: VM, outs),
        out_shape=outs,
        scratch_shapes=[pltpu.VMEM(shape, jnp.float32) for shape in scratch],
    )


def on_device(pressure_rhs, permeability, accumulation, coarse_perm, coarse_accum, run_lengths):
    up, down = call(
        pack_z1, [VM] * 4, (f32(Z1_ROWS, COLS), f32(Z1_ROWS, COLS))
    )(pressure_rhs, permeability, accumulation, coarse_perm)
    lo = shifted(up, "slab", 1)
    hi = shifted(down, "slab", -1)

    slab = lax.axis_index("slab")
    pen = lax.axis_index("pen")
    starts = jnp.cumsum(run_lengths) - run_lengths
    blocks = slab - 2 + jnp.arange(6, dtype=jnp.int32)
    begins = jnp.any(starts[None, :] == blocks[:, None], axis=1)
    masks = jnp.concatenate(
        [
            jnp.stack([pen > 0, pen < lax.axis_size("pen") - 1]).astype(jnp.float32),
            1.0 - begins.astype(jnp.float32),
        ]
    )

    up, down = call(
        pack_y1, [VM] * 6, (f32(Y1_ROWS, COLS), f32(Y1_ROWS, COLS))
    )(pressure_rhs, permeability, accumulation, coarse_perm, lo, hi)
    ylo = rotated(up, "pen", 1)
    yhi = rotated(down, "pen", -1)

    t, a, b, u, ct, ab, zup, zdn = call(
        pre_kernel,
        [SM] + [VM] * 9,
        (
            f32(8, FR, COLS), f32(6, FR, COLS), f32(6, FR, COLS), f32(6, FR, COLS),
            f32(4, CR, CCOLS), f32(4, CROWS, CCOLS),
            f32(8, CROWS, CCOLS), f32(8, CROWS, CCOLS),
        ),
        (
            (10, FR, COLS), (8, FR, COLS), (8, FR, COLS),
            (10, FR, COLS), (8, FR, COLS), (4, FR, COLS), (4, FR, CCOLS),
        ),
    )(masks, pressure_rhs, permeability, accumulation, coarse_perm, coarse_accum, lo, hi, ylo, yhi)
    r3lo = shifted(zup, "slab", 1)
    r3hi = shifted(zdn, "slab", -1)

    r4lo = shifted(jnp.concatenate([ab, r3lo[0:2], r3lo[3:4]], axis=0), "slab", 2)
    r4hi = shifted(jnp.concatenate([ab, r3hi[0:3]], axis=0), "slab", -2)

    up, down = call(
        pack_y2, [VM] * 6, (f32(Y2_ROWS, CCOLS), f32(Y2_ROWS, CCOLS))
    )(ab, u, r3lo, r3hi, r4lo, r4hi)
    ylo = rotated(up, "pen", 1)
    yhi = rotated(down, "pen", -1)

    return call(
        post_kernel,
        [SM] + [VM] * 12,
        f32(4, ROWS, COLS),
        ((8, FR, COLS), (8, FR, CCOLS), (8, FR, COLS)),
    )(masks, t, a, b, u, ct, ab, r3lo, r3hi, r4lo, r4hi, ylo, yhi)


def solution(mesh):
    return jax.shard_map(
        on_device,
        mesh=mesh,
        in_specs=(
            P("slab", "pen", None),
            P("slab", "pen", None),
            P("slab", "pen", None),
            P("slab", "pen", None),
            P("slab", "pen", None),
            P(),
        ),
        out_specs=P("slab", "pen", None),
        check_vma=False,
    )
```

time: 207 us -> 72.2 us (0.35)
  the two profiles are of different devices: /device:TPU:15 before, /device:TPU:63 now
where the time goes in v1:
time: 72.2 us; the launch traced here: 71.8 us
  starting transfers between devices  28.9 us (40%)
  waiting for transfers between devices  25.5 us (35%)
  Pallas kernels  12.3 us (17%)
  local copies, waits for them, and re-layouts  3.91 us (5%)
  other arithmetic  1.1 us (2%)
    ppermute x6, starting transfers between devices, shifted(): return lax.ppermute(x, axis, pairs)  25.9 us
    ppermute x6, waiting for transfers between devices, shifted(): return lax.ppermute(x, axis, pairs)  15.5 us
    ppermute x4, waiting for transfers between devices, rotated(): lax.ppermute(x, axis, [(i, (i + by) % devices) for i in range(devices)])  10 us
    unnamed x24, local copies, waits for them, and re-layouts  3.81 us
    pallas_call x1, Pallas kernels, on_device(): call(post_kernel, [SM] + [VM] * 12, f32(4, ROWS, COLS), ((8, FR, COLS), (...  3.52 us
    pallas_call x1, Pallas kernels, on_device(): call(pre_kernel, [SM] + [VM] * 9, (f32(8, FR, COLS), f32(6, FR, COLS), f3...  3.25 us
    ppermute x4, starting transfers between devices, rotated(): lax.ppermute(x, axis, [(i, (i + by) % devices) for i in range(devices)])  2.99 us
    pallas_call x1, Pallas kernels, on_device(): call(pack_y1, [VM] * 6, (f32(Y1_ROWS, COLS), f32(Y1_ROWS, COLS)))  1.97 us
  transfers between devices with their start and end apart: 10, of which 9 were waited for; matrix products, arithmetic and copies ran while one was open for 2% of the time, Pallas kernels for 0%

profile of v1, /device:TPU:63, one launch (start us, length us, event | category | flops | bytes accessed | tf_op | source)
XLA Modules:
  0.0 71.8 jit_solution(634201937047634607)
XLA Ops:
  0.0 1.8 %shard_map.64 = (f32[232,256]{1,0:T(8,128)}, f32[232,256]{1,0:T(8,128)}) custom-call(f32[4,32,256]{2,1,0:T(8,128)} %rhs.6, f32[4,32,256]{2,1,0:T(8,128)} %perm.5, f32[4,32,256]{2,1,0:T(8,128)} %acc.5, f32[2,16,128]{2,1,0:T(8,128)} %cperm.5), custom_call_target="tpu_custom_call" | custom-call | tf_op jit(solution)/shard_map/pallas_call | solution.py:365
  1.8 3.5 %collective-permute-start = (f32[232,256]{1,0:T(8,128)}, f32[232,256]{1,0:T(8,128)S(1)}, u32[]{:S(2)}, u32[]{:S(2)}) collective-permute-start(f32[232,256]{1,0:T(8,128)} %get-tuple-element.19), channel_id=1, source_target_pairs={{0,8},{8,16},{16,24},{24,32},{32,40},{40,48},{48,56},{56,64},{64,7... | collective-permute-start | bytes 712712 | tf_op jit(solution)/shard_map/ppermute | solution.py:23
  5.4 1.9 %collective-permute-start.1 = (f32[232,256]{1,0:T(8,128)}, f32[232,256]{1,0:T(8,128)S(1)}, u32[]{:S(2)}, u32[]{:S(2)}) collective-permute-start(f32[232,256]{1,0:T(8,128)} %get-tuple-element.20), channel_id=1, source_target_pairs={{8,0},{16,8},{24,16},{32,24},{40,32},{48,40},{56,48},{64,56},{72,6... | collective-permute-start | bytes 712712 | tf_op jit(solution)/shard_map/ppermute | solution.py:23
  7.3 0.0 copy-start.11
  7.3 0.6 copy-done.11
  8.0 0.1 copy.9
  8.1 0.1 reduce-window.9
  8.1 0.1 reduce
  8.2 0.2 compare_reduce_fusion
  8.4 0.1 add_convert_fusion
  8.5 2.1 %collective-permute-done.lo = f32[232,256]{1,0:T(8,128)S(1)} collective-permute-done((f32[232,256]{1,0:T(8,128)}, f32[232,256]{1,0:T(8,128)S(1)}, u32[]{:S(2)}, u32[]{:S(2)}) %collective-permute-start) | collective-permute-done | bytes 237600 | tf_op jit(solution)/shard_map/ppermute | solution.py:23
  10.6 0.0 copy-start
  10.6 3.6 %collective-permute-done.1.hi = f32[232,256]{1,0:T(8,128)S(1)} collective-permute-done((f32[232,256]{1,0:T(8,128)}, f32[232,256]{1,0:T(8,128)S(1)}, u32[]{:S(2)}, u32[]{:S(2)}) %collective-permute-start.1) | collective-permute-done | bytes 237600 | tf_op jit(solution)/shard_map/ppermute | solution.py:23
  14.2 0.0 copy-done
  14.2 0.0 copy-start.1
  14.2 0.7 copy-done.1
  14.9 2.0 %shard_map.65 = (f32[64,256]{1,0:T(8,128)}, f32[64,256]{1,0:T(8,128)}) custom-call(f32[4,32,256]{2,1,0:T(8,128)} %rhs.6, f32[4,32,256]{2,1,0:T(8,128)} %perm.5, f32[4,32,256]{2,1,0:T(8,128)} %acc.5, f32[2,16,128]{2,1,0:T(8,128)} %cperm.5, f32[232,256]{1,0:T(8,128)} %copy-done, f32[232,256]{1,0:T(8,128)} %copy-done.1), custom_call_target="tpu_custom_call" | custom-call | tf_op jit(solution)/shard_map/pallas_call | solution.py:383
  16.9 1.5 %collective-permute-start.2 = (f32[64,256]{1,0:T(8,128)}, f32[64,256]{1,0:T(8,128)S(1)}, u32[]{:S(2)}, u32[]{:S(2)}) collective-permute-start(f32[64,256]{1,0:T(8,128)} %get-tuple-element.21), channel_id=1, source_target_pairs={{0,1},{1,2},{2,3},{3,4},{4,5},{5,6},{6,7},{7,0},{8,9},{9,10},{10,1... | collective-permute-start | bytes 196616 | tf_op jit(solution)/shard_map/ppermute | solution.py:28
  18.4 0.2 collective-permute-start.3
  18.5 0.6 pad_maximum_fusion.2.masks
  19.2 0.8 %collective-permute-done.2.ylo = f32[64,256]{1,0:T(8,128)S(1)} collective-permute-done((f32[64,256]{1,0:T(8,128)}, f32[64,256]{1,0:T(8,128)S(1)}, u32[]{:S(2)}, u32[]{:S(2)}) %collective-permute-start.2) | collective-permute-done | bytes 65568 | tf_op jit(solution)/shard_map/ppermute | solution.py:28
  20.0 0.0 copy-start.9
  20.0 3.5 %collective-permute-done.3.yhi = f32[64,256]{1,0:T(8,128)S(1)} collective-permute-done((f32[64,256]{1,0:T(8,128)}, f32[64,256]{1,0:T(8,128)S(1)}, u32[]{:S(2)}, u32[]{:S(2)}) %collective-permute-start.3) | collective-permute-done | bytes 65568 | tf_op jit(solution)/shard_map/ppermute | solution.py:28
  23.5 0.0 copy-done.9
  23.5 0.0 copy-start.10
  23.5 0.6 copy-done.10
  24.1 3.2 %shard_map.66 = (f32[8,40,256]{2,1,0:T(8,128)}, f32[6,40,256]{2,1,0:T(8,128)}, f32[6,40,256]{2,1,0:T(8,128)}, f32[6,40,256]{2,1,0:T(8,128)}, f32[4,32,128]{2,1,0...) custom-call(f32[8]{0:T(128)} %pad_maximum_fusion.2.masks, f32[4,32,256]{2,1,0:T(8,128)} %rhs.6, ...), custom_call_target="tpu_custom_call" | custom-call | tf_op jit(solution)/shard_map/pallas_call | solution.py:389
  27.3 4.7 %collective-permute-start.4 = (f32[8,16,128]{2,1,0:T(8,128)}, f32[8,16,128]{2,1,0:T(8,128)S(1)}, u32[]{:S(2)}, u32[]{:S(2)}) collective-permute-start(f32[8,16,128]{2,1,0:T(8,128)} %get-tuple-element.29), channel_id=1, source_target_pairs={{0,8},{8,16},{16,24},{24,32},{32,40},{40,48},{48,56},{56,64},{64,7... | collective-permute-start | bytes 196616 | tf_op jit(solution)/shard_map/ppermute | solution.py:23
  32.1 4.5 %collective-permute-start.5 = (f32[8,16,128]{2,1,0:T(8,128)}, f32[8,16,128]{2,1,0:T(8,128)S(1)}, u32[]{:S(2)}, u32[]{:S(2)}) collective-permute-start(f32[8,16,128]{2,1,0:T(8,128)} %get-tuple-element.30), channel_id=1, source_target_pairs={{8,0},{16,8},{24,16},{32,24},{40,32},{48,40},{56,48},{64,56},{72,6... | collective-permute-start | bytes 196616 | tf_op jit(solution)/shard_map/ppermute | solution.py:23
  36.6 0.5 collective-permute-done.4.r3lo
  37.0 0.0 copy-start.3
  37.0 0.0 copy-start.4
  37.0 2.4 %collective-permute-done.5.r3hi = f32[8,16,128]{2,1,0:T(8,128)S(1)} collective-permute-done((f32[8,16,128]{2,1,0:T(8,128)}, f32[8,16,128]{2,1,0:T(8,128)S(1)}, u32[]{:S(2)}, u32[]{:S(2)}) %collective-permute-start.5) | collective-permute-done | bytes 65568 | tf_op jit(solution)/shard_map/ppermute | solution.py:23
  39.5 0.0 copy-start.2
  39.5 0.0 copy-done.4
  39.5 0.0 copy-done.3
  39.5 0.6 copy-done.2
  40.1 9.3 %collective-permute-start.7 = (f32[7,16,128]{2,1,0:T(8,128)S(1)}, f32[7,16,128]{2,1,0:T(8,128)S(1)}, u32[]{:S(2)}, u32[]{:S(2)}) collective-permute-start(f32[7,16,128]{2,1,0:T(8,128)S(1)} %get-tuple-element.33), channel_id=1, source_target_pairs={{16,0},{24,8},{32,16},{40,24},{48,32},{56,40},{64,48},{72,56},{80,... | collective-permute-start | bytes 172040 | tf_op jit(solution)/shard_map/ppermute | solution.py:23
  49.4 1.9 %collective-permute-start.6 = (f32[7,16,128]{2,1,0:T(8,128)S(1)}, f32[7,16,128]{2,1,0:T(8,128)S(1)}, u32[]{:S(2)}, u32[]{:S(2)}) collective-permute-start(f32[7,16,128]{2,1,0:T(8,128)S(1)} %get-tuple-element.34), channel_id=1, source_target_pairs={{0,16},{8,24},{16,32},{24,40},{32,48},{40,56},{48,64},{56,72},{64,... | collective-permute-start | bytes 172040 | tf_op jit(solution)/shard_map/ppermute | solution.py:23
  51.3 0.0 collective-permute-done.7.r4hi
  51.3 0.0 copy-start.5
  51.3 6.9 %collective-permute-done.6.r4lo = f32[7,16,128]{2,1,0:T(8,128)S(1)} collective-permute-done((f32[7,16,128]{2,1,0:T(8,128)S(1)}, f32[7,16,128]{2,1,0:T(8,128)S(1)}, u32[]{:S(2)}, u32[]{:S(2)}) %collective-permute-start.6) | collective-permute-done | bytes 57376 | tf_op jit(solution)/shard_map/ppermute | solution.py:23
  58.2 0.0 copy-start.6
  58.2 0.0 copy-done.5
  58.2 0.6 copy-done.6
  58.9 1.7 %shard_map.67 = (f32[240,128]{1,0:T(8,128)}, f32[240,128]{1,0:T(8,128)}) custom-call(f32[4,16,128]{2,1,0:T(8,128)} %get-tuple-element.28.ab, f32[6,40,256]{2,1,0:T(8,128)} %get-tuple-element.26.u.u_in, f32[8,16,128]{2,1,0:T(8,128)} %copy-done.3, f32[8,16,128]{2,1,0:T(8,128)} %copy-done.2, f32[7,16,128]{2,1,0:T(8,128)} %copy-done.6, f32[7,16,128]{2,1,0:T(8,128)} %copy-done.5), custom_call_target="tpu_custom_call" | custom-call | tf_op jit(solution)/shard_map/pallas_call | solution.py:408
  60.6 1.3 %collective-permute-start.8 = (f32[240,128]{1,0:T(8,128)}, f32[240,128]{1,0:T(8,128)S(1)}, u32[]{:S(2)}, u32[]{:S(2)}) collective-permute-start(f32[240,128]{1,0:T(8,128)} %get-tuple-element.31), channel_id=1, source_target_pairs={{0,1},{1,2},{2,3},{3,4},{4,5},{5,6},{6,7},{7,0},{8,9},{9,10},{10,1... | collective-permute-start | bytes 368648 | tf_op jit(solution)/shard_map/ppermute | solution.py:28
  61.9 0.0 collective-permute-start.9
  61.9 2.2 %collective-permute-done.8.ylo = f32[240,128]{1,0:T(8,128)S(1)} collective-permute-done((f32[240,128]{1,0:T(8,128)}, f32[240,128]{1,0:T(8,128)S(1)}, u32[]{:S(2)}, u32[]{:S(2)}) %collective-permute-start.8) | collective-permute-done | bytes 122912 | tf_op jit(solution)/shard_map/ppermute | solution.py:28
  64.1 0.0 copy-start.7
  64.1 3.5 %collective-permute-done.9.yhi = f32[240,128]{1,0:T(8,128)S(1)} collective-permute-done((f32[240,128]{1,0:T(8,128)}, f32[240,128]{1,0:T(8,128)S(1)}, u32[]{:S(2)}, u32[]{:S(2)}) %collective-permute-start.9) | collective-permute-done | bytes 122912 | tf_op jit(solution)/shard_map/ppermute | solution.py:28
  67.6 0.0 copy-start.8
  67.6 0.0 copy-done.7
  67.6 0.6 copy-done.8
  68.3 3.5 %shard_map.68 = f32[4,32,256]{2,1,0:T(8,128)} custom-call(f32[8]{0:T(128)} %pad_maximum_fusion.2.masks, f32[8,40,256]{2,1,0:T(8,128)} %get-tuple-element.23.t_in, f32[6,40,256]{2,1,0:T(8,128)} %get-tuple-element.24.a_in, f32[6,40,256]{2,1,0:T(8,128)} %get-tuple-element.25.b_in, f32[6,40,256]{2,1,0:T(8,128)} %get-tuple-element.26.u.u_in, ...), custom_call_target="tpu_custom_call" | custom-call | tf_op jit(solution)/shard_map/pallas_call | solution.py:414
  (7 shorter events, 0.0 us)
Async XLA Ops:
  1.8 8.7 %collective-permute-start = (f32[232,256]{1,0:T(8,128)}, f32[232,256]{1,0:T(8,128)S(1)}, u32[]{:S(2)}, u32[]{:S(2)}) collective-permute-start(f32[232,256]{1,0:T(8,128)} %get-tuple-element.19), channel_id=1, source_target_pairs={{0,8},{8,16},{16,24},{24,32},{32,40},{40,48},{48,56},{56,64},{64,7... | collective-permute-start | bytes 712712 | tf_op jit(solution)/shard_map/ppermute | solution.py:23
  5.4 8.8 %collective-permute-start.1 = (f32[232,256]{1,0:T(8,128)}, f32[232,256]{1,0:T(8,128)S(1)}, u32[]{:S(2)}, u32[]{:S(2)}) collective-permute-start(f32[232,256]{1,0:T(8,128)} %get-tuple-element.20), channel_id=1, source_target_pairs={{8,0},{16,8},{24,16},{32,24},{40,32},{48,40},{56,48},{64,56},{72,6... | collective-permute-start | bytes 712712 | tf_op jit(solution)/shard_map/ppermute | solution.py:23
  7.3 0.7 copy-start.11
  10.6 3.6 %copy-start = (f32[232,256]{1,0:T(8,128)}, f32[232,256]{1,0:T(8,128)S(1)}, u32[]{:S(2)}) copy-start(f32[232,256]{1,0:T(8,128)S(1)} %collective-permute-done.lo) | copy-start | bytes 712708
  14.2 0.7 copy-start.1
  16.9 3.1 %collective-permute-start.2 = (f32[64,256]{1,0:T(8,128)}, f32[64,256]{1,0:T(8,128)S(1)}, u32[]{:S(2)}, u32[]{:S(2)}) collective-permute-start(f32[64,256]{1,0:T(8,128)} %get-tuple-element.21), channel_id=1, source_target_pairs={{0,1},{1,2},{2,3},{3,4},{4,5},{5,6},{6,7},{7,0},{8,9},{9,10},{10,1... | collective-permute-start | bytes 196616 | tf_op jit(solution)/shard_map/ppermute | solution.py:28
  18.4 5.1 %collective-permute-start.3 = (f32[64,256]{1,0:T(8,128)}, f32[64,256]{1,0:T(8,128)S(1)}, u32[]{:S(2)}, u32[]{:S(2)}) collective-permute-start(f32[64,256]{1,0:T(8,128)} %get-tuple-element.22), channel_id=1, source_target_pairs={{0,7},{1,0},{2,1},{3,2},{4,3},{5,4},{6,5},{7,6},{8,15},{9,8},{10,9... | collective-permute-start | bytes 196616 | tf_op jit(solution)/shard_map/ppermute | solution.py:28
  20.0 3.5 %copy-start.9 = (f32[64,256]{1,0:T(8,128)}, f32[64,256]{1,0:T(8,128)S(1)}, u32[]{:S(2)}) copy-start(f32[64,256]{1,0:T(8,128)S(1)} %collective-permute-done.2.ylo) | copy-start | bytes 196612
  23.5 0.6 copy-start.10
  27.3 9.7 %collective-permute-start.4 = (f32[8,16,128]{2,1,0:T(8,128)}, f32[8,16,128]{2,1,0:T(8,128)S(1)}, u32[]{:S(2)}, u32[]{:S(2)}) collective-permute-start(f32[8,16,128]{2,1,0:T(8,128)} %get-tuple-element.29), channel_id=1, source_target_pairs={{0,8},{8,16},{16,24},{24,32},{32,40},{40,48},{48,56},{56,64},{64,7... | collective-permute-start | bytes 196616 | tf_op jit(solution)/shard_map/ppermute | solution.py:23
  32.1 7.4 %collective-permute-start.5 = (f32[8,16,128]{2,1,0:T(8,128)}, f32[8,16,128]{2,1,0:T(8,128)S(1)}, u32[]{:S(2)}, u32[]{:S(2)}) collective-permute-start(f32[8,16,128]{2,1,0:T(8,128)} %get-tuple-element.30), channel_id=1, source_target_pairs={{8,0},{16,8},{24,16},{32,24},{40,32},{48,40},{56,48},{64,56},{72,6... | collective-permute-start | bytes 196616 | tf_op jit(solution)/shard_map/ppermute | solution.py:23
  37.0 2.5 %copy-start.3 = (f32[8,16,128]{2,1,0:T(8,128)}, f32[8,16,128]{2,1,0:T(8,128)S(1)}, u32[]{:S(2)}) copy-start(f32[8,16,128]{2,1,0:T(8,128)S(1)} %collective-permute-done.4.r3lo) | copy-start | bytes 196612
  37.0 2.4 %copy-start.4 = (f32[4,16,128]{2,1,0:T(8,128)S(1)}, f32[4,16,128]{2,1,0:T(8,128)}, u32[]{:S(2)}) copy-start(f32[4,16,128]{2,1,0:T(8,128)} %get-tuple-element.28.ab) | copy-start | bytes 98308
  39.5 0.6 copy-start.2
  40.1 11.2 %collective-permute-start.7 = (f32[7,16,128]{2,1,0:T(8,128)S(1)}, f32[7,16,128]{2,1,0:T(8,128)S(1)}, u32[]{:S(2)}, u32[]{:S(2)}) collective-permute-start(f32[7,16,128]{2,1,0:T(8,128)S(1)} %get-tuple-element.33), channel_id=1, source_target_pairs={{16,0},{24,8},{32,16},{40,24},{48,32},{56,40},{64,48},{72,56},{80,... | collective-permute-start | bytes 172040 | tf_op jit(solution)/shard_map/ppermute | solution.py:23
  49.4 8.9 %collective-permute-start.6 = (f32[7,16,128]{2,1,0:T(8,128)S(1)}, f32[7,16,128]{2,1,0:T(8,128)S(1)}, u32[]{:S(2)}, u32[]{:S(2)}) collective-permute-start(f32[7,16,128]{2,1,0:T(8,128)S(1)} %get-tuple-element.34), channel_id=1, source_target_pairs={{0,16},{8,24},{16,32},{24,40},{32,48},{40,56},{48,64},{56,72},{64,... | collective-permute-start | bytes 172040 | tf_op jit(solution)/shard_map/ppermute | solution.py:23
  51.3 6.9 %copy-start.5 = (f32[7,16,128]{2,1,0:T(8,128)}, f32[7,16,128]{2,1,0:T(8,128)S(1)}, u32[]{:S(2)}) copy-start(f32[7,16,128]{2,1,0:T(8,128)S(1)} %collective-permute-done.7.r4hi) | copy-start | bytes 172036
  58.2 0.6 copy-start.6
  60.6 3.5 %collective-permute-start.8 = (f32[240,128]{1,0:T(8,128)}, f32[240,128]{1,0:T(8,128)S(1)}, u32[]{:S(2)}, u32[]{:S(2)}) collective-permute-start(f32[240,128]{1,0:T(8,128)} %get-tuple-element.31), channel_id=1, source_target_pairs={{0,1},{1,2},{2,3},{3,4},{4,5},{5,6},{6,7},{7,0},{8,9},{9,10},{10,1... | collective-permute-start | bytes 368648 | tf_op jit(solution)/shard_map/ppermute | solution.py:28
  61.9 5.7 %collective-permute-start.9 = (f32[240,128]{1,0:T(8,128)}, f32[240,128]{1,0:T(8,128)S(1)}, u32[]{:S(2)}, u32[]{:S(2)}) collective-permute-start(f32[240,128]{1,0:T(8,128)} %get-tuple-element.32), channel_id=1, source_target_pairs={{0,7},{1,0},{2,1},{3,2},{4,3},{5,4},{6,5},{7,6},{8,15},{9,8},{10,9... | collective-permute-start | bytes 368648 | tf_op jit(solution)/shard_map/ppermute | solution.py:28
  64.1 3.5 %copy-start.7 = (f32[240,128]{1,0:T(8,128)}, f32[240,128]{1,0:T(8,128)S(1)}, u32[]{:S(2)}) copy-start(f32[240,128]{1,0:T(8,128)S(1)} %collective-permute-done.8.ylo) | copy-start | bytes 368644
  67.6 0.6 copy-start.8

commit v2 on v1

--- a/solution.py
+++ b/solution.py
@@ -358,6 +358,7 @@
         out_specs=jax.tree.map(lambda _: VM, outs),
         out_shape=outs,
         scratch_shapes=[pltpu.VMEM(shape, jnp.float32) for shape in scratch],
+        compiler_params=pltpu.CompilerParams(vmem_limit_bytes=8 * 1024 * 1024),
     )
 
 

time: 72.2 us -> 63.7 us (0.88)
  Pallas kernels: 12.3 us -> 4.56 us
    pallas_call x1, Pallas kernels: 1.97 us -> 0.05 us  [on_device(): call(pack_y1, [VM] * 6, (f32(Y1_ROWS, COLS), f32(Y1_ROWS, COLS)))]
    pallas_call x1, Pallas kernels: 1.83 us -> 0.03 us  [on_device(): call(pack_z1, [VM] * 4, (f32(Z1_ROWS, COLS), f32(Z1_ROWS, COLS)))]
    pallas_call x1, Pallas kernels: 1.73 us -> 0.03 us  [on_device(): call(pack_y2, [VM] * 6, (f32(Y2_ROWS, CCOLS), f32(Y2_ROWS, CCOLS)))]
    pallas_call x1, Pallas kernels: 3.25 us -> 1.84 us  [on_device(): call(pre_kernel, [SM] + [VM] * 9, (f32(8, FR, COLS), f32(6, FR, COLS), f3...]
    pallas_call x1, Pallas kernels: 3.52 us -> 2.61 us  [on_device(): call(post_kernel, [SM] + [VM] * 12, f32(4, ROWS, COLS), ((8, FR, COLS), (...]
    unnamed x24 -> x20, local copies, waits for them, and re-layouts: 3.81 us -> 4.1 us
  transfers between devices with their start and end apart: 10 -> 10, of which waited for: 9 -> 8; matrix products, arithmetic and copies ran while one was open for 2% -> 1% of each run, Pallas kernels for 0% -> 0%
where the time goes in v2:
time: 63.7 us; the launch traced here: 63.3 us
  starting transfers between devices  28.8 us (45%)
  waiting for transfers between devices  25.1 us (39%)
  Pallas kernels  4.56 us (7%)
  local copies, waits for them, and re-layouts  4.19 us (7%)
    ppermute x6, starting transfers between devices, shifted(): return lax.ppermute(x, axis, pairs)  25.9 us
    ppermute x6, waiting for transfers between devices, shifted(): return lax.ppermute(x, axis, pairs)  15 us
    ppermute x4, waiting for transfers between devices, rotated(): lax.ppermute(x, axis, [(i, (i + by) % devices) for i in range(devices)])  10.1 us
    unnamed x20, local copies, waits for them, and re-layouts  4.1 us
    ppermute x4, starting transfers between devices, rotated(): lax.ppermute(x, axis, [(i, (i + by) % devices) for i in range(devices)])  2.82 us
    pallas_call x1, Pallas kernels, on_device(): call(post_kernel, [SM] + [VM] * 12, f32(4, ROWS, COLS), ((8, FR, COLS), (...  2.61 us
    pallas_call x1, Pallas kernels, on_device(): call(pre_kernel, [SM] + [VM] * 9, (f32(8, FR, COLS), f32(6, FR, COLS), f3...  1.84 us
  transfers between devices with their start and end apart: 10, of which 8 were waited for; matrix products, arithmetic and copies ran while one was open for 1% of the time, Pallas kernels for 0%

profile of v2, /device:TPU:63, one launch (start us, length us, event | category | flops | bytes accessed | tf_op | source)
XLA Modules:
  0.0 63.3 jit_solution(11370399027718105607)
XLA Ops:
  0.0 0.0 copy-start
  0.0 0.9 %copy-done = f32[4,32,256]{2,1,0:T(8,128)S(1)} copy-done((f32[4,32,256]{2,1,0:T(8,128)S(1)}, f32[4,32,256]{2,1,0:T(8,128)}, u32[]{:S(2)}) %copy-start) | copy-done | bytes 131096
  0.9 0.0 copy-start.2
  0.9 0.9 %copy-done.2 = f32[4,32,256]{2,1,0:T(8,128)S(1)} copy-done((f32[4,32,256]{2,1,0:T(8,128)S(1)}, f32[4,32,256]{2,1,0:T(8,128)}, u32[]{:S(2)}) %copy-start.2) | copy-done | bytes 131096
  1.8 0.0 copy-start.4
  1.8 0.9 %copy-done.4 = f32[4,32,256]{2,1,0:T(8,128)S(1)} copy-done((f32[4,32,256]{2,1,0:T(8,128)S(1)}, f32[4,32,256]{2,1,0:T(8,128)}, u32[]{:S(2)}) %copy-start.4) | copy-done | bytes 131096
  2.7 0.0 copy-start.6
  2.7 0.7 %copy-done.6 = f32[2,16,128]{2,1,0:T(8,128)S(1)} copy-done((f32[2,16,128]{2,1,0:T(8,128)S(1)}, f32[2,16,128]{2,1,0:T(8,128)}, u32[]{:S(2)}) %copy-start.6) | copy-done | bytes 16408
  3.4 0.0 copy-start.1
  3.4 0.0 copy-start.3
  3.4 0.0 copy-start.5
  3.5 3.7 %collective-permute-start = (f32[232,256]{1,0:T(8,128)S(1)}, f32[232,256]{1,0:T(8,128)S(1)}, u32[]{:S(2)}, u32[]{:S(2)}) collective-permute-start(f32[232,256]{1,0:T(8,128)S(1)} %get-tuple-element.19), channel_id=1, source_target_pairs={{0,8},{8,16},{16,24},{24,32},{32,40},{40,48},{48,56},{56,64},{64,7... | collective-permute-start | bytes 712712 | tf_op jit(solution)/shard_map/ppermute | solution.py:23
  7.2 1.9 %collective-permute-start.1 = (f32[232,256]{1,0:T(8,128)S(1)}, f32[232,256]{1,0:T(8,128)S(1)}, u32[]{:S(2)}, u32[]{:S(2)}) collective-permute-start(f32[232,256]{1,0:T(8,128)S(1)} %get-tuple-element.20), channel_id=1, source_target_pairs={{8,0},{16,8},{24,16},{32,24},{40,32},{48,40},{56,48},{64,56},{72,6... | collective-permute-start | bytes 712712 | tf_op jit(solution)/shard_map/ppermute | solution.py:23
  9.1 0.0 copy-start.9
  9.1 0.6 %copy-done.9 = s32[32]{0:T(128)S(1)} copy-done((s32[32]{0:T(128)S(1)}, s32[32]{0:T(128)}, u32[]{:S(2)}) %copy-start.9) | copy-done | bytes 152
  9.8 0.1 copy.9
  9.9 0.1 reduce-window.9
  9.9 0.0 copy-start.7
  9.9 0.1 reduce
  10.0 0.2 compare_reduce_fusion
  10.2 0.1 add_convert_fusion
  10.3 1.8 %collective-permute-done.lo = f32[232,256]{1,0:T(8,128)S(1)} collective-permute-done((f32[232,256]{1,0:T(8,128)S(1)}, f32[232,256]{1,0:T(8,128)S(1)}, u32[]{:S(2)}, u32[]{:S(2)}) %collective-permute-start) | collective-permute-done | bytes 237600 | tf_op jit(solution)/shard_map/ppermute | solution.py:23
  12.1 3.6 %collective-permute-done.1.hi = f32[232,256]{1,0:T(8,128)S(1)} collective-permute-done((f32[232,256]{1,0:T(8,128)S(1)}, f32[232,256]{1,0:T(8,128)S(1)}, u32[]{:S(2)}, u32[]{:S(2)}) %collective-permute-start.1) | collective-permute-done | bytes 237600 | tf_op jit(solution)/shard_map/ppermute | solution.py:23
  15.8 0.0 copy-done.1
  15.8 0.0 copy-done.3
  15.8 0.0 copy-done.5
  15.8 0.0 copy-done.7
  15.8 0.0 copy-start.8
  15.8 0.1 shard_map.65
  15.9 1.5 %collective-permute-start.2 = (f32[64,256]{1,0:T(8,128)S(1)}, f32[64,256]{1,0:T(8,128)S(1)}, u32[]{:S(2)}, u32[]{:S(2)}) collective-permute-start(f32[64,256]{1,0:T(8,128)S(1)} %get-tuple-element.21), channel_id=1, source_target_pairs={{0,1},{1,2},{2,3},{3,4},{4,5},{5,6},{6,7},{7,0},{8,9},{9,10},{10,1... | collective-permute-start | bytes 196616 | tf_op jit(solution)/shard_map/ppermute | solution.py:28
  17.4 0.2 collective-permute-start.3
  17.6 0.1 pad_maximum_fusion.2.masks
  17.6 1.1 %collective-permute-done.2.ylo = f32[64,256]{1,0:T(8,128)S(1)} collective-permute-done((f32[64,256]{1,0:T(8,128)S(1)}, f32[64,256]{1,0:T(8,128)S(1)}, u32[]{:S(2)}, u32[]{:S(2)}) %collective-permute-start.2) | collective-permute-done | bytes 65568 | tf_op jit(solution)/shard_map/ppermute | solution.py:28
  18.7 3.6 %collective-permute-done.3.yhi = f32[64,256]{1,0:T(8,128)S(1)} collective-permute-done((f32[64,256]{1,0:T(8,128)S(1)}, f32[64,256]{1,0:T(8,128)S(1)}, u32[]{:S(2)}, u32[]{:S(2)}) %collective-permute-start.3) | collective-permute-done | bytes 65568 | tf_op jit(solution)/shard_map/ppermute | solution.py:28
  22.3 0.0 copy-done.8
  22.3 1.8 %shard_map.66 = (f32[8,40,256]{2,1,0:T(8,128)S(1)}, f32[6,40,256]{2,1,0:T(8,128)S(1)}, f32[6,40,256]{2,1,0:T(8,128)S(1)}, f32[6,40,256]{2,1,0:T(8,128)S(1)}, f32...) custom-call(f32[8]{0:T(128)S(1)} %pad_maximum_fusion.2.masks, ...), custom_call_target="tpu_custom_call" | custom-call | tf_op jit(solution)/shard_map/pallas_call | solution.py:390
  24.1 4.8 %collective-permute-start.4 = (f32[8,16,128]{2,1,0:T(8,128)S(1)}, f32[8,16,128]{2,1,0:T(8,128)S(1)}, u32[]{:S(2)}, u32[]{:S(2)}) collective-permute-start(f32[8,16,128]{2,1,0:T(8,128)S(1)} %get-tuple-element.29), channel_id=1, source_target_pairs={{0,8},{8,16},{16,24},{24,32},{32,40},{40,48},{48,56},{56,64},{64,7... | collective-permute-start | bytes 196616 | tf_op jit(solution)/shard_map/ppermute | solution.py:23
  28.9 4.4 %collective-permute-start.5 = (f32[8,16,128]{2,1,0:T(8,128)S(1)}, f32[8,16,128]{2,1,0:T(8,128)S(1)}, u32[]{:S(2)}, u32[]{:S(2)}) collective-permute-start(f32[8,16,128]{2,1,0:T(8,128)S(1)} %get-tuple-element.30), channel_id=1, source_target_pairs={{8,0},{16,8},{24,16},{32,24},{40,32},{48,40},{56,48},{64,56},{72,6... | collective-permute-start | bytes 196616 | tf_op jit(solution)/shard_map/ppermute | solution.py:23
  33.2 0.0 collective-permute-done.4.r3lo
  33.3 1.9 %collective-permute-done.5.r3hi = f32[8,16,128]{2,1,0:T(8,128)S(1)} collective-permute-done((f32[8,16,128]{2,1,0:T(8,128)S(1)}, f32[8,16,128]{2,1,0:T(8,128)S(1)}, u32[]{:S(2)}, u32[]{:S(2)}) %collective-permute-start.5) | collective-permute-done | bytes 65568 | tf_op jit(solution)/shard_map/ppermute | solution.py:23
  35.2 9.3 %collective-permute-start.7 = (f32[7,16,128]{2,1,0:T(8,128)S(1)}, f32[7,16,128]{2,1,0:T(8,128)S(1)}, u32[]{:S(2)}, u32[]{:S(2)}) collective-permute-start(f32[7,16,128]{2,1,0:T(8,128)S(1)} %get-tuple-element.33), channel_id=1, source_target_pairs={{16,0},{24,8},{32,16},{40,24},{48,32},{56,40},{64,48},{72,56},{80,... | collective-permute-start | bytes 172040 | tf_op jit(solution)/shard_map/ppermute | solution.py:23
  44.5 1.9 %collective-permute-start.6 = (f32[7,16,128]{2,1,0:T(8,128)S(1)}, f32[7,16,128]{2,1,0:T(8,128)S(1)}, u32[]{:S(2)}, u32[]{:S(2)}) collective-permute-start(f32[7,16,128]{2,1,0:T(8,128)S(1)} %get-tuple-element.34), channel_id=1, source_target_pairs={{0,16},{8,24},{16,32},{24,40},{32,48},{40,56},{48,64},{56,72},{64,... | collective-permute-start | bytes 172040 | tf_op jit(solution)/shard_map/ppermute | solution.py:23
  46.5 0.0 collective-permute-done.7.r4hi
  46.5 7.5 %collective-permute-done.6.r4lo = f32[7,16,128]{2,1,0:T(8,128)S(1)} collective-permute-done((f32[7,16,128]{2,1,0:T(8,128)S(1)}, f32[7,16,128]{2,1,0:T(8,128)S(1)}, u32[]{:S(2)}, u32[]{:S(2)}) %collective-permute-start.6) | collective-permute-done | bytes 57376 | tf_op jit(solution)/shard_map/ppermute | solution.py:23
  54.1 1.1 %collective-permute-start.8 = (f32[240,128]{1,0:T(8,128)S(1)}, f32[240,128]{1,0:T(8,128)S(1)}, u32[]{:S(2)}, u32[]{:S(2)}) collective-permute-start(f32[240,128]{1,0:T(8,128)S(1)} %get-tuple-element.31), channel_id=1, source_target_pairs={{0,1},{1,2},{2,3},{3,4},{4,5},{5,6},{6,7},{7,0},{8,9},{9,10},{10,1... | collective-permute-start | bytes 368648 | tf_op jit(solution)/shard_map/ppermute | solution.py:28
  55.2 0.0 collective-permute-start.9
  55.2 1.9 %collective-permute-done.8.ylo = f32[240,128]{1,0:T(8,128)S(1)} collective-permute-done((f32[240,128]{1,0:T(8,128)S(1)}, f32[240,128]{1,0:T(8,128)S(1)}, u32[]{:S(2)}, u32[]{:S(2)}) %collective-permute-start.8) | collective-permute-done | bytes 122912 | tf_op jit(solution)/shard_map/ppermute | solution.py:28
  57.1 3.6 %collective-permute-done.9.yhi = f32[240,128]{1,0:T(8,128)S(1)} collective-permute-done((f32[240,128]{1,0:T(8,128)S(1)}, f32[240,128]{1,0:T(8,128)S(1)}, u32[]{:S(2)}, u32[]{:S(2)}) %collective-permute-start.9) | collective-permute-done | bytes 122912 | tf_op jit(solution)/shard_map/ppermute | solution.py:28
  60.7 2.6 %shard_map.68 = f32[4,32,256]{2,1,0:T(8,128)} custom-call(f32[8]{0:T(128)S(1)} %pad_maximum_fusion.2.masks, f32[8,40,256]{2,1,0:T(8,128)S(1)} %get-tuple-element.23.t_in, f32[6,40,256]{2,1,0:T(8,128)S(1)} %get-tuple-element.24.a_in, f32[6,40,256]{2,1,0:T(8,128)S(1)} %get-tuple-element.25.b_in, f32[6,40,256]{2,1,0:T(8,128)S(1)} %get-tuple-element.26.u.u_in, ...), custom_call_target="tpu_custom_call" | custom-call | tf_op jit(solution)/shard_map/pallas_call | solution.py:415
  (9 shorter events, 0.1 us)
Async XLA Ops:
  0.0 0.9 %copy-start = (f32[4,32,256]{2,1,0:T(8,128)S(1)}, f32[4,32,256]{2,1,0:T(8,128)}, u32[]{:S(2)}) copy-start(f32[4,32,256]{2,1,0:T(8,128)} %rhs.6) | copy-start | bytes 393220
  0.9 0.9 %copy-start.2 = (f32[4,32,256]{2,1,0:T(8,128)S(1)}, f32[4,32,256]{2,1,0:T(8,128)}, u32[]{:S(2)}) copy-start(f32[4,32,256]{2,1,0:T(8,128)} %perm.5) | copy-start | bytes 393220
  1.8 0.9 %copy-start.4 = (f32[4,32,256]{2,1,0:T(8,128)S(1)}, f32[4,32,256]{2,1,0:T(8,128)}, u32[]{:S(2)}) copy-start(f32[4,32,256]{2,1,0:T(8,128)} %acc.5) | copy-start | bytes 393220
  2.7 0.7 %copy-start.6 = (f32[2,16,128]{2,1,0:T(8,128)S(1)}, f32[2,16,128]{2,1,0:T(8,128)}, u32[]{:S(2)}) copy-start(f32[2,16,128]{2,1,0:T(8,128)} %cperm.5) | copy-start | bytes 49156
  3.4 12.3 %copy-start.1 = (f32[4,32,256]{2,1,0:T(8,128)S(1)}, f32[4,32,256]{2,1,0:T(8,128)}, u32[]{:S(2)}) copy-start(f32[4,32,256]{2,1,0:T(8,128)} %rhs.6) | copy-start | bytes 393220
  3.4 12.3 %copy-start.3 = (f32[4,32,256]{2,1,0:T(8,128)S(1)}, f32[4,32,256]{2,1,0:T(8,128)}, u32[]{:S(2)}) copy-start(f32[4,32,256]{2,1,0:T(8,128)} %perm.5) | copy-start | bytes 393220
  3.4 12.3 %copy-start.5 = (f32[4,32,256]{2,1,0:T(8,128)S(1)}, f32[4,32,256]{2,1,0:T(8,128)}, u32[]{:S(2)}) copy-start(f32[4,32,256]{2,1,0:T(8,128)} %acc.5) | copy-start | bytes 393220
  3.5 8.7 %collective-permute-start = (f32[232,256]{1,0:T(8,128)S(1)}, f32[232,256]{1,0:T(8,128)S(1)}, u32[]{:S(2)}, u32[]{:S(2)}) collective-permute-start(f32[232,256]{1,0:T(8,128)S(1)} %get-tuple-element.19), channel_id=1, source_target_pairs={{0,8},{8,16},{16,24},{24,32},{32,40},{40,48},{48,56},{56,64},{64,7... | collective-permute-start | bytes 712712 | tf_op jit(solution)/shard_map/ppermute | solution.py:23
  7.2 8.6 %collective-permute-start.1 = (f32[232,256]{1,0:T(8,128)S(1)}, f32[232,256]{1,0:T(8,128)S(1)}, u32[]{:S(2)}, u32[]{:S(2)}) collective-permute-start(f32[232,256]{1,0:T(8,128)S(1)} %get-tuple-element.20), channel_id=1, source_target_pairs={{8,0},{16,8},{24,16},{32,24},{40,32},{48,40},{56,48},{64,56},{72,6... | collective-permute-start | bytes 712712 | tf_op jit(solution)/shard_map/ppermute | solution.py:23
  9.1 0.7 %copy-start.9 = (s32[32]{0:T(128)S(1)}, s32[32]{0:T(128)}, u32[]{:S(2)}) copy-start(s32[32]{0:T(128)} %param.11) | copy-start | bytes 388
  9.9 5.9 %copy-start.7 = (f32[2,16,128]{2,1,0:T(8,128)S(1)}, f32[2,16,128]{2,1,0:T(8,128)}, u32[]{:S(2)}) copy-start(f32[2,16,128]{2,1,0:T(8,128)} %cperm.5) | copy-start | bytes 49156
  15.8 6.5 %copy-start.8 = (f32[2,16,128]{2,1,0:T(8,128)S(1)}, f32[2,16,128]{2,1,0:T(8,128)}, u32[]{:S(2)}) copy-start(f32[2,16,128]{2,1,0:T(8,128)} %cacc.1) | copy-start | bytes 49156
  15.9 2.8 %collective-permute-start.2 = (f32[64,256]{1,0:T(8,128)S(1)}, f32[64,256]{1,0:T(8,128)S(1)}, u32[]{:S(2)}, u32[]{:S(2)}) collective-permute-start(f32[64,256]{1,0:T(8,128)S(1)} %get-tuple-element.21), channel_id=1, source_target_pairs={{0,1},{1,2},{2,3},{3,4},{4,5},{5,6},{6,7},{7,0},{8,9},{9,10},{10,1... | collective-permute-start | bytes 196616 | tf_op jit(solution)/shard_map/ppermute | solution.py:28
  17.4 4.9 %collective-permute-start.3 = (f32[64,256]{1,0:T(8,128)S(1)}, f32[64,256]{1,0:T(8,128)S(1)}, u32[]{:S(2)}, u32[]{:S(2)}) collective-permute-start(f32[64,256]{1,0:T(8,128)S(1)} %get-tuple-element.22), channel_id=1, source_target_pairs={{0,7},{1,0},{2,1},{3,2},{4,3},{5,4},{6,5},{7,6},{8,15},{9,8},{10,9... | collective-permute-start | bytes 196616 | tf_op jit(solution)/shard_map/ppermute | solution.py:28
  24.1 9.1 %collective-permute-start.4 = (f32[8,16,128]{2,1,0:T(8,128)S(1)}, f32[8,16,128]{2,1,0:T(8,128)S(1)}, u32[]{:S(2)}, u32[]{:S(2)}) collective-permute-start(f32[8,16,128]{2,1,0:T(8,128)S(1)} %get-tuple-element.29), channel_id=1, source_target_pairs={{0,8},{8,16},{16,24},{24,32},{32,40},{40,48},{48,56},{56,64},{64,7... | collective-permute-start | bytes 196616 | tf_op jit(solution)/shard_map/ppermute | solution.py:23
  28.9 6.3 %collective-permute-start.5 = (f32[8,16,128]{2,1,0:T(8,128)S(1)}, f32[8,16,128]{2,1,0:T(8,128)S(1)}, u32[]{:S(2)}, u32[]{:S(2)}) collective-permute-start(f32[8,16,128]{2,1,0:T(8,128)S(1)} %get-tuple-element.30), channel_id=1, source_target_pairs={{8,0},{16,8},{24,16},{32,24},{40,32},{48,40},{56,48},{64,56},{72,6... | collective-permute-start | bytes 196616 | tf_op jit(solution)/shard_map/ppermute | solution.py:23
  35.2 11.2 %collective-permute-start.7 = (f32[7,16,128]{2,1,0:T(8,128)S(1)}, f32[7,16,128]{2,1,0:T(8,128)S(1)}, u32[]{:S(2)}, u32[]{:S(2)}) collective-permute-start(f32[7,16,128]{2,1,0:T(8,128)S(1)} %get-tuple-element.33), channel_id=1, source_target_pairs={{16,0},{24,8},{32,16},{40,24},{48,32},{56,40},{64,48},{72,56},{80,... | collective-permute-start | bytes 172040 | tf_op jit(solution)/shard_map/ppermute | solution.py:23
  44.5 9.5 %collective-permute-start.6 = (f32[7,16,128]{2,1,0:T(8,128)S(1)}, f32[7,16,128]{2,1,0:T(8,128)S(1)}, u32[]{:S(2)}, u32[]{:S(2)}) collective-permute-start(f32[7,16,128]{2,1,0:T(8,128)S(1)} %get-tuple-element.34), channel_id=1, source_target_pairs={{0,16},{8,24},{16,32},{24,40},{32,48},{40,56},{48,64},{56,72},{64,... | collective-permute-start | bytes 172040 | tf_op jit(solution)/shard_map/ppermute | solution.py:23
  54.1 3.0 %collective-permute-start.8 = (f32[240,128]{1,0:T(8,128)S(1)}, f32[240,128]{1,0:T(8,128)S(1)}, u32[]{:S(2)}, u32[]{:S(2)}) collective-permute-start(f32[240,128]{1,0:T(8,128)S(1)} %get-tuple-element.31), channel_id=1, source_target_pairs={{0,1},{1,2},{2,3},{3,4},{4,5},{5,6},{6,7},{7,0},{8,9},{9,10},{10,1... | collective-permute-start | bytes 368648 | tf_op jit(solution)/shard_map/ppermute | solution.py:28
  55.2 5.5 %collective-permute-start.9 = (f32[240,128]{1,0:T(8,128)S(1)}, f32[240,128]{1,0:T(8,128)S(1)}, u32[]{:S(2)}, u32[]{:S(2)}) collective-permute-start(f32[240,128]{1,0:T(8,128)S(1)} %get-tuple-element.32), channel_id=1, source_target_pairs={{0,7},{1,0},{2,1},{3,2},{4,3},{5,4},{6,5},{7,6},{8,15},{9,8},{10,9... | collective-permute-start | bytes 368648 | tf_op jit(solution)/shard_map/ppermute | solution.py:28

commit v3 on v2

--- a/solution.py
+++ b/solution.py
@@ -51,14 +51,26 @@
 Z1_ROWS = 232
 
 
-def pack_z1(rhs, perm, acc, cperm, up, down):
-    for out, first3, first2, coarse in ((up, 1, 2, 1), (down, 0, 0, 0)):
-        for k in range(3):
-            out[32 * k : 32 * k + 32, :] = perm[first3 + k]
-        for k in range(2):
-            out[Z1_RHS + 32 * k : Z1_RHS + 32 * k + 32, :] = rhs[first2 + k]
-            out[Z1_ACC + 32 * k : Z1_ACC + 32 * k + 32, :] = acc[first2 + k]
-        out[Z1_CO : Z1_CO + 8, :] = to_wide(cperm[coarse])
+def pack_z1(rhs, perm, acc, cperm, up, down, held, sems):
+    copies = [pltpu.make_async_copy(cperm, held, sems.at[0])]
+    for out, first3, first2 in ((up, 1, 2), (down, 0, 0)):
+        for base, ref, first, count in (
+            (0, perm, first3, 3), (Z1_RHS, rhs, first2, 2), (Z1_ACC, acc, first2, 2)
+        ):
+            for k in range(count):
+                copies.append(
+                    pltpu.make_async_copy(
+                        ref.at[first + k],
+                        out.at[pl.ds(base + ROWS * k, ROWS)],
+                        sems.at[len(copies)],
+                    )
+                )
+    for copy in copies:
+        copy.start()
+    for copy in copies:
+        copy.wait()
+    up[Z1_CO : Z1_CO + 8, :] = to_wide(held[1])
+    down[Z1_CO : Z1_CO + 8, :] = to_wide(held[0])
 
 
 def fine_rows(own, lo, hi, base, depth, z, first, count):
@@ -199,9 +211,20 @@
             out[4 + k] = u_out[plane, row : row + 16, lane : lane + CCOLS]
 
 
-Y2_B = 112
-Y2_U = 208
-Y2_ROWS = 240
+def pack_up2(ab, r3lo, out):
+    out[0:4] = ab[...]
+    out[4:6] = r3lo[0:2]
+    out[6] = r3lo[3]
+
+
+def pack_down2(ab, r3hi, out):
+    out[0:4] = ab[...]
+    out[4:7] = r3hi[0:3]
+
+
+Y2_B = 84
+Y2_U = 156
+Y2_ROWS = 192
 
 
 def coarse_a(ab, r3lo, r3hi, r4lo, r4hi, c):
@@ -238,13 +261,13 @@
 
 def pack_y2(ab, u, r3lo, r3hi, r4lo, r4hi, up, down):
     for out, top in ((up, True), (down, False)):
-        first = 8 if top else 0
+        first = CROWS - 6 if top else 0
         for k in range(14):
             plane = coarse_a(ab, r3lo, r3hi, r4lo, r4hi, k - 6)
-            out[8 * k : 8 * k + 8, :] = plane[first : first + 8, :]
+            out[6 * k : 6 * k + 6, :] = plane[first : first + 6, :]
         for k in range(12):
             plane = coarse_b(ab, r3lo, r3hi, r4lo, r4hi, k - 5)
-            out[Y2_B + 8 * k : Y2_B + 8 * k + 8, :] = plane[first : first + 8, :]
+            out[Y2_B + 6 * k : Y2_B + 6 * k + 6, :] = plane[first : first + 6, :]
         for k in range(8):
             at = Y2_U + 4 * k
             for half in range(2):
@@ -262,22 +285,24 @@
 
 def post_kernel(
     masks, t_in, a_in, b_in, u_in, ct, ab, r3lo, r3hi, r4lo, r4hi, ylo, yhi,
-    out, uf, cf, xs,
+    out, uf, cf, xs, ff,
 ):
     mlo = masks[0]
     mhi = masks[1]
+    tile = jnp.zeros((8, CCOLS), jnp.float32)
     a = []
-    for k in range(14):
-        own = coarse_a(ab, r3lo, r3hi, r4lo, r4hi, k - 6)[...]
-        lo = ylo[8 * k : 8 * k + 8, :] * mlo
-        hi = yhi[8 * k : 8 * k + 8, :] * mhi
-        a.append(jnp.concatenate([lo, own, hi], axis=0))
     b = [None]
-    for k in range(12):
-        own = coarse_b(ab, r3lo, r3hi, r4lo, r4hi, k - 5)[...]
-        lo = ylo[Y2_B + 8 * k : Y2_B + 8 * k + 8, :] * mlo
-        hi = yhi[Y2_B + 8 * k : Y2_B + 8 * k + 8, :] * mhi
-        b.append(jnp.concatenate([lo, own, hi], axis=0))
+    for k in range(26):
+        if k < 14:
+            own = coarse_a(ab, r3lo, r3hi, r4lo, r4hi, k - 6)
+        else:
+            own = coarse_b(ab, r3lo, r3hi, r4lo, r4hi, k - 19)
+        ff[k, 0:8, :] = tile
+        ff[k, 24:32, :] = tile
+        ff[k, 2:8, :] = ylo[6 * k : 6 * k + 6, :] * mlo
+        ff[k, 8:24, :] = own[...]
+        ff[k, 24:30, :] = yhi[6 * k : 6 * k + 6, :] * mhi
+        (a if k < 14 else b).append(ff[k])
     link = [0.5] * 13
     for j in range(6):
         link[2 * j + 1] = 0.5 * masks[2 + j]
@@ -345,6 +370,7 @@
 
 VM = pl.BlockSpec(memory_space=pltpu.VMEM)
 SM = pl.BlockSpec(memory_space=pltpu.SMEM)
+HBM = pl.BlockSpec(memory_space=pltpu.HBM)
 
 
 def f32(*shape):
@@ -357,15 +383,26 @@
         in_specs=specs,
         out_specs=jax.tree.map(lambda _: VM, outs),
         out_shape=outs,
-        scratch_shapes=[pltpu.VMEM(shape, jnp.float32) for shape in scratch],
+        scratch_shapes=[
+            pltpu.VMEM(shape, jnp.float32) if isinstance(shape, tuple) else shape
+            for shape in scratch
+        ],
         compiler_params=pltpu.CompilerParams(vmem_limit_bytes=8 * 1024 * 1024),
     )
 
 
 def on_device(pressure_rhs, permeability, accumulation, coarse_perm, coarse_accum, run_lengths):
     up, down = call(
-        pack_z1, [VM] * 4, (f32(Z1_ROWS, COLS), f32(Z1_ROWS, COLS))
-    )(pressure_rhs, permeability, accumulation, coarse_perm)
+        pack_z1,
+        [HBM] * 4,
+        (f32(Z1_ROWS, COLS), f32(Z1_ROWS, COLS)),
+        (pltpu.VMEM((2, CROWS, CCOLS), jnp.float32), pltpu.SemaphoreType.DMA((15,))),
+    )(
+        *(
+            pltpu.with_memory_space_constraint(x, pltpu.HBM)
+            for x in (pressure_rhs, permeability, accumulation, coarse_perm)
+        )
+    )
     lo = shifted(up, "slab", 1)
     hi = shifted(down, "slab", -1)
 
@@ -403,8 +440,9 @@
     r3lo = shifted(zup, "slab", 1)
     r3hi = shifted(zdn, "slab", -1)
 
-    r4lo = shifted(jnp.concatenate([ab, r3lo[0:2], r3lo[3:4]], axis=0), "slab", 2)
-    r4hi = shifted(jnp.concatenate([ab, r3hi[0:3]], axis=0), "slab", -2)
+    further = f32(7, CROWS, CCOLS)
+    r4lo = shifted(call(pack_up2, [VM] * 2, further)(ab, r3lo), "slab", 2)
+    r4hi = shifted(call(pack_down2, [VM] * 2, further)(ab, r3hi), "slab", -2)
 
     up, down = call(
         pack_y2, [VM] * 6, (f32(Y2_ROWS, CCOLS), f32(Y2_ROWS, CCOLS))
@@ -416,7 +454,7 @@
         post_kernel,
         [SM] + [VM] * 12,
         f32(4, ROWS, COLS),
-        ((8, FR, COLS), (8, FR, CCOLS), (8, FR, COLS)),
+        ((8, FR, COLS), (8, FR, CCOLS), (8, FR, COLS), (26, CR, CCOLS)),
     )(masks, t, a, b, u, ct, ab, r3lo, r3hi, r4lo, r4hi, ylo, yhi)
 
 

time: 63.7 us -> 55.5 us (0.87)
  the two profiles are of different devices: /device:TPU:63 before, /device:TPU:31 now
where the time goes in v3:
time: 55.5 us; the launch traced here: 55.2 us
  starting transfers between devices  32.4 us (58%)
  waiting for transfers between devices  15.7 us (28%)
  Pallas kernels  5.75 us (10%)
  local copies, waits for them, and re-layouts  0.76 us (1%)
    ppermute x6, starting transfers between devices, shifted(): return lax.ppermute(x, axis, pairs)  29.7 us
    ppermute x4, waiting for transfers between devices, rotated(): lax.ppermute(x, axis, [(i, (i + by) % devices) for i in range(devices)])  9.88 us
    ppermute x6, waiting for transfers between devices, shifted(): return lax.ppermute(x, axis, pairs)  5.78 us
    ppermute x4, starting transfers between devices, rotated(): lax.ppermute(x, axis, [(i, (i + by) % devices) for i in range(devices)])  2.65 us
    pallas_call x1, Pallas kernels, on_device(): call(post_kernel, [SM] + [VM] * 12, f32(4, ROWS, COLS), ((8, FR, COLS), (...  2.65 us
    pallas_call x1, Pallas kernels, on_device(): call(pre_kernel, [SM] + [VM] * 9, (f32(8, FR, COLS), f32(6, FR, COLS), f3...  1.84 us
    pallas_call x1, Pallas kernels, on_device(): call(pack_z1, [HBM] * 4, (f32(Z1_ROWS, COLS), f32(Z1_ROWS, COLS)), (pltpu...  1.16 us
  transfers between devices with their start and end apart: 10, of which 8 were waited for; matrix products, arithmetic and copies ran while one was open for 1% of the time, Pallas kernels for 0%

profile of v3, /device:TPU:31, one launch (start us, length us, event | category | flops | bytes accessed | tf_op | source)
XLA Modules:
  0.0 55.2 jit_solution(8080786143147646621)
XLA Ops:
  0.0 0.0 copy-start
  0.0 0.0 copy-start.1
  0.0 0.0 copy-start.2
  0.0 1.2 %shard_map.64 = (f32[232,256]{1,0:T(8,128)S(1)}, f32[232,256]{1,0:T(8,128)S(1)}) custom-call(f32[4,32,256]{2,1,0:T(8,128)} %rhs.6, f32[4,32,256]{2,1,0:T(8,128)} %perm.5, f32[4,32,256]{2,1,0:T(8,128)} %acc.5, f32[2,16,128]{2,1,0:T(8,128)} %cperm.5), custom_call_target="tpu_custom_call" | custom-call | tf_op jit(solution)/shard_map/pallas_call | solution.py:395
  1.2 3.5 %collective-permute-start = (f32[232,256]{1,0:T(8,128)S(1)}, f32[232,256]{1,0:T(8,128)S(1)}, u32[]{:S(2)}, u32[]{:S(2)}) collective-permute-start(f32[232,256]{1,0:T(8,128)S(1)} %get-tuple-element.19), channel_id=1, source_target_pairs={{0,8},{8,16},{16,24},{24,32},{32,40},{40,48},{48,56},{56,64},{64,7... | collective-permute-start | bytes 712712 | tf_op jit(solution)/shard_map/ppermute | solution.py:23
  4.7 9.8 %collective-permute-start.1 = (f32[232,256]{1,0:T(8,128)S(1)}, f32[232,256]{1,0:T(8,128)S(1)}, u32[]{:S(2)}, u32[]{:S(2)}) collective-permute-start(f32[232,256]{1,0:T(8,128)S(1)} %get-tuple-element.20), channel_id=1, source_target_pairs={{8,0},{16,8},{24,16},{32,24},{40,32},{48,40},{56,48},{64,56},{72,6... | collective-permute-start | bytes 712712 | tf_op jit(solution)/shard_map/ppermute | solution.py:23
  14.5 0.0 copy-start.5
  14.5 0.6 %copy-done.5 = s32[32]{0:T(128)S(1)} copy-done((s32[32]{0:T(128)S(1)}, s32[32]{0:T(128)}, u32[]{:S(2)}) %copy-start.5) | copy-done | bytes 152
  15.2 0.1 copy.9
  15.3 0.1 reduce-window.9
  15.3 0.0 copy-start.3
  15.3 0.1 reduce
  15.4 0.2 compare_reduce_fusion
  15.6 0.1 add_convert_fusion
  15.7 2.3 %collective-permute-done.lo = f32[232,256]{1,0:T(8,128)S(1)} collective-permute-done((f32[232,256]{1,0:T(8,128)S(1)}, f32[232,256]{1,0:T(8,128)S(1)}, u32[]{:S(2)}, u32[]{:S(2)}) %collective-permute-start) | collective-permute-done | bytes 237600 | tf_op jit(solution)/shard_map/ppermute | solution.py:23
  18.1 0.9 %collective-permute-done.1.hi = f32[232,256]{1,0:T(8,128)S(1)} collective-permute-done((f32[232,256]{1,0:T(8,128)S(1)}, f32[232,256]{1,0:T(8,128)S(1)}, u32[]{:S(2)}, u32[]{:S(2)}) %collective-permute-start.1) | collective-permute-done | bytes 237600 | tf_op jit(solution)/shard_map/ppermute | solution.py:23
  18.9 0.0 copy-done
  18.9 0.0 copy-done.1
  18.9 0.0 copy-done.2
  18.9 0.0 copy-done.3
  18.9 0.0 copy-start.4
  19.0 0.1 shard_map.65
  19.0 1.4 %collective-permute-start.2 = (f32[64,256]{1,0:T(8,128)S(1)}, f32[64,256]{1,0:T(8,128)S(1)}, u32[]{:S(2)}, u32[]{:S(2)}) collective-permute-start(f32[64,256]{1,0:T(8,128)S(1)} %get-tuple-element.21), channel_id=1, source_target_pairs={{0,1},{1,2},{2,3},{3,4},{4,5},{5,6},{6,7},{7,0},{8,9},{9,10},{10,1... | collective-permute-start | bytes 196616 | tf_op jit(solution)/shard_map/ppermute | solution.py:28
  20.4 0.2 collective-permute-start.3
  20.6 0.1 pad_maximum_fusion.masks
  20.7 1.1 %collective-permute-done.2.ylo = f32[64,256]{1,0:T(8,128)S(1)} collective-permute-done((f32[64,256]{1,0:T(8,128)S(1)}, f32[64,256]{1,0:T(8,128)S(1)}, u32[]{:S(2)}, u32[]{:S(2)}) %collective-permute-start.2) | collective-permute-done | bytes 65568 | tf_op jit(solution)/shard_map/ppermute | solution.py:28
  21.7 3.6 %collective-permute-done.3.yhi = f32[64,256]{1,0:T(8,128)S(1)} collective-permute-done((f32[64,256]{1,0:T(8,128)S(1)}, f32[64,256]{1,0:T(8,128)S(1)}, u32[]{:S(2)}, u32[]{:S(2)}) %collective-permute-start.3) | collective-permute-done | bytes 65568 | tf_op jit(solution)/shard_map/ppermute | solution.py:28
  25.3 0.0 copy-done.4
  25.3 1.8 %shard_map.66 = (f32[8,40,256]{2,1,0:T(8,128)S(1)}, f32[6,40,256]{2,1,0:T(8,128)S(1)}, f32[6,40,256]{2,1,0:T(8,128)S(1)}, f32[6,40,256]{2,1,0:T(8,128)S(1)}, f32...) custom-call(f32[8]{0:T(128)S(1)} %pad_maximum_fusion.masks, ...), custom_call_target="tpu_custom_call" | custom-call | tf_op jit(solution)/shard_map/pallas_call | solution.py:427
  27.1 1.9 %collective-permute-start.4 = (f32[8,16,128]{2,1,0:T(8,128)S(1)}, f32[8,16,128]{2,1,0:T(8,128)S(1)}, u32[]{:S(2)}, u32[]{:S(2)}) collective-permute-start(f32[8,16,128]{2,1,0:T(8,128)S(1)} %get-tuple-element.29), channel_id=1, source_target_pairs={{0,8},{8,16},{16,24},{24,32},{32,40},{40,48},{48,56},{56,64},{64,7... | collective-permute-start | bytes 196616 | tf_op jit(solution)/shard_map/ppermute | solution.py:23
  29.1 6.2 %collective-permute-start.5 = (f32[8,16,128]{2,1,0:T(8,128)S(1)}, f32[8,16,128]{2,1,0:T(8,128)S(1)}, u32[]{:S(2)}, u32[]{:S(2)}) collective-permute-start(f32[8,16,128]{2,1,0:T(8,128)S(1)} %get-tuple-element.30), channel_id=1, source_target_pairs={{8,0},{16,8},{24,16},{32,24},{40,32},{48,40},{56,48},{64,56},{72,6... | collective-permute-start | bytes 196616 | tf_op jit(solution)/shard_map/ppermute | solution.py:23
  35.3 0.0 collective-permute-done.4.r3lo
  35.3 1.9 %collective-permute-start.6 = (f32[7,16,128]{2,1,0:T(8,128)S(1)}, f32[7,16,128]{2,1,0:T(8,128)S(1)}, u32[]{:S(2)}, u32[]{:S(2)}) collective-permute-start(f32[7,16,128]{2,1,0:T(8,128)S(1)} %shard_map.67), channel_id=1, source_target_pairs={{0,16},{8,24},{16,32},{24,40},{32,48},{40,56},{48,64},{56,72},{64,... | collective-permute-start | bytes 172040 | tf_op jit(solution)/shard_map/ppermute | solution.py:23
  37.3 0.0 collective-permute-done.5.r3hi
  37.3 6.4 %collective-permute-start.7 = (f32[7,16,128]{2,1,0:T(8,128)S(1)}, f32[7,16,128]{2,1,0:T(8,128)S(1)}, u32[]{:S(2)}, u32[]{:S(2)}) collective-permute-start(f32[7,16,128]{2,1,0:T(8,128)S(1)} %shard_map.68), channel_id=1, source_target_pairs={{16,0},{24,8},{32,16},{40,24},{48,32},{56,40},{64,48},{72,56},{80,... | collective-permute-start | bytes 172040 | tf_op jit(solution)/shard_map/ppermute | solution.py:23
  43.7 1.5 %collective-permute-done.6.r4lo = f32[7,16,128]{2,1,0:T(8,128)S(1)} collective-permute-done((f32[7,16,128]{2,1,0:T(8,128)S(1)}, f32[7,16,128]{2,1,0:T(8,128)S(1)}, u32[]{:S(2)}, u32[]{:S(2)}) %collective-permute-start.6) | collective-permute-done | bytes 57376 | tf_op jit(solution)/shard_map/ppermute | solution.py:23
  45.2 1.0 %collective-permute-done.7.r4hi = f32[7,16,128]{2,1,0:T(8,128)S(1)} collective-permute-done((f32[7,16,128]{2,1,0:T(8,128)S(1)}, f32[7,16,128]{2,1,0:T(8,128)S(1)}, u32[]{:S(2)}, u32[]{:S(2)}) %collective-permute-start.7) | collective-permute-done | bytes 57376 | tf_op jit(solution)/shard_map/ppermute | solution.py:23
  46.3 1.1 %collective-permute-start.8 = (f32[192,128]{1,0:T(8,128)S(1)}, f32[192,128]{1,0:T(8,128)S(1)}, u32[]{:S(2)}, u32[]{:S(2)}) collective-permute-start(f32[192,128]{1,0:T(8,128)S(1)} %get-tuple-element.31), channel_id=1, source_target_pairs={{0,1},{1,2},{2,3},{3,4},{4,5},{5,6},{6,7},{7,0},{8,9},{9,10},{10,1... | collective-permute-start | bytes 294920 | tf_op jit(solution)/shard_map/ppermute | solution.py:28
  47.3 0.0 collective-permute-start.9
  47.3 1.6 %collective-permute-done.8.ylo = f32[192,128]{1,0:T(8,128)S(1)} collective-permute-done((f32[192,128]{1,0:T(8,128)S(1)}, f32[192,128]{1,0:T(8,128)S(1)}, u32[]{:S(2)}, u32[]{:S(2)}) %collective-permute-start.8) | collective-permute-done | bytes 98336 | tf_op jit(solution)/shard_map/ppermute | solution.py:28
  49.0 3.6 %collective-permute-done.9.yhi = f32[192,128]{1,0:T(8,128)S(1)} collective-permute-done((f32[192,128]{1,0:T(8,128)S(1)}, f32[192,128]{1,0:T(8,128)S(1)}, u32[]{:S(2)}, u32[]{:S(2)}) %collective-permute-start.9) | collective-permute-done | bytes 98336 | tf_op jit(solution)/shard_map/ppermute | solution.py:28
  52.6 2.6 %shard_map.70 = f32[4,32,256]{2,1,0:T(8,128)} custom-call(f32[8]{0:T(128)S(1)} %pad_maximum_fusion.masks, f32[8,40,256]{2,1,0:T(8,128)S(1)} %get-tuple-element.23.t_in, f32[6,40,256]{2,1,0:T(8,128)S(1)} %get-tuple-element.24.a_in, f32[6,40,256]{2,1,0:T(8,128)S(1)} %get-tuple-element.25.b_in, f32[6,40,256]{2,1,0:T(8,128)S(1)} %get-tuple-element.26.u.u_in, ...), custom_call_target="tpu_custom_call" | custom-call | tf_op jit(solution)/shard_map/pallas_call | solution.py:453
  (6 shorter events, 0.1 us)
Async XLA Ops:
  0.0 18.9 %copy-start = (f32[4,32,256]{2,1,0:T(8,128)S(1)}, f32[4,32,256]{2,1,0:T(8,128)}, u32[]{:S(2)}) copy-start(f32[4,32,256]{2,1,0:T(8,128)} %rhs.6) | copy-start | bytes 393220
  0.0 18.9 %copy-start.1 = (f32[4,32,256]{2,1,0:T(8,128)S(1)}, f32[4,32,256]{2,1,0:T(8,128)}, u32[]{:S(2)}) copy-start(f32[4,32,256]{2,1,0:T(8,128)} %perm.5) | copy-start | bytes 393220
  0.0 18.9 %copy-start.2 = (f32[4,32,256]{2,1,0:T(8,128)S(1)}, f32[4,32,256]{2,1,0:T(8,128)}, u32[]{:S(2)}) copy-start(f32[4,32,256]{2,1,0:T(8,128)} %acc.5) | copy-start | bytes 393220
  1.2 16.9 %collective-permute-start = (f32[232,256]{1,0:T(8,128)S(1)}, f32[232,256]{1,0:T(8,128)S(1)}, u32[]{:S(2)}, u32[]{:S(2)}) collective-permute-start(f32[232,256]{1,0:T(8,128)S(1)} %get-tuple-element.19), channel_id=1, source_target_pairs={{0,8},{8,16},{16,24},{24,32},{32,40},{40,48},{48,56},{56,64},{64,7... | collective-permute-start | bytes 712712 | tf_op jit(solution)/shard_map/ppermute | solution.py:23
  4.7 14.2 %collective-permute-start.1 = (f32[232,256]{1,0:T(8,128)S(1)}, f32[232,256]{1,0:T(8,128)S(1)}, u32[]{:S(2)}, u32[]{:S(2)}) collective-permute-start(f32[232,256]{1,0:T(8,128)S(1)} %get-tuple-element.20), channel_id=1, source_target_pairs={{8,0},{16,8},{24,16},{32,24},{40,32},{48,40},{56,48},{64,56},{72,6... | collective-permute-start | bytes 712712 | tf_op jit(solution)/shard_map/ppermute | solution.py:23
  14.5 0.7 %copy-start.5 = (s32[32]{0:T(128)S(1)}, s32[32]{0:T(128)}, u32[]{:S(2)}) copy-start(s32[32]{0:T(128)} %param.11) | copy-start | bytes 388
  15.3 3.6 %copy-start.3 = (f32[2,16,128]{2,1,0:T(8,128)S(1)}, f32[2,16,128]{2,1,0:T(8,128)}, u32[]{:S(2)}) copy-start(f32[2,16,128]{2,1,0:T(8,128)} %cperm.5) | copy-start | bytes 49156
  18.9 6.4 %copy-start.4 = (f32[2,16,128]{2,1,0:T(8,128)S(1)}, f32[2,16,128]{2,1,0:T(8,128)}, u32[]{:S(2)}) copy-start(f32[2,16,128]{2,1,0:T(8,128)} %cacc.1) | copy-start | bytes 49156
  19.0 2.7 %collective-permute-start.2 = (f32[64,256]{1,0:T(8,128)S(1)}, f32[64,256]{1,0:T(8,128)S(1)}, u32[]{:S(2)}, u32[]{:S(2)}) collective-permute-start(f32[64,256]{1,0:T(8,128)S(1)} %get-tuple-element.21), channel_id=1, source_target_pairs={{0,1},{1,2},{2,3},{3,4},{4,5},{5,6},{6,7},{7,0},{8,9},{9,10},{10,1... | collective-permute-start | bytes 196616 | tf_op jit(solution)/shard_map/ppermute | solution.py:28
  20.4 4.9 %collective-permute-start.3 = (f32[64,256]{1,0:T(8,128)S(1)}, f32[64,256]{1,0:T(8,128)S(1)}, u32[]{:S(2)}, u32[]{:S(2)}) collective-permute-start(f32[64,256]{1,0:T(8,128)S(1)} %get-tuple-element.22), channel_id=1, source_target_pairs={{0,7},{1,0},{2,1},{3,2},{4,3},{5,4},{6,5},{7,6},{8,15},{9,8},{10,9... | collective-permute-start | bytes 196616 | tf_op jit(solution)/shard_map/ppermute | solution.py:28
  27.1 8.2 %collective-permute-start.4 = (f32[8,16,128]{2,1,0:T(8,128)S(1)}, f32[8,16,128]{2,1,0:T(8,128)S(1)}, u32[]{:S(2)}, u32[]{:S(2)}) collective-permute-start(f32[8,16,128]{2,1,0:T(8,128)S(1)} %get-tuple-element.29), channel_id=1, source_target_pairs={{0,8},{8,16},{16,24},{24,32},{32,40},{40,48},{48,56},{56,64},{64,7... | collective-permute-start | bytes 196616 | tf_op jit(solution)/shard_map/ppermute | solution.py:23
  29.1 8.2 %collective-permute-start.5 = (f32[8,16,128]{2,1,0:T(8,128)S(1)}, f32[8,16,128]{2,1,0:T(8,128)S(1)}, u32[]{:S(2)}, u32[]{:S(2)}) collective-permute-start(f32[8,16,128]{2,1,0:T(8,128)S(1)} %get-tuple-element.30), channel_id=1, source_target_pairs={{8,0},{16,8},{24,16},{32,24},{40,32},{48,40},{56,48},{64,56},{72,6... | collective-permute-start | bytes 196616 | tf_op jit(solution)/shard_map/ppermute | solution.py:23
  35.3 9.9 %collective-permute-start.6 = (f32[7,16,128]{2,1,0:T(8,128)S(1)}, f32[7,16,128]{2,1,0:T(8,128)S(1)}, u32[]{:S(2)}, u32[]{:S(2)}) collective-permute-start(f32[7,16,128]{2,1,0:T(8,128)S(1)} %shard_map.67), channel_id=1, source_target_pairs={{0,16},{8,24},{16,32},{24,40},{32,48},{40,56},{48,64},{56,72},{64,... | collective-permute-start | bytes 172040 | tf_op jit(solution)/shard_map/ppermute | solution.py:23
  37.3 8.9 %collective-permute-start.7 = (f32[7,16,128]{2,1,0:T(8,128)S(1)}, f32[7,16,128]{2,1,0:T(8,128)S(1)}, u32[]{:S(2)}, u32[]{:S(2)}) collective-permute-start(f32[7,16,128]{2,1,0:T(8,128)S(1)} %shard_map.68), channel_id=1, source_target_pairs={{16,0},{24,8},{32,16},{40,24},{48,32},{56,40},{64,48},{72,56},{80,... | collective-permute-start | bytes 172040 | tf_op jit(solution)/shard_map/ppermute | solution.py:23
  46.3 2.7 %collective-permute-start.8 = (f32[192,128]{1,0:T(8,128)S(1)}, f32[192,128]{1,0:T(8,128)S(1)}, u32[]{:S(2)}, u32[]{:S(2)}) collective-permute-start(f32[192,128]{1,0:T(8,128)S(1)} %get-tuple-element.31), channel_id=1, source_target_pairs={{0,1},{1,2},{2,3},{3,4},{4,5},{5,6},{6,7},{7,0},{8,9},{9,10},{10,1... | collective-permute-start | bytes 294920 | tf_op jit(solution)/shard_map/ppermute | solution.py:28
  47.3 5.3 %collective-permute-start.9 = (f32[192,128]{1,0:T(8,128)S(1)}, f32[192,128]{1,0:T(8,128)S(1)}, u32[]{:S(2)}, u32[]{:S(2)}) collective-permute-start(f32[192,128]{1,0:T(8,128)S(1)} %get-tuple-element.32), channel_id=1, source_target_pairs={{0,7},{1,0},{2,1},{3,2},{4,3},{5,4},{6,5},{7,6},{8,15},{9,8},{10,9... | collective-permute-start | bytes 294920 | tf_op jit(solution)/shard_map/ppermute | solution.py:28

commit v4 on v3

--- a/solution.py
+++ b/solution.py
@@ -17,10 +17,55 @@
 CCOLS = 128
 
 
-def shifted(x, axis, by):
-    devices = lax.axis_size(axis)
-    pairs = [(i, i + by) for i in range(devices) if 0 <= i + by < devices]
-    return lax.ppermute(x, axis, pairs)
+LINE = 16
+
+
+def along_lines(x, by):
+    slabs, pens = lax.axis_size("slab"), lax.axis_size("pen")
+    pairs = []
+    for slab in range(slabs):
+        for pen in range(pens):
+            line, z = divmod(slab, LINE)
+            core = pen % 2
+            step = (2 * LINE - 1 - z if core else z) + by
+            step %= 2 * LINE
+            core, z = (0, step) if step < LINE else (1, 2 * LINE - 1 - step)
+            pairs.append((slab * pens + pen, (line * LINE + z) * pens + pen // 2 * 2 + core))
+    return lax.ppermute(x, ("slab", "pen"), pairs)
+
+
+def between_lines(x, partners):
+    slabs, pens = lax.axis_size("slab"), lax.axis_size("pen")
+    pairs = []
+    for line in range(1, slabs // LINE):
+        for j, k in partners:
+            for pen in range(pens):
+                here = (line * LINE + j) * pens + pen
+                there = ((line - 1) * LINE + k) * pens + pen
+                pairs += [(here, there), (there, here)]
+    return lax.ppermute(x, ("slab", "pen"), pairs)
+
+
+def place():
+    return lax.axis_index("pen") % 2 == 0, lax.axis_index("slab") % LINE
+
+
+class Picked:
+    def __init__(self, first, one, other, end, across):
+        self.parts = (first, one, other, end, across)
+
+    def __getitem__(self, index):
+        first, one, other, end, across = self.parts
+        value = jnp.where(first, one[index], other[index])
+        return jnp.where(end, across[index], value)
+
+
+def below_above(plus, minus, across):
+    first, z = place()
+    return (
+        Picked(first, plus, minus, z == 0, across),
+        Picked(first, minus, plus, z == LINE - 1, across),
+    )
 
 
 def rotated(x, axis, by):
@@ -51,16 +96,20 @@
 Z1_ROWS = 232
 
 
-def pack_z1(rhs, perm, acc, cperm, up, down, held, sems):
+def pack_z1(rhs, perm, acc, cperm, plus, minus, across, held, sems):
+    first, z = place()
+    upward = (first, jnp.logical_not(first), z == LINE - 1)
     copies = [pltpu.make_async_copy(cperm, held, sems.at[0])]
-    for out, first3, first2 in ((up, 1, 2), (down, 0, 0)):
-        for base, ref, first, count in (
-            (0, perm, first3, 3), (Z1_RHS, rhs, first2, 2), (Z1_ACC, acc, first2, 2)
+    for out, up in zip((plus, minus, across), upward):
+        for base, ref, start, count in (
+            (0, perm, jnp.where(up, 1, 0), 3),
+            (Z1_RHS, rhs, jnp.where(up, 2, 0), 2),
+            (Z1_ACC, acc, jnp.where(up, 2, 0), 2),
         ):
             for k in range(count):
                 copies.append(
                     pltpu.make_async_copy(
-                        ref.at[first + k],
+                        ref.at[start + k],
                         out.at[pl.ds(base + ROWS * k, ROWS)],
                         sems.at[len(copies)],
                     )
@@ -69,8 +118,8 @@
         copy.start()
     for copy in copies:
         copy.wait()
-    up[Z1_CO : Z1_CO + 8, :] = to_wide(held[1])
-    down[Z1_CO : Z1_CO + 8, :] = to_wide(held[0])
+    for out, up in zip((plus, minus, across), upward):
+        out[Z1_CO : Z1_CO + 8, :] = to_wide(held[jnp.where(up, 1, 0)])
 
 
 def fine_rows(own, lo, hi, base, depth, z, first, count):
@@ -97,7 +146,8 @@
 Y1_ROWS = 64
 
 
-def pack_y1(rhs, perm, acc, cperm, lo, hi, up, down):
+def pack_y1(rhs, perm, acc, cperm, plus, minus, across, up, down):
+    lo, hi = below_above(plus, minus, across)
     for out, top in ((up, True), (down, False)):
         r3 = ROWS - 3 if top else 0
         r2 = ROWS - 2 if top else 0
@@ -117,10 +167,12 @@
 
 
 def pre_kernel(
-    masks, rhs, perm, acc, cperm, cacc, lo, hi, ylo, yhi,
-    t_out, a_out, b_out, u_out, ct_out, ab_out, zup, zdn,
+    masks, rhs, perm, acc, cperm, cacc, plus, minus, across, ylo, yhi,
+    t_out, a_out, b_out, u_out, ct_out, ab_out, plus_out, minus_out, across_out,
     ts, rs, cs, xs, us, ds, fs,
 ):
+    first, place_z = place()
+    lo, hi = below_above(plus, minus, across)
     mlo = masks[0]
     mhi = masks[1]
     zeros = jnp.zeros((FR, COLS), jnp.float32)
@@ -201,25 +253,31 @@
         q = OMEGA * t / d
         a = q * res[CROWS * k : CROWS * k + CROWS]
         b = q * t
-        for out in (ab_out, zup, zdn):
+        for out in (ab_out, plus_out, minus_out, across_out):
             out[k] = a
             out[2 + k] = b
-    for out, plane in ((zup, 3), (zdn, 2)):
+    for out, up in (
+        (plus_out, first), (minus_out, jnp.logical_not(first)), (across_out, place_z == LINE - 1)
+    ):
+        plane = jnp.where(up, 3, 2)
         for k in range(4):
             row = 4 + 16 * (k // 2)
             lane = CCOLS * (k % 2)
             out[4 + k] = u_out[plane, row : row + 16, lane : lane + CCOLS]
 
 
-def pack_up2(ab, r3lo, out):
-    out[0:4] = ab[...]
-    out[4:6] = r3lo[0:2]
-    out[6] = r3lo[3]
-
-
-def pack_down2(ab, r3hi, out):
-    out[0:4] = ab[...]
-    out[4:7] = r3hi[0:3]
+def pack_plus3(held, near, far, out):
+    pack_third(place()[0], held, near, far, out)
+
+
+def pack_minus3(held, near, far, out):
+    pack_third(jnp.logical_not(place()[0]), held, near, far, out)
+
+
+def pack_third(up, held, near, far, out):
+    out[0:2] = held[0:2]
+    out[2] = held[jnp.where(up, 3, 2)]
+    out[3:7] = jnp.where(up, near[0:4], far[...])
 
 
 Y2_B = 84
@@ -227,64 +285,67 @@
 Y2_ROWS = 192
 
 
-def coarse_a(ab, r3lo, r3hi, r4lo, r4hi, c):
-    if c < -4:
-        return r4lo.at[c + 10]
-    if c < -2:
-        return r4lo.at[c + 4]
-    if c < 0:
-        return r3lo.at[c + 2]
-    if c < 2:
-        return ab.at[c]
-    if c < 4:
-        return r3hi.at[c - 2]
-    if c < 6:
-        return r4hi.at[c - 4]
-    return r4hi.at[c - 2]
-
-
-def coarse_b(ab, r3lo, r3hi, r4lo, r4hi, c):
-    if c == -5:
-        return r4lo.at[6]
-    if c < -2:
-        return r4lo.at[c + 6]
-    if c < 0:
-        return r3lo.at[c + 4]
-    if c < 2:
-        return ab.at[c + 2]
-    if c < 4:
-        return r3hi.at[c]
-    if c < 6:
-        return r4hi.at[c - 2]
-    return r4hi.at[6]
-
-
-def pack_y2(ab, u, r3lo, r3hi, r4lo, r4hi, up, down):
-    for out, top in ((up, True), (down, False)):
-        first = CROWS - 6 if top else 0
-        for k in range(14):
-            plane = coarse_a(ab, r3lo, r3hi, r4lo, r4hi, k - 6)
-            out[6 * k : 6 * k + 6, :] = plane[first : first + 6, :]
-        for k in range(12):
-            plane = coarse_b(ab, r3lo, r3hi, r4lo, r4hi, k - 5)
-            out[Y2_B + 6 * k : Y2_B + 6 * k + 6, :] = plane[first : first + 6, :]
+def pack_y2(
+    ab, u, plus1, minus1, plus2, minus2, plus3, minus3, near, far, up, down, dom, edge
+):
+    first, z = place()
+
+    def below(plus, minus, k):
+        return jnp.where(first, plus[k], minus[k])
+
+    def above(plus, minus, k):
+        return jnp.where(first, minus[k], plus[k])
+
+    def choose(value, *ends):
+        for at, other in ends:
+            value = jnp.where(z == at, other, value)
+        return value
+
+    top = LINE - 1
+    for k in range(4):
+        a = k < 2
+        dom[6 + k if a else 17 + k] = ab[k]
+        dom[4 + k if a else 15 + k] = choose(below(plus1, minus1, k), (0, near[k]))
+        dom[8 + k if a else 19 + k] = choose(above(plus1, minus1, k), (top, near[k]))
+        dom[2 + k if a else 13 + k] = choose(
+            below(plus2, minus2, k), (0, far[k]), (1, below(plus3, minus3, 3 + k))
+        )
+        dom[10 + k if a else 21 + k] = choose(
+            above(plus2, minus2, k), (top, below(plus3, minus3, 3 + k)), (top - 1, far[k])
+        )
+        edge[k] = choose(below(plus1, minus1, 4 + k), (0, near[4 + k]))
+        edge[4 + k] = choose(above(plus1, minus1, 4 + k), (top, near[4 + k]))
+    for k in range(3):
+        low = 3 if k == 2 else k
+        dom[14 if k == 2 else k] = choose(
+            below(plus3, minus3, k),
+            (0, above(plus3, minus3, 3 + low)), (1, near[low]), (2, far[low]),
+        )
+        dom[25 if k == 2 else 12 + k] = choose(
+            above(plus3, minus3, k),
+            (top, far[k]), (top - 1, near[k]), (top - 2, above(plus3, minus3, 3 + k)),
+        )
+    for out, top_rows in ((up, True), (down, False)):
+        row = CROWS - 6 if top_rows else 0
+        for k in range(26):
+            out[6 * k : 6 * k + 6, :] = dom[k, row : row + 6, :]
         for k in range(8):
             at = Y2_U + 4 * k
             for half in range(2):
                 if 0 < k < 7:
-                    row = 34 if top else 4
+                    row = 34 if top_rows else 4
                     rows = u[k - 1, row : row + 2, CCOLS * half : CCOLS * half + CCOLS]
                 else:
-                    edge = r3lo if k == 0 else r3hi
-                    if top:
-                        rows = edge[6 + half, 14:16, :]
+                    piece = (0 if k == 0 else 4) + half
+                    if top_rows:
+                        rows = edge[piece + 2, 14:16, :]
                     else:
-                        rows = edge[4 + half, 0:2, :]
+                        rows = edge[piece, 0:2, :]
                 out[at + 2 * half : at + 2 * half + 2, :] = rows
 
 
 def post_kernel(
-    masks, t_in, a_in, b_in, u_in, ct, ab, r3lo, r3hi, r4lo, r4hi, ylo, yhi,
+    masks, t_in, a_in, b_in, u_in, ct, dom, edge, ylo, yhi,
     out, uf, cf, xs, ff,
 ):
     mlo = masks[0]
@@ -293,14 +354,10 @@
     a = []
     b = [None]
     for k in range(26):
-        if k < 14:
-            own = coarse_a(ab, r3lo, r3hi, r4lo, r4hi, k - 6)
-        else:
-            own = coarse_b(ab, r3lo, r3hi, r4lo, r4hi, k - 19)
         ff[k, 0:8, :] = tile
         ff[k, 24:32, :] = tile
         ff[k, 2:8, :] = ylo[6 * k : 6 * k + 6, :] * mlo
-        ff[k, 8:24, :] = own[...]
+        ff[k, 8:24, :] = dom[k]
         ff[k, 24:30, :] = yhi[6 * k : 6 * k + 6, :] * mhi
         (a if k < 14 else b).append(ff[k])
     link = [0.5] * 13
@@ -340,11 +397,11 @@
             uf[k] = u_in[k - 1]
         else:
             uf[k] = zeros
-            edge = r3lo if k == 0 else r3hi
+            piece = 0 if k == 0 else 4
             for j in range(4):
                 row = 4 + 16 * (j // 2)
                 lane = CCOLS * (j % 2)
-                uf[k, row : row + 16, lane : lane + CCOLS] = edge[4 + j]
+                uf[k, row : row + 16, lane : lane + CCOLS] = edge[piece + j]
         at = Y2_U + 4 * k
         for half in range(2):
             lane = CCOLS * half
@@ -391,20 +448,47 @@
     )
 
 
+def pre_call(*operands):
+    return call(
+        pre_kernel,
+        [SM] + [VM] * 10,
+        (
+            f32(8, FR, COLS), f32(6, FR, COLS), f32(6, FR, COLS), f32(6, FR, COLS),
+            f32(4, CR, CCOLS), f32(4, CROWS, CCOLS),
+            f32(8, CROWS, CCOLS), f32(8, CROWS, CCOLS), f32(8, CROWS, CCOLS),
+        ),
+        (
+            (10, FR, COLS), (8, FR, COLS), (8, FR, COLS),
+            (10, FR, COLS), (8, FR, COLS), (4, FR, COLS), (4, FR, CCOLS),
+        ),
+    )(*operands)
+
+
+def post_call(*operands):
+    return call(
+        post_kernel,
+        [SM] + [VM] * 9,
+        f32(4, ROWS, COLS),
+        ((8, FR, COLS), (8, FR, CCOLS), (8, FR, COLS), (26, CR, CCOLS)),
+    )(*operands)
+
+
 def on_device(pressure_rhs, permeability, accumulation, coarse_perm, coarse_accum, run_lengths):
-    up, down = call(
+    message = f32(Z1_ROWS, COLS)
+    plus, minus, across = call(
         pack_z1,
         [HBM] * 4,
-        (f32(Z1_ROWS, COLS), f32(Z1_ROWS, COLS)),
-        (pltpu.VMEM((2, CROWS, CCOLS), jnp.float32), pltpu.SemaphoreType.DMA((15,))),
+        (message, message, message),
+        (pltpu.VMEM((2, CROWS, CCOLS), jnp.float32), pltpu.SemaphoreType.DMA((22,))),
     )(
         *(
             pltpu.with_memory_space_constraint(x, pltpu.HBM)
             for x in (pressure_rhs, permeability, accumulation, coarse_perm)
         )
     )
-    lo = shifted(up, "slab", 1)
-    hi = shifted(down, "slab", -1)
+    across = between_lines(across, ((0, LINE - 1),))
+    plus = along_lines(plus, 1)
+    minus = along_lines(minus, -1)
 
     slab = lax.axis_index("slab")
     pen = lax.axis_index("pen")
@@ -418,44 +502,35 @@
         ]
     )
 
-    up, down = call(
-        pack_y1, [VM] * 6, (f32(Y1_ROWS, COLS), f32(Y1_ROWS, COLS))
-    )(pressure_rhs, permeability, accumulation, coarse_perm, lo, hi)
+    rows = f32(Y1_ROWS, COLS)
+    up, down = call(pack_y1, [VM] * 7, (rows, rows))(
+        pressure_rhs, permeability, accumulation, coarse_perm, plus, minus, across
+    )
     ylo = rotated(up, "pen", 1)
     yhi = rotated(down, "pen", -1)
 
-    t, a, b, u, ct, ab, zup, zdn = call(
-        pre_kernel,
-        [SM] + [VM] * 9,
-        (
-            f32(8, FR, COLS), f32(6, FR, COLS), f32(6, FR, COLS), f32(6, FR, COLS),
-            f32(4, CR, CCOLS), f32(4, CROWS, CCOLS),
-            f32(8, CROWS, CCOLS), f32(8, CROWS, CCOLS),
-        ),
-        (
-            (10, FR, COLS), (8, FR, COLS), (8, FR, COLS),
-            (10, FR, COLS), (8, FR, COLS), (4, FR, COLS), (4, FR, CCOLS),
-        ),
-    )(masks, pressure_rhs, permeability, accumulation, coarse_perm, coarse_accum, lo, hi, ylo, yhi)
-    r3lo = shifted(zup, "slab", 1)
-    r3hi = shifted(zdn, "slab", -1)
-
-    further = f32(7, CROWS, CCOLS)
-    r4lo = shifted(call(pack_up2, [VM] * 2, further)(ab, r3lo), "slab", 2)
-    r4hi = shifted(call(pack_down2, [VM] * 2, further)(ab, r3hi), "slab", -2)
-
-    up, down = call(
-        pack_y2, [VM] * 6, (f32(Y2_ROWS, CCOLS), f32(Y2_ROWS, CCOLS))
-    )(ab, u, r3lo, r3hi, r4lo, r4hi)
+    t, a, b, u, ct, ab, plus, minus, across = pre_call(
+        masks, pressure_rhs, permeability, accumulation, coarse_perm, coarse_accum,
+        plus, minus, across, ylo, yhi,
+    )
+    near = between_lines(across, ((0, LINE - 1), (1, LINE - 2)))
+    far = between_lines(ab, ((0, LINE - 2), (1, LINE - 3), (2, LINE - 1)))
+    plus1 = along_lines(plus, 1)
+    minus1 = along_lines(minus, -1)
+    plus2 = along_lines(plus1[0:4], 1)
+    minus2 = along_lines(minus1[0:4], -1)
+    third = f32(7, CROWS, CCOLS)
+    plus3 = along_lines(call(pack_plus3, [VM] * 3, third)(plus2, near, far), 1)
+    minus3 = along_lines(call(pack_minus3, [VM] * 3, third)(minus2, near, far), -1)
+
+    rows = f32(Y2_ROWS, CCOLS)
+    up, down, dom, edge = call(
+        pack_y2, [VM] * 10, (rows, rows, f32(26, CROWS, CCOLS), f32(8, CROWS, CCOLS))
+    )(ab, u, plus1, minus1, plus2, minus2, plus3, minus3, near, far)
     ylo = rotated(up, "pen", 1)
     yhi = rotated(down, "pen", -1)
 
-    return call(
-        post_kernel,
-        [SM] + [VM] * 12,
-        f32(4, ROWS, COLS),
-        ((8, FR, COLS), (8, FR, CCOLS), (8, FR, COLS), (26, CR, CCOLS)),
-    )(masks, t, a, b, u, ct, ab, r3lo, r3hi, r4lo, r4hi, ylo, yhi)
+    return post_call(masks, t, a, b, u, ct, dom, edge, ylo, yhi)
 
 
 def solution(mesh):

time: 55.5 us -> 58.8 us (1.059)
  starting transfers between devices: 32.4 us -> 34.2 us
  waiting for transfers between devices: 15.7 us -> 16.9 us
    ppermute x4, starting transfers between devices: 2.65 us -> 6.82 us  [rotated(): lax.ppermute(x, axis, [(i, (i + by) % devices) for i in range(devices)])]
    ppermute x6 -> x11, starting transfers between devices: 29.7 us -> 27.4 us  [the longest x3 18.4 us: between_lines(): return lax.ppermute(x, ('slab', 'pen'), pairs)]
    ppermute x6 -> x11, waiting for transfers between devices: 5.78 us -> 7.03 us  [the longest x3 5.51 us: between_lines(): return lax.ppermute(x, ('slab', 'pen'), pairs)]
  transfers between devices with their start and end apart: 10 -> 15, of which waited for: 8 -> 7; matrix products, arithmetic and copies ran while one was open for 1% -> 1% of each run, Pallas kernels for 0% -> 0%
where the time goes in v4:
time: 58.8 us; the launch traced here: 58.6 us
  starting transfers between devices  34.2 us (58%)
  waiting for transfers between devices  16.9 us (29%)
  Pallas kernels  6 us (10%)
  local copies, waits for them, and re-layouts  0.77 us (1%)
    ppermute x3, starting transfers between devices, between_lines(): return lax.ppermute(x, ('slab', 'pen'), pairs)  18.4 us
    ppermute x4, waiting for transfers between devices, rotated(): lax.ppermute(x, axis, [(i, (i + by) % devices) for i in range(devices)])  9.88 us
    ppermute x8, starting transfers between devices, along_lines(): return lax.ppermute(x, ('slab', 'pen'), pairs)  8.95 us
    ppermute x4, starting transfers between devices, rotated(): lax.ppermute(x, axis, [(i, (i + by) % devices) for i in range(devices)])  6.82 us
    ppermute x3, waiting for transfers between devices, between_lines(): return lax.ppermute(x, ('slab', 'pen'), pairs)  5.51 us
    pallas_call x1, Pallas kernels, post_call(): call(post_kernel, [SM] + [VM] * 9, f32(4, ROWS, COLS), ((8, FR, COLS), (8...  2.65 us
    pallas_call x1, Pallas kernels, pre_call(): call(pre_kernel, [SM] + [VM] * 10, (f32(8, FR, COLS), f32(6, FR, COLS), f...  1.89 us
    ppermute x8, waiting for transfers between devices, along_lines(): return lax.ppermute(x, ('slab', 'pen'), pairs)  1.52 us
  transfers between devices with their start and end apart: 15, of which 7 were waited for; matrix products, arithmetic and copies ran while one was open for 1% of the time, Pallas kernels for 0%

profile of v4, /device:TPU:31, one launch (start us, length us, event | category | flops | bytes accessed | tf_op | source)
XLA Modules:
  0.0 58.6 jit_solution(12748334707966496878)
XLA Ops:
  0.0 0.0 copy-start
  0.0 0.0 copy-start.1
  0.0 0.0 copy-start.2
  0.0 1.3 %shard_map.64 = (f32[232,256]{1,0:T(8,128)S(1)}, f32[232,256]{1,0:T(8,128)S(1)}, f32[232,256]{1,0:T(8,128)S(1)}) custom-call(f32[4,32,256]{2,1,0:T(8,128)} %rhs.6, f32[4,32,256]{2,1,0:T(8,128)} %perm.5, f32[4,32,256]{2,1,0:T(8,128)} %acc.5, f32[2,16,128]{2,1,0:T(8,128)} %cperm.5), custom_call_target="tpu_custom_call" | custom-call | tf_op jit(solution)/shard_map/pallas_call | solution.py:478
  1.3 0.7 %collective-permute-start = (f32[232,256]{1,0:T(8,128)S(1)}, f32[232,256]{1,0:T(8,128)S(1)}, u32[]{:S(2)}, u32[]{:S(2)}) collective-permute-start(f32[232,256]{1,0:T(8,128)S(1)} %get-tuple-element.23), channel_id=1, source_target_pairs={{0,8},{1,0},{2,10},{3,2},{4,12},{5,4},{6,14},{7,6},{8,16},{9,1},{1... | collective-permute-start | bytes 712712 | tf_op jit(solution)/shard_map/ppermute | solution.py:34
  2.0 1.0 %collective-permute-start.1 = (f32[232,256]{1,0:T(8,128)S(1)}, f32[232,256]{1,0:T(8,128)S(1)}, u32[]{:S(2)}, u32[]{:S(2)}) collective-permute-start(f32[232,256]{1,0:T(8,128)S(1)} %get-tuple-element.24), channel_id=1, source_target_pairs={{0,1},{1,9},{2,3},{3,11},{4,5},{5,13},{6,7},{7,15},{8,0},{9,17},{1... | collective-permute-start | bytes 712712 | tf_op jit(solution)/shard_map/ppermute | solution.py:34
  3.0 10.4 %collective-permute-start.2 = (f32[232,256]{1,0:T(8,128)S(1)}, f32[232,256]{1,0:T(8,128)S(1)}, u32[]{:S(2)}, u32[]{:S(2)}) collective-permute-start(f32[232,256]{1,0:T(8,128)S(1)} %get-tuple-element.25), channel_id=1, source_target_pairs={{128,120},{120,128},{129,121},{121,129},{130,122},{122,130},{131,1... | collective-permute-start | bytes 712712 | tf_op jit(solution)/shard_map/ppermute | solution.py:46
  13.5 0.0 copy-start.5
  13.5 0.6 %copy-done.5 = s32[32]{0:T(128)S(1)} copy-done((s32[32]{0:T(128)S(1)}, s32[32]{0:T(128)}, u32[]{:S(2)}) %copy-start.5) | copy-done | bytes 152
  14.1 0.1 copy.9
  14.2 0.1 reduce-window.9
  14.3 0.0 copy-start.3
  14.3 0.1 reduce
  14.4 0.2 compare_reduce_fusion
  14.6 0.1 add_convert_fusion
  14.7 0.0 collective-permute-done.plus
  14.7 0.0 collective-permute-done.1.minus
  14.7 2.9 %collective-permute-done.2.across = f32[232,256]{1,0:T(8,128)S(1)} collective-permute-done((f32[232,256]{1,0:T(8,128)S(1)}, f32[232,256]{1,0:T(8,128)S(1)}, u32[]{:S(2)}, u32[]{:S(2)}) %collective-permute-start.2) | collective-permute-done | bytes 237600 | tf_op jit(solution)/shard_map/ppermute | solution.py:46
  17.6 0.0 copy-done
  17.6 0.0 copy-done.1
  17.6 0.0 copy-done.2
  17.6 0.0 copy-done.3
  17.6 0.0 copy-start.4
  17.6 0.1 shard_map.65
  17.7 2.5 %collective-permute-start.3 = (f32[64,256]{1,0:T(8,128)S(1)}, f32[64,256]{1,0:T(8,128)S(1)}, u32[]{:S(2)}, u32[]{:S(2)}) collective-permute-start(f32[64,256]{1,0:T(8,128)S(1)} %get-tuple-element.26), channel_id=1, source_target_pairs={{0,1},{1,2},{2,3},{3,4},{4,5},{5,6},{6,7},{7,0},{8,9},{9,10},{10,1... | collective-permute-start | bytes 196616 | tf_op jit(solution)/shard_map/ppermute | solution.py:73
  20.1 0.2 collective-permute-start.4
  20.3 0.1 pad_maximum_fusion.masks
  20.4 1.1 %collective-permute-done.3.ylo = f32[64,256]{1,0:T(8,128)S(1)} collective-permute-done((f32[64,256]{1,0:T(8,128)S(1)}, f32[64,256]{1,0:T(8,128)S(1)}, u32[]{:S(2)}, u32[]{:S(2)}) %collective-permute-start.3) | collective-permute-done | bytes 65568 | tf_op jit(solution)/shard_map/ppermute | solution.py:73
  21.5 3.6 %collective-permute-done.4.yhi = f32[64,256]{1,0:T(8,128)S(1)} collective-permute-done((f32[64,256]{1,0:T(8,128)S(1)}, f32[64,256]{1,0:T(8,128)S(1)}, u32[]{:S(2)}, u32[]{:S(2)}) %collective-permute-start.4) | collective-permute-done | bytes 65568 | tf_op jit(solution)/shard_map/ppermute | solution.py:73
  25.0 0.0 copy-done.4
  25.0 1.9 %shard_map.66 = (f32[8,40,256]{2,1,0:T(8,128)S(1)}, f32[6,40,256]{2,1,0:T(8,128)S(1)}, f32[6,40,256]{2,1,0:T(8,128)S(1)}, f32[6,40,256]{2,1,0:T(8,128)S(1)}, f32...) custom-call(f32[8]{0:T(128)S(1)} %pad_maximum_fusion.masks, ...), custom_call_target="tpu_custom_call" | custom-call | tf_op jit(solution)/shard_map/pallas_call | solution.py:452
  26.9 0.0 collective-permute-start.5
  27.0 1.5 %collective-permute-start.6 = (f32[8,16,128]{2,1,0:T(8,128)S(1)}, f32[8,16,128]{2,1,0:T(8,128)S(1)}, u32[]{:S(2)}, u32[]{:S(2)}) collective-permute-start(f32[8,16,128]{2,1,0:T(8,128)S(1)} %get-tuple-element.35), channel_id=1, source_target_pairs={{0,1},{1,9},{2,3},{3,11},{4,5},{5,13},{6,7},{7,15},{8,0},{9,17},{1... | collective-permute-start | bytes 196616 | tf_op jit(solution)/shard_map/ppermute | solution.py:34
  28.4 4.5 %collective-permute-start.9 = (f32[8,16,128]{2,1,0:T(8,128)S(1)}, f32[8,16,128]{2,1,0:T(8,128)S(1)}, u32[]{:S(2)}, u32[]{:S(2)}) collective-permute-start(f32[8,16,128]{2,1,0:T(8,128)S(1)} %get-tuple-element.36), channel_id=1, source_target_pairs={{128,120},{120,128},{129,121},{121,129},{130,122},{122,130},{131,1... | collective-permute-start | bytes 196616 | tf_op jit(solution)/shard_map/ppermute | solution.py:46
  32.9 3.5 %collective-permute-start.10 = (f32[4,16,128]{2,1,0:T(8,128)S(1)}, f32[4,16,128]{2,1,0:T(8,128)S(1)}, u32[]{:S(2)}, u32[]{:S(2)}) collective-permute-start(f32[4,16,128]{2,1,0:T(8,128)S(1)} %get-tuple-element.33.ab), channel_id=1, source_target_pairs={{128,112},{112,128},{129,113},{113,129},{130,114},{114,130},{131,1... | collective-permute-start | bytes 98312 | tf_op jit(solution)/shard_map/ppermute | solution.py:46
  36.4 0.0 collective-permute-done.5.plus1
  36.4 0.0 collective-permute-start.7
  36.5 0.0 collective-permute-done.6.minus1
  36.5 1.5 %collective-permute-start.8 = (f32[4,16,128]{2,1,0:T(8,128)S(1)}, f32[4,16,128]{2,1,0:T(8,128)S(1)}, u32[]{:S(2)}, u32[]{:S(2)}) collective-permute-start(f32[4,16,128]{2,1,0:T(8,128)S(1)} %slice.9), channel_id=1, source_target_pairs={{0,1},{1,9},{2,3},{3,11},{4,5},{5,13},{6,7},{7,15},{8,0},{9,17},{1... | collective-permute-start | bytes 98312 | tf_op jit(solution)/shard_map/ppermute | solution.py:34
  38.0 2.6 %collective-permute-done.10.far = f32[4,16,128]{2,1,0:T(8,128)S(1)} collective-permute-done((f32[4,16,128]{2,1,0:T(8,128)S(1)}, f32[4,16,128]{2,1,0:T(8,128)S(1)}, u32[]{:S(2)}, u32[]{:S(2)}) %collective-permute-start.10) | collective-permute-done | bytes 32800 | tf_op jit(solution)/shard_map/ppermute | solution.py:46
  40.6 0.0 collective-permute-done.9.near
  40.6 0.0 collective-permute-done.7.held.plus2
  40.6 1.9 %collective-permute-start.11 = (f32[7,16,128]{2,1,0:T(8,128)S(1)}, f32[7,16,128]{2,1,0:T(8,128)S(1)}, u32[]{:S(2)}, u32[]{:S(2)}) collective-permute-start(f32[7,16,128]{2,1,0:T(8,128)S(1)} %shard_map.67), channel_id=1, source_target_pairs={{0,8},{1,0},{2,10},{3,2},{4,12},{5,4},{6,14},{7,6},{8,16},{9,1},{1... | collective-permute-start | bytes 172040 | tf_op jit(solution)/shard_map/ppermute | solution.py:34
  42.5 0.0 collective-permute-done.8.held.minus2
  42.6 2.4 %collective-permute-start.12 = (f32[7,16,128]{2,1,0:T(8,128)S(1)}, f32[7,16,128]{2,1,0:T(8,128)S(1)}, u32[]{:S(2)}, u32[]{:S(2)}) collective-permute-start(f32[7,16,128]{2,1,0:T(8,128)S(1)} %shard_map.68), channel_id=1, source_target_pairs={{0,1},{1,9},{2,3},{3,11},{4,5},{5,13},{6,7},{7,15},{8,0},{9,17},{1... | collective-permute-start | bytes 172040 | tf_op jit(solution)/shard_map/ppermute | solution.py:34
  44.9 1.5 %collective-permute-done.11.plus3 = f32[7,16,128]{2,1,0:T(8,128)S(1)} collective-permute-done((f32[7,16,128]{2,1,0:T(8,128)S(1)}, f32[7,16,128]{2,1,0:T(8,128)S(1)}, u32[]{:S(2)}, u32[]{:S(2)}) %collective-permute-start.11) | collective-permute-done | bytes 57376 | tf_op jit(solution)/shard_map/ppermute | solution.py:34
  46.4 0.0 collective-permute-done.12.minus3
  46.4 0.1 shard_map.69
  46.5 4.2 %collective-permute-start.13 = (f32[192,128]{1,0:T(8,128)S(1)}, f32[192,128]{1,0:T(8,128)S(1)}, u32[]{:S(2)}, u32[]{:S(2)}) collective-permute-start(f32[192,128]{1,0:T(8,128)S(1)} %get-tuple-element.39), channel_id=1, source_target_pairs={{0,1},{1,2},{2,3},{3,4},{4,5},{5,6},{6,7},{7,0},{8,9},{9,10},{10,1... | collective-permute-start | bytes 294920 | tf_op jit(solution)/shard_map/ppermute | solution.py:73
  50.7 0.0 collective-permute-start.14
  50.7 1.6 %collective-permute-done.13.ylo = f32[192,128]{1,0:T(8,128)S(1)} collective-permute-done((f32[192,128]{1,0:T(8,128)S(1)}, f32[192,128]{1,0:T(8,128)S(1)}, u32[]{:S(2)}, u32[]{:S(2)}) %collective-permute-start.13) | collective-permute-done | bytes 98336 | tf_op jit(solution)/shard_map/ppermute | solution.py:73
  52.3 3.6 %collective-permute-done.14.yhi = f32[192,128]{1,0:T(8,128)S(1)} collective-permute-done((f32[192,128]{1,0:T(8,128)S(1)}, f32[192,128]{1,0:T(8,128)S(1)}, u32[]{:S(2)}, u32[]{:S(2)}) %collective-permute-start.14) | collective-permute-done | bytes 98336 | tf_op jit(solution)/shard_map/ppermute | solution.py:73
  55.9 2.6 %shard_map.70 = f32[4,32,256]{2,1,0:T(8,128)} custom-call(f32[8]{0:T(128)S(1)} %pad_maximum_fusion.masks, f32[8,40,256]{2,1,0:T(8,128)S(1)} %get-tuple-element.28.t_in, f32[6,40,256]{2,1,0:T(8,128)S(1)} %get-tuple-element.29.a_in, f32[6,40,256]{2,1,0:T(8,128)S(1)} %get-tuple-element.30.b_in, f32[6,40,256]{2,1,0:T(8,128)S(1)} %get-tuple-element.31.u.u_in, ...), custom_call_target="tpu_custom_call" | custom-call | tf_op jit(solution)/shard_map/pallas_call | solution.py:468
  (7 shorter events, 0.0 us)
Async XLA Ops:
  0.0 17.6 %copy-start = (f32[4,32,256]{2,1,0:T(8,128)S(1)}, f32[4,32,256]{2,1,0:T(8,128)}, u32[]{:S(2)}) copy-start(f32[4,32,256]{2,1,0:T(8,128)} %rhs.6) | copy-start | bytes 393220
  0.0 17.6 %copy-start.1 = (f32[4,32,256]{2,1,0:T(8,128)S(1)}, f32[4,32,256]{2,1,0:T(8,128)}, u32[]{:S(2)}) copy-start(f32[4,32,256]{2,1,0:T(8,128)} %perm.5) | copy-start | bytes 393220
  0.0 17.6 %copy-start.2 = (f32[4,32,256]{2,1,0:T(8,128)S(1)}, f32[4,32,256]{2,1,0:T(8,128)}, u32[]{:S(2)}) copy-start(f32[4,32,256]{2,1,0:T(8,128)} %acc.5) | copy-start | bytes 393220
  1.3 13.3 %collective-permute-start = (f32[232,256]{1,0:T(8,128)S(1)}, f32[232,256]{1,0:T(8,128)S(1)}, u32[]{:S(2)}, u32[]{:S(2)}) collective-permute-start(f32[232,256]{1,0:T(8,128)S(1)} %get-tuple-element.23), channel_id=1, source_target_pairs={{0,8},{1,0},{2,10},{3,2},{4,12},{5,4},{6,14},{7,6},{8,16},{9,1},{1... | collective-permute-start | bytes 712712 | tf_op jit(solution)/shard_map/ppermute | solution.py:34
  2.0 12.7 %collective-permute-start.1 = (f32[232,256]{1,0:T(8,128)S(1)}, f32[232,256]{1,0:T(8,128)S(1)}, u32[]{:S(2)}, u32[]{:S(2)}) collective-permute-start(f32[232,256]{1,0:T(8,128)S(1)} %get-tuple-element.24), channel_id=1, source_target_pairs={{0,1},{1,9},{2,3},{3,11},{4,5},{5,13},{6,7},{7,15},{8,0},{9,17},{1... | collective-permute-start | bytes 712712 | tf_op jit(solution)/shard_map/ppermute | solution.py:34
  3.0 14.5 %collective-permute-start.2 = (f32[232,256]{1,0:T(8,128)S(1)}, f32[232,256]{1,0:T(8,128)S(1)}, u32[]{:S(2)}, u32[]{:S(2)}) collective-permute-start(f32[232,256]{1,0:T(8,128)S(1)} %get-tuple-element.25), channel_id=1, source_target_pairs={{128,120},{120,128},{129,121},{121,129},{130,122},{122,130},{131,1... | collective-permute-start | bytes 712712 | tf_op jit(solution)/shard_map/ppermute | solution.py:46
  13.5 0.7 %copy-start.5 = (s32[32]{0:T(128)S(1)}, s32[32]{0:T(128)}, u32[]{:S(2)}) copy-start(s32[32]{0:T(128)} %param.11) | copy-start | bytes 388
  14.3 3.3 %copy-start.3 = (f32[2,16,128]{2,1,0:T(8,128)S(1)}, f32[2,16,128]{2,1,0:T(8,128)}, u32[]{:S(2)}) copy-start(f32[2,16,128]{2,1,0:T(8,128)} %cperm.5) | copy-start | bytes 49156
  17.6 7.4 %copy-start.4 = (f32[2,16,128]{2,1,0:T(8,128)S(1)}, f32[2,16,128]{2,1,0:T(8,128)}, u32[]{:S(2)}) copy-start(f32[2,16,128]{2,1,0:T(8,128)} %cacc.1) | copy-start | bytes 49156
  17.7 3.8 %collective-permute-start.3 = (f32[64,256]{1,0:T(8,128)S(1)}, f32[64,256]{1,0:T(8,128)S(1)}, u32[]{:S(2)}, u32[]{:S(2)}) collective-permute-start(f32[64,256]{1,0:T(8,128)S(1)} %get-tuple-element.26), channel_id=1, source_target_pairs={{0,1},{1,2},{2,3},{3,4},{4,5},{5,6},{6,7},{7,0},{8,9},{9,10},{10,1... | collective-permute-start | bytes 196616 | tf_op jit(solution)/shard_map/ppermute | solution.py:73
  20.1 4.9 %collective-permute-start.4 = (f32[64,256]{1,0:T(8,128)S(1)}, f32[64,256]{1,0:T(8,128)S(1)}, u32[]{:S(2)}, u32[]{:S(2)}) collective-permute-start(f32[64,256]{1,0:T(8,128)S(1)} %get-tuple-element.27), channel_id=1, source_target_pairs={{0,7},{1,0},{2,1},{3,2},{4,3},{5,4},{6,5},{7,6},{8,15},{9,8},{10,9... | collective-permute-start | bytes 196616 | tf_op jit(solution)/shard_map/ppermute | solution.py:73
  26.9 9.5 %collective-permute-start.5 = (f32[8,16,128]{2,1,0:T(8,128)S(1)}, f32[8,16,128]{2,1,0:T(8,128)S(1)}, u32[]{:S(2)}, u32[]{:S(2)}) collective-permute-start(f32[8,16,128]{2,1,0:T(8,128)S(1)} %get-tuple-element.34), channel_id=1, source_target_pairs={{0,8},{1,0},{2,10},{3,2},{4,12},{5,4},{6,14},{7,6},{8,16},{9,1},{1... | collective-permute-start | bytes 196616 | tf_op jit(solution)/shard_map/ppermute | solution.py:34
  27.0 9.5 %collective-permute-start.6 = (f32[8,16,128]{2,1,0:T(8,128)S(1)}, f32[8,16,128]{2,1,0:T(8,128)S(1)}, u32[]{:S(2)}, u32[]{:S(2)}) collective-permute-start(f32[8,16,128]{2,1,0:T(8,128)S(1)} %get-tuple-element.35), channel_id=1, source_target_pairs={{0,1},{1,9},{2,3},{3,11},{4,5},{5,13},{6,7},{7,15},{8,0},{9,17},{1... | collective-permute-start | bytes 196616 | tf_op jit(solution)/shard_map/ppermute | solution.py:34
  28.4 12.2 %collective-permute-start.9 = (f32[8,16,128]{2,1,0:T(8,128)S(1)}, f32[8,16,128]{2,1,0:T(8,128)S(1)}, u32[]{:S(2)}, u32[]{:S(2)}) collective-permute-start(f32[8,16,128]{2,1,0:T(8,128)S(1)} %get-tuple-element.36), channel_id=1, source_target_pairs={{128,120},{120,128},{129,121},{121,129},{130,122},{122,130},{131,1... | collective-permute-start | bytes 196616 | tf_op jit(solution)/shard_map/ppermute | solution.py:46
  32.9 7.7 %collective-permute-start.10 = (f32[4,16,128]{2,1,0:T(8,128)S(1)}, f32[4,16,128]{2,1,0:T(8,128)S(1)}, u32[]{:S(2)}, u32[]{:S(2)}) collective-permute-start(f32[4,16,128]{2,1,0:T(8,128)S(1)} %get-tuple-element.33.ab), channel_id=1, source_target_pairs={{128,112},{112,128},{129,113},{113,129},{130,114},{114,130},{131,1... | collective-permute-start | bytes 98312 | tf_op jit(solution)/shard_map/ppermute | solution.py:46
  36.4 4.1 %collective-permute-start.7 = (f32[4,16,128]{2,1,0:T(8,128)S(1)}, f32[4,16,128]{2,1,0:T(8,128)S(1)}, u32[]{:S(2)}, u32[]{:S(2)}) collective-permute-start(f32[4,16,128]{2,1,0:T(8,128)S(1)} %slice.8), channel_id=1, source_target_pairs={{0,8},{1,0},{2,10},{3,2},{4,12},{5,4},{6,14},{7,6},{8,16},{9,1},{1... | collective-permute-start | bytes 98312 | tf_op jit(solution)/shard_map/ppermute | solution.py:34
  36.5 6.1 %collective-permute-start.8 = (f32[4,16,128]{2,1,0:T(8,128)S(1)}, f32[4,16,128]{2,1,0:T(8,128)S(1)}, u32[]{:S(2)}, u32[]{:S(2)}) collective-permute-start(f32[4,16,128]{2,1,0:T(8,128)S(1)} %slice.9), channel_id=1, source_target_pairs={{0,1},{1,9},{2,3},{3,11},{4,5},{5,13},{6,7},{7,15},{8,0},{9,17},{1... | collective-permute-start | bytes 98312 | tf_op jit(solution)/shard_map/ppermute | solution.py:34
  40.6 5.8 %collective-permute-start.11 = (f32[7,16,128]{2,1,0:T(8,128)S(1)}, f32[7,16,128]{2,1,0:T(8,128)S(1)}, u32[]{:S(2)}, u32[]{:S(2)}) collective-permute-start(f32[7,16,128]{2,1,0:T(8,128)S(1)} %shard_map.67), channel_id=1, source_target_pairs={{0,8},{1,0},{2,10},{3,2},{4,12},{5,4},{6,14},{7,6},{8,16},{9,1},{1... | collective-permute-start | bytes 172040 | tf_op jit(solution)/shard_map/ppermute | solution.py:34
  42.6 3.9 %collective-permute-start.12 = (f32[7,16,128]{2,1,0:T(8,128)S(1)}, f32[7,16,128]{2,1,0:T(8,128)S(1)}, u32[]{:S(2)}, u32[]{:S(2)}) collective-permute-start(f32[7,16,128]{2,1,0:T(8,128)S(1)} %shard_map.68), channel_id=1, source_target_pairs={{0,1},{1,9},{2,3},{3,11},{4,5},{5,13},{6,7},{7,15},{8,0},{9,17},{1... | collective-permute-start | bytes 172040 | tf_op jit(solution)/shard_map/ppermute | solution.py:34
  46.5 5.8 %collective-permute-start.13 = (f32[192,128]{1,0:T(8,128)S(1)}, f32[192,128]{1,0:T(8,128)S(1)}, u32[]{:S(2)}, u32[]{:S(2)}) collective-permute-start(f32[192,128]{1,0:T(8,128)S(1)} %get-tuple-element.39), channel_id=1, source_target_pairs={{0,1},{1,2},{2,3},{3,4},{4,5},{5,6},{6,7},{7,0},{8,9},{9,10},{10,1... | collective-permute-start | bytes 294920 | tf_op jit(solution)/shard_map/ppermute | solution.py:73
  50.7 5.3 %collective-permute-start.14 = (f32[192,128]{1,0:T(8,128)S(1)}, f32[192,128]{1,0:T(8,128)S(1)}, u32[]{:S(2)}, u32[]{:S(2)}) collective-permute-start(f32[192,128]{1,0:T(8,128)S(1)} %get-tuple-element.40), channel_id=1, source_target_pairs={{0,7},{1,0},{2,1},{3,2},{4,3},{5,4},{6,5},{7,6},{8,15},{9,8},{10,9... | collective-permute-start | bytes 294920 | tf_op jit(solution)/shard_map/ppermute | solution.py:73

commit v5 on v4

--- a/solution.py
+++ b/solution.py
@@ -15,6 +15,12 @@
 CR = 32
 CROWS = 16
 CCOLS = 128
+
+
+def shifted(x, axis, by):
+    devices = lax.axis_size(axis)
+    pairs = [(i, i + by) for i in range(devices) if 0 <= i + by < devices]
+    return lax.ppermute(x, axis, pairs)
 
 
 LINE = 16
@@ -34,14 +40,14 @@
     return lax.ppermute(x, ("slab", "pen"), pairs)
 
 
-def between_lines(x, partners):
+def between_lines(x, by):
     slabs, pens = lax.axis_size("slab"), lax.axis_size("pen")
     pairs = []
-    for line in range(1, slabs // LINE):
-        for j, k in partners:
+    for source in range(slabs):
+        target = source + by
+        if 0 <= target < slabs and source // LINE != target // LINE:
             for pen in range(pens):
-                here = (line * LINE + j) * pens + pen
-                there = ((line - 1) * LINE + k) * pens + pen
+                here, there = source * pens + pen, target * pens + pen
                 pairs += [(here, there), (there, here)]
     return lax.ppermute(x, ("slab", "pen"), pairs)
 
@@ -60,11 +66,11 @@
         return jnp.where(end, across[index], value)
 
 
-def below_above(plus, minus, across):
+def below_above(plus, minus, rising, falling):
     first, z = place()
     return (
-        Picked(first, plus, minus, z == 0, across),
-        Picked(first, minus, plus, z == LINE - 1, across),
+        Picked(first, plus, minus, z == 0, rising),
+        Picked(first, minus, plus, z == LINE - 1, falling),
     )
 
 
@@ -146,8 +152,8 @@
 Y1_ROWS = 64
 
 
-def pack_y1(rhs, perm, acc, cperm, plus, minus, across, up, down):
-    lo, hi = below_above(plus, minus, across)
+def pack_y1(rhs, perm, acc, cperm, plus, minus, rising, falling, up, down):
+    lo, hi = below_above(plus, minus, rising, falling)
     for out, top in ((up, True), (down, False)):
         r3 = ROWS - 3 if top else 0
         r2 = ROWS - 2 if top else 0
@@ -167,12 +173,12 @@
 
 
 def pre_kernel(
-    masks, rhs, perm, acc, cperm, cacc, plus, minus, across, ylo, yhi,
+    masks, rhs, perm, acc, cperm, cacc, plus, minus, rising, falling, ylo, yhi,
     t_out, a_out, b_out, u_out, ct_out, ab_out, plus_out, minus_out, across_out,
     ts, rs, cs, xs, us, ds, fs,
 ):
     first, place_z = place()
-    lo, hi = below_above(plus, minus, across)
+    lo, hi = below_above(plus, minus, rising, falling)
     mlo = masks[0]
     mhi = masks[1]
     zeros = jnp.zeros((FR, COLS), jnp.float32)
@@ -266,18 +272,13 @@
             out[4 + k] = u_out[plane, row : row + 16, lane : lane + CCOLS]
 
 
-def pack_plus3(held, near, far, out):
-    pack_third(place()[0], held, near, far, out)
-
-
-def pack_minus3(held, near, far, out):
-    pack_third(jnp.logical_not(place()[0]), held, near, far, out)
-
-
-def pack_third(up, held, near, far, out):
-    out[0:2] = held[0:2]
-    out[2] = held[jnp.where(up, 3, 2)]
-    out[3:7] = jnp.where(up, near[0:4], far[...])
+def pack_second(ab, plus1, minus1, rising1, falling1, up, down):
+    lo, hi = below_above(plus1, minus1, rising1, falling1)
+    up[0:4] = ab[...]
+    up[4:6] = lo[0:2]
+    up[6] = lo[3]
+    down[0:4] = ab[...]
+    down[4:7] = hi[0:3]
 
 
 Y2_B = 84
@@ -286,45 +287,21 @@
 
 
 def pack_y2(
-    ab, u, plus1, minus1, plus2, minus2, plus3, minus3, near, far, up, down, dom, edge
+    ab, u, plus1, minus1, rising1, falling1, lo2, hi2, up, down, dom, edge
 ):
-    first, z = place()
-
-    def below(plus, minus, k):
-        return jnp.where(first, plus[k], minus[k])
-
-    def above(plus, minus, k):
-        return jnp.where(first, minus[k], plus[k])
-
-    def choose(value, *ends):
-        for at, other in ends:
-            value = jnp.where(z == at, other, value)
-        return value
-
-    top = LINE - 1
+    lo, hi = below_above(plus1, minus1, rising1, falling1)
     for k in range(4):
         a = k < 2
         dom[6 + k if a else 17 + k] = ab[k]
-        dom[4 + k if a else 15 + k] = choose(below(plus1, minus1, k), (0, near[k]))
-        dom[8 + k if a else 19 + k] = choose(above(plus1, minus1, k), (top, near[k]))
-        dom[2 + k if a else 13 + k] = choose(
-            below(plus2, minus2, k), (0, far[k]), (1, below(plus3, minus3, 3 + k))
-        )
-        dom[10 + k if a else 21 + k] = choose(
-            above(plus2, minus2, k), (top, below(plus3, minus3, 3 + k)), (top - 1, far[k])
-        )
-        edge[k] = choose(below(plus1, minus1, 4 + k), (0, near[4 + k]))
-        edge[4 + k] = choose(above(plus1, minus1, 4 + k), (top, near[4 + k]))
+        dom[4 + k if a else 15 + k] = lo[k]
+        dom[8 + k if a else 19 + k] = hi[k]
+        dom[2 + k if a else 13 + k] = lo2[k]
+        dom[10 + k if a else 21 + k] = hi2[k]
+        edge[k] = lo[4 + k]
+        edge[4 + k] = hi[4 + k]
     for k in range(3):
-        low = 3 if k == 2 else k
-        dom[14 if k == 2 else k] = choose(
-            below(plus3, minus3, k),
-            (0, above(plus3, minus3, 3 + low)), (1, near[low]), (2, far[low]),
-        )
-        dom[25 if k == 2 else 12 + k] = choose(
-            above(plus3, minus3, k),
-            (top, far[k]), (top - 1, near[k]), (top - 2, above(plus3, minus3, 3 + k)),
-        )
+        dom[14 if k == 2 else k] = lo2[4 + k]
+        dom[25 if k == 2 else 12 + k] = hi2[4 + k]
     for out, top_rows in ((up, True), (down, False)):
         row = CROWS - 6 if top_rows else 0
         for k in range(26):
@@ -451,7 +428,7 @@
 def pre_call(*operands):
     return call(
         pre_kernel,
-        [SM] + [VM] * 10,
+        [SM] + [VM] * 11,
         (
             f32(8, FR, COLS), f32(6, FR, COLS), f32(6, FR, COLS), f32(6, FR, COLS),
             f32(4, CR, CCOLS), f32(4, CROWS, CCOLS),
@@ -486,7 +463,7 @@
             for x in (pressure_rhs, permeability, accumulation, coarse_perm)
         )
     )
-    across = between_lines(across, ((0, LINE - 1),))
+    falling = rising = between_lines(across, 1)
     plus = along_lines(plus, 1)
     minus = along_lines(minus, -1)
 
@@ -503,30 +480,28 @@
     )
 
     rows = f32(Y1_ROWS, COLS)
-    up, down = call(pack_y1, [VM] * 7, (rows, rows))(
-        pressure_rhs, permeability, accumulation, coarse_perm, plus, minus, across
+    up, down = call(pack_y1, [VM] * 8, (rows, rows))(
+        pressure_rhs, permeability, accumulation, coarse_perm, plus, minus, rising, falling
     )
     ylo = rotated(up, "pen", 1)
     yhi = rotated(down, "pen", -1)
 
     t, a, b, u, ct, ab, plus, minus, across = pre_call(
         masks, pressure_rhs, permeability, accumulation, coarse_perm, coarse_accum,
-        plus, minus, across, ylo, yhi,
-    )
-    near = between_lines(across, ((0, LINE - 1), (1, LINE - 2)))
-    far = between_lines(ab, ((0, LINE - 2), (1, LINE - 3), (2, LINE - 1)))
-    plus1 = along_lines(plus, 1)
-    minus1 = along_lines(minus, -1)
-    plus2 = along_lines(plus1[0:4], 1)
-    minus2 = along_lines(minus1[0:4], -1)
-    third = f32(7, CROWS, CCOLS)
-    plus3 = along_lines(call(pack_plus3, [VM] * 3, third)(plus2, near, far), 1)
-    minus3 = along_lines(call(pack_minus3, [VM] * 3, third)(minus2, near, far), -1)
+        plus, minus, rising, falling, ylo, yhi,
+    )
+    falling = rising = between_lines(across, 1)
+    plus = along_lines(plus, 1)
+    minus = along_lines(minus, -1)
+    second = f32(7, CROWS, CCOLS)
+    up, down = call(pack_second, [VM] * 5, (second, second))(ab, plus, minus, rising, falling)
+    lo2 = shifted(up, "slab", 2)
+    hi2 = shifted(down, "slab", -2)
 
     rows = f32(Y2_ROWS, CCOLS)
     up, down, dom, edge = call(
-        pack_y2, [VM] * 10, (rows, rows, f32(26, CROWS, CCOLS), f32(8, CROWS, CCOLS))
-    )(ab, u, plus1, minus1, plus2, minus2, plus3, minus3, near, far)
+        pack_y2, [VM] * 8, (rows, rows, f32(26, CROWS, CCOLS), f32(8, CROWS, CCOLS))
+    )(ab, u, plus, minus, rising, falling, lo2, hi2)
     ylo = rotated(up, "pen", 1)
     yhi = rotated(down, "pen", -1)
 

time: 58.8 us -> 56.3 us (0.957)
  starting transfers between devices: 34.2 us -> 31.7 us
    ppermute x0 -> x2, starting transfers between devices: none -> 8.29 us  [shifted(): return lax.ppermute(x, axis, pairs)]
    ppermute x8 -> x4, starting transfers between devices: 8.95 us -> 3.16 us  [along_lines(): return lax.ppermute(x, ('slab', 'pen'), pairs)]
    ppermute x3 -> x2, starting transfers between devices: 18.4 us -> 14.9 us  [between_lines(): return lax.ppermute(x, ('slab', 'pen'), pairs)]
    ppermute x8 -> x4, waiting for transfers between devices: 1.52 us -> 0.01 us  [along_lines(): return lax.ppermute(x, ('slab', 'pen'), pairs)]
    ppermute x4, starting transfers between devices: 6.82 us -> 5.34 us  [rotated(): lax.ppermute(x, axis, [(i, (i + by) % devices) for i in range(devices)])]
    ppermute x0 -> x2, waiting for transfers between devices: none -> 1.23 us  [shifted(): return lax.ppermute(x, axis, pairs)]
    ppermute x3 -> x2, waiting for transfers between devices: 5.51 us -> 5.86 us  [between_lines(): return lax.ppermute(x, ('slab', 'pen'), pairs)]
    pallas_call x5 -> x4, Pallas kernels: 2.04 us -> 2.03 us  [the longest x1 1.89 us: pre_call(): call(pre_kernel, [SM] + [VM] * 11, (f32(8, FR, COLS), f32(6, FR, COLS), f...]
  transfers between devices with their start and end apart: 15 -> 12, of which waited for: 7 -> 8; matrix products, arithmetic and copies ran while one was open for 1% -> 1% of each run, Pallas kernels for 0% -> 0%
where the time goes in v5:
time: 56.3 us; the launch traced here: 56.1 us
  starting transfers between devices  31.7 us (56%)
  waiting for transfers between devices  17 us (30%)
  Pallas kernels  5.99 us (11%)
  local copies, waits for them, and re-layouts  0.76 us (1%)
    ppermute x2, starting transfers between devices, between_lines(): return lax.ppermute(x, ('slab', 'pen'), pairs)  14.9 us
    ppermute x4, waiting for transfers between devices, rotated(): lax.ppermute(x, axis, [(i, (i + by) % devices) for i in range(devices)])  9.88 us
    ppermute x2, starting transfers between devices, shifted(): return lax.ppermute(x, axis, pairs)  8.29 us
    ppermute x2, waiting for transfers between devices, between_lines(): return lax.ppermute(x, ('slab', 'pen'), pairs)  5.86 us
    ppermute x4, starting transfers between devices, rotated(): lax.ppermute(x, axis, [(i, (i + by) % devices) for i in range(devices)])  5.34 us
    ppermute x4, starting transfers between devices, along_lines(): return lax.ppermute(x, ('slab', 'pen'), pairs)  3.16 us
    pallas_call x1, Pallas kernels, post_call(): call(post_kernel, [SM] + [VM] * 9, f32(4, ROWS, COLS), ((8, FR, COLS), (8...  2.65 us
    pallas_call x1, Pallas kernels, pre_call(): call(pre_kernel, [SM] + [VM] * 11, (f32(8, FR, COLS), f32(6, FR, COLS), f...  1.89 us
  transfers between devices with their start and end apart: 12, of which 8 were waited for; matrix products, arithmetic and copies ran while one was open for 1% of the time, Pallas kernels for 0%

profile of v5, /device:TPU:31, one launch (start us, length us, event | category | flops | bytes accessed | tf_op | source)
XLA Modules:
  0.0 56.1 jit_solution(17867481810187929406)
XLA Ops:
  0.0 0.0 copy-start
  0.0 0.0 copy-start.1
  0.0 0.0 copy-start.2
  0.0 1.3 %shard_map.64 = (f32[232,256]{1,0:T(8,128)S(1)}, f32[232,256]{1,0:T(8,128)S(1)}, f32[232,256]{1,0:T(8,128)S(1)}) custom-call(f32[4,32,256]{2,1,0:T(8,128)} %rhs.6, f32[4,32,256]{2,1,0:T(8,128)} %perm.5, f32[4,32,256]{2,1,0:T(8,128)} %acc.5, f32[2,16,128]{2,1,0:T(8,128)} %cperm.5), custom_call_target="tpu_custom_call" | custom-call | tf_op jit(solution)/shard_map/pallas_call | solution.py:455
  1.3 0.7 %collective-permute-start = (f32[232,256]{1,0:T(8,128)S(1)}, f32[232,256]{1,0:T(8,128)S(1)}, u32[]{:S(2)}, u32[]{:S(2)}) collective-permute-start(f32[232,256]{1,0:T(8,128)S(1)} %get-tuple-element.25), channel_id=1, source_target_pairs={{0,8},{1,0},{2,10},{3,2},{4,12},{5,4},{6,14},{7,6},{8,16},{9,1},{1... | collective-permute-start | bytes 712712 | tf_op jit(solution)/shard_map/ppermute | solution.py:40
  2.0 1.0 %collective-permute-start.1 = (f32[232,256]{1,0:T(8,128)S(1)}, f32[232,256]{1,0:T(8,128)S(1)}, u32[]{:S(2)}, u32[]{:S(2)}) collective-permute-start(f32[232,256]{1,0:T(8,128)S(1)} %get-tuple-element.26), channel_id=1, source_target_pairs={{0,1},{1,9},{2,3},{3,11},{4,5},{5,13},{6,7},{7,15},{8,0},{9,17},{1... | collective-permute-start | bytes 712712 | tf_op jit(solution)/shard_map/ppermute | solution.py:40
  3.0 10.4 %collective-permute-start.2 = (f32[232,256]{1,0:T(8,128)S(1)}, f32[232,256]{1,0:T(8,128)S(1)}, u32[]{:S(2)}, u32[]{:S(2)}) collective-permute-start(f32[232,256]{1,0:T(8,128)S(1)} %get-tuple-element.27), channel_id=1, source_target_pairs={{120,128},{128,120},{121,129},{129,121},{122,130},{130,122},{123,1... | collective-permute-start | bytes 712712 | tf_op jit(solution)/shard_map/ppermute | solution.py:52
  13.5 0.0 copy-start.5
  13.5 0.6 %copy-done.5 = s32[32]{0:T(128)S(1)} copy-done((s32[32]{0:T(128)S(1)}, s32[32]{0:T(128)}, u32[]{:S(2)}) %copy-start.5) | copy-done | bytes 152
  14.1 0.1 copy.9
  14.2 0.1 reduce-window.9
  14.3 0.0 copy-start.3
  14.3 0.1 reduce
  14.4 0.2 compare_reduce_fusion
  14.6 0.1 add_convert_fusion
  14.7 0.0 collective-permute-done.plus
  14.7 0.0 collective-permute-done.1.minus
  14.7 2.9 %collective-permute-done.2.rising.falling = f32[232,256]{1,0:T(8,128)S(1)} collective-permute-done((f32[232,256]{1,0:T(8,128)S(1)}, f32[232,256]{1,0:T(8,128)S(1)}, u32[]{:S(2)}, u32[]{:S(2)}) %collective-permute-start.2) | collective-permute-done | bytes 237600 | tf_op jit(solution)/shard_map/ppermute | solution.py:52
  17.6 0.0 copy-done
  17.6 0.0 copy-done.1
  17.6 0.0 copy-done.2
  17.6 0.0 copy-done.3
  17.6 0.0 copy-start.4
  17.6 0.1 shard_map.65
  17.7 2.5 %collective-permute-start.3 = (f32[64,256]{1,0:T(8,128)S(1)}, f32[64,256]{1,0:T(8,128)S(1)}, u32[]{:S(2)}, u32[]{:S(2)}) collective-permute-start(f32[64,256]{1,0:T(8,128)S(1)} %get-tuple-element.28), channel_id=1, source_target_pairs={{0,1},{1,2},{2,3},{3,4},{4,5},{5,6},{6,7},{7,0},{8,9},{9,10},{10,1... | collective-permute-start | bytes 196616 | tf_op jit(solution)/shard_map/ppermute | solution.py:79
  20.1 0.2 collective-permute-start.4
  20.3 0.1 pad_maximum_fusion.masks
  20.4 1.1 %collective-permute-done.3.ylo = f32[64,256]{1,0:T(8,128)S(1)} collective-permute-done((f32[64,256]{1,0:T(8,128)S(1)}, f32[64,256]{1,0:T(8,128)S(1)}, u32[]{:S(2)}, u32[]{:S(2)}) %collective-permute-start.3) | collective-permute-done | bytes 65568 | tf_op jit(solution)/shard_map/ppermute | solution.py:79
  21.5 3.6 %collective-permute-done.4.yhi = f32[64,256]{1,0:T(8,128)S(1)} collective-permute-done((f32[64,256]{1,0:T(8,128)S(1)}, f32[64,256]{1,0:T(8,128)S(1)}, u32[]{:S(2)}, u32[]{:S(2)}) %collective-permute-start.4) | collective-permute-done | bytes 65568 | tf_op jit(solution)/shard_map/ppermute | solution.py:79
  25.0 0.0 copy-done.4
  25.0 1.9 %shard_map.66 = (f32[8,40,256]{2,1,0:T(8,128)S(1)}, f32[6,40,256]{2,1,0:T(8,128)S(1)}, f32[6,40,256]{2,1,0:T(8,128)S(1)}, f32[6,40,256]{2,1,0:T(8,128)S(1)}, f32...) custom-call(f32[8]{0:T(128)S(1)} %pad_maximum_fusion.masks, ...), custom_call_target="tpu_custom_call" | custom-call | tf_op jit(solution)/shard_map/pallas_call | solution.py:429
  26.9 0.0 collective-permute-start.5
  27.0 1.5 %collective-permute-start.6 = (f32[8,16,128]{2,1,0:T(8,128)S(1)}, f32[8,16,128]{2,1,0:T(8,128)S(1)}, u32[]{:S(2)}, u32[]{:S(2)}) collective-permute-start(f32[8,16,128]{2,1,0:T(8,128)S(1)} %get-tuple-element.37), channel_id=1, source_target_pairs={{0,1},{1,9},{2,3},{3,11},{4,5},{5,13},{6,7},{7,15},{8,0},{9,17},{1... | collective-permute-start | bytes 196616 | tf_op jit(solution)/shard_map/ppermute | solution.py:40
  28.4 4.5 %collective-permute-start.7 = (f32[8,16,128]{2,1,0:T(8,128)S(1)}, f32[8,16,128]{2,1,0:T(8,128)S(1)}, u32[]{:S(2)}, u32[]{:S(2)}) collective-permute-start(f32[8,16,128]{2,1,0:T(8,128)S(1)} %get-tuple-element.38), channel_id=1, source_target_pairs={{120,128},{128,120},{121,129},{129,121},{122,130},{130,122},{123,1... | collective-permute-start | bytes 196616 | tf_op jit(solution)/shard_map/ppermute | solution.py:52
  32.9 0.0 collective-permute-done.5.plus1
  32.9 0.0 collective-permute-done.6.minus1
  32.9 3.0 %collective-permute-done.7.rising1.falling1 = f32[8,16,128]{2,1,0:T(8,128)S(1)} collective-permute-done((f32[8,16,128]{2,1,0:T(8,128)S(1)}, f32[8,16,128]{2,1,0:T(8,128)S(1)}, u32[]{:S(2)}, u32[]{:S(2)}) %collective-permute-start.7) | collective-permute-done | bytes 65568 | tf_op jit(solution)/shard_map/ppermute | solution.py:52
  36.0 1.9 %collective-permute-start.8 = (f32[7,16,128]{2,1,0:T(8,128)S(1)}, f32[7,16,128]{2,1,0:T(8,128)S(1)}, u32[]{:S(2)}, u32[]{:S(2)}) collective-permute-start(f32[7,16,128]{2,1,0:T(8,128)S(1)} %get-tuple-element.39), channel_id=1, source_target_pairs={{0,16},{8,24},{16,32},{24,40},{32,48},{40,56},{48,64},{56,72},{64,... | collective-permute-start | bytes 172040 | tf_op jit(solution)/shard_map/ppermute | solution.py:23
  37.9 6.4 %collective-permute-start.9 = (f32[7,16,128]{2,1,0:T(8,128)S(1)}, f32[7,16,128]{2,1,0:T(8,128)S(1)}, u32[]{:S(2)}, u32[]{:S(2)}) collective-permute-start(f32[7,16,128]{2,1,0:T(8,128)S(1)} %get-tuple-element.40), channel_id=1, source_target_pairs={{16,0},{24,8},{32,16},{40,24},{48,32},{56,40},{64,48},{72,56},{80,... | collective-permute-start | bytes 172040 | tf_op jit(solution)/shard_map/ppermute | solution.py:23
  44.3 0.5 collective-permute-done.8.lo2
  44.8 0.7 %collective-permute-done.9.hi2 = f32[7,16,128]{2,1,0:T(8,128)S(1)} collective-permute-done((f32[7,16,128]{2,1,0:T(8,128)S(1)}, f32[7,16,128]{2,1,0:T(8,128)S(1)}, u32[]{:S(2)}, u32[]{:S(2)}) %collective-permute-start.9) | collective-permute-done | bytes 57376 | tf_op jit(solution)/shard_map/ppermute | solution.py:23
  45.5 0.1 shard_map.68
  45.6 2.7 %collective-permute-start.10 = (f32[192,128]{1,0:T(8,128)S(1)}, f32[192,128]{1,0:T(8,128)S(1)}, u32[]{:S(2)}, u32[]{:S(2)}) collective-permute-start(f32[192,128]{1,0:T(8,128)S(1)} %get-tuple-element.43), channel_id=1, source_target_pairs={{0,1},{1,2},{2,3},{3,4},{4,5},{5,6},{6,7},{7,0},{8,9},{9,10},{10,1... | collective-permute-start | bytes 294920 | tf_op jit(solution)/shard_map/ppermute | solution.py:79
  48.2 0.0 collective-permute-start.11
  48.2 1.6 %collective-permute-done.10.ylo = f32[192,128]{1,0:T(8,128)S(1)} collective-permute-done((f32[192,128]{1,0:T(8,128)S(1)}, f32[192,128]{1,0:T(8,128)S(1)}, u32[]{:S(2)}, u32[]{:S(2)}) %collective-permute-start.10) | collective-permute-done | bytes 98336 | tf_op jit(solution)/shard_map/ppermute | solution.py:79
  49.9 3.6 %collective-permute-done.11.yhi = f32[192,128]{1,0:T(8,128)S(1)} collective-permute-done((f32[192,128]{1,0:T(8,128)S(1)}, f32[192,128]{1,0:T(8,128)S(1)}, u32[]{:S(2)}, u32[]{:S(2)}) %collective-permute-start.11) | collective-permute-done | bytes 98336 | tf_op jit(solution)/shard_map/ppermute | solution.py:79
  53.5 2.6 %shard_map.69 = f32[4,32,256]{2,1,0:T(8,128)} custom-call(f32[8]{0:T(128)S(1)} %pad_maximum_fusion.masks, f32[8,40,256]{2,1,0:T(8,128)S(1)} %get-tuple-element.30.t_in, f32[6,40,256]{2,1,0:T(8,128)S(1)} %get-tuple-element.31.a_in, f32[6,40,256]{2,1,0:T(8,128)S(1)} %get-tuple-element.32.b_in, f32[6,40,256]{2,1,0:T(8,128)S(1)} %get-tuple-element.33.u.u_in, ...), custom_call_target="tpu_custom_call" | custom-call | tf_op jit(solution)/shard_map/pallas_call | solution.py:445
  (4 shorter events, 0.0 us)
Async XLA Ops:
  0.0 17.6 %copy-start = (f32[4,32,256]{2,1,0:T(8,128)S(1)}, f32[4,32,256]{2,1,0:T(8,128)}, u32[]{:S(2)}) copy-start(f32[4,32,256]{2,1,0:T(8,128)} %rhs.6) | copy-start | bytes 393220
  0.0 17.6 %copy-start.1 = (f32[4,32,256]{2,1,0:T(8,128)S(1)}, f32[4,32,256]{2,1,0:T(8,128)}, u32[]{:S(2)}) copy-start(f32[4,32,256]{2,1,0:T(8,128)} %perm.5) | copy-start | bytes 393220
  0.0 17.6 %copy-start.2 = (f32[4,32,256]{2,1,0:T(8,128)S(1)}, f32[4,32,256]{2,1,0:T(8,128)}, u32[]{:S(2)}) copy-start(f32[4,32,256]{2,1,0:T(8,128)} %acc.5) | copy-start | bytes 393220
  1.3 13.3 %collective-permute-start = (f32[232,256]{1,0:T(8,128)S(1)}, f32[232,256]{1,0:T(8,128)S(1)}, u32[]{:S(2)}, u32[]{:S(2)}) collective-permute-start(f32[232,256]{1,0:T(8,128)S(1)} %get-tuple-element.25), channel_id=1, source_target_pairs={{0,8},{1,0},{2,10},{3,2},{4,12},{5,4},{6,14},{7,6},{8,16},{9,1},{1... | collective-permute-start | bytes 712712 | tf_op jit(solution)/shard_map/ppermute | solution.py:40
  2.0 12.7 %collective-permute-start.1 = (f32[232,256]{1,0:T(8,128)S(1)}, f32[232,256]{1,0:T(8,128)S(1)}, u32[]{:S(2)}, u32[]{:S(2)}) collective-permute-start(f32[232,256]{1,0:T(8,128)S(1)} %get-tuple-element.26), channel_id=1, source_target_pairs={{0,1},{1,9},{2,3},{3,11},{4,5},{5,13},{6,7},{7,15},{8,0},{9,17},{1... | collective-permute-start | bytes 712712 | tf_op jit(solution)/shard_map/ppermute | solution.py:40
  3.0 14.5 %collective-permute-start.2 = (f32[232,256]{1,0:T(8,128)S(1)}, f32[232,256]{1,0:T(8,128)S(1)}, u32[]{:S(2)}, u32[]{:S(2)}) collective-permute-start(f32[232,256]{1,0:T(8,128)S(1)} %get-tuple-element.27), channel_id=1, source_target_pairs={{120,128},{128,120},{121,129},{129,121},{122,130},{130,122},{123,1... | collective-permute-start | bytes 712712 | tf_op jit(solution)/shard_map/ppermute | solution.py:52
  13.5 0.7 %copy-start.5 = (s32[32]{0:T(128)S(1)}, s32[32]{0:T(128)}, u32[]{:S(2)}) copy-start(s32[32]{0:T(128)} %param.11) | copy-start | bytes 388
  14.3 3.3 %copy-start.3 = (f32[2,16,128]{2,1,0:T(8,128)S(1)}, f32[2,16,128]{2,1,0:T(8,128)}, u32[]{:S(2)}) copy-start(f32[2,16,128]{2,1,0:T(8,128)} %cperm.5) | copy-start | bytes 49156
  17.6 7.4 %copy-start.4 = (f32[2,16,128]{2,1,0:T(8,128)S(1)}, f32[2,16,128]{2,1,0:T(8,128)}, u32[]{:S(2)}) copy-start(f32[2,16,128]{2,1,0:T(8,128)} %cacc.1) | copy-start | bytes 49156
  17.7 3.8 %collective-permute-start.3 = (f32[64,256]{1,0:T(8,128)S(1)}, f32[64,256]{1,0:T(8,128)S(1)}, u32[]{:S(2)}, u32[]{:S(2)}) collective-permute-start(f32[64,256]{1,0:T(8,128)S(1)} %get-tuple-element.28), channel_id=1, source_target_pairs={{0,1},{1,2},{2,3},{3,4},{4,5},{5,6},{6,7},{7,0},{8,9},{9,10},{10,1... | collective-permute-start | bytes 196616 | tf_op jit(solution)/shard_map/ppermute | solution.py:79
  20.1 4.9 %collective-permute-start.4 = (f32[64,256]{1,0:T(8,128)S(1)}, f32[64,256]{1,0:T(8,128)S(1)}, u32[]{:S(2)}, u32[]{:S(2)}) collective-permute-start(f32[64,256]{1,0:T(8,128)S(1)} %get-tuple-element.29), channel_id=1, source_target_pairs={{0,7},{1,0},{2,1},{3,2},{4,3},{5,4},{6,5},{7,6},{8,15},{9,8},{10,9... | collective-permute-start | bytes 196616 | tf_op jit(solution)/shard_map/ppermute | solution.py:79
  26.9 6.0 %collective-permute-start.5 = (f32[8,16,128]{2,1,0:T(8,128)S(1)}, f32[8,16,128]{2,1,0:T(8,128)S(1)}, u32[]{:S(2)}, u32[]{:S(2)}) collective-permute-start(f32[8,16,128]{2,1,0:T(8,128)S(1)} %get-tuple-element.36), channel_id=1, source_target_pairs={{0,8},{1,0},{2,10},{3,2},{4,12},{5,4},{6,14},{7,6},{8,16},{9,1},{1... | collective-permute-start | bytes 196616 | tf_op jit(solution)/shard_map/ppermute | solution.py:40
  27.0 6.0 %collective-permute-start.6 = (f32[8,16,128]{2,1,0:T(8,128)S(1)}, f32[8,16,128]{2,1,0:T(8,128)S(1)}, u32[]{:S(2)}, u32[]{:S(2)}) collective-permute-start(f32[8,16,128]{2,1,0:T(8,128)S(1)} %get-tuple-element.37), channel_id=1, source_target_pairs={{0,1},{1,9},{2,3},{3,11},{4,5},{5,13},{6,7},{7,15},{8,0},{9,17},{1... | collective-permute-start | bytes 196616 | tf_op jit(solution)/shard_map/ppermute | solution.py:40
  28.4 7.5 %collective-permute-start.7 = (f32[8,16,128]{2,1,0:T(8,128)S(1)}, f32[8,16,128]{2,1,0:T(8,128)S(1)}, u32[]{:S(2)}, u32[]{:S(2)}) collective-permute-start(f32[8,16,128]{2,1,0:T(8,128)S(1)} %get-tuple-element.38), channel_id=1, source_target_pairs={{120,128},{128,120},{121,129},{129,121},{122,130},{130,122},{123,1... | collective-permute-start | bytes 196616 | tf_op jit(solution)/shard_map/ppermute | solution.py:52
  36.0 8.8 %collective-permute-start.8 = (f32[7,16,128]{2,1,0:T(8,128)S(1)}, f32[7,16,128]{2,1,0:T(8,128)S(1)}, u32[]{:S(2)}, u32[]{:S(2)}) collective-permute-start(f32[7,16,128]{2,1,0:T(8,128)S(1)} %get-tuple-element.39), channel_id=1, source_target_pairs={{0,16},{8,24},{16,32},{24,40},{32,48},{40,56},{48,64},{56,72},{64,... | collective-permute-start | bytes 172040 | tf_op jit(solution)/shard_map/ppermute | solution.py:23
  37.9 7.6 %collective-permute-start.9 = (f32[7,16,128]{2,1,0:T(8,128)S(1)}, f32[7,16,128]{2,1,0:T(8,128)S(1)}, u32[]{:S(2)}, u32[]{:S(2)}) collective-permute-start(f32[7,16,128]{2,1,0:T(8,128)S(1)} %get-tuple-element.40), channel_id=1, source_target_pairs={{16,0},{24,8},{32,16},{40,24},{48,32},{56,40},{64,48},{72,56},{80,... | collective-permute-start | bytes 172040 | tf_op jit(solution)/shard_map/ppermute | solution.py:23
  45.6 4.3 %collective-permute-start.10 = (f32[192,128]{1,0:T(8,128)S(1)}, f32[192,128]{1,0:T(8,128)S(1)}, u32[]{:S(2)}, u32[]{:S(2)}) collective-permute-start(f32[192,128]{1,0:T(8,128)S(1)} %get-tuple-element.43), channel_id=1, source_target_pairs={{0,1},{1,2},{2,3},{3,4},{4,5},{5,6},{6,7},{7,0},{8,9},{9,10},{10,1... | collective-permute-start | bytes 294920 | tf_op jit(solution)/shard_map/ppermute | solution.py:79
  48.2 5.3 %collective-permute-start.11 = (f32[192,128]{1,0:T(8,128)S(1)}, f32[192,128]{1,0:T(8,128)S(1)}, u32[]{:S(2)}, u32[]{:S(2)}) collective-permute-start(f32[192,128]{1,0:T(8,128)S(1)} %get-tuple-element.44), channel_id=1, source_target_pairs={{0,7},{1,0},{2,1},{3,2},{4,3},{5,4},{6,5},{7,6},{8,15},{9,8},{10,9... | collective-permute-start | bytes 294920 | tf_op jit(solution)/shard_map/ppermute | solution.py:79

commit v6 on v4

--- a/solution.py
+++ b/solution.py
@@ -34,14 +34,13 @@
     return lax.ppermute(x, ("slab", "pen"), pairs)
 
 
-def between_lines(x, partners):
+def between_lines(x, apart):
     slabs, pens = lax.axis_size("slab"), lax.axis_size("pen")
     pairs = []
-    for line in range(1, slabs // LINE):
-        for j, k in partners:
+    for low in range(slabs - apart):
+        if low // LINE != (low + apart) // LINE:
             for pen in range(pens):
-                here = (line * LINE + j) * pens + pen
-                there = ((line - 1) * LINE + k) * pens + pen
+                here, there = low * pens + pen, (low + apart) * pens + pen
                 pairs += [(here, there), (there, here)]
     return lax.ppermute(x, ("slab", "pen"), pairs)
 
@@ -266,18 +265,11 @@
             out[4 + k] = u_out[plane, row : row + 16, lane : lane + CCOLS]
 
 
-def pack_plus3(held, near, far, out):
-    pack_third(place()[0], held, near, far, out)
-
-
-def pack_minus3(held, near, far, out):
-    pack_third(jnp.logical_not(place()[0]), held, near, far, out)
-
-
-def pack_third(up, held, near, far, out):
-    out[0:2] = held[0:2]
-    out[2] = held[jnp.where(up, 3, 2)]
-    out[3:7] = jnp.where(up, near[0:4], far[...])
+def pack_far(ab, plus1, minus1, out):
+    first, z = place()
+    near_start = z < LINE // 2
+    out[0:4] = ab[...]
+    out[4:8] = jnp.where(first == near_start, plus1[0:4], minus1[0:4])
 
 
 Y2_B = 84
@@ -286,45 +278,29 @@
 
 
 def pack_y2(
-    ab, u, plus1, minus1, plus2, minus2, plus3, minus3, near, far, up, down, dom, edge
+    ab, u, plus1, minus1, across, plus2, minus2, plus3, minus3, far, up, down, dom, edge
 ):
     first, z = place()
 
-    def below(plus, minus, k):
-        return jnp.where(first, plus[k], minus[k])
-
-    def above(plus, minus, k):
-        return jnp.where(first, minus[k], plus[k])
-
-    def choose(value, *ends):
-        for at, other in ends:
-            value = jnp.where(z == at, other, value)
-        return value
-
-    top = LINE - 1
+    def below(plus, minus, k, places, other):
+        return jnp.where(z < places, other, jnp.where(first, plus[k], minus[k]))
+
+    def above(plus, minus, k, places, other):
+        return jnp.where(z >= LINE - places, other, jnp.where(first, minus[k], plus[k]))
+
     for k in range(4):
         a = k < 2
         dom[6 + k if a else 17 + k] = ab[k]
-        dom[4 + k if a else 15 + k] = choose(below(plus1, minus1, k), (0, near[k]))
-        dom[8 + k if a else 19 + k] = choose(above(plus1, minus1, k), (top, near[k]))
-        dom[2 + k if a else 13 + k] = choose(
-            below(plus2, minus2, k), (0, far[k]), (1, below(plus3, minus3, 3 + k))
-        )
-        dom[10 + k if a else 21 + k] = choose(
-            above(plus2, minus2, k), (top, below(plus3, minus3, 3 + k)), (top - 1, far[k])
-        )
-        edge[k] = choose(below(plus1, minus1, 4 + k), (0, near[4 + k]))
-        edge[4 + k] = choose(above(plus1, minus1, 4 + k), (top, near[4 + k]))
+        dom[4 + k if a else 15 + k] = below(plus1, minus1, k, 1, across[k])
+        dom[8 + k if a else 19 + k] = above(plus1, minus1, k, 1, across[k])
+        dom[2 + k if a else 13 + k] = below(plus2, minus2, k, 2, far[4 + k])
+        dom[10 + k if a else 21 + k] = above(plus2, minus2, k, 2, far[4 + k])
+        edge[k] = below(plus1, minus1, 4 + k, 1, across[4 + k])
+        edge[4 + k] = above(plus1, minus1, 4 + k, 1, across[4 + k])
     for k in range(3):
         low = 3 if k == 2 else k
-        dom[14 if k == 2 else k] = choose(
-            below(plus3, minus3, k),
-            (0, above(plus3, minus3, 3 + low)), (1, near[low]), (2, far[low]),
-        )
-        dom[25 if k == 2 else 12 + k] = choose(
-            above(plus3, minus3, k),
-            (top, far[k]), (top - 1, near[k]), (top - 2, above(plus3, minus3, 3 + k)),
-        )
+        dom[14 if k == 2 else k] = below(plus3, minus3, low, 3, far[low])
+        dom[25 if k == 2 else 12 + k] = above(plus3, minus3, k, 3, far[k])
     for out, top_rows in ((up, True), (down, False)):
         row = CROWS - 6 if top_rows else 0
         for k in range(26):
@@ -486,7 +462,7 @@
             for x in (pressure_rhs, permeability, accumulation, coarse_perm)
         )
     )
-    across = between_lines(across, ((0, LINE - 1),))
+    across = between_lines(across, 1)
     plus = along_lines(plus, 1)
     minus = along_lines(minus, -1)
 
@@ -513,20 +489,21 @@
         masks, pressure_rhs, permeability, accumulation, coarse_perm, coarse_accum,
         plus, minus, across, ylo, yhi,
     )
-    near = between_lines(across, ((0, LINE - 1), (1, LINE - 2)))
-    far = between_lines(ab, ((0, LINE - 2), (1, LINE - 3), (2, LINE - 1)))
+    across = between_lines(across, 1)
     plus1 = along_lines(plus, 1)
     minus1 = along_lines(minus, -1)
+    far = between_lines(
+        call(pack_far, [VM] * 3, f32(8, CROWS, CCOLS))(ab, plus1, minus1), 3
+    )
     plus2 = along_lines(plus1[0:4], 1)
     minus2 = along_lines(minus1[0:4], -1)
-    third = f32(7, CROWS, CCOLS)
-    plus3 = along_lines(call(pack_plus3, [VM] * 3, third)(plus2, near, far), 1)
-    minus3 = along_lines(call(pack_minus3, [VM] * 3, third)(minus2, near, far), -1)
+    plus3 = along_lines(plus2, 1)
+    minus3 = along_lines(minus2, -1)
 
     rows = f32(Y2_ROWS, CCOLS)
     up, down, dom, edge = call(
         pack_y2, [VM] * 10, (rows, rows, f32(26, CROWS, CCOLS), f32(8, CROWS, CCOLS))
-    )(ab, u, plus1, minus1, plus2, minus2, plus3, minus3, near, far)
+    )(ab, u, plus1, minus1, across, plus2, minus2, plus3, minus3, far)
     ylo = rotated(up, "pen", 1)
     yhi = rotated(down, "pen", -1)
 

time: 58.8 us -> 53.9 us (0.917)
  the two profiles are of different devices: /device:TPU:31 before, /device:TPU:63 now
where the time goes in v6:
time: 53.9 us; the launch traced here: 53.7 us
  starting transfers between devices  28.9 us (54%)
  waiting for transfers between devices  17.4 us (32%)
  Pallas kernels  5.99 us (11%)
  local copies, waits for them, and re-layouts  0.76 us (1%)
    ppermute x8, starting transfers between devices, along_lines(): return lax.ppermute(x, ('slab', 'pen'), pairs)  17.8 us
    ppermute x4, waiting for transfers between devices, rotated(): lax.ppermute(x, axis, [(i, (i + by) % devices) for i in range(devices)])  9.88 us
    ppermute x4, starting transfers between devices, rotated(): lax.ppermute(x, axis, [(i, (i + by) % devices) for i in range(devices)])  6.01 us
    ppermute x8, waiting for transfers between devices, along_lines(): return lax.ppermute(x, ('slab', 'pen'), pairs)  5.25 us
    ppermute x3, starting transfers between devices, between_lines(): return lax.ppermute(x, ('slab', 'pen'), pairs)  5.11 us
    pallas_call x1, Pallas kernels, post_call(): call(post_kernel, [SM] + [VM] * 9, f32(4, ROWS, COLS), ((8, FR, COLS), (8...  2.65 us
    ppermute x3, waiting for transfers between devices, between_lines(): return lax.ppermute(x, ('slab', 'pen'), pairs)  2.24 us
    pallas_call x1, Pallas kernels, pre_call(): call(pre_kernel, [SM] + [VM] * 10, (f32(8, FR, COLS), f32(6, FR, COLS), f...  1.89 us
  transfers between devices with their start and end apart: 15, of which 9 were waited for; matrix products, arithmetic and copies ran while one was open for 1% of the time, Pallas kernels for 0%

profile of v6, /device:TPU:63, one launch (start us, length us, event | category | flops | bytes accessed | tf_op | source)
XLA Modules:
  0.0 53.7 jit_solution(9522566967028595248)
XLA Ops:
  0.0 0.0 copy-start
  0.0 0.0 copy-start.1
  0.0 0.0 copy-start.2
  0.0 1.3 %shard_map.64 = (f32[232,256]{1,0:T(8,128)S(1)}, f32[232,256]{1,0:T(8,128)S(1)}, f32[232,256]{1,0:T(8,128)S(1)}) custom-call(f32[4,32,256]{2,1,0:T(8,128)} %rhs.6, f32[4,32,256]{2,1,0:T(8,128)} %perm.5, f32[4,32,256]{2,1,0:T(8,128)} %acc.5, f32[2,16,128]{2,1,0:T(8,128)} %cperm.5), custom_call_target="tpu_custom_call" | custom-call | tf_op jit(solution)/shard_map/pallas_call | solution.py:454
  1.3 0.0 collective-permute-start
  1.4 1.7 %collective-permute-start.1 = (f32[232,256]{1,0:T(8,128)S(1)}, f32[232,256]{1,0:T(8,128)S(1)}, u32[]{:S(2)}, u32[]{:S(2)}) collective-permute-start(f32[232,256]{1,0:T(8,128)S(1)} %get-tuple-element.24), channel_id=1, source_target_pairs={{0,1},{1,9},{2,3},{3,11},{4,5},{5,13},{6,7},{7,15},{8,0},{9,17},{1... | collective-permute-start | bytes 712712 | tf_op jit(solution)/shard_map/ppermute | solution.py:34
  3.0 0.7 %collective-permute-start.2 = (f32[232,256]{1,0:T(8,128)S(1)}, f32[232,256]{1,0:T(8,128)S(1)}, u32[]{:S(2)}, u32[]{:S(2)}) collective-permute-start(f32[232,256]{1,0:T(8,128)S(1)} %get-tuple-element.25), channel_id=1, source_target_pairs={{120,128},{128,120},{121,129},{129,121},{122,130},{130,122},{123,1... | collective-permute-start | bytes 712712 | tf_op jit(solution)/shard_map/ppermute | solution.py:45
  3.7 0.0 copy-start.5
  3.7 0.6 %copy-done.5 = s32[32]{0:T(128)S(1)} copy-done((s32[32]{0:T(128)S(1)}, s32[32]{0:T(128)}, u32[]{:S(2)}) %copy-start.5) | copy-done | bytes 152
  4.4 0.1 copy.9
  4.5 0.1 reduce-window.9
  4.5 0.0 copy-start.3
  4.5 0.1 reduce
  4.6 0.2 compare_reduce_fusion
  4.8 0.1 add_convert_fusion
  4.9 1.9 %collective-permute-done.plus = f32[232,256]{1,0:T(8,128)S(1)} collective-permute-done((f32[232,256]{1,0:T(8,128)S(1)}, f32[232,256]{1,0:T(8,128)S(1)}, u32[]{:S(2)}, u32[]{:S(2)}) %collective-permute-start) | collective-permute-done | bytes 237600 | tf_op jit(solution)/shard_map/ppermute | solution.py:34
  6.8 1.3 %collective-permute-done.1.minus = f32[232,256]{1,0:T(8,128)S(1)} collective-permute-done((f32[232,256]{1,0:T(8,128)S(1)}, f32[232,256]{1,0:T(8,128)S(1)}, u32[]{:S(2)}, u32[]{:S(2)}) %collective-permute-start.1) | collective-permute-done | bytes 237600 | tf_op jit(solution)/shard_map/ppermute | solution.py:34
  8.1 0.0 collective-permute-done.2.across
  8.1 0.0 copy-done
  8.1 0.0 copy-done.1
  8.1 0.0 copy-done.2
  8.1 0.0 copy-done.3
  8.1 0.0 copy-start.4
  8.1 0.1 shard_map.65
  8.2 1.8 %collective-permute-start.3 = (f32[64,256]{1,0:T(8,128)S(1)}, f32[64,256]{1,0:T(8,128)S(1)}, u32[]{:S(2)}, u32[]{:S(2)}) collective-permute-start(f32[64,256]{1,0:T(8,128)S(1)} %get-tuple-element.26), channel_id=1, source_target_pairs={{0,1},{1,2},{2,3},{3,4},{4,5},{5,6},{6,7},{7,0},{8,9},{9,10},{10,1... | collective-permute-start | bytes 196616 | tf_op jit(solution)/shard_map/ppermute | solution.py:72
  10.0 0.2 collective-permute-start.4
  10.2 0.1 pad_maximum_fusion.masks
  10.3 1.1 %collective-permute-done.3.ylo = f32[64,256]{1,0:T(8,128)S(1)} collective-permute-done((f32[64,256]{1,0:T(8,128)S(1)}, f32[64,256]{1,0:T(8,128)S(1)}, u32[]{:S(2)}, u32[]{:S(2)}) %collective-permute-start.3) | collective-permute-done | bytes 65568 | tf_op jit(solution)/shard_map/ppermute | solution.py:72
  11.3 3.6 %collective-permute-done.4.yhi = f32[64,256]{1,0:T(8,128)S(1)} collective-permute-done((f32[64,256]{1,0:T(8,128)S(1)}, f32[64,256]{1,0:T(8,128)S(1)}, u32[]{:S(2)}, u32[]{:S(2)}) %collective-permute-start.4) | collective-permute-done | bytes 65568 | tf_op jit(solution)/shard_map/ppermute | solution.py:72
  14.9 0.0 copy-done.4
  14.9 1.9 %shard_map.66 = (f32[8,40,256]{2,1,0:T(8,128)S(1)}, f32[6,40,256]{2,1,0:T(8,128)S(1)}, f32[6,40,256]{2,1,0:T(8,128)S(1)}, f32[6,40,256]{2,1,0:T(8,128)S(1)}, f32...) custom-call(f32[8]{0:T(128)S(1)} %pad_maximum_fusion.masks, ...), custom_call_target="tpu_custom_call" | custom-call | tf_op jit(solution)/shard_map/pallas_call | solution.py:428
  16.8 10.0 %collective-permute-start.5 = (f32[8,16,128]{2,1,0:T(8,128)S(1)}, f32[8,16,128]{2,1,0:T(8,128)S(1)}, u32[]{:S(2)}, u32[]{:S(2)}) collective-permute-start(f32[8,16,128]{2,1,0:T(8,128)S(1)} %get-tuple-element.34), channel_id=1, source_target_pairs={{0,8},{1,0},{2,10},{3,2},{4,12},{5,4},{6,14},{7,6},{8,16},{9,1},{1... | collective-permute-start | bytes 196616 | tf_op jit(solution)/shard_map/ppermute | solution.py:34
  26.8 0.0 collective-permute-start.6
  26.8 0.7 %collective-permute-start.7 = (f32[8,16,128]{2,1,0:T(8,128)S(1)}, f32[8,16,128]{2,1,0:T(8,128)S(1)}, u32[]{:S(2)}, u32[]{:S(2)}) collective-permute-start(f32[8,16,128]{2,1,0:T(8,128)S(1)} %get-tuple-element.36), channel_id=1, source_target_pairs={{120,128},{128,120},{121,129},{129,121},{122,130},{130,122},{123,1... | collective-permute-start | bytes 196616 | tf_op jit(solution)/shard_map/ppermute | solution.py:45
  27.4 0.7 %collective-permute-done.5.plus1 = f32[8,16,128]{2,1,0:T(8,128)S(1)} collective-permute-done((f32[8,16,128]{2,1,0:T(8,128)S(1)}, f32[8,16,128]{2,1,0:T(8,128)S(1)}, u32[]{:S(2)}, u32[]{:S(2)}) %collective-permute-start.5) | collective-permute-done | bytes 65568 | tf_op jit(solution)/shard_map/ppermute | solution.py:34
  28.1 4.6 %collective-permute-start.8 = (f32[4,16,128]{2,1,0:T(8,128)S(1)}, f32[4,16,128]{2,1,0:T(8,128)S(1)}, u32[]{:S(2)}, u32[]{:S(2)}) collective-permute-start(f32[4,16,128]{2,1,0:T(8,128)S(1)} %slice.8), channel_id=1, source_target_pairs={{0,8},{1,0},{2,10},{3,2},{4,12},{5,4},{6,14},{7,6},{8,16},{9,1},{1... | collective-permute-start | bytes 98312 | tf_op jit(solution)/shard_map/ppermute | solution.py:34
  32.8 0.0 collective-permute-done.6.minus1
  32.8 0.0 collective-permute-start.9
  32.8 3.8 %collective-permute-start.12 = (f32[8,16,128]{2,1,0:T(8,128)S(1)}, f32[8,16,128]{2,1,0:T(8,128)S(1)}, u32[]{:S(2)}, u32[]{:S(2)}) collective-permute-start(f32[8,16,128]{2,1,0:T(8,128)S(1)} %shard_map.67), channel_id=1, source_target_pairs={{104,128},{128,104},{105,129},{129,105},{106,130},{130,106},{107,1... | collective-permute-start | bytes 196616 | tf_op jit(solution)/shard_map/ppermute | solution.py:45
  36.6 0.0 collective-permute-done.8.plus2
  36.6 0.0 collective-permute-start.10
  36.7 0.0 collective-permute-done.9.minus2
  36.7 1.4 %collective-permute-start.11 = (f32[4,16,128]{2,1,0:T(8,128)S(1)}, f32[4,16,128]{2,1,0:T(8,128)S(1)}, u32[]{:S(2)}, u32[]{:S(2)}) collective-permute-start(f32[4,16,128]{2,1,0:T(8,128)S(1)} %collective-permute-done.9.minus2), channel_id=1, source_target_pairs={{0,1},{1,9},{2,3},{3,11},{4,5},{5,13},{6,7},{7,15},{8,0},{9,17},{1... | collective-permute-start | bytes 98312 | tf_op jit(solution)/shard_map/ppermute | solution.py:34
  38.1 0.0 collective-permute-done.7.across
  38.1 1.4 %collective-permute-done.10.plus3 = f32[4,16,128]{2,1,0:T(8,128)S(1)} collective-permute-done((f32[4,16,128]{2,1,0:T(8,128)S(1)}, f32[4,16,128]{2,1,0:T(8,128)S(1)}, u32[]{:S(2)}, u32[]{:S(2)}) %collective-permute-start.10) | collective-permute-done | bytes 32800 | tf_op jit(solution)/shard_map/ppermute | solution.py:34
  39.5 0.0 collective-permute-done.11.minus3
  39.5 2.2 %collective-permute-done.12.far = f32[8,16,128]{2,1,0:T(8,128)S(1)} collective-permute-done((f32[8,16,128]{2,1,0:T(8,128)S(1)}, f32[8,16,128]{2,1,0:T(8,128)S(1)}, u32[]{:S(2)}, u32[]{:S(2)}) %collective-permute-start.12) | collective-permute-done | bytes 65568 | tf_op jit(solution)/shard_map/ppermute | solution.py:45
  41.7 0.1 shard_map.68
  41.8 4.0 %collective-permute-start.13 = (f32[192,128]{1,0:T(8,128)S(1)}, f32[192,128]{1,0:T(8,128)S(1)}, u32[]{:S(2)}, u32[]{:S(2)}) collective-permute-start(f32[192,128]{1,0:T(8,128)S(1)} %get-tuple-element.39), channel_id=1, source_target_pairs={{0,1},{1,2},{2,3},{3,4},{4,5},{5,6},{6,7},{7,0},{8,9},{9,10},{10,1... | collective-permute-start | bytes 294920 | tf_op jit(solution)/shard_map/ppermute | solution.py:72
  45.8 0.0 collective-permute-start.14
  45.8 1.6 %collective-permute-done.13.ylo = f32[192,128]{1,0:T(8,128)S(1)} collective-permute-done((f32[192,128]{1,0:T(8,128)S(1)}, f32[192,128]{1,0:T(8,128)S(1)}, u32[]{:S(2)}, u32[]{:S(2)}) %collective-permute-start.13) | collective-permute-done | bytes 98336 | tf_op jit(solution)/shard_map/ppermute | solution.py:72
  47.4 3.6 %collective-permute-done.14.yhi = f32[192,128]{1,0:T(8,128)S(1)} collective-permute-done((f32[192,128]{1,0:T(8,128)S(1)}, f32[192,128]{1,0:T(8,128)S(1)}, u32[]{:S(2)}, u32[]{:S(2)}) %collective-permute-start.14) | collective-permute-done | bytes 98336 | tf_op jit(solution)/shard_map/ppermute | solution.py:72
  51.0 2.6 %shard_map.69 = f32[4,32,256]{2,1,0:T(8,128)} custom-call(f32[8]{0:T(128)S(1)} %pad_maximum_fusion.masks, f32[8,40,256]{2,1,0:T(8,128)S(1)} %get-tuple-element.28.t_in, f32[6,40,256]{2,1,0:T(8,128)S(1)} %get-tuple-element.29.a_in, f32[6,40,256]{2,1,0:T(8,128)S(1)} %get-tuple-element.30.b_in, f32[6,40,256]{2,1,0:T(8,128)S(1)} %get-tuple-element.31.u.u_in, ...), custom_call_target="tpu_custom_call" | custom-call | tf_op jit(solution)/shard_map/pallas_call | solution.py:444
  (6 shorter events, 0.0 us)
Async XLA Ops:
  0.0 8.1 %copy-start = (f32[4,32,256]{2,1,0:T(8,128)S(1)}, f32[4,32,256]{2,1,0:T(8,128)}, u32[]{:S(2)}) copy-start(f32[4,32,256]{2,1,0:T(8,128)} %rhs.6) | copy-start | bytes 393220
  0.0 8.1 %copy-start.1 = (f32[4,32,256]{2,1,0:T(8,128)S(1)}, f32[4,32,256]{2,1,0:T(8,128)}, u32[]{:S(2)}) copy-start(f32[4,32,256]{2,1,0:T(8,128)} %perm.5) | copy-start | bytes 393220
  0.0 8.1 %copy-start.2 = (f32[4,32,256]{2,1,0:T(8,128)S(1)}, f32[4,32,256]{2,1,0:T(8,128)}, u32[]{:S(2)}) copy-start(f32[4,32,256]{2,1,0:T(8,128)} %acc.5) | copy-start | bytes 393220
  1.3 5.4 %collective-permute-start = (f32[232,256]{1,0:T(8,128)S(1)}, f32[232,256]{1,0:T(8,128)S(1)}, u32[]{:S(2)}, u32[]{:S(2)}) collective-permute-start(f32[232,256]{1,0:T(8,128)S(1)} %get-tuple-element.23), channel_id=1, source_target_pairs={{0,8},{1,0},{2,10},{3,2},{4,12},{5,4},{6,14},{7,6},{8,16},{9,1},{1... | collective-permute-start | bytes 712712 | tf_op jit(solution)/shard_map/ppermute | solution.py:34
  1.4 6.7 %collective-permute-start.1 = (f32[232,256]{1,0:T(8,128)S(1)}, f32[232,256]{1,0:T(8,128)S(1)}, u32[]{:S(2)}, u32[]{:S(2)}) collective-permute-start(f32[232,256]{1,0:T(8,128)S(1)} %get-tuple-element.24), channel_id=1, source_target_pairs={{0,1},{1,9},{2,3},{3,11},{4,5},{5,13},{6,7},{7,15},{8,0},{9,17},{1... | collective-permute-start | bytes 712712 | tf_op jit(solution)/shard_map/ppermute | solution.py:34
  3.0 5.0 %collective-permute-start.2 = (f32[232,256]{1,0:T(8,128)S(1)}, f32[232,256]{1,0:T(8,128)S(1)}, u32[]{:S(2)}, u32[]{:S(2)}) collective-permute-start(f32[232,256]{1,0:T(8,128)S(1)} %get-tuple-element.25), channel_id=1, source_target_pairs={{120,128},{128,120},{121,129},{129,121},{122,130},{130,122},{123,1... | collective-permute-start | bytes 712712 | tf_op jit(solution)/shard_map/ppermute | solution.py:45
  3.7 0.7 %copy-start.5 = (s32[32]{0:T(128)S(1)}, s32[32]{0:T(128)}, u32[]{:S(2)}) copy-start(s32[32]{0:T(128)} %param.11) | copy-start | bytes 388
  4.5 3.6 %copy-start.3 = (f32[2,16,128]{2,1,0:T(8,128)S(1)}, f32[2,16,128]{2,1,0:T(8,128)}, u32[]{:S(2)}) copy-start(f32[2,16,128]{2,1,0:T(8,128)} %cperm.5) | copy-start | bytes 49156
  8.1 6.8 %copy-start.4 = (f32[2,16,128]{2,1,0:T(8,128)S(1)}, f32[2,16,128]{2,1,0:T(8,128)}, u32[]{:S(2)}) copy-start(f32[2,16,128]{2,1,0:T(8,128)} %cacc.1) | copy-start | bytes 49156
  8.2 3.2 %collective-permute-start.3 = (f32[64,256]{1,0:T(8,128)S(1)}, f32[64,256]{1,0:T(8,128)S(1)}, u32[]{:S(2)}, u32[]{:S(2)}) collective-permute-start(f32[64,256]{1,0:T(8,128)S(1)} %get-tuple-element.26), channel_id=1, source_target_pairs={{0,1},{1,2},{2,3},{3,4},{4,5},{5,6},{6,7},{7,0},{8,9},{9,10},{10,1... | collective-permute-start | bytes 196616 | tf_op jit(solution)/shard_map/ppermute | solution.py:72
  10.0 4.9 %collective-permute-start.4 = (f32[64,256]{1,0:T(8,128)S(1)}, f32[64,256]{1,0:T(8,128)S(1)}, u32[]{:S(2)}, u32[]{:S(2)}) collective-permute-start(f32[64,256]{1,0:T(8,128)S(1)} %get-tuple-element.27), channel_id=1, source_target_pairs={{0,7},{1,0},{2,1},{3,2},{4,3},{5,4},{6,5},{7,6},{8,15},{9,8},{10,9... | collective-permute-start | bytes 196616 | tf_op jit(solution)/shard_map/ppermute | solution.py:72
  16.8 11.3 %collective-permute-start.5 = (f32[8,16,128]{2,1,0:T(8,128)S(1)}, f32[8,16,128]{2,1,0:T(8,128)S(1)}, u32[]{:S(2)}, u32[]{:S(2)}) collective-permute-start(f32[8,16,128]{2,1,0:T(8,128)S(1)} %get-tuple-element.34), channel_id=1, source_target_pairs={{0,8},{1,0},{2,10},{3,2},{4,12},{5,4},{6,14},{7,6},{8,16},{9,1},{1... | collective-permute-start | bytes 196616 | tf_op jit(solution)/shard_map/ppermute | solution.py:34
  26.8 6.0 %collective-permute-start.6 = (f32[8,16,128]{2,1,0:T(8,128)S(1)}, f32[8,16,128]{2,1,0:T(8,128)S(1)}, u32[]{:S(2)}, u32[]{:S(2)}) collective-permute-start(f32[8,16,128]{2,1,0:T(8,128)S(1)} %get-tuple-element.35), channel_id=1, source_target_pairs={{0,1},{1,9},{2,3},{3,11},{4,5},{5,13},{6,7},{7,15},{8,0},{9,17},{1... | collective-permute-start | bytes 196616 | tf_op jit(solution)/shard_map/ppermute | solution.py:34
  26.8 11.4 %collective-permute-start.7 = (f32[8,16,128]{2,1,0:T(8,128)S(1)}, f32[8,16,128]{2,1,0:T(8,128)S(1)}, u32[]{:S(2)}, u32[]{:S(2)}) collective-permute-start(f32[8,16,128]{2,1,0:T(8,128)S(1)} %get-tuple-element.36), channel_id=1, source_target_pairs={{120,128},{128,120},{121,129},{129,121},{122,130},{130,122},{123,1... | collective-permute-start | bytes 196616 | tf_op jit(solution)/shard_map/ppermute | solution.py:45
  28.1 8.5 %collective-permute-start.8 = (f32[4,16,128]{2,1,0:T(8,128)S(1)}, f32[4,16,128]{2,1,0:T(8,128)S(1)}, u32[]{:S(2)}, u32[]{:S(2)}) collective-permute-start(f32[4,16,128]{2,1,0:T(8,128)S(1)} %slice.8), channel_id=1, source_target_pairs={{0,8},{1,0},{2,10},{3,2},{4,12},{5,4},{6,14},{7,6},{8,16},{9,1},{1... | collective-permute-start | bytes 98312 | tf_op jit(solution)/shard_map/ppermute | solution.py:34
  32.8 3.9 %collective-permute-start.9 = (f32[4,16,128]{2,1,0:T(8,128)S(1)}, f32[4,16,128]{2,1,0:T(8,128)S(1)}, u32[]{:S(2)}, u32[]{:S(2)}) collective-permute-start(f32[4,16,128]{2,1,0:T(8,128)S(1)} %slice.9), channel_id=1, source_target_pairs={{0,1},{1,9},{2,3},{3,11},{4,5},{5,13},{6,7},{7,15},{8,0},{9,17},{1... | collective-permute-start | bytes 98312 | tf_op jit(solution)/shard_map/ppermute | solution.py:34
  32.8 8.9 %collective-permute-start.12 = (f32[8,16,128]{2,1,0:T(8,128)S(1)}, f32[8,16,128]{2,1,0:T(8,128)S(1)}, u32[]{:S(2)}, u32[]{:S(2)}) collective-permute-start(f32[8,16,128]{2,1,0:T(8,128)S(1)} %shard_map.67), channel_id=1, source_target_pairs={{104,128},{128,104},{105,129},{129,105},{106,130},{130,106},{107,1... | collective-permute-start | bytes 196616 | tf_op jit(solution)/shard_map/ppermute | solution.py:45
  36.6 2.9 %collective-permute-start.10 = (f32[4,16,128]{2,1,0:T(8,128)S(1)}, f32[4,16,128]{2,1,0:T(8,128)S(1)}, u32[]{:S(2)}, u32[]{:S(2)}) collective-permute-start(f32[4,16,128]{2,1,0:T(8,128)S(1)} %collective-permute-done.8.plus2), channel_id=1, source_target_pairs={{0,8},{1,0},{2,10},{3,2},{4,12},{5,4},{6,14},{7,6},{8,16},{9,1},{1... | collective-permute-start | bytes 98312 | tf_op jit(solution)/shard_map/ppermute | solution.py:34
  36.7 2.8 %collective-permute-start.11 = (f32[4,16,128]{2,1,0:T(8,128)S(1)}, f32[4,16,128]{2,1,0:T(8,128)S(1)}, u32[]{:S(2)}, u32[]{:S(2)}) collective-permute-start(f32[4,16,128]{2,1,0:T(8,128)S(1)} %collective-permute-done.9.minus2), channel_id=1, source_target_pairs={{0,1},{1,9},{2,3},{3,11},{4,5},{5,13},{6,7},{7,15},{8,0},{9,17},{1... | collective-permute-start | bytes 98312 | tf_op jit(solution)/shard_map/ppermute | solution.py:34
  41.8 5.6 %collective-permute-start.13 = (f32[192,128]{1,0:T(8,128)S(1)}, f32[192,128]{1,0:T(8,128)S(1)}, u32[]{:S(2)}, u32[]{:S(2)}) collective-permute-start(f32[192,128]{1,0:T(8,128)S(1)} %get-tuple-element.39), channel_id=1, source_target_pairs={{0,1},{1,2},{2,3},{3,4},{4,5},{5,6},{6,7},{7,0},{8,9},{9,10},{10,1... | collective-permute-start | bytes 294920 | tf_op jit(solution)/shard_map/ppermute | solution.py:72
  45.8 5.3 %collective-permute-start.14 = (f32[192,128]{1,0:T(8,128)S(1)}, f32[192,128]{1,0:T(8,128)S(1)}, u32[]{:S(2)}, u32[]{:S(2)}) collective-permute-start(f32[192,128]{1,0:T(8,128)S(1)} %get-tuple-element.40), channel_id=1, source_target_pairs={{0,7},{1,0},{2,1},{3,2},{4,3},{5,4},{6,5},{7,6},{8,15},{9,8},{10,9... | collective-permute-start | bytes 294920 | tf_op jit(solution)/shard_map/ppermute | solution.py:72

commit v7 on v6

--- a/solution.py
+++ b/solution.py
@@ -101,18 +101,17 @@
     copies = [pltpu.make_async_copy(cperm, held, sems.at[0])]
     for out, up in zip((plus, minus, across), upward):
         for base, ref, start, count in (
-            (0, perm, jnp.where(up, 1, 0), 3),
-            (Z1_RHS, rhs, jnp.where(up, 2, 0), 2),
-            (Z1_ACC, acc, jnp.where(up, 2, 0), 2),
+            (0, perm, jnp.where(up, ROWS, 0), 3),
+            (Z1_RHS, rhs, jnp.where(up, 2 * ROWS, 0), 2),
+            (Z1_ACC, acc, jnp.where(up, 2 * ROWS, 0), 2),
         ):
-            for k in range(count):
-                copies.append(
-                    pltpu.make_async_copy(
-                        ref.at[start + k],
-                        out.at[pl.ds(base + ROWS * k, ROWS)],
-                        sems.at[len(copies)],
-                    )
+            copies.append(
+                pltpu.make_async_copy(
+                    ref.at[pl.ds(pl.multiple_of(start, ROWS), ROWS * count)],
+                    out.at[pl.ds(base, ROWS * count)],
+                    sems.at[len(copies)],
                 )
+            )
     for copy in copies:
         copy.start()
     for copy in copies:
@@ -268,8 +267,9 @@
 def pack_far(ab, plus1, minus1, out):
     first, z = place()
     near_start = z < LINE // 2
-    out[0:4] = ab[...]
-    out[4:8] = jnp.where(first == near_start, plus1[0:4], minus1[0:4])
+    out[0:2] = ab[0:2]
+    out[2] = ab[jnp.where(near_start, 2, 3)]
+    out[3:7] = jnp.where(first == near_start, plus1[0:4], minus1[0:4])
 
 
 Y2_B = 84
@@ -293,13 +293,13 @@
         dom[6 + k if a else 17 + k] = ab[k]
         dom[4 + k if a else 15 + k] = below(plus1, minus1, k, 1, across[k])
         dom[8 + k if a else 19 + k] = above(plus1, minus1, k, 1, across[k])
-        dom[2 + k if a else 13 + k] = below(plus2, minus2, k, 2, far[4 + k])
-        dom[10 + k if a else 21 + k] = above(plus2, minus2, k, 2, far[4 + k])
+        dom[2 + k if a else 13 + k] = below(plus2, minus2, k, 2, far[3 + k])
+        dom[10 + k if a else 21 + k] = above(plus2, minus2, k, 2, far[3 + k])
         edge[k] = below(plus1, minus1, 4 + k, 1, across[4 + k])
         edge[4 + k] = above(plus1, minus1, 4 + k, 1, across[4 + k])
     for k in range(3):
         low = 3 if k == 2 else k
-        dom[14 if k == 2 else k] = below(plus3, minus3, low, 3, far[low])
+        dom[14 if k == 2 else k] = below(plus3, minus3, low, 3, far[k])
         dom[25 if k == 2 else 12 + k] = above(plus3, minus3, k, 3, far[k])
     for out, top_rows in ((up, True), (down, False)):
         row = CROWS - 6 if top_rows else 0
@@ -455,11 +455,16 @@
         pack_z1,
         [HBM] * 4,
         (message, message, message),
-        (pltpu.VMEM((2, CROWS, CCOLS), jnp.float32), pltpu.SemaphoreType.DMA((22,))),
+        (pltpu.VMEM((2, CROWS, CCOLS), jnp.float32), pltpu.SemaphoreType.DMA((10,))),
     )(
         *(
             pltpu.with_memory_space_constraint(x, pltpu.HBM)
-            for x in (pressure_rhs, permeability, accumulation, coarse_perm)
+            for x in (
+                pressure_rhs.reshape(-1, COLS),
+                permeability.reshape(-1, COLS),
+                accumulation.reshape(-1, COLS),
+                coarse_perm,
+            )
         )
     )
     across = between_lines(across, 1)
@@ -493,7 +498,7 @@
     plus1 = along_lines(plus, 1)
     minus1 = along_lines(minus, -1)
     far = between_lines(
-        call(pack_far, [VM] * 3, f32(8, CROWS, CCOLS))(ab, plus1, minus1), 3
+        call(pack_far, [VM] * 3, f32(7, CROWS, CCOLS))(ab, plus1, minus1), 3
     )
     plus2 = along_lines(plus1[0:4], 1)
     minus2 = along_lines(minus1[0:4], -1)

time: 53.9 us -> 53.6 us (level)
    ppermute x8, waiting for transfers between devices: 5.25 us -> 3.87 us  [along_lines(): return lax.ppermute(x, ('slab', 'pen'), pairs)]
    ppermute x3, waiting for transfers between devices: 2.24 us -> 3.53 us  [between_lines(): return lax.ppermute(x, ('slab', 'pen'), pairs)]
  transfers between devices with their start and end apart: 15 -> 15, of which waited for: 9 -> 8; matrix products, arithmetic and copies ran while one was open for 1% -> 1% of each run, Pallas kernels for 0% -> 0%
where the time goes in v7:
time: 53.6 us; the launch traced here: 53.4 us
  starting transfers between devices  28.7 us (54%)
  waiting for transfers between devices  17.3 us (32%)
  Pallas kernels  5.97 us (11%)
  local copies, waits for them, and re-layouts  0.76 us (1%)
    ppermute x8, starting transfers between devices, along_lines(): return lax.ppermute(x, ('slab', 'pen'), pairs)  17.8 us
    ppermute x4, waiting for transfers between devices, rotated(): lax.ppermute(x, axis, [(i, (i + by) % devices) for i in range(devices)])  9.88 us
    ppermute x4, starting transfers between devices, rotated(): lax.ppermute(x, axis, [(i, (i + by) % devices) for i in range(devices)])  5.83 us
    ppermute x3, starting transfers between devices, between_lines(): return lax.ppermute(x, ('slab', 'pen'), pairs)  5.11 us
    ppermute x8, waiting for transfers between devices, along_lines(): return lax.ppermute(x, ('slab', 'pen'), pairs)  3.87 us
    ppermute x3, waiting for transfers between devices, between_lines(): return lax.ppermute(x, ('slab', 'pen'), pairs)  3.53 us
    pallas_call x1, Pallas kernels, post_call(): call(post_kernel, [SM] + [VM] * 9, f32(4, ROWS, COLS), ((8, FR, COLS), (8...  2.65 us
    pallas_call x1, Pallas kernels, pre_call(): call(pre_kernel, [SM] + [VM] * 10, (f32(8, FR, COLS), f32(6, FR, COLS), f...  1.89 us
  transfers between devices with their start and end apart: 15, of which 8 were waited for; matrix products, arithmetic and copies ran while one was open for 1% of the time, Pallas kernels for 0%

profile of v7, /device:TPU:63, one launch (start us, length us, event | category | flops | bytes accessed | tf_op | source)
XLA Modules:
  0.0 53.4 jit_solution(5235096421435779295)
XLA Ops:
  0.0 0.0 copy-start
  0.0 0.0 copy-start.1
  0.0 0.0 copy-start.2
  0.0 1.3 %shard_map.64 = (f32[232,256]{1,0:T(8,128)S(1)}, f32[232,256]{1,0:T(8,128)S(1)}, f32[232,256]{1,0:T(8,128)S(1)}) custom-call(f32[128,256]{1,0:T(8,128)} %bitcast.6, f32[128,256]{1,0:T(8,128)} %bitcast.7, f32[128,256]{1,0:T(8,128)} %bitcast.8, f32[2,16,128]{2,1,0:T(8,128)} %cperm.5), custom_call_target="tpu_custom_call" | custom-call | tf_op jit(solution)/shard_map/pallas_call | solution.py:454
  1.3 0.0 collective-permute-start
  1.3 1.7 %collective-permute-start.1 = (f32[232,256]{1,0:T(8,128)S(1)}, f32[232,256]{1,0:T(8,128)S(1)}, u32[]{:S(2)}, u32[]{:S(2)}) collective-permute-start(f32[232,256]{1,0:T(8,128)S(1)} %get-tuple-element.24), channel_id=1, source_target_pairs={{0,1},{1,9},{2,3},{3,11},{4,5},{5,13},{6,7},{7,15},{8,0},{9,17},{1... | collective-permute-start | bytes 712712 | tf_op jit(solution)/shard_map/ppermute | solution.py:34
  3.0 0.7 %collective-permute-start.2 = (f32[232,256]{1,0:T(8,128)S(1)}, f32[232,256]{1,0:T(8,128)S(1)}, u32[]{:S(2)}, u32[]{:S(2)}) collective-permute-start(f32[232,256]{1,0:T(8,128)S(1)} %get-tuple-element.25), channel_id=1, source_target_pairs={{120,128},{128,120},{121,129},{129,121},{122,130},{130,122},{123,1... | collective-permute-start | bytes 712712 | tf_op jit(solution)/shard_map/ppermute | solution.py:45
  3.7 0.0 copy-start.5
  3.7 0.6 %copy-done.5 = s32[32]{0:T(128)S(1)} copy-done((s32[32]{0:T(128)S(1)}, s32[32]{0:T(128)}, u32[]{:S(2)}) %copy-start.5) | copy-done | bytes 152
  4.3 0.1 copy.9
  4.4 0.1 reduce-window.9
  4.5 0.0 copy-start.3
  4.5 0.1 reduce
  4.6 0.2 compare_reduce_fusion
  4.8 0.1 add_convert_fusion
  4.9 1.9 %collective-permute-done.plus = f32[232,256]{1,0:T(8,128)S(1)} collective-permute-done((f32[232,256]{1,0:T(8,128)S(1)}, f32[232,256]{1,0:T(8,128)S(1)}, u32[]{:S(2)}, u32[]{:S(2)}) %collective-permute-start) | collective-permute-done | bytes 237600 | tf_op jit(solution)/shard_map/ppermute | solution.py:34
  6.8 1.3 %collective-permute-done.1.minus = f32[232,256]{1,0:T(8,128)S(1)} collective-permute-done((f32[232,256]{1,0:T(8,128)S(1)}, f32[232,256]{1,0:T(8,128)S(1)}, u32[]{:S(2)}, u32[]{:S(2)}) %collective-permute-start.1) | collective-permute-done | bytes 237600 | tf_op jit(solution)/shard_map/ppermute | solution.py:34
  8.0 0.0 collective-permute-done.2.across
  8.0 0.0 copy-done
  8.0 0.0 copy-done.1
  8.0 0.0 copy-done.2
  8.1 0.0 copy-done.3
  8.1 0.0 copy-start.4
  8.1 0.1 shard_map.65
  8.1 1.8 %collective-permute-start.3 = (f32[64,256]{1,0:T(8,128)S(1)}, f32[64,256]{1,0:T(8,128)S(1)}, u32[]{:S(2)}, u32[]{:S(2)}) collective-permute-start(f32[64,256]{1,0:T(8,128)S(1)} %get-tuple-element.26), channel_id=1, source_target_pairs={{0,1},{1,2},{2,3},{3,4},{4,5},{5,6},{6,7},{7,0},{8,9},{9,10},{10,1... | collective-permute-start | bytes 196616 | tf_op jit(solution)/shard_map/ppermute | solution.py:72
  10.0 0.2 collective-permute-start.4
  10.2 0.1 pad_maximum_fusion.masks
  10.2 1.1 %collective-permute-done.3.ylo = f32[64,256]{1,0:T(8,128)S(1)} collective-permute-done((f32[64,256]{1,0:T(8,128)S(1)}, f32[64,256]{1,0:T(8,128)S(1)}, u32[]{:S(2)}, u32[]{:S(2)}) %collective-permute-start.3) | collective-permute-done | bytes 65568 | tf_op jit(solution)/shard_map/ppermute | solution.py:72
  11.3 3.6 %collective-permute-done.4.yhi = f32[64,256]{1,0:T(8,128)S(1)} collective-permute-done((f32[64,256]{1,0:T(8,128)S(1)}, f32[64,256]{1,0:T(8,128)S(1)}, u32[]{:S(2)}, u32[]{:S(2)}) %collective-permute-start.4) | collective-permute-done | bytes 65568 | tf_op jit(solution)/shard_map/ppermute | solution.py:72
  14.9 0.0 copy-done.4
  14.9 1.9 %shard_map.66 = (f32[8,40,256]{2,1,0:T(8,128)S(1)}, f32[6,40,256]{2,1,0:T(8,128)S(1)}, f32[6,40,256]{2,1,0:T(8,128)S(1)}, f32[6,40,256]{2,1,0:T(8,128)S(1)}, f32...) custom-call(f32[8]{0:T(128)S(1)} %pad_maximum_fusion.masks, ...), custom_call_target="tpu_custom_call" | custom-call | tf_op jit(solution)/shard_map/pallas_call | solution.py:428
  16.8 10.0 %collective-permute-start.5 = (f32[8,16,128]{2,1,0:T(8,128)S(1)}, f32[8,16,128]{2,1,0:T(8,128)S(1)}, u32[]{:S(2)}, u32[]{:S(2)}) collective-permute-start(f32[8,16,128]{2,1,0:T(8,128)S(1)} %get-tuple-element.34), channel_id=1, source_target_pairs={{0,8},{1,0},{2,10},{3,2},{4,12},{5,4},{6,14},{7,6},{8,16},{9,1},{1... | collective-permute-start | bytes 196616 | tf_op jit(solution)/shard_map/ppermute | solution.py:34
  26.7 0.0 collective-permute-start.6
  26.7 0.7 %collective-permute-start.7 = (f32[8,16,128]{2,1,0:T(8,128)S(1)}, f32[8,16,128]{2,1,0:T(8,128)S(1)}, u32[]{:S(2)}, u32[]{:S(2)}) collective-permute-start(f32[8,16,128]{2,1,0:T(8,128)S(1)} %get-tuple-element.36), channel_id=1, source_target_pairs={{120,128},{128,120},{121,129},{129,121},{122,130},{130,122},{123,1... | collective-permute-start | bytes 196616 | tf_op jit(solution)/shard_map/ppermute | solution.py:45
  27.4 0.7 %collective-permute-done.5.plus1 = f32[8,16,128]{2,1,0:T(8,128)S(1)} collective-permute-done((f32[8,16,128]{2,1,0:T(8,128)S(1)}, f32[8,16,128]{2,1,0:T(8,128)S(1)}, u32[]{:S(2)}, u32[]{:S(2)}) %collective-permute-start.5) | collective-permute-done | bytes 65568 | tf_op jit(solution)/shard_map/ppermute | solution.py:34
  28.1 4.6 %collective-permute-start.8 = (f32[4,16,128]{2,1,0:T(8,128)S(1)}, f32[4,16,128]{2,1,0:T(8,128)S(1)}, u32[]{:S(2)}, u32[]{:S(2)}) collective-permute-start(f32[4,16,128]{2,1,0:T(8,128)S(1)} %slice.8), channel_id=1, source_target_pairs={{0,8},{1,0},{2,10},{3,2},{4,12},{5,4},{6,14},{7,6},{8,16},{9,1},{1... | collective-permute-start | bytes 98312 | tf_op jit(solution)/shard_map/ppermute | solution.py:34
  32.8 0.0 collective-permute-done.6.minus1
  32.8 0.0 collective-permute-start.9
  32.8 3.8 %collective-permute-start.12 = (f32[7,16,128]{2,1,0:T(8,128)S(1)}, f32[7,16,128]{2,1,0:T(8,128)S(1)}, u32[]{:S(2)}, u32[]{:S(2)}) collective-permute-start(f32[7,16,128]{2,1,0:T(8,128)S(1)} %shard_map.67), channel_id=1, source_target_pairs={{104,128},{128,104},{105,129},{129,105},{106,130},{130,106},{107,1... | collective-permute-start | bytes 172040 | tf_op jit(solution)/shard_map/ppermute | solution.py:45
  36.6 0.0 collective-permute-done.8.plus2
  36.6 0.0 collective-permute-start.10
  36.6 0.0 collective-permute-done.9.minus2
  36.7 1.4 %collective-permute-start.11 = (f32[4,16,128]{2,1,0:T(8,128)S(1)}, f32[4,16,128]{2,1,0:T(8,128)S(1)}, u32[]{:S(2)}, u32[]{:S(2)}) collective-permute-start(f32[4,16,128]{2,1,0:T(8,128)S(1)} %collective-permute-done.9.minus2), channel_id=1, source_target_pairs={{0,1},{1,9},{2,3},{3,11},{4,5},{5,13},{6,7},{7,15},{8,0},{9,17},{1... | collective-permute-start | bytes 98312 | tf_op jit(solution)/shard_map/ppermute | solution.py:34
  38.1 0.0 collective-permute-done.7.across
  38.1 3.5 %collective-permute-done.12.far = f32[7,16,128]{2,1,0:T(8,128)S(1)} collective-permute-done((f32[7,16,128]{2,1,0:T(8,128)S(1)}, f32[7,16,128]{2,1,0:T(8,128)S(1)}, u32[]{:S(2)}, u32[]{:S(2)}) %collective-permute-start.12) | collective-permute-done | bytes 57376 | tf_op jit(solution)/shard_map/ppermute | solution.py:45
  41.6 0.0 collective-permute-done.10.plus3
  41.6 0.0 collective-permute-done.11.minus3
  41.6 0.1 shard_map.68
  41.7 3.8 %collective-permute-start.13 = (f32[192,128]{1,0:T(8,128)S(1)}, f32[192,128]{1,0:T(8,128)S(1)}, u32[]{:S(2)}, u32[]{:S(2)}) collective-permute-start(f32[192,128]{1,0:T(8,128)S(1)} %get-tuple-element.39), channel_id=1, source_target_pairs={{0,1},{1,2},{2,3},{3,4},{4,5},{5,6},{6,7},{7,0},{8,9},{9,10},{10,1... | collective-permute-start | bytes 294920 | tf_op jit(solution)/shard_map/ppermute | solution.py:72
  45.5 0.0 collective-permute-start.14
  45.5 1.6 %collective-permute-done.13.ylo = f32[192,128]{1,0:T(8,128)S(1)} collective-permute-done((f32[192,128]{1,0:T(8,128)S(1)}, f32[192,128]{1,0:T(8,128)S(1)}, u32[]{:S(2)}, u32[]{:S(2)}) %collective-permute-start.13) | collective-permute-done | bytes 98336 | tf_op jit(solution)/shard_map/ppermute | solution.py:72
  47.1 3.6 %collective-permute-done.14.yhi = f32[192,128]{1,0:T(8,128)S(1)} collective-permute-done((f32[192,128]{1,0:T(8,128)S(1)}, f32[192,128]{1,0:T(8,128)S(1)}, u32[]{:S(2)}, u32[]{:S(2)}) %collective-permute-start.14) | collective-permute-done | bytes 98336 | tf_op jit(solution)/shard_map/ppermute | solution.py:72
  50.8 2.6 %shard_map.69 = f32[4,32,256]{2,1,0:T(8,128)} custom-call(f32[8]{0:T(128)S(1)} %pad_maximum_fusion.masks, f32[8,40,256]{2,1,0:T(8,128)S(1)} %get-tuple-element.28.t_in, f32[6,40,256]{2,1,0:T(8,128)S(1)} %get-tuple-element.29.a_in, f32[6,40,256]{2,1,0:T(8,128)S(1)} %get-tuple-element.30.b_in, f32[6,40,256]{2,1,0:T(8,128)S(1)} %get-tuple-element.31.u.u_in, ...), custom_call_target="tpu_custom_call" | custom-call | tf_op jit(solution)/shard_map/pallas_call | solution.py:444
  (6 shorter events, 0.0 us)
Async XLA Ops:
  0.0 8.0 %copy-start = (f32[4,32,256]{2,1,0:T(8,128)S(1)}, f32[4,32,256]{2,1,0:T(8,128)}, u32[]{:S(2)}) copy-start(f32[4,32,256]{2,1,0:T(8,128)} %rhs.4) | copy-start | bytes 393220
  0.0 8.0 %copy-start.1 = (f32[4,32,256]{2,1,0:T(8,128)S(1)}, f32[4,32,256]{2,1,0:T(8,128)}, u32[]{:S(2)}) copy-start(f32[4,32,256]{2,1,0:T(8,128)} %perm.3) | copy-start | bytes 393220
  0.0 8.0 %copy-start.2 = (f32[4,32,256]{2,1,0:T(8,128)S(1)}, f32[4,32,256]{2,1,0:T(8,128)}, u32[]{:S(2)}) copy-start(f32[4,32,256]{2,1,0:T(8,128)} %acc.3) | copy-start | bytes 393220
  1.3 5.4 %collective-permute-start = (f32[232,256]{1,0:T(8,128)S(1)}, f32[232,256]{1,0:T(8,128)S(1)}, u32[]{:S(2)}, u32[]{:S(2)}) collective-permute-start(f32[232,256]{1,0:T(8,128)S(1)} %get-tuple-element.23), channel_id=1, source_target_pairs={{0,8},{1,0},{2,10},{3,2},{4,12},{5,4},{6,14},{7,6},{8,16},{9,1},{1... | collective-permute-start | bytes 712712 | tf_op jit(solution)/shard_map/ppermute | solution.py:34
  1.3 6.7 %collective-permute-start.1 = (f32[232,256]{1,0:T(8,128)S(1)}, f32[232,256]{1,0:T(8,128)S(1)}, u32[]{:S(2)}, u32[]{:S(2)}) collective-permute-start(f32[232,256]{1,0:T(8,128)S(1)} %get-tuple-element.24), channel_id=1, source_target_pairs={{0,1},{1,9},{2,3},{3,11},{4,5},{5,13},{6,7},{7,15},{8,0},{9,17},{1... | collective-permute-start | bytes 712712 | tf_op jit(solution)/shard_map/ppermute | solution.py:34
  3.0 5.0 %collective-permute-start.2 = (f32[232,256]{1,0:T(8,128)S(1)}, f32[232,256]{1,0:T(8,128)S(1)}, u32[]{:S(2)}, u32[]{:S(2)}) collective-permute-start(f32[232,256]{1,0:T(8,128)S(1)} %get-tuple-element.25), channel_id=1, source_target_pairs={{120,128},{128,120},{121,129},{129,121},{122,130},{130,122},{123,1... | collective-permute-start | bytes 712712 | tf_op jit(solution)/shard_map/ppermute | solution.py:45
  3.7 0.7 %copy-start.5 = (s32[32]{0:T(128)S(1)}, s32[32]{0:T(128)}, u32[]{:S(2)}) copy-start(s32[32]{0:T(128)} %param.11) | copy-start | bytes 388
  4.5 3.6 %copy-start.3 = (f32[2,16,128]{2,1,0:T(8,128)S(1)}, f32[2,16,128]{2,1,0:T(8,128)}, u32[]{:S(2)}) copy-start(f32[2,16,128]{2,1,0:T(8,128)} %cperm.5) | copy-start | bytes 49156
  8.1 6.8 %copy-start.4 = (f32[2,16,128]{2,1,0:T(8,128)S(1)}, f32[2,16,128]{2,1,0:T(8,128)}, u32[]{:S(2)}) copy-start(f32[2,16,128]{2,1,0:T(8,128)} %cacc.1) | copy-start | bytes 49156
  8.1 3.2 %collective-permute-start.3 = (f32[64,256]{1,0:T(8,128)S(1)}, f32[64,256]{1,0:T(8,128)S(1)}, u32[]{:S(2)}, u32[]{:S(2)}) collective-permute-start(f32[64,256]{1,0:T(8,128)S(1)} %get-tuple-element.26), channel_id=1, source_target_pairs={{0,1},{1,2},{2,3},{3,4},{4,5},{5,6},{6,7},{7,0},{8,9},{9,10},{10,1... | collective-permute-start | bytes 196616 | tf_op jit(solution)/shard_map/ppermute | solution.py:72
  10.0 4.9 %collective-permute-start.4 = (f32[64,256]{1,0:T(8,128)S(1)}, f32[64,256]{1,0:T(8,128)S(1)}, u32[]{:S(2)}, u32[]{:S(2)}) collective-permute-start(f32[64,256]{1,0:T(8,128)S(1)} %get-tuple-element.27), channel_id=1, source_target_pairs={{0,7},{1,0},{2,1},{3,2},{4,3},{5,4},{6,5},{7,6},{8,15},{9,8},{10,9... | collective-permute-start | bytes 196616 | tf_op jit(solution)/shard_map/ppermute | solution.py:72
  16.8 11.3 %collective-permute-start.5 = (f32[8,16,128]{2,1,0:T(8,128)S(1)}, f32[8,16,128]{2,1,0:T(8,128)S(1)}, u32[]{:S(2)}, u32[]{:S(2)}) collective-permute-start(f32[8,16,128]{2,1,0:T(8,128)S(1)} %get-tuple-element.34), channel_id=1, source_target_pairs={{0,8},{1,0},{2,10},{3,2},{4,12},{5,4},{6,14},{7,6},{8,16},{9,1},{1... | collective-permute-start | bytes 196616 | tf_op jit(solution)/shard_map/ppermute | solution.py:34
  26.7 6.0 %collective-permute-start.6 = (f32[8,16,128]{2,1,0:T(8,128)S(1)}, f32[8,16,128]{2,1,0:T(8,128)S(1)}, u32[]{:S(2)}, u32[]{:S(2)}) collective-permute-start(f32[8,16,128]{2,1,0:T(8,128)S(1)} %get-tuple-element.35), channel_id=1, source_target_pairs={{0,1},{1,9},{2,3},{3,11},{4,5},{5,13},{6,7},{7,15},{8,0},{9,17},{1... | collective-permute-start | bytes 196616 | tf_op jit(solution)/shard_map/ppermute | solution.py:34
  26.7 11.4 %collective-permute-start.7 = (f32[8,16,128]{2,1,0:T(8,128)S(1)}, f32[8,16,128]{2,1,0:T(8,128)S(1)}, u32[]{:S(2)}, u32[]{:S(2)}) collective-permute-start(f32[8,16,128]{2,1,0:T(8,128)S(1)} %get-tuple-element.36), channel_id=1, source_target_pairs={{120,128},{128,120},{121,129},{129,121},{122,130},{130,122},{123,1... | collective-permute-start | bytes 196616 | tf_op jit(solution)/shard_map/ppermute | solution.py:45
  28.1 8.5 %collective-permute-start.8 = (f32[4,16,128]{2,1,0:T(8,128)S(1)}, f32[4,16,128]{2,1,0:T(8,128)S(1)}, u32[]{:S(2)}, u32[]{:S(2)}) collective-permute-start(f32[4,16,128]{2,1,0:T(8,128)S(1)} %slice.8), channel_id=1, source_target_pairs={{0,8},{1,0},{2,10},{3,2},{4,12},{5,4},{6,14},{7,6},{8,16},{9,1},{1... | collective-permute-start | bytes 98312 | tf_op jit(solution)/shard_map/ppermute | solution.py:34
  32.8 3.9 %collective-permute-start.9 = (f32[4,16,128]{2,1,0:T(8,128)S(1)}, f32[4,16,128]{2,1,0:T(8,128)S(1)}, u32[]{:S(2)}, u32[]{:S(2)}) collective-permute-start(f32[4,16,128]{2,1,0:T(8,128)S(1)} %slice.9), channel_id=1, source_target_pairs={{0,1},{1,9},{2,3},{3,11},{4,5},{5,13},{6,7},{7,15},{8,0},{9,17},{1... | collective-permute-start | bytes 98312 | tf_op jit(solution)/shard_map/ppermute | solution.py:34
  32.8 8.8 %collective-permute-start.12 = (f32[7,16,128]{2,1,0:T(8,128)S(1)}, f32[7,16,128]{2,1,0:T(8,128)S(1)}, u32[]{:S(2)}, u32[]{:S(2)}) collective-permute-start(f32[7,16,128]{2,1,0:T(8,128)S(1)} %shard_map.67), channel_id=1, source_target_pairs={{104,128},{128,104},{105,129},{129,105},{106,130},{130,106},{107,1... | collective-permute-start | bytes 172040 | tf_op jit(solution)/shard_map/ppermute | solution.py:45
  36.6 5.0 %collective-permute-start.10 = (f32[4,16,128]{2,1,0:T(8,128)S(1)}, f32[4,16,128]{2,1,0:T(8,128)S(1)}, u32[]{:S(2)}, u32[]{:S(2)}) collective-permute-start(f32[4,16,128]{2,1,0:T(8,128)S(1)} %collective-permute-done.8.plus2), channel_id=1, source_target_pairs={{0,8},{1,0},{2,10},{3,2},{4,12},{5,4},{6,14},{7,6},{8,16},{9,1},{1... | collective-permute-start | bytes 98312 | tf_op jit(solution)/shard_map/ppermute | solution.py:34
  36.7 5.0 %collective-permute-start.11 = (f32[4,16,128]{2,1,0:T(8,128)S(1)}, f32[4,16,128]{2,1,0:T(8,128)S(1)}, u32[]{:S(2)}, u32[]{:S(2)}) collective-permute-start(f32[4,16,128]{2,1,0:T(8,128)S(1)} %collective-permute-done.9.minus2), channel_id=1, source_target_pairs={{0,1},{1,9},{2,3},{3,11},{4,5},{5,13},{6,7},{7,15},{8,0},{9,17},{1... | collective-permute-start | bytes 98312 | tf_op jit(solution)/shard_map/ppermute | solution.py:34
  41.7 5.4 %collective-permute-start.13 = (f32[192,128]{1,0:T(8,128)S(1)}, f32[192,128]{1,0:T(8,128)S(1)}, u32[]{:S(2)}, u32[]{:S(2)}) collective-permute-start(f32[192,128]{1,0:T(8,128)S(1)} %get-tuple-element.39), channel_id=1, source_target_pairs={{0,1},{1,2},{2,3},{3,4},{4,5},{5,6},{6,7},{7,0},{8,9},{9,10},{10,1... | collective-permute-start | bytes 294920 | tf_op jit(solution)/shard_map/ppermute | solution.py:72
  45.5 5.3 %collective-permute-start.14 = (f32[192,128]{1,0:T(8,128)S(1)}, f32[192,128]{1,0:T(8,128)S(1)}, u32[]{:S(2)}, u32[]{:S(2)}) collective-permute-start(f32[192,128]{1,0:T(8,128)S(1)} %get-tuple-element.40), channel_id=1, source_target_pairs={{0,7},{1,0},{2,1},{3,2},{4,3},{5,4},{6,5},{7,6},{8,15},{9,8},{10,9... | collective-permute-start | bytes 294920 | tf_op jit(solution)/shard_map/ppermute | solution.py:72

commit v8 on v7

--- a/solution.py
+++ b/solution.py
@@ -42,6 +42,28 @@
             for pen in range(pens):
                 here, there = low * pens + pen, (low + apart) * pens + pen
                 pairs += [(here, there), (there, here)]
+    return lax.ppermute(x, ("slab", "pen"), pairs)
+
+
+def first_to_first(x):
+    slabs, pens = lax.axis_size("slab"), lax.axis_size("pen")
+    pairs = [
+        (slab * pens + pen, (slab - LINE) * pens + pen)
+        for slab in range(LINE, slabs, LINE)
+        for pen in range(pens)
+    ]
+    return lax.ppermute(x, ("slab", "pen"), pairs)
+
+
+def ends_onward(x):
+    slabs, pens = lax.axis_size("slab"), lax.axis_size("pen")
+    pairs = []
+    for slab in range(0, slabs - LINE, LINE):
+        for pen in range(pens):
+            first, last, onward = (
+                at * pens + pen for at in (slab, slab + LINE - 1, slab + LINE)
+            )
+            pairs += [(first, last), (last, onward)]
     return lax.ppermute(x, ("slab", "pen"), pairs)
 
 
@@ -120,6 +142,12 @@
         out[Z1_CO : Z1_CO + 8, :] = to_wide(held[jnp.where(up, 1, 0)])
 
 
+def hand_on(across, handed, out):
+    @pl.when(place()[1] == 0)
+    def _():
+        out[...] = handed[...]
+
+
 def fine_rows(own, lo, hi, base, depth, z, first, count):
     if z < 0:
         at = base + 32 * (z + depth)
@@ -141,7 +169,7 @@
 Y1_RHS = 30
 Y1_ACC = 46
 Y1_CO = 62
-Y1_ROWS = 64
+Y1_ROWS = 72
 
 
 def pack_y1(rhs, perm, acc, cperm, plus, minus, across, up, down):
@@ -274,7 +302,7 @@
 
 Y2_B = 84
 Y2_U = 156
-Y2_ROWS = 192
+Y2_ROWS = 200
 
 
 def pack_y2(
@@ -384,7 +412,7 @@
             uf[k, 2:4, lane : lane + CCOLS] = ylo[at + 2 * half : at + 2 * half + 2, :] * mlo
             uf[k, 36:38, lane : lane + CCOLS] = yhi[at + 2 * half : at + 2 * half + 2, :] * mhi
         both = 2 * (k // 2)
-        uf[k] = uf[k] + t_in[k] * jnp.concatenate([cf[both], cf[both + 1]], axis=1)
+        uf[k] = uf[k] + t_in[k] * jnp.concatenate([cf[both, 0:FR], cf[both + 1, 0:FR]], axis=1)
     for k in range(8):
         xs[k] = smooth_xy(uf[k])
     for k in range(6):
@@ -445,7 +473,7 @@
         post_kernel,
         [SM] + [VM] * 9,
         f32(4, ROWS, COLS),
-        ((8, FR, COLS), (8, FR, CCOLS), (8, FR, COLS), (26, CR, CCOLS)),
+        ((8, FR, COLS), (8, FR + 8, CCOLS), (8, FR, COLS), (26, CR, CCOLS)),
     )(*operands)
 
 
@@ -467,7 +495,15 @@
             )
         )
     )
-    across = between_lines(across, 1)
+    across = pl.pallas_call(
+        hand_on,
+        in_specs=[VM] * 2,
+        out_specs=VM,
+        out_shape=message,
+        input_output_aliases={0: 0},
+        compiler_params=pltpu.CompilerParams(vmem_limit_bytes=8 * 1024 * 1024),
+    )(across, first_to_first(across))
+    across = ends_onward(across)
     plus = along_lines(plus, 1)
     minus = along_lines(minus, -1)
 

time: 53.6 us -> 54.9 us (1.024)
  waiting for transfers between devices: 17.3 us -> 18.3 us
    ppermute x8, waiting for transfers between devices: 3.87 us -> 5.75 us  [along_lines(): return lax.ppermute(x, ('slab', 'pen'), pairs)]
    ppermute x4, starting transfers between devices: 5.83 us -> 4.32 us  [rotated(): lax.ppermute(x, axis, [(i, (i + by) % devices) for i in range(devices)])]
    ppermute x0 -> x2, starting transfers between devices: none -> 1.48 us  [the longest x1 0.81 us: ends_onward(): return lax.ppermute(x, ('slab', 'pen'), pairs)]
    ppermute x3 -> x2, waiting for transfers between devices: 3.53 us -> 2.63 us  [between_lines(): return lax.ppermute(x, ('slab', 'pen'), pairs)]
    ppermute x3 -> x2, starting transfers between devices: 5.11 us -> 5.34 us  [between_lines(): return lax.ppermute(x, ('slab', 'pen'), pairs)]
  transfers between devices with their start and end apart: 15 -> 16, of which waited for: 8 -> 8; matrix products, arithmetic and copies ran while one was open for 1% -> 1% of each run, Pallas kernels for 0% -> 0%
where the time goes in v8:
time: 54.9 us; the launch traced here: 54.6 us
  starting transfers between devices  28.9 us (53%)
  waiting for transfers between devices  18.3 us (33%)
  Pallas kernels  5.96 us (11%)
  local copies, waits for them, and re-layouts  0.78 us (1%)
    ppermute x8, starting transfers between devices, along_lines(): return lax.ppermute(x, ('slab', 'pen'), pairs)  17.7 us
    ppermute x4, waiting for transfers between devices, rotated(): lax.ppermute(x, axis, [(i, (i + by) % devices) for i in range(devices)])  9.89 us
    ppermute x8, waiting for transfers between devices, along_lines(): return lax.ppermute(x, ('slab', 'pen'), pairs)  5.75 us
    ppermute x2, starting transfers between devices, between_lines(): return lax.ppermute(x, ('slab', 'pen'), pairs)  5.34 us
    ppermute x4, starting transfers between devices, rotated(): lax.ppermute(x, axis, [(i, (i + by) % devices) for i in range(devices)])  4.32 us
    pallas_call x1, Pallas kernels, post_call(): call(post_kernel, [SM] + [VM] * 9, f32(4, ROWS, COLS), ((8, FR, COLS), (8...  2.66 us
    ppermute x2, waiting for transfers between devices, between_lines(): return lax.ppermute(x, ('slab', 'pen'), pairs)  2.63 us
    pallas_call x1, Pallas kernels, pre_call(): call(pre_kernel, [SM] + [VM] * 10, (f32(8, FR, COLS), f32(6, FR, COLS), f...  1.9 us
  transfers between devices with their start and end apart: 16, of which 8 were waited for; matrix products, arithmetic and copies ran while one was open for 1% of the time, Pallas kernels for 0%

profile of v8, /device:TPU:63, one launch (start us, length us, event | category | flops | bytes accessed | tf_op | source)
XLA Modules:
  0.0 54.6 jit_solution(17380576168851169884)
XLA Ops:
  0.0 1.2 %shard_map.64 = (f32[232,256]{1,0:T(8,128)S(1)}, f32[232,256]{1,0:T(8,128)S(1)}, f32[232,256]{1,0:T(8,128)S(1)}) custom-call(f32[128,256]{1,0:T(8,128)} %bitcast.6, f32[128,256]{1,0:T(8,128)} %bitcast.7, f32[128,256]{1,0:T(8,128)} %bitcast.8, f32[2,16,128]{2,1,0:T(8,128)} %cperm.5), custom_call_target="tpu_custom_call" | custom-call | tf_op jit(solution)/shard_map/pallas_call | solution.py:482
  1.2 0.7 %collective-permute-start.2 = (f32[232,256]{1,0:T(8,128)S(1)}, f32[232,256]{1,0:T(8,128)S(1)}, u32[]{:S(2)}, u32[]{:S(2)}) collective-permute-start(f32[232,256]{1,0:T(8,128)S(1)} %get-tuple-element.25.across), channel_id=1, source_target_pairs={{128,0},{129,1},{130,2},{131,3},{132,4},{133,5},{134,6},{135,7},{2... | collective-permute-start | bytes 712712 | tf_op jit(solution)/shard_map/ppermute | solution.py:55
  1.9 1.6 %collective-permute-start = (f32[232,256]{1,0:T(8,128)S(1)}, f32[232,256]{1,0:T(8,128)S(1)}, u32[]{:S(2)}, u32[]{:S(2)}) collective-permute-start(f32[232,256]{1,0:T(8,128)S(1)} %get-tuple-element.23), channel_id=1, source_target_pairs={{0,8},{1,0},{2,10},{3,2},{4,12},{5,4},{6,14},{7,6},{8,16},{9,1},{1... | collective-permute-start | bytes 712712 | tf_op jit(solution)/shard_map/ppermute | solution.py:34
  3.6 0.0 collective-permute-start.1
  3.6 0.0 copy-start.5
  3.6 0.7 %copy-done.5 = s32[32]{0:T(128)S(1)} copy-done((s32[32]{0:T(128)S(1)}, s32[32]{0:T(128)}, u32[]{:S(2)}) %copy-start.5) | copy-done | bytes 152
  4.3 0.1 copy.10
  4.3 0.1 reduce-window.9
  4.4 0.1 reduce
  4.5 0.2 compare_reduce_fusion
  4.7 0.0 copy-start
  4.7 0.0 copy-start.1
  4.7 0.0 copy-start.2
  4.8 0.0 collective-permute-done.2.handed
  4.8 0.0 copy-start.3
  4.8 0.8 %collective-permute-start.3 = (f32[232,256]{1,0:T(8,128)S(1)}, f32[232,256]{1,0:T(8,128)S(1)}, u32[]{:S(2)}, u32[]{:S(2)}) collective-permute-start(f32[232,256]{1,0:T(8,128)S(1)} %shard_map.65), channel_id=1, source_target_pairs={{0,120},{120,128},{1,121},{121,129},{2,122},{122,130},{3,123},{123... | collective-permute-start | bytes 712712 | tf_op jit(solution)/shard_map/ppermute | solution.py:67
  5.6 0.1 add_convert_fusion
  5.7 1.9 %collective-permute-done.plus = f32[232,256]{1,0:T(8,128)S(1)} collective-permute-done((f32[232,256]{1,0:T(8,128)S(1)}, f32[232,256]{1,0:T(8,128)S(1)}, u32[]{:S(2)}, u32[]{:S(2)}) %collective-permute-start) | collective-permute-done | bytes 237600 | tf_op jit(solution)/shard_map/ppermute | solution.py:34
  7.7 3.1 %collective-permute-done.1.minus = f32[232,256]{1,0:T(8,128)S(1)} collective-permute-done((f32[232,256]{1,0:T(8,128)S(1)}, f32[232,256]{1,0:T(8,128)S(1)}, u32[]{:S(2)}, u32[]{:S(2)}) %collective-permute-start.1) | collective-permute-done | bytes 237600 | tf_op jit(solution)/shard_map/ppermute | solution.py:34
  10.7 0.0 collective-permute-done.3.across
  10.7 0.0 copy-done
  10.7 0.0 copy-done.1
  10.8 0.0 copy-done.2
  10.8 0.0 copy-done.3
  10.8 0.0 copy-start.4
  10.8 0.1 shard_map.66
  10.8 0.2 collective-permute-start.4
  11.1 0.3 collective-permute-start.5
  11.4 0.1 pad_maximum_fusion.masks
  11.4 1.0 %collective-permute-done.4.ylo = f32[72,256]{1,0:T(8,128)S(1)} collective-permute-done((f32[72,256]{1,0:T(8,128)S(1)}, f32[72,256]{1,0:T(8,128)S(1)}, u32[]{:S(2)}, u32[]{:S(2)}) %collective-permute-start.4) | collective-permute-done | bytes 73760 | tf_op jit(solution)/shard_map/ppermute | solution.py:94
  12.5 3.6 %collective-permute-done.5.yhi = f32[72,256]{1,0:T(8,128)S(1)} collective-permute-done((f32[72,256]{1,0:T(8,128)S(1)}, f32[72,256]{1,0:T(8,128)S(1)}, u32[]{:S(2)}, u32[]{:S(2)}) %collective-permute-start.5) | collective-permute-done | bytes 73760 | tf_op jit(solution)/shard_map/ppermute | solution.py:94
  16.1 0.0 copy-done.4
  16.1 1.9 %shard_map.67 = (f32[8,40,256]{2,1,0:T(8,128)S(1)}, f32[6,40,256]{2,1,0:T(8,128)S(1)}, f32[6,40,256]{2,1,0:T(8,128)S(1)}, f32[6,40,256]{2,1,0:T(8,128)S(1)}, f32...) custom-call(f32[8]{0:T(128)S(1)} %pad_maximum_fusion.masks, ...), custom_call_target="tpu_custom_call" | custom-call | tf_op jit(solution)/shard_map/pallas_call | solution.py:456
  18.0 10.8 %collective-permute-start.6 = (f32[8,16,128]{2,1,0:T(8,128)S(1)}, f32[8,16,128]{2,1,0:T(8,128)S(1)}, u32[]{:S(2)}, u32[]{:S(2)}) collective-permute-start(f32[8,16,128]{2,1,0:T(8,128)S(1)} %get-tuple-element.34), channel_id=1, source_target_pairs={{0,8},{1,0},{2,10},{3,2},{4,12},{5,4},{6,14},{7,6},{8,16},{9,1},{1... | collective-permute-start | bytes 196616 | tf_op jit(solution)/shard_map/ppermute | solution.py:34
  28.8 0.0 collective-permute-start.7
  28.8 0.7 %collective-permute-start.8 = (f32[8,16,128]{2,1,0:T(8,128)S(1)}, f32[8,16,128]{2,1,0:T(8,128)S(1)}, u32[]{:S(2)}, u32[]{:S(2)}) collective-permute-start(f32[8,16,128]{2,1,0:T(8,128)S(1)} %get-tuple-element.36), channel_id=1, source_target_pairs={{120,128},{128,120},{121,129},{129,121},{122,130},{130,122},{123,1... | collective-permute-start | bytes 196616 | tf_op jit(solution)/shard_map/ppermute | solution.py:45
  29.5 0.7 %collective-permute-done.6.plus1 = f32[8,16,128]{2,1,0:T(8,128)S(1)} collective-permute-done((f32[8,16,128]{2,1,0:T(8,128)S(1)}, f32[8,16,128]{2,1,0:T(8,128)S(1)}, u32[]{:S(2)}, u32[]{:S(2)}) %collective-permute-start.6) | collective-permute-done | bytes 65568 | tf_op jit(solution)/shard_map/ppermute | solution.py:34
  30.2 3.7 %collective-permute-start.9 = (f32[4,16,128]{2,1,0:T(8,128)S(1)}, f32[4,16,128]{2,1,0:T(8,128)S(1)}, u32[]{:S(2)}, u32[]{:S(2)}) collective-permute-start(f32[4,16,128]{2,1,0:T(8,128)S(1)} %slice.8), channel_id=1, source_target_pairs={{0,8},{1,0},{2,10},{3,2},{4,12},{5,4},{6,14},{7,6},{8,16},{9,1},{1... | collective-permute-start | bytes 98312 | tf_op jit(solution)/shard_map/ppermute | solution.py:34
  33.9 0.0 collective-permute-done.7.minus1
  33.9 0.0 collective-permute-start.10
  34.0 4.7 %collective-permute-start.13 = (f32[7,16,128]{2,1,0:T(8,128)S(1)}, f32[7,16,128]{2,1,0:T(8,128)S(1)}, u32[]{:S(2)}, u32[]{:S(2)}) collective-permute-start(f32[7,16,128]{2,1,0:T(8,128)S(1)} %shard_map.68), channel_id=1, source_target_pairs={{104,128},{128,104},{105,129},{129,105},{106,130},{130,106},{107,1... | collective-permute-start | bytes 172040 | tf_op jit(solution)/shard_map/ppermute | solution.py:45
  38.7 0.0 collective-permute-done.9.plus2
  38.7 0.0 collective-permute-start.11
  38.7 0.0 collective-permute-done.10.minus2
  38.7 1.4 %collective-permute-start.12 = (f32[4,16,128]{2,1,0:T(8,128)S(1)}, f32[4,16,128]{2,1,0:T(8,128)S(1)}, u32[]{:S(2)}, u32[]{:S(2)}) collective-permute-start(f32[4,16,128]{2,1,0:T(8,128)S(1)} %collective-permute-done.10.minus2), channel_id=1, source_target_pairs={{0,1},{1,9},{2,3},{3,11},{4,5},{5,13},{6,7},{7,15},{8,0},{9,17},{1... | collective-permute-start | bytes 98312 | tf_op jit(solution)/shard_map/ppermute | solution.py:34
  40.2 0.0 collective-permute-done.8.across
  40.2 2.6 %collective-permute-done.13.far = f32[7,16,128]{2,1,0:T(8,128)S(1)} collective-permute-done((f32[7,16,128]{2,1,0:T(8,128)S(1)}, f32[7,16,128]{2,1,0:T(8,128)S(1)}, u32[]{:S(2)}, u32[]{:S(2)}) %collective-permute-start.13) | collective-permute-done | bytes 57376 | tf_op jit(solution)/shard_map/ppermute | solution.py:45
  42.8 0.0 collective-permute-done.11.plus3
  42.8 0.0 collective-permute-done.12.minus3
  42.8 0.1 shard_map.69
  42.9 3.8 %collective-permute-start.14 = (f32[200,128]{1,0:T(8,128)S(1)}, f32[200,128]{1,0:T(8,128)S(1)}, u32[]{:S(2)}, u32[]{:S(2)}) collective-permute-start(f32[200,128]{1,0:T(8,128)S(1)} %get-tuple-element.39), channel_id=1, source_target_pairs={{0,1},{1,2},{2,3},{3,4},{4,5},{5,6},{6,7},{7,0},{8,9},{9,10},{10,1... | collective-permute-start | bytes 307208 | tf_op jit(solution)/shard_map/ppermute | solution.py:94
  46.7 0.0 collective-permute-start.15
  46.7 1.7 %collective-permute-done.14.ylo = f32[200,128]{1,0:T(8,128)S(1)} collective-permute-done((f32[200,128]{1,0:T(8,128)S(1)}, f32[200,128]{1,0:T(8,128)S(1)}, u32[]{:S(2)}, u32[]{:S(2)}) %collective-permute-start.14) | collective-permute-done | bytes 102432 | tf_op jit(solution)/shard_map/ppermute | solution.py:94
  48.4 3.6 %collective-permute-done.15.yhi = f32[200,128]{1,0:T(8,128)S(1)} collective-permute-done((f32[200,128]{1,0:T(8,128)S(1)}, f32[200,128]{1,0:T(8,128)S(1)}, u32[]{:S(2)}, u32[]{:S(2)}) %collective-permute-start.15) | collective-permute-done | bytes 102432 | tf_op jit(solution)/shard_map/ppermute | solution.py:94
  52.0 2.7 %shard_map.70 = f32[4,32,256]{2,1,0:T(8,128)} custom-call(f32[8]{0:T(128)S(1)} %pad_maximum_fusion.masks, f32[8,40,256]{2,1,0:T(8,128)S(1)} %get-tuple-element.28.t_in, f32[6,40,256]{2,1,0:T(8,128)S(1)} %get-tuple-element.29.a_in, f32[6,40,256]{2,1,0:T(8,128)S(1)} %get-tuple-element.30.b_in, f32[6,40,256]{2,1,0:T(8,128)S(1)} %get-tuple-element.31.u.u_in, ...), custom_call_target="tpu_custom_call" | custom-call | tf_op jit(solution)/shard_map/pallas_call | solution.py:472
  (7 shorter events, 0.1 us)
Async XLA Ops:
  1.2 3.5 %collective-permute-start.2 = (f32[232,256]{1,0:T(8,128)S(1)}, f32[232,256]{1,0:T(8,128)S(1)}, u32[]{:S(2)}, u32[]{:S(2)}) collective-permute-start(f32[232,256]{1,0:T(8,128)S(1)} %get-tuple-element.25.across), channel_id=1, source_target_pairs={{128,0},{129,1},{130,2},{131,3},{132,4},{133,5},{134,6},{135,7},{2... | collective-permute-start | bytes 712712 | tf_op jit(solution)/shard_map/ppermute | solution.py:55
  1.9 5.7 %collective-permute-start = (f32[232,256]{1,0:T(8,128)S(1)}, f32[232,256]{1,0:T(8,128)S(1)}, u32[]{:S(2)}, u32[]{:S(2)}) collective-permute-start(f32[232,256]{1,0:T(8,128)S(1)} %get-tuple-element.23), channel_id=1, source_target_pairs={{0,8},{1,0},{2,10},{3,2},{4,12},{5,4},{6,14},{7,6},{8,16},{9,1},{1... | collective-permute-start | bytes 712712 | tf_op jit(solution)/shard_map/ppermute | solution.py:34
  3.6 7.2 %collective-permute-start.1 = (f32[232,256]{1,0:T(8,128)S(1)}, f32[232,256]{1,0:T(8,128)S(1)}, u32[]{:S(2)}, u32[]{:S(2)}) collective-permute-start(f32[232,256]{1,0:T(8,128)S(1)} %get-tuple-element.24), channel_id=1, source_target_pairs={{0,1},{1,9},{2,3},{3,11},{4,5},{5,13},{6,7},{7,15},{8,0},{9,17},{1... | collective-permute-start | bytes 712712 | tf_op jit(solution)/shard_map/ppermute | solution.py:34
  3.6 0.7 %copy-start.5 = (s32[32]{0:T(128)S(1)}, s32[32]{0:T(128)}, u32[]{:S(2)}) copy-start(s32[32]{0:T(128)} %param.11) | copy-start | bytes 388
  4.7 6.0 %copy-start = (f32[4,32,256]{2,1,0:T(8,128)S(1)}, f32[4,32,256]{2,1,0:T(8,128)}, u32[]{:S(2)}) copy-start(f32[4,32,256]{2,1,0:T(8,128)} %rhs.4) | copy-start | bytes 393220
  4.7 6.0 %copy-start.1 = (f32[4,32,256]{2,1,0:T(8,128)S(1)}, f32[4,32,256]{2,1,0:T(8,128)}, u32[]{:S(2)}) copy-start(f32[4,32,256]{2,1,0:T(8,128)} %perm.3) | copy-start | bytes 393220
  4.7 6.0 %copy-start.2 = (f32[4,32,256]{2,1,0:T(8,128)S(1)}, f32[4,32,256]{2,1,0:T(8,128)}, u32[]{:S(2)}) copy-start(f32[4,32,256]{2,1,0:T(8,128)} %acc.3) | copy-start | bytes 393220
  4.8 6.0 %copy-start.3 = (f32[2,16,128]{2,1,0:T(8,128)S(1)}, f32[2,16,128]{2,1,0:T(8,128)}, u32[]{:S(2)}) copy-start(f32[2,16,128]{2,1,0:T(8,128)} %cperm.5) | copy-start | bytes 49156
  4.8 5.9 %collective-permute-start.3 = (f32[232,256]{1,0:T(8,128)S(1)}, f32[232,256]{1,0:T(8,128)S(1)}, u32[]{:S(2)}, u32[]{:S(2)}) collective-permute-start(f32[232,256]{1,0:T(8,128)S(1)} %shard_map.65), channel_id=1, source_target_pairs={{0,120},{120,128},{1,121},{121,129},{2,122},{122,130},{3,123},{123... | collective-permute-start | bytes 712712 | tf_op jit(solution)/shard_map/ppermute | solution.py:67
  10.8 5.3 %copy-start.4 = (f32[2,16,128]{2,1,0:T(8,128)S(1)}, f32[2,16,128]{2,1,0:T(8,128)}, u32[]{:S(2)}) copy-start(f32[2,16,128]{2,1,0:T(8,128)} %cacc.1) | copy-start | bytes 49156
  10.8 1.6 %collective-permute-start.4 = (f32[72,256]{1,0:T(8,128)S(1)}, f32[72,256]{1,0:T(8,128)S(1)}, u32[]{:S(2)}, u32[]{:S(2)}) collective-permute-start(f32[72,256]{1,0:T(8,128)S(1)} %get-tuple-element.26), channel_id=1, source_target_pairs={{0,1},{1,2},{2,3},{3,4},{4,5},{5,6},{6,7},{7,0},{8,9},{9,10},{10,1... | collective-permute-start | bytes 221192 | tf_op jit(solution)/shard_map/ppermute | solution.py:94
  11.1 5.0 %collective-permute-start.5 = (f32[72,256]{1,0:T(8,128)S(1)}, f32[72,256]{1,0:T(8,128)S(1)}, u32[]{:S(2)}, u32[]{:S(2)}) collective-permute-start(f32[72,256]{1,0:T(8,128)S(1)} %get-tuple-element.27), channel_id=1, source_target_pairs={{0,7},{1,0},{2,1},{3,2},{4,3},{5,4},{6,5},{7,6},{8,15},{9,8},{10,9... | collective-permute-start | bytes 221192 | tf_op jit(solution)/shard_map/ppermute | solution.py:94
  18.0 12.2 %collective-permute-start.6 = (f32[8,16,128]{2,1,0:T(8,128)S(1)}, f32[8,16,128]{2,1,0:T(8,128)S(1)}, u32[]{:S(2)}, u32[]{:S(2)}) collective-permute-start(f32[8,16,128]{2,1,0:T(8,128)S(1)} %get-tuple-element.34), channel_id=1, source_target_pairs={{0,8},{1,0},{2,10},{3,2},{4,12},{5,4},{6,14},{7,6},{8,16},{9,1},{1... | collective-permute-start | bytes 196616 | tf_op jit(solution)/shard_map/ppermute | solution.py:34
  28.8 5.1 %collective-permute-start.7 = (f32[8,16,128]{2,1,0:T(8,128)S(1)}, f32[8,16,128]{2,1,0:T(8,128)S(1)}, u32[]{:S(2)}, u32[]{:S(2)}) collective-permute-start(f32[8,16,128]{2,1,0:T(8,128)S(1)} %get-tuple-element.35), channel_id=1, source_target_pairs={{0,1},{1,9},{2,3},{3,11},{4,5},{5,13},{6,7},{7,15},{8,0},{9,17},{1... | collective-permute-start | bytes 196616 | tf_op jit(solution)/shard_map/ppermute | solution.py:34
  28.8 11.4 %collective-permute-start.8 = (f32[8,16,128]{2,1,0:T(8,128)S(1)}, f32[8,16,128]{2,1,0:T(8,128)S(1)}, u32[]{:S(2)}, u32[]{:S(2)}) collective-permute-start(f32[8,16,128]{2,1,0:T(8,128)S(1)} %get-tuple-element.36), channel_id=1, source_target_pairs={{120,128},{128,120},{121,129},{129,121},{122,130},{130,122},{123,1... | collective-permute-start | bytes 196616 | tf_op jit(solution)/shard_map/ppermute | solution.py:45
  30.2 8.5 %collective-permute-start.9 = (f32[4,16,128]{2,1,0:T(8,128)S(1)}, f32[4,16,128]{2,1,0:T(8,128)S(1)}, u32[]{:S(2)}, u32[]{:S(2)}) collective-permute-start(f32[4,16,128]{2,1,0:T(8,128)S(1)} %slice.8), channel_id=1, source_target_pairs={{0,8},{1,0},{2,10},{3,2},{4,12},{5,4},{6,14},{7,6},{8,16},{9,1},{1... | collective-permute-start | bytes 98312 | tf_op jit(solution)/shard_map/ppermute | solution.py:34
  33.9 4.8 %collective-permute-start.10 = (f32[4,16,128]{2,1,0:T(8,128)S(1)}, f32[4,16,128]{2,1,0:T(8,128)S(1)}, u32[]{:S(2)}, u32[]{:S(2)}) collective-permute-start(f32[4,16,128]{2,1,0:T(8,128)S(1)} %slice.9), channel_id=1, source_target_pairs={{0,1},{1,9},{2,3},{3,11},{4,5},{5,13},{6,7},{7,15},{8,0},{9,17},{1... | collective-permute-start | bytes 98312 | tf_op jit(solution)/shard_map/ppermute | solution.py:34
  34.0 8.8 %collective-permute-start.13 = (f32[7,16,128]{2,1,0:T(8,128)S(1)}, f32[7,16,128]{2,1,0:T(8,128)S(1)}, u32[]{:S(2)}, u32[]{:S(2)}) collective-permute-start(f32[7,16,128]{2,1,0:T(8,128)S(1)} %shard_map.68), channel_id=1, source_target_pairs={{104,128},{128,104},{105,129},{129,105},{106,130},{130,106},{107,1... | collective-permute-start | bytes 172040 | tf_op jit(solution)/shard_map/ppermute | solution.py:45
  38.7 4.1 %collective-permute-start.11 = (f32[4,16,128]{2,1,0:T(8,128)S(1)}, f32[4,16,128]{2,1,0:T(8,128)S(1)}, u32[]{:S(2)}, u32[]{:S(2)}) collective-permute-start(f32[4,16,128]{2,1,0:T(8,128)S(1)} %collective-permute-done.9.plus2), channel_id=1, source_target_pairs={{0,8},{1,0},{2,10},{3,2},{4,12},{5,4},{6,14},{7,6},{8,16},{9,1},{1... | collective-permute-start | bytes 98312 | tf_op jit(solution)/shard_map/ppermute | solution.py:34
  38.7 4.1 %collective-permute-start.12 = (f32[4,16,128]{2,1,0:T(8,128)S(1)}, f32[4,16,128]{2,1,0:T(8,128)S(1)}, u32[]{:S(2)}, u32[]{:S(2)}) collective-permute-start(f32[4,16,128]{2,1,0:T(8,128)S(1)} %collective-permute-done.10.minus2), channel_id=1, source_target_pairs={{0,1},{1,9},{2,3},{3,11},{4,5},{5,13},{6,7},{7,15},{8,0},{9,17},{1... | collective-permute-start | bytes 98312 | tf_op jit(solution)/shard_map/ppermute | solution.py:34
  42.9 5.5 %collective-permute-start.14 = (f32[200,128]{1,0:T(8,128)S(1)}, f32[200,128]{1,0:T(8,128)S(1)}, u32[]{:S(2)}, u32[]{:S(2)}) collective-permute-start(f32[200,128]{1,0:T(8,128)S(1)} %get-tuple-element.39), channel_id=1, source_target_pairs={{0,1},{1,2},{2,3},{3,4},{4,5},{5,6},{6,7},{7,0},{8,9},{9,10},{10,1... | collective-permute-start | bytes 307208 | tf_op jit(solution)/shard_map/ppermute | solution.py:94
  46.7 5.3 %collective-permute-start.15 = (f32[200,128]{1,0:T(8,128)S(1)}, f32[200,128]{1,0:T(8,128)S(1)}, u32[]{:S(2)}, u32[]{:S(2)}) collective-permute-start(f32[200,128]{1,0:T(8,128)S(1)} %get-tuple-element.40), channel_id=1, source_target_pairs={{0,7},{1,0},{2,1},{3,2},{4,3},{5,4},{6,5},{7,6},{8,15},{9,8},{10,9... | collective-permute-start | bytes 307208 | tf_op jit(solution)/shard_map/ppermute | solution.py:94

commit v9 on v7

--- a/solution.py
+++ b/solution.py
@@ -141,7 +141,7 @@
 Y1_RHS = 30
 Y1_ACC = 46
 Y1_CO = 62
-Y1_ROWS = 64
+Y1_ROWS = 72
 
 
 def pack_y1(rhs, perm, acc, cperm, plus, minus, across, up, down):
@@ -274,7 +274,7 @@
 
 Y2_B = 84
 Y2_U = 156
-Y2_ROWS = 192
+Y2_ROWS = 200
 
 
 def pack_y2(
@@ -384,7 +384,7 @@
             uf[k, 2:4, lane : lane + CCOLS] = ylo[at + 2 * half : at + 2 * half + 2, :] * mlo
             uf[k, 36:38, lane : lane + CCOLS] = yhi[at + 2 * half : at + 2 * half + 2, :] * mhi
         both = 2 * (k // 2)
-        uf[k] = uf[k] + t_in[k] * jnp.concatenate([cf[both], cf[both + 1]], axis=1)
+        uf[k] = uf[k] + t_in[k] * jnp.concatenate([cf[both, 0:FR], cf[both + 1, 0:FR]], axis=1)
     for k in range(8):
         xs[k] = smooth_xy(uf[k])
     for k in range(6):
@@ -445,7 +445,7 @@
         post_kernel,
         [SM] + [VM] * 9,
         f32(4, ROWS, COLS),
-        ((8, FR, COLS), (8, FR, CCOLS), (8, FR, COLS), (26, CR, CCOLS)),
+        ((8, FR, COLS), (8, FR + 8, CCOLS), (8, FR, COLS), (26, CR, CCOLS)),
     )(*operands)
 
 

time: 53.6 us -> 53.7 us (level)
  no operation moved by 1% of the time
where the time goes in v9:
time: 53.7 us; the launch traced here: 53.5 us
  starting transfers between devices  28.7 us (53%)
  waiting for transfers between devices  17.4 us (32%)
  Pallas kernels  5.98 us (11%)
  local copies, waits for them, and re-layouts  0.76 us (1%)
    ppermute x8, starting transfers between devices, along_lines(): return lax.ppermute(x, ('slab', 'pen'), pairs)  17.8 us
    ppermute x4, waiting for transfers between devices, rotated(): lax.ppermute(x, axis, [(i, (i + by) % devices) for i in range(devices)])  10 us
    ppermute x4, starting transfers between devices, rotated(): lax.ppermute(x, axis, [(i, (i + by) % devices) for i in range(devices)])  5.83 us
    ppermute x3, starting transfers between devices, between_lines(): return lax.ppermute(x, ('slab', 'pen'), pairs)  5.11 us
    ppermute x8, waiting for transfers between devices, along_lines(): return lax.ppermute(x, ('slab', 'pen'), pairs)  3.87 us
    ppermute x3, waiting for transfers between devices, between_lines(): return lax.ppermute(x, ('slab', 'pen'), pairs)  3.53 us
    pallas_call x1, Pallas kernels, post_call(): call(post_kernel, [SM] + [VM] * 9, f32(4, ROWS, COLS), ((8, FR, COLS), (8...  2.65 us
    pallas_call x1, Pallas kernels, pre_call(): call(pre_kernel, [SM] + [VM] * 10, (f32(8, FR, COLS), f32(6, FR, COLS), f...  1.89 us
  transfers between devices with their start and end apart: 15, of which 8 were waited for; matrix products, arithmetic and copies ran while one was open for 1% of the time, Pallas kernels for 0%

profile of v9, /device:TPU:63, one launch (start us, length us, event | category | flops | bytes accessed | tf_op | source)
XLA Modules:
  0.0 53.5 jit_solution(5262934184831786553)
XLA Ops:
  0.0 0.0 copy-start
  0.0 0.0 copy-start.1
  0.0 0.0 copy-start.2
  0.0 1.3 %shard_map.64 = (f32[232,256]{1,0:T(8,128)S(1)}, f32[232,256]{1,0:T(8,128)S(1)}, f32[232,256]{1,0:T(8,128)S(1)}) custom-call(f32[128,256]{1,0:T(8,128)} %bitcast.6, f32[128,256]{1,0:T(8,128)} %bitcast.7, f32[128,256]{1,0:T(8,128)} %bitcast.8, f32[2,16,128]{2,1,0:T(8,128)} %cperm.5), custom_call_target="tpu_custom_call" | custom-call | tf_op jit(solution)/shard_map/pallas_call | solution.py:454
  1.3 0.0 collective-permute-start
  1.3 1.7 %collective-permute-start.1 = (f32[232,256]{1,0:T(8,128)S(1)}, f32[232,256]{1,0:T(8,128)S(1)}, u32[]{:S(2)}, u32[]{:S(2)}) collective-permute-start(f32[232,256]{1,0:T(8,128)S(1)} %get-tuple-element.24), channel_id=1, source_target_pairs={{0,1},{1,9},{2,3},{3,11},{4,5},{5,13},{6,7},{7,15},{8,0},{9,17},{1... | collective-permute-start | bytes 712712 | tf_op jit(solution)/shard_map/ppermute | solution.py:34
  3.0 0.7 %collective-permute-start.2 = (f32[232,256]{1,0:T(8,128)S(1)}, f32[232,256]{1,0:T(8,128)S(1)}, u32[]{:S(2)}, u32[]{:S(2)}) collective-permute-start(f32[232,256]{1,0:T(8,128)S(1)} %get-tuple-element.25), channel_id=1, source_target_pairs={{120,128},{128,120},{121,129},{129,121},{122,130},{130,122},{123,1... | collective-permute-start | bytes 712712 | tf_op jit(solution)/shard_map/ppermute | solution.py:45
  3.7 0.0 copy-start.5
  3.7 0.6 %copy-done.5 = s32[32]{0:T(128)S(1)} copy-done((s32[32]{0:T(128)S(1)}, s32[32]{0:T(128)}, u32[]{:S(2)}) %copy-start.5) | copy-done | bytes 152
  4.3 0.1 copy.9
  4.4 0.1 reduce-window.9
  4.5 0.0 copy-start.3
  4.5 0.1 reduce
  4.6 0.2 compare_reduce_fusion
  4.8 0.1 add_convert_fusion
  4.9 1.9 %collective-permute-done.plus = f32[232,256]{1,0:T(8,128)S(1)} collective-permute-done((f32[232,256]{1,0:T(8,128)S(1)}, f32[232,256]{1,0:T(8,128)S(1)}, u32[]{:S(2)}, u32[]{:S(2)}) %collective-permute-start) | collective-permute-done | bytes 237600 | tf_op jit(solution)/shard_map/ppermute | solution.py:34
  6.8 1.3 %collective-permute-done.1.minus = f32[232,256]{1,0:T(8,128)S(1)} collective-permute-done((f32[232,256]{1,0:T(8,128)S(1)}, f32[232,256]{1,0:T(8,128)S(1)}, u32[]{:S(2)}, u32[]{:S(2)}) %collective-permute-start.1) | collective-permute-done | bytes 237600 | tf_op jit(solution)/shard_map/ppermute | solution.py:34
  8.0 0.0 collective-permute-done.2.across
  8.0 0.0 copy-done
  8.0 0.0 copy-done.1
  8.0 0.0 copy-done.2
  8.1 0.0 copy-done.3
  8.1 0.0 copy-start.4
  8.1 0.1 shard_map.65
  8.1 1.8 %collective-permute-start.3 = (f32[72,256]{1,0:T(8,128)S(1)}, f32[72,256]{1,0:T(8,128)S(1)}, u32[]{:S(2)}, u32[]{:S(2)}) collective-permute-start(f32[72,256]{1,0:T(8,128)S(1)} %get-tuple-element.26), channel_id=1, source_target_pairs={{0,1},{1,2},{2,3},{3,4},{4,5},{5,6},{6,7},{7,0},{8,9},{9,10},{10,1... | collective-permute-start | bytes 221192 | tf_op jit(solution)/shard_map/ppermute | solution.py:72
  10.0 0.2 collective-permute-start.4
  10.2 0.1 pad_maximum_fusion.masks
  10.2 1.1 %collective-permute-done.3.ylo = f32[72,256]{1,0:T(8,128)S(1)} collective-permute-done((f32[72,256]{1,0:T(8,128)S(1)}, f32[72,256]{1,0:T(8,128)S(1)}, u32[]{:S(2)}, u32[]{:S(2)}) %collective-permute-start.3) | collective-permute-done | bytes 73760 | tf_op jit(solution)/shard_map/ppermute | solution.py:72
  11.4 3.6 %collective-permute-done.4.yhi = f32[72,256]{1,0:T(8,128)S(1)} collective-permute-done((f32[72,256]{1,0:T(8,128)S(1)}, f32[72,256]{1,0:T(8,128)S(1)}, u32[]{:S(2)}, u32[]{:S(2)}) %collective-permute-start.4) | collective-permute-done | bytes 73760 | tf_op jit(solution)/shard_map/ppermute | solution.py:72
  15.0 0.0 copy-done.4
  15.0 1.9 %shard_map.66 = (f32[8,40,256]{2,1,0:T(8,128)S(1)}, f32[6,40,256]{2,1,0:T(8,128)S(1)}, f32[6,40,256]{2,1,0:T(8,128)S(1)}, f32[6,40,256]{2,1,0:T(8,128)S(1)}, f32...) custom-call(f32[8]{0:T(128)S(1)} %pad_maximum_fusion.masks, ...), custom_call_target="tpu_custom_call" | custom-call | tf_op jit(solution)/shard_map/pallas_call | solution.py:428
  16.9 10.0 %collective-permute-start.5 = (f32[8,16,128]{2,1,0:T(8,128)S(1)}, f32[8,16,128]{2,1,0:T(8,128)S(1)}, u32[]{:S(2)}, u32[]{:S(2)}) collective-permute-start(f32[8,16,128]{2,1,0:T(8,128)S(1)} %get-tuple-element.34), channel_id=1, source_target_pairs={{0,8},{1,0},{2,10},{3,2},{4,12},{5,4},{6,14},{7,6},{8,16},{9,1},{1... | collective-permute-start | bytes 196616 | tf_op jit(solution)/shard_map/ppermute | solution.py:34
  26.8 0.0 collective-permute-start.6
  26.8 0.7 %collective-permute-start.7 = (f32[8,16,128]{2,1,0:T(8,128)S(1)}, f32[8,16,128]{2,1,0:T(8,128)S(1)}, u32[]{:S(2)}, u32[]{:S(2)}) collective-permute-start(f32[8,16,128]{2,1,0:T(8,128)S(1)} %get-tuple-element.36), channel_id=1, source_target_pairs={{120,128},{128,120},{121,129},{129,121},{122,130},{130,122},{123,1... | collective-permute-start | bytes 196616 | tf_op jit(solution)/shard_map/ppermute | solution.py:45
  27.5 0.7 %collective-permute-done.5.plus1 = f32[8,16,128]{2,1,0:T(8,128)S(1)} collective-permute-done((f32[8,16,128]{2,1,0:T(8,128)S(1)}, f32[8,16,128]{2,1,0:T(8,128)S(1)}, u32[]{:S(2)}, u32[]{:S(2)}) %collective-permute-start.5) | collective-permute-done | bytes 65568 | tf_op jit(solution)/shard_map/ppermute | solution.py:34
  28.2 4.6 %collective-permute-start.8 = (f32[4,16,128]{2,1,0:T(8,128)S(1)}, f32[4,16,128]{2,1,0:T(8,128)S(1)}, u32[]{:S(2)}, u32[]{:S(2)}) collective-permute-start(f32[4,16,128]{2,1,0:T(8,128)S(1)} %slice.8), channel_id=1, source_target_pairs={{0,8},{1,0},{2,10},{3,2},{4,12},{5,4},{6,14},{7,6},{8,16},{9,1},{1... | collective-permute-start | bytes 98312 | tf_op jit(solution)/shard_map/ppermute | solution.py:34
  32.8 0.0 collective-permute-done.6.minus1
  32.9 0.0 collective-permute-start.9
  32.9 3.8 %collective-permute-start.12 = (f32[7,16,128]{2,1,0:T(8,128)S(1)}, f32[7,16,128]{2,1,0:T(8,128)S(1)}, u32[]{:S(2)}, u32[]{:S(2)}) collective-permute-start(f32[7,16,128]{2,1,0:T(8,128)S(1)} %shard_map.67), channel_id=1, source_target_pairs={{104,128},{128,104},{105,129},{129,105},{106,130},{130,106},{107,1... | collective-permute-start | bytes 172040 | tf_op jit(solution)/shard_map/ppermute | solution.py:45
  36.7 0.0 collective-permute-done.8.plus2
  36.7 0.0 collective-permute-start.10
  36.7 0.0 collective-permute-done.9.minus2
  36.7 1.4 %collective-permute-start.11 = (f32[4,16,128]{2,1,0:T(8,128)S(1)}, f32[4,16,128]{2,1,0:T(8,128)S(1)}, u32[]{:S(2)}, u32[]{:S(2)}) collective-permute-start(f32[4,16,128]{2,1,0:T(8,128)S(1)} %collective-permute-done.9.minus2), channel_id=1, source_target_pairs={{0,1},{1,9},{2,3},{3,11},{4,5},{5,13},{6,7},{7,15},{8,0},{9,17},{1... | collective-permute-start | bytes 98312 | tf_op jit(solution)/shard_map/ppermute | solution.py:34
  38.2 0.0 collective-permute-done.7.across
  38.2 3.5 %collective-permute-done.12.far = f32[7,16,128]{2,1,0:T(8,128)S(1)} collective-permute-done((f32[7,16,128]{2,1,0:T(8,128)S(1)}, f32[7,16,128]{2,1,0:T(8,128)S(1)}, u32[]{:S(2)}, u32[]{:S(2)}) %collective-permute-start.12) | collective-permute-done | bytes 57376 | tf_op jit(solution)/shard_map/ppermute | solution.py:45
  41.7 0.0 collective-permute-done.10.plus3
  41.7 0.0 collective-permute-done.11.minus3
  41.7 0.1 shard_map.68
  41.8 3.8 %collective-permute-start.13 = (f32[200,128]{1,0:T(8,128)S(1)}, f32[200,128]{1,0:T(8,128)S(1)}, u32[]{:S(2)}, u32[]{:S(2)}) collective-permute-start(f32[200,128]{1,0:T(8,128)S(1)} %get-tuple-element.39), channel_id=1, source_target_pairs={{0,1},{1,2},{2,3},{3,4},{4,5},{5,6},{6,7},{7,0},{8,9},{9,10},{10,1... | collective-permute-start | bytes 307208 | tf_op jit(solution)/shard_map/ppermute | solution.py:72
  45.6 0.0 collective-permute-start.14
  45.6 1.7 %collective-permute-done.13.ylo = f32[200,128]{1,0:T(8,128)S(1)} collective-permute-done((f32[200,128]{1,0:T(8,128)S(1)}, f32[200,128]{1,0:T(8,128)S(1)}, u32[]{:S(2)}, u32[]{:S(2)}) %collective-permute-start.13) | collective-permute-done | bytes 102432 | tf_op jit(solution)/shard_map/ppermute | solution.py:72
  47.3 3.6 %collective-permute-done.14.yhi = f32[200,128]{1,0:T(8,128)S(1)} collective-permute-done((f32[200,128]{1,0:T(8,128)S(1)}, f32[200,128]{1,0:T(8,128)S(1)}, u32[]{:S(2)}, u32[]{:S(2)}) %collective-permute-start.14) | collective-permute-done | bytes 102432 | tf_op jit(solution)/shard_map/ppermute | solution.py:72
  50.9 2.6 %shard_map.69 = f32[4,32,256]{2,1,0:T(8,128)} custom-call(f32[8]{0:T(128)S(1)} %pad_maximum_fusion.masks, f32[8,40,256]{2,1,0:T(8,128)S(1)} %get-tuple-element.28.t_in, f32[6,40,256]{2,1,0:T(8,128)S(1)} %get-tuple-element.29.a_in, f32[6,40,256]{2,1,0:T(8,128)S(1)} %get-tuple-element.30.b_in, f32[6,40,256]{2,1,0:T(8,128)S(1)} %get-tuple-element.31.u.u_in, ...), custom_call_target="tpu_custom_call" | custom-call | tf_op jit(solution)/shard_map/pallas_call | solution.py:444
  (6 shorter events, 0.0 us)
Async XLA Ops:
  0.0 8.0 %copy-start = (f32[4,32,256]{2,1,0:T(8,128)S(1)}, f32[4,32,256]{2,1,0:T(8,128)}, u32[]{:S(2)}) copy-start(f32[4,32,256]{2,1,0:T(8,128)} %rhs.4) | copy-start | bytes 393220
  0.0 8.0 %copy-start.1 = (f32[4,32,256]{2,1,0:T(8,128)S(1)}, f32[4,32,256]{2,1,0:T(8,128)}, u32[]{:S(2)}) copy-start(f32[4,32,256]{2,1,0:T(8,128)} %perm.3) | copy-start | bytes 393220
  0.0 8.0 %copy-start.2 = (f32[4,32,256]{2,1,0:T(8,128)S(1)}, f32[4,32,256]{2,1,0:T(8,128)}, u32[]{:S(2)}) copy-start(f32[4,32,256]{2,1,0:T(8,128)} %acc.3) | copy-start | bytes 393220
  1.3 5.4 %collective-permute-start = (f32[232,256]{1,0:T(8,128)S(1)}, f32[232,256]{1,0:T(8,128)S(1)}, u32[]{:S(2)}, u32[]{:S(2)}) collective-permute-start(f32[232,256]{1,0:T(8,128)S(1)} %get-tuple-element.23), channel_id=1, source_target_pairs={{0,8},{1,0},{2,10},{3,2},{4,12},{5,4},{6,14},{7,6},{8,16},{9,1},{1... | collective-permute-start | bytes 712712 | tf_op jit(solution)/shard_map/ppermute | solution.py:34
  1.3 6.7 %collective-permute-start.1 = (f32[232,256]{1,0:T(8,128)S(1)}, f32[232,256]{1,0:T(8,128)S(1)}, u32[]{:S(2)}, u32[]{:S(2)}) collective-permute-start(f32[232,256]{1,0:T(8,128)S(1)} %get-tuple-element.24), channel_id=1, source_target_pairs={{0,1},{1,9},{2,3},{3,11},{4,5},{5,13},{6,7},{7,15},{8,0},{9,17},{1... | collective-permute-start | bytes 712712 | tf_op jit(solution)/shard_map/ppermute | solution.py:34
  3.0 5.0 %collective-permute-start.2 = (f32[232,256]{1,0:T(8,128)S(1)}, f32[232,256]{1,0:T(8,128)S(1)}, u32[]{:S(2)}, u32[]{:S(2)}) collective-permute-start(f32[232,256]{1,0:T(8,128)S(1)} %get-tuple-element.25), channel_id=1, source_target_pairs={{120,128},{128,120},{121,129},{129,121},{122,130},{130,122},{123,1... | collective-permute-start | bytes 712712 | tf_op jit(solution)/shard_map/ppermute | solution.py:45
  3.7 0.7 %copy-start.5 = (s32[32]{0:T(128)S(1)}, s32[32]{0:T(128)}, u32[]{:S(2)}) copy-start(s32[32]{0:T(128)} %param.11) | copy-start | bytes 388
  4.5 3.6 %copy-start.3 = (f32[2,16,128]{2,1,0:T(8,128)S(1)}, f32[2,16,128]{2,1,0:T(8,128)}, u32[]{:S(2)}) copy-start(f32[2,16,128]{2,1,0:T(8,128)} %cperm.5) | copy-start | bytes 49156
  8.1 6.9 %copy-start.4 = (f32[2,16,128]{2,1,0:T(8,128)S(1)}, f32[2,16,128]{2,1,0:T(8,128)}, u32[]{:S(2)}) copy-start(f32[2,16,128]{2,1,0:T(8,128)} %cacc.1) | copy-start | bytes 49156
  8.1 3.2 %collective-permute-start.3 = (f32[72,256]{1,0:T(8,128)S(1)}, f32[72,256]{1,0:T(8,128)S(1)}, u32[]{:S(2)}, u32[]{:S(2)}) collective-permute-start(f32[72,256]{1,0:T(8,128)S(1)} %get-tuple-element.26), channel_id=1, source_target_pairs={{0,1},{1,2},{2,3},{3,4},{4,5},{5,6},{6,7},{7,0},{8,9},{9,10},{10,1... | collective-permute-start | bytes 221192 | tf_op jit(solution)/shard_map/ppermute | solution.py:72
  10.0 5.0 %collective-permute-start.4 = (f32[72,256]{1,0:T(8,128)S(1)}, f32[72,256]{1,0:T(8,128)S(1)}, u32[]{:S(2)}, u32[]{:S(2)}) collective-permute-start(f32[72,256]{1,0:T(8,128)S(1)} %get-tuple-element.27), channel_id=1, source_target_pairs={{0,7},{1,0},{2,1},{3,2},{4,3},{5,4},{6,5},{7,6},{8,15},{9,8},{10,9... | collective-permute-start | bytes 221192 | tf_op jit(solution)/shard_map/ppermute | solution.py:72
  16.9 11.3 %collective-permute-start.5 = (f32[8,16,128]{2,1,0:T(8,128)S(1)}, f32[8,16,128]{2,1,0:T(8,128)S(1)}, u32[]{:S(2)}, u32[]{:S(2)}) collective-permute-start(f32[8,16,128]{2,1,0:T(8,128)S(1)} %get-tuple-element.34), channel_id=1, source_target_pairs={{0,8},{1,0},{2,10},{3,2},{4,12},{5,4},{6,14},{7,6},{8,16},{9,1},{1... | collective-permute-start | bytes 196616 | tf_op jit(solution)/shard_map/ppermute | solution.py:34
  26.8 6.0 %collective-permute-start.6 = (f32[8,16,128]{2,1,0:T(8,128)S(1)}, f32[8,16,128]{2,1,0:T(8,128)S(1)}, u32[]{:S(2)}, u32[]{:S(2)}) collective-permute-start(f32[8,16,128]{2,1,0:T(8,128)S(1)} %get-tuple-element.35), channel_id=1, source_target_pairs={{0,1},{1,9},{2,3},{3,11},{4,5},{5,13},{6,7},{7,15},{8,0},{9,17},{1... | collective-permute-start | bytes 196616 | tf_op jit(solution)/shard_map/ppermute | solution.py:34
  26.8 11.4 %collective-permute-start.7 = (f32[8,16,128]{2,1,0:T(8,128)S(1)}, f32[8,16,128]{2,1,0:T(8,128)S(1)}, u32[]{:S(2)}, u32[]{:S(2)}) collective-permute-start(f32[8,16,128]{2,1,0:T(8,128)S(1)} %get-tuple-element.36), channel_id=1, source_target_pairs={{120,128},{128,120},{121,129},{129,121},{122,130},{130,122},{123,1... | collective-permute-start | bytes 196616 | tf_op jit(solution)/shard_map/ppermute | solution.py:45
  28.2 8.5 %collective-permute-start.8 = (f32[4,16,128]{2,1,0:T(8,128)S(1)}, f32[4,16,128]{2,1,0:T(8,128)S(1)}, u32[]{:S(2)}, u32[]{:S(2)}) collective-permute-start(f32[4,16,128]{2,1,0:T(8,128)S(1)} %slice.8), channel_id=1, source_target_pairs={{0,8},{1,0},{2,10},{3,2},{4,12},{5,4},{6,14},{7,6},{8,16},{9,1},{1... | collective-permute-start | bytes 98312 | tf_op jit(solution)/shard_map/ppermute | solution.py:34
  32.9 3.9 %collective-permute-start.9 = (f32[4,16,128]{2,1,0:T(8,128)S(1)}, f32[4,16,128]{2,1,0:T(8,128)S(1)}, u32[]{:S(2)}, u32[]{:S(2)}) collective-permute-start(f32[4,16,128]{2,1,0:T(8,128)S(1)} %slice.9), channel_id=1, source_target_pairs={{0,1},{1,9},{2,3},{3,11},{4,5},{5,13},{6,7},{7,15},{8,0},{9,17},{1... | collective-permute-start | bytes 98312 | tf_op jit(solution)/shard_map/ppermute | solution.py:34
  32.9 8.8 %collective-permute-start.12 = (f32[7,16,128]{2,1,0:T(8,128)S(1)}, f32[7,16,128]{2,1,0:T(8,128)S(1)}, u32[]{:S(2)}, u32[]{:S(2)}) collective-permute-start(f32[7,16,128]{2,1,0:T(8,128)S(1)} %shard_map.67), channel_id=1, source_target_pairs={{104,128},{128,104},{105,129},{129,105},{106,130},{130,106},{107,1... | collective-permute-start | bytes 172040 | tf_op jit(solution)/shard_map/ppermute | solution.py:45
  36.7 5.0 %collective-permute-start.10 = (f32[4,16,128]{2,1,0:T(8,128)S(1)}, f32[4,16,128]{2,1,0:T(8,128)S(1)}, u32[]{:S(2)}, u32[]{:S(2)}) collective-permute-start(f32[4,16,128]{2,1,0:T(8,128)S(1)} %collective-permute-done.8.plus2), channel_id=1, source_target_pairs={{0,8},{1,0},{2,10},{3,2},{4,12},{5,4},{6,14},{7,6},{8,16},{9,1},{1... | collective-permute-start | bytes 98312 | tf_op jit(solution)/shard_map/ppermute | solution.py:34
  36.7 5.0 %collective-permute-start.11 = (f32[4,16,128]{2,1,0:T(8,128)S(1)}, f32[4,16,128]{2,1,0:T(8,128)S(1)}, u32[]{:S(2)}, u32[]{:S(2)}) collective-permute-start(f32[4,16,128]{2,1,0:T(8,128)S(1)} %collective-permute-done.9.minus2), channel_id=1, source_target_pairs={{0,1},{1,9},{2,3},{3,11},{4,5},{5,13},{6,7},{7,15},{8,0},{9,17},{1... | collective-permute-start | bytes 98312 | tf_op jit(solution)/shard_map/ppermute | solution.py:34
  41.8 5.5 %collective-permute-start.13 = (f32[200,128]{1,0:T(8,128)S(1)}, f32[200,128]{1,0:T(8,128)S(1)}, u32[]{:S(2)}, u32[]{:S(2)}) collective-permute-start(f32[200,128]{1,0:T(8,128)S(1)} %get-tuple-element.39), channel_id=1, source_target_pairs={{0,1},{1,2},{2,3},{3,4},{4,5},{5,6},{6,7},{7,0},{8,9},{9,10},{10,1... | collective-permute-start | bytes 307208 | tf_op jit(solution)/shard_map/ppermute | solution.py:72
  45.6 5.3 %collective-permute-start.14 = (f32[200,128]{1,0:T(8,128)S(1)}, f32[200,128]{1,0:T(8,128)S(1)}, u32[]{:S(2)}, u32[]{:S(2)}) collective-permute-start(f32[200,128]{1,0:T(8,128)S(1)} %get-tuple-element.40), channel_id=1, source_target_pairs={{0,7},{1,0},{2,1},{3,2},{4,3},{5,4},{6,5},{7,6},{8,15},{9,8},{10,9... | collective-permute-start | bytes 307208 | tf_op jit(solution)/shard_map/ppermute | solution.py:72

commit v10 on v9

--- a/solution.py
+++ b/solution.py
@@ -251,17 +251,25 @@
         q = OMEGA * t / d
         a = q * res[CROWS * k : CROWS * k + CROWS]
         b = q * t
-        for out in (ab_out, plus_out, minus_out, across_out):
+        for out in (ab_out, across_out):
             out[k] = a
             out[2 + k] = b
-    for out, up in (
-        (plus_out, first), (minus_out, jnp.logical_not(first)), (across_out, place_z == LINE - 1)
+    for out, up, at in (
+        (plus_out, first, 0),
+        (minus_out, jnp.logical_not(first), 0),
+        (across_out, place_z == LINE - 1, 4),
     ):
         plane = jnp.where(up, 3, 2)
         for k in range(4):
             row = 4 + 16 * (k // 2)
             lane = CCOLS * (k % 2)
-            out[4 + k] = u_out[plane, row : row + 16, lane : lane + CCOLS]
+            out[at + k] = u_out[plane, row : row + 16, lane : lane + CCOLS]
+
+
+def pass_on(plus2, minus2, across, plus_out, minus_out):
+    del across
+    plus_out[...] = plus2[0:4]
+    minus_out[...] = minus2[0:4]
 
 
 def pack_far(ab, plus1, minus1, out):
@@ -295,8 +303,8 @@
         dom[8 + k if a else 19 + k] = above(plus1, minus1, k, 1, across[k])
         dom[2 + k if a else 13 + k] = below(plus2, minus2, k, 2, far[3 + k])
         dom[10 + k if a else 21 + k] = above(plus2, minus2, k, 2, far[3 + k])
-        edge[k] = below(plus1, minus1, 4 + k, 1, across[4 + k])
-        edge[4 + k] = above(plus1, minus1, 4 + k, 1, across[4 + k])
+        edge[k] = below(plus2, minus2, 4 + k, 1, across[4 + k])
+        edge[4 + k] = above(plus2, minus2, 4 + k, 1, across[4 + k])
     for k in range(3):
         low = 3 if k == 2 else k
         dom[14 if k == 2 else k] = below(plus3, minus3, low, 3, far[k])
@@ -431,7 +439,7 @@
         (
             f32(8, FR, COLS), f32(6, FR, COLS), f32(6, FR, COLS), f32(6, FR, COLS),
             f32(4, CR, CCOLS), f32(4, CROWS, CCOLS),
-            f32(8, CROWS, CCOLS), f32(8, CROWS, CCOLS), f32(8, CROWS, CCOLS),
+            f32(4, CROWS, CCOLS), f32(4, CROWS, CCOLS), f32(8, CROWS, CCOLS),
         ),
         (
             (10, FR, COLS), (8, FR, COLS), (8, FR, COLS),
@@ -495,15 +503,17 @@
         plus, minus, across, ylo, yhi,
     )
     across = between_lines(across, 1)
-    plus1 = along_lines(plus, 1)
-    minus1 = along_lines(minus, -1)
+    plus1 = along_lines(ab, 1)
+    minus1 = along_lines(ab, -1)
     far = between_lines(
         call(pack_far, [VM] * 3, f32(7, CROWS, CCOLS))(ab, plus1, minus1), 3
     )
-    plus2 = along_lines(plus1[0:4], 1)
-    minus2 = along_lines(minus1[0:4], -1)
-    plus3 = along_lines(plus2, 1)
-    minus3 = along_lines(minus2, -1)
+    plus2 = along_lines(jnp.concatenate([plus1, plus], axis=0), 1)
+    minus2 = along_lines(jnp.concatenate([minus1, minus], axis=0), -1)
+    block = f32(4, CROWS, CCOLS)
+    plus, minus = call(pass_on, [VM] * 3, (block, block))(plus2, minus2, across)
+    plus3 = along_lines(plus, 1)
+    minus3 = along_lines(minus, -1)
 
     rows = f32(Y2_ROWS, CCOLS)
     up, down, dom, edge = call(

time: 53.7 us -> 53.8 us (level)
  no operation moved by 1% of the time
where the time goes in v10:
time: 53.8 us; the launch traced here: 53.6 us
  starting transfers between devices  29 us (54%)
  waiting for transfers between devices  17.1 us (32%)
  Pallas kernels  5.98 us (11%)
  local copies, waits for them, and re-layouts  0.76 us (1%)
    ppermute x8, starting transfers between devices, along_lines(): return lax.ppermute(x, ('slab', 'pen'), pairs)  18.1 us
    ppermute x4, waiting for transfers between devices, rotated(): lax.ppermute(x, axis, [(i, (i + by) % devices) for i in range(devices)])  10 us
    ppermute x4, starting transfers between devices, rotated(): lax.ppermute(x, axis, [(i, (i + by) % devices) for i in range(devices)])  5.83 us
    ppermute x3, starting transfers between devices, between_lines(): return lax.ppermute(x, ('slab', 'pen'), pairs)  5.09 us
    ppermute x8, waiting for transfers between devices, along_lines(): return lax.ppermute(x, ('slab', 'pen'), pairs)  3.53 us
    ppermute x3, waiting for transfers between devices, between_lines(): return lax.ppermute(x, ('slab', 'pen'), pairs)  3.53 us
    pallas_call x1, Pallas kernels, post_call(): call(post_kernel, [SM] + [VM] * 9, f32(4, ROWS, COLS), ((8, FR, COLS), (8...  2.65 us
    pallas_call x1, Pallas kernels, pre_call(): call(pre_kernel, [SM] + [VM] * 10, (f32(8, FR, COLS), f32(6, FR, COLS), f...  1.89 us
  transfers between devices with their start and end apart: 15, of which 8 were waited for; matrix products, arithmetic and copies ran while one was open for 1% of the time, Pallas kernels for 0%

profile of v10, /device:TPU:63, one launch (start us, length us, event | category | flops | bytes accessed | tf_op | source)
XLA Modules:
  0.0 53.6 jit_solution(15147909863245259230)
XLA Ops:
  0.0 0.0 copy-start
  0.0 0.0 copy-start.1
  0.0 0.0 copy-start.2
  0.0 1.3 %shard_map.64 = (f32[232,256]{1,0:T(8,128)S(1)}, f32[232,256]{1,0:T(8,128)S(1)}, f32[232,256]{1,0:T(8,128)S(1)}) custom-call(f32[128,256]{1,0:T(8,128)} %bitcast.6, f32[128,256]{1,0:T(8,128)} %bitcast.7, f32[128,256]{1,0:T(8,128)} %bitcast.8, f32[2,16,128]{2,1,0:T(8,128)} %cperm.5), custom_call_target="tpu_custom_call" | custom-call | tf_op jit(solution)/shard_map/pallas_call | solution.py:462
  1.3 0.0 collective-permute-start
  1.3 1.7 %collective-permute-start.1 = (f32[232,256]{1,0:T(8,128)S(1)}, f32[232,256]{1,0:T(8,128)S(1)}, u32[]{:S(2)}, u32[]{:S(2)}) collective-permute-start(f32[232,256]{1,0:T(8,128)S(1)} %get-tuple-element.26), channel_id=1, source_target_pairs={{0,1},{1,9},{2,3},{3,11},{4,5},{5,13},{6,7},{7,15},{8,0},{9,17},{1... | collective-permute-start | bytes 712712 | tf_op jit(solution)/shard_map/ppermute | solution.py:34
  3.0 0.7 %collective-permute-start.2 = (f32[232,256]{1,0:T(8,128)S(1)}, f32[232,256]{1,0:T(8,128)S(1)}, u32[]{:S(2)}, u32[]{:S(2)}) collective-permute-start(f32[232,256]{1,0:T(8,128)S(1)} %get-tuple-element.27), channel_id=1, source_target_pairs={{120,128},{128,120},{121,129},{129,121},{122,130},{130,122},{123,1... | collective-permute-start | bytes 712712 | tf_op jit(solution)/shard_map/ppermute | solution.py:45
  3.7 0.0 copy-start.5
  3.7 0.6 %copy-done.5 = s32[32]{0:T(128)S(1)} copy-done((s32[32]{0:T(128)S(1)}, s32[32]{0:T(128)}, u32[]{:S(2)}) %copy-start.5) | copy-done | bytes 152
  4.3 0.1 copy.9
  4.4 0.1 reduce-window.9
  4.5 0.0 copy-start.3
  4.5 0.1 reduce
  4.6 0.2 compare_reduce_fusion
  4.8 0.1 add_convert_fusion
  4.9 1.9 %collective-permute-done.plus = f32[232,256]{1,0:T(8,128)S(1)} collective-permute-done((f32[232,256]{1,0:T(8,128)S(1)}, f32[232,256]{1,0:T(8,128)S(1)}, u32[]{:S(2)}, u32[]{:S(2)}) %collective-permute-start) | collective-permute-done | bytes 237600 | tf_op jit(solution)/shard_map/ppermute | solution.py:34
  6.8 1.3 %collective-permute-done.1.minus = f32[232,256]{1,0:T(8,128)S(1)} collective-permute-done((f32[232,256]{1,0:T(8,128)S(1)}, f32[232,256]{1,0:T(8,128)S(1)}, u32[]{:S(2)}, u32[]{:S(2)}) %collective-permute-start.1) | collective-permute-done | bytes 237600 | tf_op jit(solution)/shard_map/ppermute | solution.py:34
  8.0 0.0 collective-permute-done.2.across
  8.0 0.0 copy-done
  8.0 0.0 copy-done.1
  8.0 0.0 copy-done.2
  8.1 0.0 copy-done.3
  8.1 0.0 copy-start.4
  8.1 0.1 shard_map.65
  8.1 1.8 %collective-permute-start.3 = (f32[72,256]{1,0:T(8,128)S(1)}, f32[72,256]{1,0:T(8,128)S(1)}, u32[]{:S(2)}, u32[]{:S(2)}) collective-permute-start(f32[72,256]{1,0:T(8,128)S(1)} %get-tuple-element.28), channel_id=1, source_target_pairs={{0,1},{1,2},{2,3},{3,4},{4,5},{5,6},{6,7},{7,0},{8,9},{9,10},{10,1... | collective-permute-start | bytes 221192 | tf_op jit(solution)/shard_map/ppermute | solution.py:72
  10.0 0.2 collective-permute-start.4
  10.2 0.1 pad_maximum_fusion.2.masks
  10.2 1.1 %collective-permute-done.3.ylo = f32[72,256]{1,0:T(8,128)S(1)} collective-permute-done((f32[72,256]{1,0:T(8,128)S(1)}, f32[72,256]{1,0:T(8,128)S(1)}, u32[]{:S(2)}, u32[]{:S(2)}) %collective-permute-start.3) | collective-permute-done | bytes 73760 | tf_op jit(solution)/shard_map/ppermute | solution.py:72
  11.4 3.6 %collective-permute-done.4.yhi = f32[72,256]{1,0:T(8,128)S(1)} collective-permute-done((f32[72,256]{1,0:T(8,128)S(1)}, f32[72,256]{1,0:T(8,128)S(1)}, u32[]{:S(2)}, u32[]{:S(2)}) %collective-permute-start.4) | collective-permute-done | bytes 73760 | tf_op jit(solution)/shard_map/ppermute | solution.py:72
  15.0 0.0 copy-done.4
  15.0 1.9 %shard_map.66 = (f32[8,40,256]{2,1,0:T(8,128)S(1)}, f32[6,40,256]{2,1,0:T(8,128)S(1)}, f32[6,40,256]{2,1,0:T(8,128)S(1)}, f32[6,40,256]{2,1,0:T(8,128)S(1)}, f32...) custom-call(f32[8]{0:T(128)S(1)} %pad_maximum_fusion.2.masks, ...), custom_call_target="tpu_custom_call" | custom-call | tf_op jit(solution)/shard_map/pallas_call | solution.py:436
  16.9 10.0 %collective-permute-start.5 = (f32[4,16,128]{2,1,0:T(8,128)S(1)}, f32[4,16,128]{2,1,0:T(8,128)S(1)}, u32[]{:S(2)}, u32[]{:S(2)}) collective-permute-start(f32[4,16,128]{2,1,0:T(8,128)S(1)} %get-tuple-element.35.ab), channel_id=1, source_target_pairs={{0,8},{1,0},{2,10},{3,2},{4,12},{5,4},{6,14},{7,6},{8,16},{9,1},{1... | collective-permute-start | bytes 98312 | tf_op jit(solution)/shard_map/ppermute | solution.py:34
  26.8 0.0 collective-permute-start.6
  26.8 0.7 %collective-permute-start.7 = (f32[8,16,128]{2,1,0:T(8,128)S(1)}, f32[8,16,128]{2,1,0:T(8,128)S(1)}, u32[]{:S(2)}, u32[]{:S(2)}) collective-permute-start(f32[8,16,128]{2,1,0:T(8,128)S(1)} %get-tuple-element.36), channel_id=1, source_target_pairs={{120,128},{128,120},{121,129},{129,121},{122,130},{130,122},{123,1... | collective-permute-start | bytes 196616 | tf_op jit(solution)/shard_map/ppermute | solution.py:45
  27.5 0.4 collective-permute-done.5.plus1
  27.9 5.0 %collective-permute-start.8 = (f32[8,16,128]{2,1,0:T(8,128)S(1)}, f32[8,16,128]{2,1,0:T(8,128)S(1)}, u32[]{:S(2)}, u32[]{:S(2)}) collective-permute-start(f32[8,16,128]{2,1,0:T(8,128)S(1)} %pad_maximum_fusion), channel_id=1, source_target_pairs={{0,8},{1,0},{2,10},{3,2},{4,12},{5,4},{6,14},{7,6},{8,16},{9,1},{1... | collective-permute-start | bytes 196616 | tf_op jit(solution)/shard_map/ppermute | solution.py:34
  32.8 0.0 collective-permute-done.6.minus1
  32.9 0.0 collective-permute-start.9
  32.9 3.8 %collective-permute-start.12 = (f32[7,16,128]{2,1,0:T(8,128)S(1)}, f32[7,16,128]{2,1,0:T(8,128)S(1)}, u32[]{:S(2)}, u32[]{:S(2)}) collective-permute-start(f32[7,16,128]{2,1,0:T(8,128)S(1)} %shard_map.68), channel_id=1, source_target_pairs={{104,128},{128,104},{105,129},{129,105},{106,130},{130,106},{107,1... | collective-permute-start | bytes 172040 | tf_op jit(solution)/shard_map/ppermute | solution.py:45
  36.7 0.0 collective-permute-done.7.across
  36.7 0.0 collective-permute-done.8.plus2
  36.7 0.0 collective-permute-done.9.minus2
  36.7 0.0 collective-permute-start.10
  36.8 1.5 %collective-permute-start.11 = (f32[4,16,128]{2,1,0:T(8,128)S(1)}, f32[4,16,128]{2,1,0:T(8,128)S(1)}, u32[]{:S(2)}, u32[]{:S(2)}) collective-permute-start(f32[4,16,128]{2,1,0:T(8,128)S(1)} %get-tuple-element.40), channel_id=1, source_target_pairs={{0,1},{1,9},{2,3},{3,11},{4,5},{5,13},{6,7},{7,15},{8,0},{9,17},{1... | collective-permute-start | bytes 98312 | tf_op jit(solution)/shard_map/ppermute | solution.py:34
  38.2 3.5 %collective-permute-done.12.far = f32[7,16,128]{2,1,0:T(8,128)S(1)} collective-permute-done((f32[7,16,128]{2,1,0:T(8,128)S(1)}, f32[7,16,128]{2,1,0:T(8,128)S(1)}, u32[]{:S(2)}, u32[]{:S(2)}) %collective-permute-start.12) | collective-permute-done | bytes 57376 | tf_op jit(solution)/shard_map/ppermute | solution.py:45
  41.7 0.0 collective-permute-done.10.plus3
  41.8 0.0 collective-permute-done.11.minus3
  41.8 0.1 shard_map.69
  41.8 3.8 %collective-permute-start.13 = (f32[200,128]{1,0:T(8,128)S(1)}, f32[200,128]{1,0:T(8,128)S(1)}, u32[]{:S(2)}, u32[]{:S(2)}) collective-permute-start(f32[200,128]{1,0:T(8,128)S(1)} %get-tuple-element.43), channel_id=1, source_target_pairs={{0,1},{1,2},{2,3},{3,4},{4,5},{5,6},{6,7},{7,0},{8,9},{9,10},{10,1... | collective-permute-start | bytes 307208 | tf_op jit(solution)/shard_map/ppermute | solution.py:72
  45.6 0.0 collective-permute-start.14
  45.6 1.7 %collective-permute-done.13.ylo = f32[200,128]{1,0:T(8,128)S(1)} collective-permute-done((f32[200,128]{1,0:T(8,128)S(1)}, f32[200,128]{1,0:T(8,128)S(1)}, u32[]{:S(2)}, u32[]{:S(2)}) %collective-permute-start.13) | collective-permute-done | bytes 102432 | tf_op jit(solution)/shard_map/ppermute | solution.py:72
  47.3 3.6 %collective-permute-done.14.yhi = f32[200,128]{1,0:T(8,128)S(1)} collective-permute-done((f32[200,128]{1,0:T(8,128)S(1)}, f32[200,128]{1,0:T(8,128)S(1)}, u32[]{:S(2)}, u32[]{:S(2)}) %collective-permute-start.14) | collective-permute-done | bytes 102432 | tf_op jit(solution)/shard_map/ppermute | solution.py:72
  50.9 2.7 %shard_map.70 = f32[4,32,256]{2,1,0:T(8,128)} custom-call(f32[8]{0:T(128)S(1)} %pad_maximum_fusion.2.masks, f32[8,40,256]{2,1,0:T(8,128)S(1)} %get-tuple-element.30.t_in, f32[6,40,256]{2,1,0:T(8,128)S(1)} %get-tuple-element.31.a_in, f32[6,40,256]{2,1,0:T(8,128)S(1)} %get-tuple-element.32.b_in, f32[6,40,256]{2,1,0:T(8,128)S(1)} %get-tuple-element.33.u.u_in, ...), custom_call_target="tpu_custom_call" | custom-call | tf_op jit(solution)/shard_map/pallas_call | solution.py:452
  (7 shorter events, 0.1 us)
Async XLA Ops:
  0.0 8.0 %copy-start = (f32[4,32,256]{2,1,0:T(8,128)S(1)}, f32[4,32,256]{2,1,0:T(8,128)}, u32[]{:S(2)}) copy-start(f32[4,32,256]{2,1,0:T(8,128)} %rhs.4) | copy-start | bytes 393220
  0.0 8.0 %copy-start.1 = (f32[4,32,256]{2,1,0:T(8,128)S(1)}, f32[4,32,256]{2,1,0:T(8,128)}, u32[]{:S(2)}) copy-start(f32[4,32,256]{2,1,0:T(8,128)} %perm.3) | copy-start | bytes 393220
  0.0 8.0 %copy-start.2 = (f32[4,32,256]{2,1,0:T(8,128)S(1)}, f32[4,32,256]{2,1,0:T(8,128)}, u32[]{:S(2)}) copy-start(f32[4,32,256]{2,1,0:T(8,128)} %acc.3) | copy-start | bytes 393220
  1.3 5.4 %collective-permute-start = (f32[232,256]{1,0:T(8,128)S(1)}, f32[232,256]{1,0:T(8,128)S(1)}, u32[]{:S(2)}, u32[]{:S(2)}) collective-permute-start(f32[232,256]{1,0:T(8,128)S(1)} %get-tuple-element.25), channel_id=1, source_target_pairs={{0,8},{1,0},{2,10},{3,2},{4,12},{5,4},{6,14},{7,6},{8,16},{9,1},{1... | collective-permute-start | bytes 712712 | tf_op jit(solution)/shard_map/ppermute | solution.py:34
  1.3 6.7 %collective-permute-start.1 = (f32[232,256]{1,0:T(8,128)S(1)}, f32[232,256]{1,0:T(8,128)S(1)}, u32[]{:S(2)}, u32[]{:S(2)}) collective-permute-start(f32[232,256]{1,0:T(8,128)S(1)} %get-tuple-element.26), channel_id=1, source_target_pairs={{0,1},{1,9},{2,3},{3,11},{4,5},{5,13},{6,7},{7,15},{8,0},{9,17},{1... | collective-permute-start | bytes 712712 | tf_op jit(solution)/shard_map/ppermute | solution.py:34
  3.0 5.0 %collective-permute-start.2 = (f32[232,256]{1,0:T(8,128)S(1)}, f32[232,256]{1,0:T(8,128)S(1)}, u32[]{:S(2)}, u32[]{:S(2)}) collective-permute-start(f32[232,256]{1,0:T(8,128)S(1)} %get-tuple-element.27), channel_id=1, source_target_pairs={{120,128},{128,120},{121,129},{129,121},{122,130},{130,122},{123,1... | collective-permute-start | bytes 712712 | tf_op jit(solution)/shard_map/ppermute | solution.py:45
  3.7 0.7 %copy-start.5 = (s32[32]{0:T(128)S(1)}, s32[32]{0:T(128)}, u32[]{:S(2)}) copy-start(s32[32]{0:T(128)} %param.11) | copy-start | bytes 388
  4.5 3.6 %copy-start.3 = (f32[2,16,128]{2,1,0:T(8,128)S(1)}, f32[2,16,128]{2,1,0:T(8,128)}, u32[]{:S(2)}) copy-start(f32[2,16,128]{2,1,0:T(8,128)} %cperm.5) | copy-start | bytes 49156
  8.1 6.9 %copy-start.4 = (f32[2,16,128]{2,1,0:T(8,128)S(1)}, f32[2,16,128]{2,1,0:T(8,128)}, u32[]{:S(2)}) copy-start(f32[2,16,128]{2,1,0:T(8,128)} %cacc.1) | copy-start | bytes 49156
  8.1 3.2 %collective-permute-start.3 = (f32[72,256]{1,0:T(8,128)S(1)}, f32[72,256]{1,0:T(8,128)S(1)}, u32[]{:S(2)}, u32[]{:S(2)}) collective-permute-start(f32[72,256]{1,0:T(8,128)S(1)} %get-tuple-element.28), channel_id=1, source_target_pairs={{0,1},{1,2},{2,3},{3,4},{4,5},{5,6},{6,7},{7,0},{8,9},{9,10},{10,1... | collective-permute-start | bytes 221192 | tf_op jit(solution)/shard_map/ppermute | solution.py:72
  10.0 5.0 %collective-permute-start.4 = (f32[72,256]{1,0:T(8,128)S(1)}, f32[72,256]{1,0:T(8,128)S(1)}, u32[]{:S(2)}, u32[]{:S(2)}) collective-permute-start(f32[72,256]{1,0:T(8,128)S(1)} %get-tuple-element.29), channel_id=1, source_target_pairs={{0,7},{1,0},{2,1},{3,2},{4,3},{5,4},{6,5},{7,6},{8,15},{9,8},{10,9... | collective-permute-start | bytes 221192 | tf_op jit(solution)/shard_map/ppermute | solution.py:72
  16.9 11.0 %collective-permute-start.5 = (f32[4,16,128]{2,1,0:T(8,128)S(1)}, f32[4,16,128]{2,1,0:T(8,128)S(1)}, u32[]{:S(2)}, u32[]{:S(2)}) collective-permute-start(f32[4,16,128]{2,1,0:T(8,128)S(1)} %get-tuple-element.35.ab), channel_id=1, source_target_pairs={{0,8},{1,0},{2,10},{3,2},{4,12},{5,4},{6,14},{7,6},{8,16},{9,1},{1... | collective-permute-start | bytes 98312 | tf_op jit(solution)/shard_map/ppermute | solution.py:34
  26.8 6.0 %collective-permute-start.6 = (f32[4,16,128]{2,1,0:T(8,128)S(1)}, f32[4,16,128]{2,1,0:T(8,128)S(1)}, u32[]{:S(2)}, u32[]{:S(2)}) collective-permute-start(f32[4,16,128]{2,1,0:T(8,128)S(1)} %get-tuple-element.35.ab), channel_id=1, source_target_pairs={{0,1},{1,9},{2,3},{3,11},{4,5},{5,13},{6,7},{7,15},{8,0},{9,17},{1... | collective-permute-start | bytes 98312 | tf_op jit(solution)/shard_map/ppermute | solution.py:34
  26.8 9.9 %collective-permute-start.7 = (f32[8,16,128]{2,1,0:T(8,128)S(1)}, f32[8,16,128]{2,1,0:T(8,128)S(1)}, u32[]{:S(2)}, u32[]{:S(2)}) collective-permute-start(f32[8,16,128]{2,1,0:T(8,128)S(1)} %get-tuple-element.36), channel_id=1, source_target_pairs={{120,128},{128,120},{121,129},{129,121},{122,130},{130,122},{123,1... | collective-permute-start | bytes 196616 | tf_op jit(solution)/shard_map/ppermute | solution.py:45
  27.9 8.9 %collective-permute-start.8 = (f32[8,16,128]{2,1,0:T(8,128)S(1)}, f32[8,16,128]{2,1,0:T(8,128)S(1)}, u32[]{:S(2)}, u32[]{:S(2)}) collective-permute-start(f32[8,16,128]{2,1,0:T(8,128)S(1)} %pad_maximum_fusion), channel_id=1, source_target_pairs={{0,8},{1,0},{2,10},{3,2},{4,12},{5,4},{6,14},{7,6},{8,16},{9,1},{1... | collective-permute-start | bytes 196616 | tf_op jit(solution)/shard_map/ppermute | solution.py:34
  32.9 3.9 %collective-permute-start.9 = (f32[8,16,128]{2,1,0:T(8,128)S(1)}, f32[8,16,128]{2,1,0:T(8,128)S(1)}, u32[]{:S(2)}, u32[]{:S(2)}) collective-permute-start(f32[8,16,128]{2,1,0:T(8,128)S(1)} %pad_maximum_fusion.1), channel_id=1, source_target_pairs={{0,1},{1,9},{2,3},{3,11},{4,5},{5,13},{6,7},{7,15},{8,0},{9,17},{1... | collective-permute-start | bytes 196616 | tf_op jit(solution)/shard_map/ppermute | solution.py:34
  32.9 8.8 %collective-permute-start.12 = (f32[7,16,128]{2,1,0:T(8,128)S(1)}, f32[7,16,128]{2,1,0:T(8,128)S(1)}, u32[]{:S(2)}, u32[]{:S(2)}) collective-permute-start(f32[7,16,128]{2,1,0:T(8,128)S(1)} %shard_map.68), channel_id=1, source_target_pairs={{104,128},{128,104},{105,129},{129,105},{106,130},{130,106},{107,1... | collective-permute-start | bytes 172040 | tf_op jit(solution)/shard_map/ppermute | solution.py:45
  36.7 5.0 %collective-permute-start.10 = (f32[4,16,128]{2,1,0:T(8,128)S(1)}, f32[4,16,128]{2,1,0:T(8,128)S(1)}, u32[]{:S(2)}, u32[]{:S(2)}) collective-permute-start(f32[4,16,128]{2,1,0:T(8,128)S(1)} %get-tuple-element.39), channel_id=1, source_target_pairs={{0,8},{1,0},{2,10},{3,2},{4,12},{5,4},{6,14},{7,6},{8,16},{9,1},{1... | collective-permute-start | bytes 98312 | tf_op jit(solution)/shard_map/ppermute | solution.py:34
  36.8 5.0 %collective-permute-start.11 = (f32[4,16,128]{2,1,0:T(8,128)S(1)}, f32[4,16,128]{2,1,0:T(8,128)S(1)}, u32[]{:S(2)}, u32[]{:S(2)}) collective-permute-start(f32[4,16,128]{2,1,0:T(8,128)S(1)} %get-tuple-element.40), channel_id=1, source_target_pairs={{0,1},{1,9},{2,3},{3,11},{4,5},{5,13},{6,7},{7,15},{8,0},{9,17},{1... | collective-permute-start | bytes 98312 | tf_op jit(solution)/shard_map/ppermute | solution.py:34
  41.8 5.5 %collective-permute-start.13 = (f32[200,128]{1,0:T(8,128)S(1)}, f32[200,128]{1,0:T(8,128)S(1)}, u32[]{:S(2)}, u32[]{:S(2)}) collective-permute-start(f32[200,128]{1,0:T(8,128)S(1)} %get-tuple-element.43), channel_id=1, source_target_pairs={{0,1},{1,2},{2,3},{3,4},{4,5},{5,6},{6,7},{7,0},{8,9},{9,10},{10,1... | collective-permute-start | bytes 307208 | tf_op jit(solution)/shard_map/ppermute | solution.py:72
  45.6 5.3 %collective-permute-start.14 = (f32[200,128]{1,0:T(8,128)S(1)}, f32[200,128]{1,0:T(8,128)S(1)}, u32[]{:S(2)}, u32[]{:S(2)}) collective-permute-start(f32[200,128]{1,0:T(8,128)S(1)} %get-tuple-element.44), channel_id=1, source_target_pairs={{0,7},{1,0},{2,1},{3,2},{4,3},{5,4},{6,5},{7,6},{8,15},{9,8},{10,9... | collective-permute-start | bytes 307208 | tf_op jit(solution)/shard_map/ppermute | solution.py:72

commit v11 on v10

--- a/solution.py
+++ b/solution.py
@@ -164,27 +164,35 @@
             out[at : at + 1, lane : lane + CCOLS] = plane[rc : rc + 1, :]
 
 
+def frame_kernel(rhs, perm, acc, cperm, plus, minus, across, ts, rs, cs, ct):
+    lo, hi = below_above(plus, minus, across)
+    zeros = jnp.zeros((FR, COLS), jnp.float32)
+    for k in range(10):
+        ts[k] = zeros
+        ts[k, 4:36, :] = jnp.sqrt(fine_rows(perm, lo, hi, 0, 3, k - 3, 0, ROWS))
+    for k in range(8):
+        for ref, own, base in ((rs, rhs, Z1_RHS), (cs, acc, Z1_ACC)):
+            ref[k] = zeros
+            ref[k, 4:36, :] = fine_rows(own, lo, hi, base, 2, k - 2, 0, ROWS)
+    for k in range(4):
+        ct[k] = jnp.zeros((CR, CCOLS), jnp.float32)
+        ct[k, 8:24, :] = jnp.sqrt(coarse_plane(cperm, lo, hi, k - 1))
+
+
 def pre_kernel(
-    masks, rhs, perm, acc, cperm, cacc, plus, minus, across, ylo, yhi,
-    t_out, a_out, b_out, u_out, ct_out, ab_out, plus_out, minus_out, across_out,
-    ts, rs, cs, xs, us, ds, fs,
+    masks, ts_in, rs_in, cs_in, ct_in, cacc, ylo, yhi,
+    ts, rs, cs, ct_out, a_out, b_out, u_out, ab_out, plus_out, minus_out, across_out,
+    xs, us, ds, fs,
 ):
+    del ts_in, rs_in, cs_in, ct_in
     first, place_z = place()
-    lo, hi = below_above(plus, minus, across)
     mlo = masks[0]
     mhi = masks[1]
-    zeros = jnp.zeros((FR, COLS), jnp.float32)
     for k in range(10):
-        z = k - 3
-        ts[k] = zeros
-        ts[k, 4:36, :] = jnp.sqrt(fine_rows(perm, lo, hi, 0, 3, z, 0, ROWS))
         ts[k, 1:4, :] = jnp.sqrt(ylo[3 * k : 3 * k + 3, :] * mlo)
         ts[k, 36:39, :] = jnp.sqrt(yhi[3 * k : 3 * k + 3, :] * mhi)
     for k in range(8):
-        z = k - 2
-        for ref, own, base, ybase in ((rs, rhs, Z1_RHS, Y1_RHS), (cs, acc, Z1_ACC, Y1_ACC)):
-            ref[k] = zeros
-            ref[k, 4:36, :] = fine_rows(own, lo, hi, base, 2, z, 0, ROWS)
+        for ref, ybase in ((rs, Y1_RHS), (cs, Y1_ACC)):
             ref[k, 2:4, :] = ylo[ybase + 2 * k : ybase + 2 * k + 2, :] * mlo
             ref[k, 36:38, :] = yhi[ybase + 2 * k : ybase + 2 * k + 2, :] * mhi
     for k in range(10):
@@ -197,7 +205,6 @@
         q = OMEGA * t / d
         if 2 <= k < 6:
             ds[k - 2] = d
-        t_out[k] = t
         rs_k = rs[k]
         us[k] = q * rs_k
         cs[k] = q * t
@@ -236,8 +243,6 @@
         stacked, fold, precision=lax.Precision.HIGHEST, preferred_element_type=jnp.float32
     )
     for k in range(4):
-        ct_out[k] = jnp.zeros((CR, CCOLS), jnp.float32)
-        ct_out[k, 8:24, :] = jnp.sqrt(coarse_plane(cperm, lo, hi, k - 1))
         at = Y1_CO + k // 2
         lane = CCOLS * (k % 2)
         ct_out[k, 7:8, :] = jnp.sqrt(ylo[at : at + 1, lane : lane + CCOLS] * mlo)
@@ -392,7 +397,7 @@
             uf[k, 2:4, lane : lane + CCOLS] = ylo[at + 2 * half : at + 2 * half + 2, :] * mlo
             uf[k, 36:38, lane : lane + CCOLS] = yhi[at + 2 * half : at + 2 * half + 2, :] * mhi
         both = 2 * (k // 2)
-        uf[k] = uf[k] + t_in[k] * jnp.concatenate([cf[both, 0:FR], cf[both + 1, 0:FR]], axis=1)
+        uf[k] = uf[k] + t_in[k + 1] * jnp.concatenate([cf[both, 0:FR], cf[both + 1, 0:FR]], axis=1)
     for k in range(8):
         xs[k] = smooth_xy(uf[k])
     for k in range(6):
@@ -405,7 +410,7 @@
         v = uf[k + 2]
         w = 2.0 * (xs[k + 1] + 0.5 * (xs[k] + xs[k + 2]) - v)
         new = KEEP * v + a_in[k + 1] + b_in[k + 1] * w
-        uf[k + 2] = new / t_in[k + 2]
+        uf[k + 2] = new / t_in[k + 3]
         out[k] = uf[k + 2, 4:36, :]
 
 
@@ -418,9 +423,10 @@
     return jax.ShapeDtypeStruct(shape, jnp.float32)
 
 
-def call(kernel, specs, outs, scratch=()):
+def call(kernel, specs, outs, scratch=(), in_place=0):
     return pl.pallas_call(
         kernel,
+        input_output_aliases={k + 1: k for k in range(in_place)},
         in_specs=specs,
         out_specs=jax.tree.map(lambda _: VM, outs),
         out_shape=outs,
@@ -432,19 +438,25 @@
     )
 
 
+def frame_call(*operands):
+    return call(
+        frame_kernel,
+        [VM] * 7,
+        (f32(10, FR, COLS), f32(8, FR, COLS), f32(8, FR, COLS), f32(4, CR, CCOLS)),
+    )(*operands)
+
+
 def pre_call(*operands):
     return call(
         pre_kernel,
-        [SM] + [VM] * 10,
+        [SM] + [VM] * 7,
         (
-            f32(8, FR, COLS), f32(6, FR, COLS), f32(6, FR, COLS), f32(6, FR, COLS),
-            f32(4, CR, CCOLS), f32(4, CROWS, CCOLS),
+            f32(10, FR, COLS), f32(8, FR, COLS), f32(8, FR, COLS), f32(4, CR, CCOLS),
+            f32(6, FR, COLS), f32(6, FR, COLS), f32(6, FR, COLS), f32(4, CROWS, CCOLS),
             f32(4, CROWS, CCOLS), f32(4, CROWS, CCOLS), f32(8, CROWS, CCOLS),
         ),
-        (
-            (10, FR, COLS), (8, FR, COLS), (8, FR, COLS),
-            (10, FR, COLS), (8, FR, COLS), (4, FR, COLS), (4, FR, CCOLS),
-        ),
+        ((10, FR, COLS), (8, FR, COLS), (4, FR, COLS), (4, FR, CCOLS)),
+        in_place=4,
     )(*operands)
 
 
@@ -498,9 +510,11 @@
     ylo = rotated(up, "pen", 1)
     yhi = rotated(down, "pen", -1)
 
-    t, a, b, u, ct, ab, plus, minus, across = pre_call(
-        masks, pressure_rhs, permeability, accumulation, coarse_perm, coarse_accum,
-        plus, minus, across, ylo, yhi,
+    frames = frame_call(
+        pressure_rhs, permeability, accumulation, coarse_perm, plus, minus, across
+    )
+    t, _, _, ct, a, b, u, ab, plus, minus, across = pre_call(
+        masks, *frames, coarse_accum, ylo, yhi
     )
     across = between_lines(across, 1)
     plus1 = along_lines(ab, 1)

time: 53.8 us -> 53.6 us (level)
    pallas_call x1 -> x2, Pallas kernels: 1.89 us -> 1.91 us  [the longest x1 1.71 us: pre_call(): call(pre_kernel, [SM] + [VM] * 7, (f32(10, FR, COLS), f32(8, FR, COLS), f...]
where the time goes in v11:
time: 53.6 us; the launch traced here: 53.4 us
  starting transfers between devices  29 us (54%)
  waiting for transfers between devices  16.9 us (32%)
  Pallas kernels  6.01 us (11%)
  local copies, waits for them, and re-layouts  0.76 us (1%)
    ppermute x8, starting transfers between devices, along_lines(): return lax.ppermute(x, ('slab', 'pen'), pairs)  18.1 us
    ppermute x4, waiting for transfers between devices, rotated(): lax.ppermute(x, axis, [(i, (i + by) % devices) for i in range(devices)])  9.8 us
    ppermute x4, starting transfers between devices, rotated(): lax.ppermute(x, axis, [(i, (i + by) % devices) for i in range(devices)])  5.83 us
    ppermute x3, starting transfers between devices, between_lines(): return lax.ppermute(x, ('slab', 'pen'), pairs)  5.08 us
    ppermute x3, waiting for transfers between devices, between_lines(): return lax.ppermute(x, ('slab', 'pen'), pairs)  3.53 us
    ppermute x8, waiting for transfers between devices, along_lines(): return lax.ppermute(x, ('slab', 'pen'), pairs)  3.53 us
    pallas_call x1, Pallas kernels, post_call(): call(post_kernel, [SM] + [VM] * 9, f32(4, ROWS, COLS), ((8, FR, COLS), (8...  2.65 us
    pallas_call x1, Pallas kernels, pre_call(): call(pre_kernel, [SM] + [VM] * 7, (f32(10, FR, COLS), f32(8, FR, COLS), f...  1.71 us
  transfers between devices with their start and end apart: 15, of which 8 were waited for; matrix products, arithmetic and copies ran while one was open for 1% of the time, Pallas kernels for 0%

profile of v11, /device:TPU:63, one launch (start us, length us, event | category | flops | bytes accessed | tf_op | source)
XLA Modules:
  0.0 53.4 jit_solution(12000710465611229749)
XLA Ops:
  0.0 0.0 copy-start
  0.0 0.0 copy-start.1
  0.0 0.0 copy-start.2
  0.0 1.3 %shard_map.64 = (f32[232,256]{1,0:T(8,128)S(1)}, f32[232,256]{1,0:T(8,128)S(1)}, f32[232,256]{1,0:T(8,128)S(1)}) custom-call(f32[128,256]{1,0:T(8,128)} %bitcast.6, f32[128,256]{1,0:T(8,128)} %bitcast.7, f32[128,256]{1,0:T(8,128)} %bitcast.8, f32[2,16,128]{2,1,0:T(8,128)} %cperm.5), custom_call_target="tpu_custom_call" | custom-call | tf_op jit(solution)/shard_map/pallas_call | solution.py:474
  1.3 0.0 collective-permute-start
  1.3 1.7 %collective-permute-start.1 = (f32[232,256]{1,0:T(8,128)S(1)}, f32[232,256]{1,0:T(8,128)S(1)}, u32[]{:S(2)}, u32[]{:S(2)}) collective-permute-start(f32[232,256]{1,0:T(8,128)S(1)} %get-tuple-element.30), channel_id=1, source_target_pairs={{0,1},{1,9},{2,3},{3,11},{4,5},{5,13},{6,7},{7,15},{8,0},{9,17},{1... | collective-permute-start | bytes 712712 | tf_op jit(solution)/shard_map/ppermute | solution.py:34
  3.0 0.7 %collective-permute-start.2 = (f32[232,256]{1,0:T(8,128)S(1)}, f32[232,256]{1,0:T(8,128)S(1)}, u32[]{:S(2)}, u32[]{:S(2)}) collective-permute-start(f32[232,256]{1,0:T(8,128)S(1)} %get-tuple-element.31), channel_id=1, source_target_pairs={{120,128},{128,120},{121,129},{129,121},{122,130},{130,122},{123,1... | collective-permute-start | bytes 712712 | tf_op jit(solution)/shard_map/ppermute | solution.py:45
  3.7 0.0 copy-start.5
  3.7 0.6 %copy-done.5 = s32[32]{0:T(128)S(1)} copy-done((s32[32]{0:T(128)S(1)}, s32[32]{0:T(128)}, u32[]{:S(2)}) %copy-start.5) | copy-done | bytes 152
  4.3 0.1 copy.13
  4.4 0.1 reduce-window.9
  4.5 0.0 copy-start.3
  4.5 0.1 reduce
  4.6 0.2 compare_reduce_fusion
  4.8 0.1 add_convert_fusion
  4.9 1.9 %collective-permute-done.plus = f32[232,256]{1,0:T(8,128)S(1)} collective-permute-done((f32[232,256]{1,0:T(8,128)S(1)}, f32[232,256]{1,0:T(8,128)S(1)}, u32[]{:S(2)}, u32[]{:S(2)}) %collective-permute-start) | collective-permute-done | bytes 237600 | tf_op jit(solution)/shard_map/ppermute | solution.py:34
  6.8 1.3 %collective-permute-done.1.minus = f32[232,256]{1,0:T(8,128)S(1)} collective-permute-done((f32[232,256]{1,0:T(8,128)S(1)}, f32[232,256]{1,0:T(8,128)S(1)}, u32[]{:S(2)}, u32[]{:S(2)}) %collective-permute-start.1) | collective-permute-done | bytes 237600 | tf_op jit(solution)/shard_map/ppermute | solution.py:34
  8.0 0.0 collective-permute-done.2.across
  8.0 0.0 copy-done
  8.0 0.0 copy-done.1
  8.0 0.0 copy-done.2
  8.1 0.0 copy-done.3
  8.1 0.1 shard_map.66
  8.1 1.8 %collective-permute-start.3 = (f32[72,256]{1,0:T(8,128)S(1)}, f32[72,256]{1,0:T(8,128)S(1)}, u32[]{:S(2)}, u32[]{:S(2)}) collective-permute-start(f32[72,256]{1,0:T(8,128)S(1)} %get-tuple-element.36), channel_id=1, source_target_pairs={{0,1},{1,2},{2,3},{3,4},{4,5},{5,6},{6,7},{7,0},{8,9},{9,10},{10,1... | collective-permute-start | bytes 221192 | tf_op jit(solution)/shard_map/ppermute | solution.py:72
  10.0 0.2 collective-permute-start.4
  10.2 0.1 pad_maximum_fusion.2.masks
  10.2 0.0 copy-start.4
  10.2 0.2 shard_map.65
  10.4 0.9 %collective-permute-done.3.ylo = f32[72,256]{1,0:T(8,128)S(1)} collective-permute-done((f32[72,256]{1,0:T(8,128)S(1)}, f32[72,256]{1,0:T(8,128)S(1)}, u32[]{:S(2)}, u32[]{:S(2)}) %collective-permute-start.3) | collective-permute-done | bytes 73760 | tf_op jit(solution)/shard_map/ppermute | solution.py:72
  11.4 3.6 %collective-permute-done.4.yhi = f32[72,256]{1,0:T(8,128)S(1)} collective-permute-done((f32[72,256]{1,0:T(8,128)S(1)}, f32[72,256]{1,0:T(8,128)S(1)}, u32[]{:S(2)}, u32[]{:S(2)}) %collective-permute-start.4) | collective-permute-done | bytes 73760 | tf_op jit(solution)/shard_map/ppermute | solution.py:72
  14.9 0.0 copy-done.4
  15.0 1.7 %shard_map.67 = (f32[10,40,256]{2,1,0:T(8,128)S(1)}, f32[8,40,256]{2,1,0:T(8,128)S(1)}, f32[8,40,256]{2,1,0:T(8,128)S(1)}, f32[4,32,128]{2,1,0:T(8,128)S(1)}, f3...) custom-call(f32[8]{0:T(128)S(1)} %pad_maximum_fusion.2.masks, ...), custom_call_target="tpu_custom_call", output_to_operand_aliasing={{0}: (1, {}), {1}: (2, {}), {2}: (3, {}), {3}: (4, {})} | custom-call | tf_op jit(solution)/shard_map/pallas_call | solution.py:450
  16.7 10.0 %collective-permute-start.5 = (f32[4,16,128]{2,1,0:T(8,128)S(1)}, f32[4,16,128]{2,1,0:T(8,128)S(1)}, u32[]{:S(2)}, u32[]{:S(2)}) collective-permute-start(f32[4,16,128]{2,1,0:T(8,128)S(1)} %get-tuple-element.43.ab), channel_id=1, source_target_pairs={{0,8},{1,0},{2,10},{3,2},{4,12},{5,4},{6,14},{7,6},{8,16},{9,1},{1... | collective-permute-start | bytes 98312 | tf_op jit(solution)/shard_map/ppermute | solution.py:34
  26.6 0.0 collective-permute-start.6
  26.6 0.7 %collective-permute-start.7 = (f32[8,16,128]{2,1,0:T(8,128)S(1)}, f32[8,16,128]{2,1,0:T(8,128)S(1)}, u32[]{:S(2)}, u32[]{:S(2)}) collective-permute-start(f32[8,16,128]{2,1,0:T(8,128)S(1)} %get-tuple-element.44), channel_id=1, source_target_pairs={{120,128},{128,120},{121,129},{129,121},{122,130},{130,122},{123,1... | collective-permute-start | bytes 196616 | tf_op jit(solution)/shard_map/ppermute | solution.py:45
  27.3 0.4 collective-permute-done.5.plus1
  27.7 5.0 %collective-permute-start.8 = (f32[8,16,128]{2,1,0:T(8,128)S(1)}, f32[8,16,128]{2,1,0:T(8,128)S(1)}, u32[]{:S(2)}, u32[]{:S(2)}) collective-permute-start(f32[8,16,128]{2,1,0:T(8,128)S(1)} %pad_maximum_fusion), channel_id=1, source_target_pairs={{0,8},{1,0},{2,10},{3,2},{4,12},{5,4},{6,14},{7,6},{8,16},{9,1},{1... | collective-permute-start | bytes 196616 | tf_op jit(solution)/shard_map/ppermute | solution.py:34
  32.7 0.0 collective-permute-done.6.minus1
  32.7 0.0 collective-permute-start.9
  32.7 3.8 %collective-permute-start.12 = (f32[7,16,128]{2,1,0:T(8,128)S(1)}, f32[7,16,128]{2,1,0:T(8,128)S(1)}, u32[]{:S(2)}, u32[]{:S(2)}) collective-permute-start(f32[7,16,128]{2,1,0:T(8,128)S(1)} %shard_map.69), channel_id=1, source_target_pairs={{104,128},{128,104},{105,129},{129,105},{106,130},{130,106},{107,1... | collective-permute-start | bytes 172040 | tf_op jit(solution)/shard_map/ppermute | solution.py:45
  36.5 0.0 collective-permute-done.7.across
  36.5 0.0 collective-permute-done.8.plus2
  36.5 0.0 collective-permute-done.9.minus2
  36.5 0.0 collective-permute-start.10
  36.6 1.5 %collective-permute-start.11 = (f32[4,16,128]{2,1,0:T(8,128)S(1)}, f32[4,16,128]{2,1,0:T(8,128)S(1)}, u32[]{:S(2)}, u32[]{:S(2)}) collective-permute-start(f32[4,16,128]{2,1,0:T(8,128)S(1)} %get-tuple-element.48), channel_id=1, source_target_pairs={{0,1},{1,9},{2,3},{3,11},{4,5},{5,13},{6,7},{7,15},{8,0},{9,17},{1... | collective-permute-start | bytes 98312 | tf_op jit(solution)/shard_map/ppermute | solution.py:34
  38.0 3.5 %collective-permute-done.12.far = f32[7,16,128]{2,1,0:T(8,128)S(1)} collective-permute-done((f32[7,16,128]{2,1,0:T(8,128)S(1)}, f32[7,16,128]{2,1,0:T(8,128)S(1)}, u32[]{:S(2)}, u32[]{:S(2)}) %collective-permute-start.12) | collective-permute-done | bytes 57376 | tf_op jit(solution)/shard_map/ppermute | solution.py:45
  41.6 0.0 collective-permute-done.10.plus3
  41.6 0.0 collective-permute-done.11.minus3
  41.6 0.1 shard_map.70
  41.6 3.8 %collective-permute-start.13 = (f32[200,128]{1,0:T(8,128)S(1)}, f32[200,128]{1,0:T(8,128)S(1)}, u32[]{:S(2)}, u32[]{:S(2)}) collective-permute-start(f32[200,128]{1,0:T(8,128)S(1)} %get-tuple-element.51), channel_id=1, source_target_pairs={{0,1},{1,2},{2,3},{3,4},{4,5},{5,6},{6,7},{7,0},{8,9},{9,10},{10,1... | collective-permute-start | bytes 307208 | tf_op jit(solution)/shard_map/ppermute | solution.py:72
  45.4 0.0 collective-permute-start.14
  45.4 1.7 %collective-permute-done.13.ylo = f32[200,128]{1,0:T(8,128)S(1)} collective-permute-done((f32[200,128]{1,0:T(8,128)S(1)}, f32[200,128]{1,0:T(8,128)S(1)}, u32[]{:S(2)}, u32[]{:S(2)}) %collective-permute-start.13) | collective-permute-done | bytes 102432 | tf_op jit(solution)/shard_map/ppermute | solution.py:72
  47.1 3.6 %collective-permute-done.14.yhi = f32[200,128]{1,0:T(8,128)S(1)} collective-permute-done((f32[200,128]{1,0:T(8,128)S(1)}, f32[200,128]{1,0:T(8,128)S(1)}, u32[]{:S(2)}, u32[]{:S(2)}) %collective-permute-start.14) | collective-permute-done | bytes 102432 | tf_op jit(solution)/shard_map/ppermute | solution.py:72
  50.7 2.7 %shard_map.71 = f32[4,32,256]{2,1,0:T(8,128)} custom-call(f32[8]{0:T(128)S(1)} %pad_maximum_fusion.2.masks, f32[10,40,256]{2,1,0:T(8,128)S(1)} %get-tuple-element.38.t_in, f32[6,40,256]{2,1,0:T(8,128)S(1)} %get-tuple-element.39.a_in, f32[6,40,256]{2,1,0:T(8,128)S(1)} %get-tuple-element.40.b_in, f32[6,40,256]{2,1,0:T(8,128)S(1)} %get-tuple-element.41.u.u_in, ...), custom_call_target="tpu_custom_call" | custom-call | tf_op jit(solution)/shard_map/pallas_call | solution.py:464
  (7 shorter events, 0.1 us)
Async XLA Ops:
  0.0 8.0 %copy-start = (f32[4,32,256]{2,1,0:T(8,128)S(1)}, f32[4,32,256]{2,1,0:T(8,128)}, u32[]{:S(2)}) copy-start(f32[4,32,256]{2,1,0:T(8,128)} %rhs.4) | copy-start | bytes 393220
  0.0 8.0 %copy-start.1 = (f32[4,32,256]{2,1,0:T(8,128)S(1)}, f32[4,32,256]{2,1,0:T(8,128)}, u32[]{:S(2)}) copy-start(f32[4,32,256]{2,1,0:T(8,128)} %perm.3) | copy-start | bytes 393220
  0.0 8.0 %copy-start.2 = (f32[4,32,256]{2,1,0:T(8,128)S(1)}, f32[4,32,256]{2,1,0:T(8,128)}, u32[]{:S(2)}) copy-start(f32[4,32,256]{2,1,0:T(8,128)} %acc.3) | copy-start | bytes 393220
  1.3 5.4 %collective-permute-start = (f32[232,256]{1,0:T(8,128)S(1)}, f32[232,256]{1,0:T(8,128)S(1)}, u32[]{:S(2)}, u32[]{:S(2)}) collective-permute-start(f32[232,256]{1,0:T(8,128)S(1)} %get-tuple-element.29), channel_id=1, source_target_pairs={{0,8},{1,0},{2,10},{3,2},{4,12},{5,4},{6,14},{7,6},{8,16},{9,1},{1... | collective-permute-start | bytes 712712 | tf_op jit(solution)/shard_map/ppermute | solution.py:34
  1.3 6.7 %collective-permute-start.1 = (f32[232,256]{1,0:T(8,128)S(1)}, f32[232,256]{1,0:T(8,128)S(1)}, u32[]{:S(2)}, u32[]{:S(2)}) collective-permute-start(f32[232,256]{1,0:T(8,128)S(1)} %get-tuple-element.30), channel_id=1, source_target_pairs={{0,1},{1,9},{2,3},{3,11},{4,5},{5,13},{6,7},{7,15},{8,0},{9,17},{1... | collective-permute-start | bytes 712712 | tf_op jit(solution)/shard_map/ppermute | solution.py:34
  3.0 5.0 %collective-permute-start.2 = (f32[232,256]{1,0:T(8,128)S(1)}, f32[232,256]{1,0:T(8,128)S(1)}, u32[]{:S(2)}, u32[]{:S(2)}) collective-permute-start(f32[232,256]{1,0:T(8,128)S(1)} %get-tuple-element.31), channel_id=1, source_target_pairs={{120,128},{128,120},{121,129},{129,121},{122,130},{130,122},{123,1... | collective-permute-start | bytes 712712 | tf_op jit(solution)/shard_map/ppermute | solution.py:45
  3.7 0.7 %copy-start.5 = (s32[32]{0:T(128)S(1)}, s32[32]{0:T(128)}, u32[]{:S(2)}) copy-start(s32[32]{0:T(128)} %param.11) | copy-start | bytes 388
  4.5 3.6 %copy-start.3 = (f32[2,16,128]{2,1,0:T(8,128)S(1)}, f32[2,16,128]{2,1,0:T(8,128)}, u32[]{:S(2)}) copy-start(f32[2,16,128]{2,1,0:T(8,128)} %cperm.5) | copy-start | bytes 49156
  8.1 3.2 %collective-permute-start.3 = (f32[72,256]{1,0:T(8,128)S(1)}, f32[72,256]{1,0:T(8,128)S(1)}, u32[]{:S(2)}, u32[]{:S(2)}) collective-permute-start(f32[72,256]{1,0:T(8,128)S(1)} %get-tuple-element.36), channel_id=1, source_target_pairs={{0,1},{1,2},{2,3},{3,4},{4,5},{5,6},{6,7},{7,0},{8,9},{9,10},{10,1... | collective-permute-start | bytes 221192 | tf_op jit(solution)/shard_map/ppermute | solution.py:72
  10.0 5.0 %collective-permute-start.4 = (f32[72,256]{1,0:T(8,128)S(1)}, f32[72,256]{1,0:T(8,128)S(1)}, u32[]{:S(2)}, u32[]{:S(2)}) collective-permute-start(f32[72,256]{1,0:T(8,128)S(1)} %get-tuple-element.37), channel_id=1, source_target_pairs={{0,7},{1,0},{2,1},{3,2},{4,3},{5,4},{6,5},{7,6},{8,15},{9,8},{10,9... | collective-permute-start | bytes 221192 | tf_op jit(solution)/shard_map/ppermute | solution.py:72
  10.2 4.7 %copy-start.4 = (f32[2,16,128]{2,1,0:T(8,128)S(1)}, f32[2,16,128]{2,1,0:T(8,128)}, u32[]{:S(2)}) copy-start(f32[2,16,128]{2,1,0:T(8,128)} %cacc.1) | copy-start | bytes 49156
  16.7 11.0 %collective-permute-start.5 = (f32[4,16,128]{2,1,0:T(8,128)S(1)}, f32[4,16,128]{2,1,0:T(8,128)S(1)}, u32[]{:S(2)}, u32[]{:S(2)}) collective-permute-start(f32[4,16,128]{2,1,0:T(8,128)S(1)} %get-tuple-element.43.ab), channel_id=1, source_target_pairs={{0,8},{1,0},{2,10},{3,2},{4,12},{5,4},{6,14},{7,6},{8,16},{9,1},{1... | collective-permute-start | bytes 98312 | tf_op jit(solution)/shard_map/ppermute | solution.py:34
  26.6 6.0 %collective-permute-start.6 = (f32[4,16,128]{2,1,0:T(8,128)S(1)}, f32[4,16,128]{2,1,0:T(8,128)S(1)}, u32[]{:S(2)}, u32[]{:S(2)}) collective-permute-start(f32[4,16,128]{2,1,0:T(8,128)S(1)} %get-tuple-element.43.ab), channel_id=1, source_target_pairs={{0,1},{1,9},{2,3},{3,11},{4,5},{5,13},{6,7},{7,15},{8,0},{9,17},{1... | collective-permute-start | bytes 98312 | tf_op jit(solution)/shard_map/ppermute | solution.py:34
  26.6 9.9 %collective-permute-start.7 = (f32[8,16,128]{2,1,0:T(8,128)S(1)}, f32[8,16,128]{2,1,0:T(8,128)S(1)}, u32[]{:S(2)}, u32[]{:S(2)}) collective-permute-start(f32[8,16,128]{2,1,0:T(8,128)S(1)} %get-tuple-element.44), channel_id=1, source_target_pairs={{120,128},{128,120},{121,129},{129,121},{122,130},{130,122},{123,1... | collective-permute-start | bytes 196616 | tf_op jit(solution)/shard_map/ppermute | solution.py:45
  27.7 8.9 %collective-permute-start.8 = (f32[8,16,128]{2,1,0:T(8,128)S(1)}, f32[8,16,128]{2,1,0:T(8,128)S(1)}, u32[]{:S(2)}, u32[]{:S(2)}) collective-permute-start(f32[8,16,128]{2,1,0:T(8,128)S(1)} %pad_maximum_fusion), channel_id=1, source_target_pairs={{0,8},{1,0},{2,10},{3,2},{4,12},{5,4},{6,14},{7,6},{8,16},{9,1},{1... | collective-permute-start | bytes 196616 | tf_op jit(solution)/shard_map/ppermute | solution.py:34
  32.7 3.9 %collective-permute-start.9 = (f32[8,16,128]{2,1,0:T(8,128)S(1)}, f32[8,16,128]{2,1,0:T(8,128)S(1)}, u32[]{:S(2)}, u32[]{:S(2)}) collective-permute-start(f32[8,16,128]{2,1,0:T(8,128)S(1)} %pad_maximum_fusion.1), channel_id=1, source_target_pairs={{0,1},{1,9},{2,3},{3,11},{4,5},{5,13},{6,7},{7,15},{8,0},{9,17},{1... | collective-permute-start | bytes 196616 | tf_op jit(solution)/shard_map/ppermute | solution.py:34
  32.7 8.8 %collective-permute-start.12 = (f32[7,16,128]{2,1,0:T(8,128)S(1)}, f32[7,16,128]{2,1,0:T(8,128)S(1)}, u32[]{:S(2)}, u32[]{:S(2)}) collective-permute-start(f32[7,16,128]{2,1,0:T(8,128)S(1)} %shard_map.69), channel_id=1, source_target_pairs={{104,128},{128,104},{105,129},{129,105},{106,130},{130,106},{107,1... | collective-permute-start | bytes 172040 | tf_op jit(solution)/shard_map/ppermute | solution.py:45
  36.5 5.0 %collective-permute-start.10 = (f32[4,16,128]{2,1,0:T(8,128)S(1)}, f32[4,16,128]{2,1,0:T(8,128)S(1)}, u32[]{:S(2)}, u32[]{:S(2)}) collective-permute-start(f32[4,16,128]{2,1,0:T(8,128)S(1)} %get-tuple-element.47), channel_id=1, source_target_pairs={{0,8},{1,0},{2,10},{3,2},{4,12},{5,4},{6,14},{7,6},{8,16},{9,1},{1... | collective-permute-start | bytes 98312 | tf_op jit(solution)/shard_map/ppermute | solution.py:34
  36.6 5.0 %collective-permute-start.11 = (f32[4,16,128]{2,1,0:T(8,128)S(1)}, f32[4,16,128]{2,1,0:T(8,128)S(1)}, u32[]{:S(2)}, u32[]{:S(2)}) collective-permute-start(f32[4,16,128]{2,1,0:T(8,128)S(1)} %get-tuple-element.48), channel_id=1, source_target_pairs={{0,1},{1,9},{2,3},{3,11},{4,5},{5,13},{6,7},{7,15},{8,0},{9,17},{1... | collective-permute-start | bytes 98312 | tf_op jit(solution)/shard_map/ppermute | solution.py:34
  41.6 5.5 %collective-permute-start.13 = (f32[200,128]{1,0:T(8,128)S(1)}, f32[200,128]{1,0:T(8,128)S(1)}, u32[]{:S(2)}, u32[]{:S(2)}) collective-permute-start(f32[200,128]{1,0:T(8,128)S(1)} %get-tuple-element.51), channel_id=1, source_target_pairs={{0,1},{1,2},{2,3},{3,4},{4,5},{5,6},{6,7},{7,0},{8,9},{9,10},{10,1... | collective-permute-start | bytes 307208 | tf_op jit(solution)/shard_map/ppermute | solution.py:72
  45.4 5.3 %collective-permute-start.14 = (f32[200,128]{1,0:T(8,128)S(1)}, f32[200,128]{1,0:T(8,128)S(1)}, u32[]{:S(2)}, u32[]{:S(2)}) collective-permute-start(f32[200,128]{1,0:T(8,128)S(1)} %get-tuple-element.52), channel_id=1, source_target_pairs={{0,7},{1,0},{2,1},{3,2},{4,3},{5,4},{6,5},{7,6},{8,15},{9,8},{10,9... | collective-permute-start | bytes 307208 | tf_op jit(solution)/shard_map/ppermute | solution.py:72

commit v12 on v11

--- a/solution.py
+++ b/solution.py
@@ -333,20 +333,33 @@
                 out[at + 2 * half : at + 2 * half + 2, :] = rows
 
 
+def window_kernel(u_in, dom, edge, ff, uf):
+    for k in range(26):
+        ff[k] = jnp.zeros((CR, CCOLS), jnp.float32)
+        ff[k, 8:24, :] = dom[k]
+    for k in range(8):
+        if 0 < k < 7:
+            uf[k] = u_in[k - 1]
+        else:
+            uf[k] = jnp.zeros((FR, COLS), jnp.float32)
+            piece = 0 if k == 0 else 4
+            for j in range(4):
+                row = 4 + 16 * (j // 2)
+                lane = CCOLS * (j % 2)
+                uf[k, row : row + 16, lane : lane + CCOLS] = edge[piece + j]
+
+
 def post_kernel(
-    masks, t_in, a_in, b_in, u_in, ct, dom, edge, ylo, yhi,
-    out, uf, cf, xs, ff,
+    masks, ff_in, uf_in, t_in, a_in, b_in, ct, ylo, yhi,
+    ff, uf, out, cf, xs,
 ):
+    del ff_in, uf_in
     mlo = masks[0]
     mhi = masks[1]
-    tile = jnp.zeros((8, CCOLS), jnp.float32)
     a = []
     b = [None]
     for k in range(26):
-        ff[k, 0:8, :] = tile
-        ff[k, 24:32, :] = tile
         ff[k, 2:8, :] = ylo[6 * k : 6 * k + 6, :] * mlo
-        ff[k, 8:24, :] = dom[k]
         ff[k, 24:30, :] = yhi[6 * k : 6 * k + 6, :] * mhi
         (a if k < 14 else b).append(ff[k])
     link = [0.5] * 13
@@ -380,17 +393,7 @@
             rows = wide[CR * k + 6 : CR * k + 26, CCOLS * half : CCOLS * half + CCOLS]
             cf[2 * k + half, pl.ds(0, 20, 2), :] = rows
             cf[2 * k + half, pl.ds(1, 20, 2), :] = rows
-    zeros = jnp.zeros((FR, COLS), jnp.float32)
-    for k in range(8):
-        if 0 < k < 7:
-            uf[k] = u_in[k - 1]
-        else:
-            uf[k] = zeros
-            piece = 0 if k == 0 else 4
-            for j in range(4):
-                row = 4 + 16 * (j // 2)
-                lane = CCOLS * (j % 2)
-                uf[k, row : row + 16, lane : lane + CCOLS] = edge[piece + j]
+    for k in range(8):
         at = Y2_U + 4 * k
         for half in range(2):
             lane = CCOLS * half
@@ -460,12 +463,19 @@
     )(*operands)
 
 
+def window_call(*operands):
+    return call(
+        window_kernel, [VM] * 3, (f32(26, CR, CCOLS), f32(8, FR, COLS))
+    )(*operands)
+
+
 def post_call(*operands):
     return call(
         post_kernel,
-        [SM] + [VM] * 9,
-        f32(4, ROWS, COLS),
-        ((8, FR, COLS), (8, FR + 8, CCOLS), (8, FR, COLS), (26, CR, CCOLS)),
+        [SM] + [VM] * 8,
+        (f32(26, CR, CCOLS), f32(8, FR, COLS), f32(4, ROWS, COLS)),
+        ((8, FR + 8, CCOLS), (8, FR, COLS)),
+        in_place=2,
     )(*operands)
 
 
@@ -536,7 +546,7 @@
     ylo = rotated(up, "pen", 1)
     yhi = rotated(down, "pen", -1)
 
-    return post_call(masks, t, a, b, u, ct, dom, edge, ylo, yhi)
+    return post_call(masks, *window_call(u, dom, edge), t, a, b, ct, ylo, yhi)[2]
 
 
 def solution(mesh):

time: 53.6 us -> 53.5 us (level)
    pallas_call x1 -> x2, Pallas kernels: 2.65 us -> 2.7 us  [the longest x1 2.64 us: post_call(): call(post_kernel, [SM] + [VM] * 8, (f32(26, CR, CCOLS), f32(8, FR, COLS),...]
  transfers between devices with their start and end apart: 15 -> 15, of which waited for: 8 -> 8; matrix products, arithmetic and copies ran while one was open for 1% -> 1% of each run, Pallas kernels for 0% -> 1%
where the time goes in v12:
time: 53.5 us; the launch traced here: 53.4 us
  starting transfers between devices  29 us (54%)
  waiting for transfers between devices  16.8 us (31%)
  Pallas kernels  6.05 us (11%)
  local copies, waits for them, and re-layouts  0.76 us (1%)
    ppermute x8, starting transfers between devices, along_lines(): return lax.ppermute(x, ('slab', 'pen'), pairs)  18.1 us
    ppermute x4, waiting for transfers between devices, rotated(): lax.ppermute(x, axis, [(i, (i + by) % devices) for i in range(devices)])  9.74 us
    ppermute x4, starting transfers between devices, rotated(): lax.ppermute(x, axis, [(i, (i + by) % devices) for i in range(devices)])  5.83 us
    ppermute x3, starting transfers between devices, between_lines(): return lax.ppermute(x, ('slab', 'pen'), pairs)  5.08 us
    ppermute x3, waiting for transfers between devices, between_lines(): return lax.ppermute(x, ('slab', 'pen'), pairs)  3.53 us
    ppermute x8, waiting for transfers between devices, along_lines(): return lax.ppermute(x, ('slab', 'pen'), pairs)  3.53 us
    pallas_call x1, Pallas kernels, post_call(): call(post_kernel, [SM] + [VM] * 8, (f32(26, CR, CCOLS), f32(8, FR, COLS),...  2.64 us
    pallas_call x1, Pallas kernels, pre_call(): call(pre_kernel, [SM] + [VM] * 7, (f32(10, FR, COLS), f32(8, FR, COLS), f...  1.71 us
  transfers between devices with their start and end apart: 15, of which 8 were waited for; matrix products, arithmetic and copies ran while one was open for 1% of the time, Pallas kernels for 1%

profile of v12, /device:TPU:63, one launch (start us, length us, event | category | flops | bytes accessed | tf_op | source)
XLA Modules:
  0.0 53.4 jit_solution(17239494904438745666)
XLA Ops:
  0.0 0.0 copy-start
  0.0 0.0 copy-start.1
  0.0 0.0 copy-start.2
  0.0 1.3 %shard_map.64 = (f32[232,256]{1,0:T(8,128)S(1)}, f32[232,256]{1,0:T(8,128)S(1)}, f32[232,256]{1,0:T(8,128)S(1)}) custom-call(f32[128,256]{1,0:T(8,128)} %bitcast.6, f32[128,256]{1,0:T(8,128)} %bitcast.7, f32[128,256]{1,0:T(8,128)} %bitcast.8, f32[2,16,128]{2,1,0:T(8,128)} %cperm.5), custom_call_target="tpu_custom_call" | custom-call | tf_op jit(solution)/shard_map/pallas_call | solution.py:484
  1.3 0.0 collective-permute-start
  1.3 1.7 %collective-permute-start.1 = (f32[232,256]{1,0:T(8,128)S(1)}, f32[232,256]{1,0:T(8,128)S(1)}, u32[]{:S(2)}, u32[]{:S(2)}) collective-permute-start(f32[232,256]{1,0:T(8,128)S(1)} %get-tuple-element.33), channel_id=1, source_target_pairs={{0,1},{1,9},{2,3},{3,11},{4,5},{5,13},{6,7},{7,15},{8,0},{9,17},{1... | collective-permute-start | bytes 712712 | tf_op jit(solution)/shard_map/ppermute | solution.py:34
  3.0 0.7 %collective-permute-start.2 = (f32[232,256]{1,0:T(8,128)S(1)}, f32[232,256]{1,0:T(8,128)S(1)}, u32[]{:S(2)}, u32[]{:S(2)}) collective-permute-start(f32[232,256]{1,0:T(8,128)S(1)} %get-tuple-element.34), channel_id=1, source_target_pairs={{120,128},{128,120},{121,129},{129,121},{122,130},{130,122},{123,1... | collective-permute-start | bytes 712712 | tf_op jit(solution)/shard_map/ppermute | solution.py:45
  3.7 0.0 copy-start.5
  3.7 0.6 %copy-done.5 = s32[32]{0:T(128)S(1)} copy-done((s32[32]{0:T(128)S(1)}, s32[32]{0:T(128)}, u32[]{:S(2)}) %copy-start.5) | copy-done | bytes 152
  4.3 0.1 copy.15
  4.4 0.1 reduce-window.9
  4.5 0.0 copy-start.3
  4.5 0.1 reduce
  4.6 0.2 compare_reduce_fusion
  4.8 0.1 add_convert_fusion
  4.9 1.9 %collective-permute-done.plus = f32[232,256]{1,0:T(8,128)S(1)} collective-permute-done((f32[232,256]{1,0:T(8,128)S(1)}, f32[232,256]{1,0:T(8,128)S(1)}, u32[]{:S(2)}, u32[]{:S(2)}) %collective-permute-start) | collective-permute-done | bytes 237600 | tf_op jit(solution)/shard_map/ppermute | solution.py:34
  6.8 1.3 %collective-permute-done.1.minus = f32[232,256]{1,0:T(8,128)S(1)} collective-permute-done((f32[232,256]{1,0:T(8,128)S(1)}, f32[232,256]{1,0:T(8,128)S(1)}, u32[]{:S(2)}, u32[]{:S(2)}) %collective-permute-start.1) | collective-permute-done | bytes 237600 | tf_op jit(solution)/shard_map/ppermute | solution.py:34
  8.0 0.0 collective-permute-done.2.across
  8.0 0.0 copy-done
  8.0 0.0 copy-done.1
  8.0 0.0 copy-done.2
  8.1 0.0 copy-done.3
  8.1 0.1 shard_map.66
  8.1 1.8 %collective-permute-start.3 = (f32[72,256]{1,0:T(8,128)S(1)}, f32[72,256]{1,0:T(8,128)S(1)}, u32[]{:S(2)}, u32[]{:S(2)}) collective-permute-start(f32[72,256]{1,0:T(8,128)S(1)} %get-tuple-element.39), channel_id=1, source_target_pairs={{0,1},{1,2},{2,3},{3,4},{4,5},{5,6},{6,7},{7,0},{8,9},{9,10},{10,1... | collective-permute-start | bytes 221192 | tf_op jit(solution)/shard_map/ppermute | solution.py:72
  10.0 0.2 collective-permute-start.4
  10.2 0.1 pad_maximum_fusion.2.masks
  10.2 0.0 copy-start.4
  10.2 0.2 shard_map.65
  10.4 0.9 %collective-permute-done.3.ylo = f32[72,256]{1,0:T(8,128)S(1)} collective-permute-done((f32[72,256]{1,0:T(8,128)S(1)}, f32[72,256]{1,0:T(8,128)S(1)}, u32[]{:S(2)}, u32[]{:S(2)}) %collective-permute-start.3) | collective-permute-done | bytes 73760 | tf_op jit(solution)/shard_map/ppermute | solution.py:72
  11.4 3.6 %collective-permute-done.4.yhi = f32[72,256]{1,0:T(8,128)S(1)} collective-permute-done((f32[72,256]{1,0:T(8,128)S(1)}, f32[72,256]{1,0:T(8,128)S(1)}, u32[]{:S(2)}, u32[]{:S(2)}) %collective-permute-start.4) | collective-permute-done | bytes 73760 | tf_op jit(solution)/shard_map/ppermute | solution.py:72
  14.9 0.0 copy-done.4
  15.0 1.7 %shard_map.67 = (f32[10,40,256]{2,1,0:T(8,128)S(1)}, f32[8,40,256]{2,1,0:T(8,128)S(1)}, f32[8,40,256]{2,1,0:T(8,128)S(1)}, f32[4,32,128]{2,1,0:T(8,128)S(1)}, f3...) custom-call(f32[8]{0:T(128)S(1)} %pad_maximum_fusion.2.masks, ...), custom_call_target="tpu_custom_call", output_to_operand_aliasing={{0}: (1, {}), {1}: (2, {}), {2}: (3, {}), {3}: (4, {})} | custom-call | tf_op jit(solution)/shard_map/pallas_call | solution.py:453
  16.7 10.0 %collective-permute-start.5 = (f32[4,16,128]{2,1,0:T(8,128)S(1)}, f32[4,16,128]{2,1,0:T(8,128)S(1)}, u32[]{:S(2)}, u32[]{:S(2)}) collective-permute-start(f32[4,16,128]{2,1,0:T(8,128)S(1)} %get-tuple-element.42.ab), channel_id=1, source_target_pairs={{0,8},{1,0},{2,10},{3,2},{4,12},{5,4},{6,14},{7,6},{8,16},{9,1},{1... | collective-permute-start | bytes 98312 | tf_op jit(solution)/shard_map/ppermute | solution.py:34
  26.6 0.0 collective-permute-start.6
  26.6 0.7 %collective-permute-start.7 = (f32[8,16,128]{2,1,0:T(8,128)S(1)}, f32[8,16,128]{2,1,0:T(8,128)S(1)}, u32[]{:S(2)}, u32[]{:S(2)}) collective-permute-start(f32[8,16,128]{2,1,0:T(8,128)S(1)} %get-tuple-element.43), channel_id=1, source_target_pairs={{120,128},{128,120},{121,129},{129,121},{122,130},{130,122},{123,1... | collective-permute-start | bytes 196616 | tf_op jit(solution)/shard_map/ppermute | solution.py:45
  27.3 0.4 collective-permute-done.5.plus1
  27.7 5.0 %collective-permute-start.8 = (f32[8,16,128]{2,1,0:T(8,128)S(1)}, f32[8,16,128]{2,1,0:T(8,128)S(1)}, u32[]{:S(2)}, u32[]{:S(2)}) collective-permute-start(f32[8,16,128]{2,1,0:T(8,128)S(1)} %pad_maximum_fusion), channel_id=1, source_target_pairs={{0,8},{1,0},{2,10},{3,2},{4,12},{5,4},{6,14},{7,6},{8,16},{9,1},{1... | collective-permute-start | bytes 196616 | tf_op jit(solution)/shard_map/ppermute | solution.py:34
  32.7 0.0 collective-permute-done.6.minus1
  32.7 0.0 collective-permute-start.9
  32.7 3.8 %collective-permute-start.12 = (f32[7,16,128]{2,1,0:T(8,128)S(1)}, f32[7,16,128]{2,1,0:T(8,128)S(1)}, u32[]{:S(2)}, u32[]{:S(2)}) collective-permute-start(f32[7,16,128]{2,1,0:T(8,128)S(1)} %shard_map.69), channel_id=1, source_target_pairs={{104,128},{128,104},{105,129},{129,105},{106,130},{130,106},{107,1... | collective-permute-start | bytes 172040 | tf_op jit(solution)/shard_map/ppermute | solution.py:45
  36.5 0.0 collective-permute-done.7.across
  36.5 0.0 collective-permute-done.8.plus2
  36.5 0.0 collective-permute-done.9.minus2
  36.5 0.0 collective-permute-start.10
  36.6 1.5 %collective-permute-start.11 = (f32[4,16,128]{2,1,0:T(8,128)S(1)}, f32[4,16,128]{2,1,0:T(8,128)S(1)}, u32[]{:S(2)}, u32[]{:S(2)}) collective-permute-start(f32[4,16,128]{2,1,0:T(8,128)S(1)} %get-tuple-element.47), channel_id=1, source_target_pairs={{0,1},{1,9},{2,3},{3,11},{4,5},{5,13},{6,7},{7,15},{8,0},{9,17},{1... | collective-permute-start | bytes 98312 | tf_op jit(solution)/shard_map/ppermute | solution.py:34
  38.0 3.5 %collective-permute-done.12.far = f32[7,16,128]{2,1,0:T(8,128)S(1)} collective-permute-done((f32[7,16,128]{2,1,0:T(8,128)S(1)}, f32[7,16,128]{2,1,0:T(8,128)S(1)}, u32[]{:S(2)}, u32[]{:S(2)}) %collective-permute-start.12) | collective-permute-done | bytes 57376 | tf_op jit(solution)/shard_map/ppermute | solution.py:45
  41.6 0.0 collective-permute-done.10.plus3
  41.6 0.0 collective-permute-done.11.minus3
  41.6 0.1 shard_map.70
  41.6 3.8 %collective-permute-start.13 = (f32[200,128]{1,0:T(8,128)S(1)}, f32[200,128]{1,0:T(8,128)S(1)}, u32[]{:S(2)}, u32[]{:S(2)}) collective-permute-start(f32[200,128]{1,0:T(8,128)S(1)} %get-tuple-element.56), channel_id=1, source_target_pairs={{0,1},{1,2},{2,3},{3,4},{4,5},{5,6},{6,7},{7,0},{8,9},{9,10},{10,1... | collective-permute-start | bytes 307208 | tf_op jit(solution)/shard_map/ppermute | solution.py:72
  45.4 0.0 collective-permute-start.14
  45.4 0.1 shard_map.71
  45.5 1.6 %collective-permute-done.13.ylo = f32[200,128]{1,0:T(8,128)S(1)} collective-permute-done((f32[200,128]{1,0:T(8,128)S(1)}, f32[200,128]{1,0:T(8,128)S(1)}, u32[]{:S(2)}, u32[]{:S(2)}) %collective-permute-start.13) | collective-permute-done | bytes 102432 | tf_op jit(solution)/shard_map/ppermute | solution.py:72
  47.1 3.6 %collective-permute-done.14.yhi = f32[200,128]{1,0:T(8,128)S(1)} collective-permute-done((f32[200,128]{1,0:T(8,128)S(1)}, f32[200,128]{1,0:T(8,128)S(1)}, u32[]{:S(2)}, u32[]{:S(2)}) %collective-permute-start.14) | collective-permute-done | bytes 102432 | tf_op jit(solution)/shard_map/ppermute | solution.py:72
  50.7 2.6 %shard_map.72 = (f32[26,32,128]{2,1,0:T(8,128)S(1)}, f32[8,40,256]{2,1,0:T(8,128)S(1)}, f32[4,32,256]{2,1,0:T(8,128)}) custom-call(f32[8]{0:T(128)S(1)} %pad_maximum_fusion.2.masks, f32[26,32,128]{2,1,0:T(8,128)S(1)} %get-tuple-element.50.ff_in, f32[8,40,256]{2,1,0:T(8,128)S(1)} %get-tuple-element.51.uf_in, ...), custom_call_target="tpu_custom_call", output_to_operand_aliasing={{0}: (1, {}), {1}: (2, {})} | custom-call | tf_op jit(solution)/shard_map/pallas_call | solution.py:473
  (7 shorter events, 0.1 us)
Async XLA Ops:
  0.0 8.0 %copy-start = (f32[4,32,256]{2,1,0:T(8,128)S(1)}, f32[4,32,256]{2,1,0:T(8,128)}, u32[]{:S(2)}) copy-start(f32[4,32,256]{2,1,0:T(8,128)} %rhs.4) | copy-start | bytes 393220
  0.0 8.0 %copy-start.1 = (f32[4,32,256]{2,1,0:T(8,128)S(1)}, f32[4,32,256]{2,1,0:T(8,128)}, u32[]{:S(2)}) copy-start(f32[4,32,256]{2,1,0:T(8,128)} %perm.3) | copy-start | bytes 393220
  0.0 8.0 %copy-start.2 = (f32[4,32,256]{2,1,0:T(8,128)S(1)}, f32[4,32,256]{2,1,0:T(8,128)}, u32[]{:S(2)}) copy-start(f32[4,32,256]{2,1,0:T(8,128)} %acc.3) | copy-start | bytes 393220
  1.3 5.4 %collective-permute-start = (f32[232,256]{1,0:T(8,128)S(1)}, f32[232,256]{1,0:T(8,128)S(1)}, u32[]{:S(2)}, u32[]{:S(2)}) collective-permute-start(f32[232,256]{1,0:T(8,128)S(1)} %get-tuple-element.32), channel_id=1, source_target_pairs={{0,8},{1,0},{2,10},{3,2},{4,12},{5,4},{6,14},{7,6},{8,16},{9,1},{1... | collective-permute-start | bytes 712712 | tf_op jit(solution)/shard_map/ppermute | solution.py:34
  1.3 6.7 %collective-permute-start.1 = (f32[232,256]{1,0:T(8,128)S(1)}, f32[232,256]{1,0:T(8,128)S(1)}, u32[]{:S(2)}, u32[]{:S(2)}) collective-permute-start(f32[232,256]{1,0:T(8,128)S(1)} %get-tuple-element.33), channel_id=1, source_target_pairs={{0,1},{1,9},{2,3},{3,11},{4,5},{5,13},{6,7},{7,15},{8,0},{9,17},{1... | collective-permute-start | bytes 712712 | tf_op jit(solution)/shard_map/ppermute | solution.py:34
  3.0 5.0 %collective-permute-start.2 = (f32[232,256]{1,0:T(8,128)S(1)}, f32[232,256]{1,0:T(8,128)S(1)}, u32[]{:S(2)}, u32[]{:S(2)}) collective-permute-start(f32[232,256]{1,0:T(8,128)S(1)} %get-tuple-element.34), channel_id=1, source_target_pairs={{120,128},{128,120},{121,129},{129,121},{122,130},{130,122},{123,1... | collective-permute-start | bytes 712712 | tf_op jit(solution)/shard_map/ppermute | solution.py:45
  3.7 0.7 %copy-start.5 = (s32[32]{0:T(128)S(1)}, s32[32]{0:T(128)}, u32[]{:S(2)}) copy-start(s32[32]{0:T(128)} %param.11) | copy-start | bytes 388
  4.5 3.6 %copy-start.3 = (f32[2,16,128]{2,1,0:T(8,128)S(1)}, f32[2,16,128]{2,1,0:T(8,128)}, u32[]{:S(2)}) copy-start(f32[2,16,128]{2,1,0:T(8,128)} %cperm.5) | copy-start | bytes 49156
  8.1 3.2 %collective-permute-start.3 = (f32[72,256]{1,0:T(8,128)S(1)}, f32[72,256]{1,0:T(8,128)S(1)}, u32[]{:S(2)}, u32[]{:S(2)}) collective-permute-start(f32[72,256]{1,0:T(8,128)S(1)} %get-tuple-element.39), channel_id=1, source_target_pairs={{0,1},{1,2},{2,3},{3,4},{4,5},{5,6},{6,7},{7,0},{8,9},{9,10},{10,1... | collective-permute-start | bytes 221192 | tf_op jit(solution)/shard_map/ppermute | solution.py:72
  10.0 5.0 %collective-permute-start.4 = (f32[72,256]{1,0:T(8,128)S(1)}, f32[72,256]{1,0:T(8,128)S(1)}, u32[]{:S(2)}, u32[]{:S(2)}) collective-permute-start(f32[72,256]{1,0:T(8,128)S(1)} %get-tuple-element.40), channel_id=1, source_target_pairs={{0,7},{1,0},{2,1},{3,2},{4,3},{5,4},{6,5},{7,6},{8,15},{9,8},{10,9... | collective-permute-start | bytes 221192 | tf_op jit(solution)/shard_map/ppermute | solution.py:72
  10.2 4.7 %copy-start.4 = (f32[2,16,128]{2,1,0:T(8,128)S(1)}, f32[2,16,128]{2,1,0:T(8,128)}, u32[]{:S(2)}) copy-start(f32[2,16,128]{2,1,0:T(8,128)} %cacc.1) | copy-start | bytes 49156
  16.7 11.0 %collective-permute-start.5 = (f32[4,16,128]{2,1,0:T(8,128)S(1)}, f32[4,16,128]{2,1,0:T(8,128)S(1)}, u32[]{:S(2)}, u32[]{:S(2)}) collective-permute-start(f32[4,16,128]{2,1,0:T(8,128)S(1)} %get-tuple-element.42.ab), channel_id=1, source_target_pairs={{0,8},{1,0},{2,10},{3,2},{4,12},{5,4},{6,14},{7,6},{8,16},{9,1},{1... | collective-permute-start | bytes 98312 | tf_op jit(solution)/shard_map/ppermute | solution.py:34
  26.6 6.0 %collective-permute-start.6 = (f32[4,16,128]{2,1,0:T(8,128)S(1)}, f32[4,16,128]{2,1,0:T(8,128)S(1)}, u32[]{:S(2)}, u32[]{:S(2)}) collective-permute-start(f32[4,16,128]{2,1,0:T(8,128)S(1)} %get-tuple-element.42.ab), channel_id=1, source_target_pairs={{0,1},{1,9},{2,3},{3,11},{4,5},{5,13},{6,7},{7,15},{8,0},{9,17},{1... | collective-permute-start | bytes 98312 | tf_op jit(solution)/shard_map/ppermute | solution.py:34
  26.6 9.9 %collective-permute-start.7 = (f32[8,16,128]{2,1,0:T(8,128)S(1)}, f32[8,16,128]{2,1,0:T(8,128)S(1)}, u32[]{:S(2)}, u32[]{:S(2)}) collective-permute-start(f32[8,16,128]{2,1,0:T(8,128)S(1)} %get-tuple-element.43), channel_id=1, source_target_pairs={{120,128},{128,120},{121,129},{129,121},{122,130},{130,122},{123,1... | collective-permute-start | bytes 196616 | tf_op jit(solution)/shard_map/ppermute | solution.py:45
  27.7 8.9 %collective-permute-start.8 = (f32[8,16,128]{2,1,0:T(8,128)S(1)}, f32[8,16,128]{2,1,0:T(8,128)S(1)}, u32[]{:S(2)}, u32[]{:S(2)}) collective-permute-start(f32[8,16,128]{2,1,0:T(8,128)S(1)} %pad_maximum_fusion), channel_id=1, source_target_pairs={{0,8},{1,0},{2,10},{3,2},{4,12},{5,4},{6,14},{7,6},{8,16},{9,1},{1... | collective-permute-start | bytes 196616 | tf_op jit(solution)/shard_map/ppermute | solution.py:34
  32.7 3.9 %collective-permute-start.9 = (f32[8,16,128]{2,1,0:T(8,128)S(1)}, f32[8,16,128]{2,1,0:T(8,128)S(1)}, u32[]{:S(2)}, u32[]{:S(2)}) collective-permute-start(f32[8,16,128]{2,1,0:T(8,128)S(1)} %pad_maximum_fusion.1), channel_id=1, source_target_pairs={{0,1},{1,9},{2,3},{3,11},{4,5},{5,13},{6,7},{7,15},{8,0},{9,17},{1... | collective-permute-start | bytes 196616 | tf_op jit(solution)/shard_map/ppermute | solution.py:34
  32.7 8.8 %collective-permute-start.12 = (f32[7,16,128]{2,1,0:T(8,128)S(1)}, f32[7,16,128]{2,1,0:T(8,128)S(1)}, u32[]{:S(2)}, u32[]{:S(2)}) collective-permute-start(f32[7,16,128]{2,1,0:T(8,128)S(1)} %shard_map.69), channel_id=1, source_target_pairs={{104,128},{128,104},{105,129},{129,105},{106,130},{130,106},{107,1... | collective-permute-start | bytes 172040 | tf_op jit(solution)/shard_map/ppermute | solution.py:45
  36.5 5.0 %collective-permute-start.10 = (f32[4,16,128]{2,1,0:T(8,128)S(1)}, f32[4,16,128]{2,1,0:T(8,128)S(1)}, u32[]{:S(2)}, u32[]{:S(2)}) collective-permute-start(f32[4,16,128]{2,1,0:T(8,128)S(1)} %get-tuple-element.46), channel_id=1, source_target_pairs={{0,8},{1,0},{2,10},{3,2},{4,12},{5,4},{6,14},{7,6},{8,16},{9,1},{1... | collective-permute-start | bytes 98312 | tf_op jit(solution)/shard_map/ppermute | solution.py:34
  36.6 5.0 %collective-permute-start.11 = (f32[4,16,128]{2,1,0:T(8,128)S(1)}, f32[4,16,128]{2,1,0:T(8,128)S(1)}, u32[]{:S(2)}, u32[]{:S(2)}) collective-permute-start(f32[4,16,128]{2,1,0:T(8,128)S(1)} %get-tuple-element.47), channel_id=1, source_target_pairs={{0,1},{1,9},{2,3},{3,11},{4,5},{5,13},{6,7},{7,15},{8,0},{9,17},{1... | collective-permute-start | bytes 98312 | tf_op jit(solution)/shard_map/ppermute | solution.py:34
  41.6 5.5 %collective-permute-start.13 = (f32[200,128]{1,0:T(8,128)S(1)}, f32[200,128]{1,0:T(8,128)S(1)}, u32[]{:S(2)}, u32[]{:S(2)}) collective-permute-start(f32[200,128]{1,0:T(8,128)S(1)} %get-tuple-element.56), channel_id=1, source_target_pairs={{0,1},{1,2},{2,3},{3,4},{4,5},{5,6},{6,7},{7,0},{8,9},{9,10},{10,1... | collective-permute-start | bytes 307208 | tf_op jit(solution)/shard_map/ppermute | solution.py:72
  45.4 5.3 %collective-permute-start.14 = (f32[200,128]{1,0:T(8,128)S(1)}, f32[200,128]{1,0:T(8,128)S(1)}, u32[]{:S(2)}, u32[]{:S(2)}) collective-permute-start(f32[200,128]{1,0:T(8,128)S(1)} %get-tuple-element.57), channel_id=1, source_target_pairs={{0,7},{1,0},{2,1},{3,2},{4,3},{5,4},{6,5},{7,6},{8,15},{9,8},{10,9... | collective-permute-start | bytes 307208 | tf_op jit(solution)/shard_map/ppermute | solution.py:72

commit v13 on v12

--- a/solution.py
+++ b/solution.py
@@ -269,12 +269,6 @@
             row = 4 + 16 * (k // 2)
             lane = CCOLS * (k % 2)
             out[at + k] = u_out[plane, row : row + 16, lane : lane + CCOLS]
-
-
-def pass_on(plus2, minus2, across, plus_out, minus_out):
-    del across
-    plus_out[...] = plus2[0:4]
-    minus_out[...] = minus2[0:4]
 
 
 def pack_far(ab, plus1, minus1, out):
@@ -534,10 +528,8 @@
     )
     plus2 = along_lines(jnp.concatenate([plus1, plus], axis=0), 1)
     minus2 = along_lines(jnp.concatenate([minus1, minus], axis=0), -1)
-    block = f32(4, CROWS, CCOLS)
-    plus, minus = call(pass_on, [VM] * 3, (block, block))(plus2, minus2, across)
-    plus3 = along_lines(plus, 1)
-    minus3 = along_lines(minus, -1)
+    plus3 = along_lines(plus2[0:4], 1)
+    minus3 = along_lines(minus2[0:4], -1)
 
     rows = f32(Y2_ROWS, CCOLS)
     up, down, dom, edge = call(

time: 53.5 us -> 56.7 us (1.060)
  the two profiles are of different devices: /device:TPU:63 before, /device:TPU:31 now
where the time goes in v13:
time: 56.7 us; the launch traced here: 56.6 us
  starting transfers between devices  30.5 us (54%)
  waiting for transfers between devices  18.5 us (33%)
  Pallas kernels  6.04 us (11%)
  local copies, waits for them, and re-layouts  0.76 us (1%)
    ppermute x3, starting transfers between devices, between_lines(): return lax.ppermute(x, ('slab', 'pen'), pairs)  16.5 us
    ppermute x4, waiting for transfers between devices, rotated(): lax.ppermute(x, axis, [(i, (i + by) % devices) for i in range(devices)])  9.74 us
    ppermute x3, waiting for transfers between devices, between_lines(): return lax.ppermute(x, ('slab', 'pen'), pairs)  7.45 us
    ppermute x4, starting transfers between devices, rotated(): lax.ppermute(x, axis, [(i, (i + by) % devices) for i in range(devices)])  7.11 us
    ppermute x8, starting transfers between devices, along_lines(): return lax.ppermute(x, ('slab', 'pen'), pairs)  6.92 us
    pallas_call x1, Pallas kernels, post_call(): call(post_kernel, [SM] + [VM] * 8, (f32(26, CR, CCOLS), f32(8, FR, COLS),...  2.64 us
    pallas_call x1, Pallas kernels, pre_call(): call(pre_kernel, [SM] + [VM] * 7, (f32(10, FR, COLS), f32(8, FR, COLS), f...  1.71 us
    ppermute x8, waiting for transfers between devices, along_lines(): return lax.ppermute(x, ('slab', 'pen'), pairs)  1.32 us
  transfers between devices with their start and end apart: 15, of which 7 were waited for; matrix products, arithmetic and copies ran while one was open for 1% of the time, Pallas kernels for 1%

profile of v13, /device:TPU:31, one launch (start us, length us, event | category | flops | bytes accessed | tf_op | source)
XLA Modules:
  0.0 56.6 jit_solution(8796047988072619995)
XLA Ops:
  0.0 0.0 copy-start
  0.0 0.0 copy-start.1
  0.0 0.0 copy-start.2
  0.0 1.3 %shard_map.64 = (f32[232,256]{1,0:T(8,128)S(1)}, f32[232,256]{1,0:T(8,128)S(1)}, f32[232,256]{1,0:T(8,128)S(1)}) custom-call(f32[128,256]{1,0:T(8,128)} %bitcast.6, f32[128,256]{1,0:T(8,128)} %bitcast.7, f32[128,256]{1,0:T(8,128)} %bitcast.8, f32[2,16,128]{2,1,0:T(8,128)} %cperm.5), custom_call_target="tpu_custom_call" | custom-call | tf_op jit(solution)/shard_map/pallas_call | solution.py:478
  1.3 0.7 %collective-permute-start = (f32[232,256]{1,0:T(8,128)S(1)}, f32[232,256]{1,0:T(8,128)S(1)}, u32[]{:S(2)}, u32[]{:S(2)}) collective-permute-start(f32[232,256]{1,0:T(8,128)S(1)} %get-tuple-element.30), channel_id=1, source_target_pairs={{0,8},{1,0},{2,10},{3,2},{4,12},{5,4},{6,14},{7,6},{8,16},{9,1},{1... | collective-permute-start | bytes 712712 | tf_op jit(solution)/shard_map/ppermute | solution.py:34
  2.0 1.0 %collective-permute-start.1 = (f32[232,256]{1,0:T(8,128)S(1)}, f32[232,256]{1,0:T(8,128)S(1)}, u32[]{:S(2)}, u32[]{:S(2)}) collective-permute-start(f32[232,256]{1,0:T(8,128)S(1)} %get-tuple-element.31), channel_id=1, source_target_pairs={{0,1},{1,9},{2,3},{3,11},{4,5},{5,13},{6,7},{7,15},{8,0},{9,17},{1... | collective-permute-start | bytes 712712 | tf_op jit(solution)/shard_map/ppermute | solution.py:34
  3.0 10.4 %collective-permute-start.2 = (f32[232,256]{1,0:T(8,128)S(1)}, f32[232,256]{1,0:T(8,128)S(1)}, u32[]{:S(2)}, u32[]{:S(2)}) collective-permute-start(f32[232,256]{1,0:T(8,128)S(1)} %get-tuple-element.32), channel_id=1, source_target_pairs={{120,128},{128,120},{121,129},{129,121},{122,130},{130,122},{123,1... | collective-permute-start | bytes 712712 | tf_op jit(solution)/shard_map/ppermute | solution.py:45
  13.5 0.0 copy-start.5
  13.5 0.6 %copy-done.5 = s32[32]{0:T(128)S(1)} copy-done((s32[32]{0:T(128)S(1)}, s32[32]{0:T(128)}, u32[]{:S(2)}) %copy-start.5) | copy-done | bytes 152
  14.1 0.1 copy.15
  14.2 0.1 reduce-window.9
  14.3 0.0 copy-start.3
  14.3 0.1 reduce
  14.4 0.2 compare_reduce_fusion
  14.6 0.1 add_convert_fusion
  14.6 0.0 collective-permute-done.plus
  14.7 0.0 collective-permute-done.1.minus
  14.7 2.9 %collective-permute-done.2.across = f32[232,256]{1,0:T(8,128)S(1)} collective-permute-done((f32[232,256]{1,0:T(8,128)S(1)}, f32[232,256]{1,0:T(8,128)S(1)}, u32[]{:S(2)}, u32[]{:S(2)}) %collective-permute-start.2) | collective-permute-done | bytes 237600 | tf_op jit(solution)/shard_map/ppermute | solution.py:45
  17.5 0.0 copy-done
  17.5 0.0 copy-done.1
  17.5 0.0 copy-done.2
  17.5 0.0 copy-done.3
  17.6 0.1 shard_map.66
  17.6 2.5 %collective-permute-start.3 = (f32[72,256]{1,0:T(8,128)S(1)}, f32[72,256]{1,0:T(8,128)S(1)}, u32[]{:S(2)}, u32[]{:S(2)}) collective-permute-start(f32[72,256]{1,0:T(8,128)S(1)} %get-tuple-element.37), channel_id=1, source_target_pairs={{0,1},{1,2},{2,3},{3,4},{4,5},{5,6},{6,7},{7,0},{8,9},{9,10},{10,1... | collective-permute-start | bytes 221192 | tf_op jit(solution)/shard_map/ppermute | solution.py:72
  20.1 0.2 collective-permute-start.4
  20.3 0.1 pad_maximum_fusion.2.masks
  20.4 0.0 copy-start.4
  20.4 0.2 shard_map.65
  20.6 0.9 %collective-permute-done.3.ylo = f32[72,256]{1,0:T(8,128)S(1)} collective-permute-done((f32[72,256]{1,0:T(8,128)S(1)}, f32[72,256]{1,0:T(8,128)S(1)}, u32[]{:S(2)}, u32[]{:S(2)}) %collective-permute-start.3) | collective-permute-done | bytes 73760 | tf_op jit(solution)/shard_map/ppermute | solution.py:72
  21.5 3.6 %collective-permute-done.4.yhi = f32[72,256]{1,0:T(8,128)S(1)} collective-permute-done((f32[72,256]{1,0:T(8,128)S(1)}, f32[72,256]{1,0:T(8,128)S(1)}, u32[]{:S(2)}, u32[]{:S(2)}) %collective-permute-start.4) | collective-permute-done | bytes 73760 | tf_op jit(solution)/shard_map/ppermute | solution.py:72
  25.1 0.0 copy-done.4
  25.1 1.7 %shard_map.67 = (f32[10,40,256]{2,1,0:T(8,128)S(1)}, f32[8,40,256]{2,1,0:T(8,128)S(1)}, f32[8,40,256]{2,1,0:T(8,128)S(1)}, f32[4,32,128]{2,1,0:T(8,128)S(1)}, f3...) custom-call(f32[8]{0:T(128)S(1)} %pad_maximum_fusion.2.masks, ...), custom_call_target="tpu_custom_call", output_to_operand_aliasing={{0}: (1, {}), {1}: (2, {}), {2}: (3, {}), {3}: (4, {})} | custom-call | tf_op jit(solution)/shard_map/pallas_call | solution.py:447
  26.8 0.0 collective-permute-start.5
  26.8 1.5 %collective-permute-start.6 = (f32[4,16,128]{2,1,0:T(8,128)S(1)}, f32[4,16,128]{2,1,0:T(8,128)S(1)}, u32[]{:S(2)}, u32[]{:S(2)}) collective-permute-start(f32[4,16,128]{2,1,0:T(8,128)S(1)} %get-tuple-element.40.ab), channel_id=1, source_target_pairs={{0,1},{1,9},{2,3},{3,11},{4,5},{5,13},{6,7},{7,15},{8,0},{9,17},{1... | collective-permute-start | bytes 98312 | tf_op jit(solution)/shard_map/ppermute | solution.py:34
  28.3 1.3 %collective-permute-done.5.plus1 = f32[4,16,128]{2,1,0:T(8,128)S(1)} collective-permute-done((f32[4,16,128]{2,1,0:T(8,128)S(1)}, f32[4,16,128]{2,1,0:T(8,128)S(1)}, u32[]{:S(2)}, u32[]{:S(2)}) %collective-permute-start.5) | collective-permute-done | bytes 32800 | tf_op jit(solution)/shard_map/ppermute | solution.py:34
  29.6 0.0 collective-permute-start.8
  29.6 0.0 collective-permute-done.6.minus1
  29.6 1.5 %collective-permute-start.9 = (f32[8,16,128]{2,1,0:T(8,128)S(1)}, f32[8,16,128]{2,1,0:T(8,128)S(1)}, u32[]{:S(2)}, u32[]{:S(2)}) collective-permute-start(f32[8,16,128]{2,1,0:T(8,128)S(1)} %pad_maximum_fusion.1), channel_id=1, source_target_pairs={{0,1},{1,9},{2,3},{3,11},{4,5},{5,13},{6,7},{7,15},{8,0},{9,17},{1... | collective-permute-start | bytes 196616 | tf_op jit(solution)/shard_map/ppermute | solution.py:34
  31.1 4.1 %collective-permute-start.7 = (f32[8,16,128]{2,1,0:T(8,128)S(1)}, f32[8,16,128]{2,1,0:T(8,128)S(1)}, u32[]{:S(2)}, u32[]{:S(2)}) collective-permute-start(f32[8,16,128]{2,1,0:T(8,128)S(1)} %get-tuple-element.41), channel_id=1, source_target_pairs={{120,128},{128,120},{121,129},{129,121},{122,130},{130,122},{123,1... | collective-permute-start | bytes 196616 | tf_op jit(solution)/shard_map/ppermute | solution.py:45
  35.2 1.9 %collective-permute-start.12 = (f32[7,16,128]{2,1,0:T(8,128)S(1)}, f32[7,16,128]{2,1,0:T(8,128)S(1)}, u32[]{:S(2)}, u32[]{:S(2)}) collective-permute-start(f32[7,16,128]{2,1,0:T(8,128)S(1)} %shard_map.68), channel_id=1, source_target_pairs={{104,128},{128,104},{105,129},{129,105},{106,130},{130,106},{107,1... | collective-permute-start | bytes 172040 | tf_op jit(solution)/shard_map/ppermute | solution.py:45
  37.2 0.0 collective-permute-done.8.plus2
  37.2 2.3 %collective-permute-start.10 = (f32[4,16,128]{2,1,0:T(8,128)S(1)}, f32[4,16,128]{2,1,0:T(8,128)S(1)}, u32[]{:S(2)}, u32[]{:S(2)}) collective-permute-start(f32[4,16,128]{2,1,0:T(8,128)S(1)} %slice.8), channel_id=1, source_target_pairs={{0,8},{1,0},{2,10},{3,2},{4,12},{5,4},{6,14},{7,6},{8,16},{9,1},{1... | collective-permute-start | bytes 98312 | tf_op jit(solution)/shard_map/ppermute | solution.py:34
  39.5 0.0 collective-permute-done.9.minus2
  39.5 0.0 collective-permute-start.11
  39.5 0.0 collective-permute-done.7.across
  39.5 4.6 %collective-permute-done.12.far = f32[7,16,128]{2,1,0:T(8,128)S(1)} collective-permute-done((f32[7,16,128]{2,1,0:T(8,128)S(1)}, f32[7,16,128]{2,1,0:T(8,128)S(1)}, u32[]{:S(2)}, u32[]{:S(2)}) %collective-permute-start.12) | collective-permute-done | bytes 57376 | tf_op jit(solution)/shard_map/ppermute | solution.py:45
  44.1 0.0 collective-permute-done.10.plus3
  44.1 0.0 collective-permute-done.11.minus3
  44.1 0.1 shard_map.69
  44.2 4.5 %collective-permute-start.13 = (f32[200,128]{1,0:T(8,128)S(1)}, f32[200,128]{1,0:T(8,128)S(1)}, u32[]{:S(2)}, u32[]{:S(2)}) collective-permute-start(f32[200,128]{1,0:T(8,128)S(1)} %get-tuple-element.52), channel_id=1, source_target_pairs={{0,1},{1,2},{2,3},{3,4},{4,5},{5,6},{6,7},{7,0},{8,9},{9,10},{10,1... | collective-permute-start | bytes 307208 | tf_op jit(solution)/shard_map/ppermute | solution.py:72
  48.6 0.0 collective-permute-start.14
  48.6 0.1 shard_map.70
  48.7 1.6 %collective-permute-done.13.ylo = f32[200,128]{1,0:T(8,128)S(1)} collective-permute-done((f32[200,128]{1,0:T(8,128)S(1)}, f32[200,128]{1,0:T(8,128)S(1)}, u32[]{:S(2)}, u32[]{:S(2)}) %collective-permute-start.13) | collective-permute-done | bytes 102432 | tf_op jit(solution)/shard_map/ppermute | solution.py:72
  50.3 3.6 %collective-permute-done.14.yhi = f32[200,128]{1,0:T(8,128)S(1)} collective-permute-done((f32[200,128]{1,0:T(8,128)S(1)}, f32[200,128]{1,0:T(8,128)S(1)}, u32[]{:S(2)}, u32[]{:S(2)}) %collective-permute-start.14) | collective-permute-done | bytes 102432 | tf_op jit(solution)/shard_map/ppermute | solution.py:72
  53.9 2.6 %shard_map.71 = (f32[26,32,128]{2,1,0:T(8,128)S(1)}, f32[8,40,256]{2,1,0:T(8,128)S(1)}, f32[4,32,256]{2,1,0:T(8,128)}) custom-call(f32[8]{0:T(128)S(1)} %pad_maximum_fusion.2.masks, f32[26,32,128]{2,1,0:T(8,128)S(1)} %get-tuple-element.46.ff_in, f32[8,40,256]{2,1,0:T(8,128)S(1)} %get-tuple-element.47.uf_in, ...), custom_call_target="tpu_custom_call", output_to_operand_aliasing={{0}: (1, {}), {1}: (2, {})} | custom-call | tf_op jit(solution)/shard_map/pallas_call | solution.py:467
  (8 shorter events, 0.1 us)
Async XLA Ops:
  0.0 17.5 %copy-start = (f32[4,32,256]{2,1,0:T(8,128)S(1)}, f32[4,32,256]{2,1,0:T(8,128)}, u32[]{:S(2)}) copy-start(f32[4,32,256]{2,1,0:T(8,128)} %rhs.4) | copy-start | bytes 393220
  0.0 17.5 %copy-start.1 = (f32[4,32,256]{2,1,0:T(8,128)S(1)}, f32[4,32,256]{2,1,0:T(8,128)}, u32[]{:S(2)}) copy-start(f32[4,32,256]{2,1,0:T(8,128)} %perm.3) | copy-start | bytes 393220
  0.0 17.5 %copy-start.2 = (f32[4,32,256]{2,1,0:T(8,128)S(1)}, f32[4,32,256]{2,1,0:T(8,128)}, u32[]{:S(2)}) copy-start(f32[4,32,256]{2,1,0:T(8,128)} %acc.3) | copy-start | bytes 393220
  1.3 13.3 %collective-permute-start = (f32[232,256]{1,0:T(8,128)S(1)}, f32[232,256]{1,0:T(8,128)S(1)}, u32[]{:S(2)}, u32[]{:S(2)}) collective-permute-start(f32[232,256]{1,0:T(8,128)S(1)} %get-tuple-element.30), channel_id=1, source_target_pairs={{0,8},{1,0},{2,10},{3,2},{4,12},{5,4},{6,14},{7,6},{8,16},{9,1},{1... | collective-permute-start | bytes 712712 | tf_op jit(solution)/shard_map/ppermute | solution.py:34
  2.0 12.7 %collective-permute-start.1 = (f32[232,256]{1,0:T(8,128)S(1)}, f32[232,256]{1,0:T(8,128)S(1)}, u32[]{:S(2)}, u32[]{:S(2)}) collective-permute-start(f32[232,256]{1,0:T(8,128)S(1)} %get-tuple-element.31), channel_id=1, source_target_pairs={{0,1},{1,9},{2,3},{3,11},{4,5},{5,13},{6,7},{7,15},{8,0},{9,17},{1... | collective-permute-start | bytes 712712 | tf_op jit(solution)/shard_map/ppermute | solution.py:34
  3.0 14.5 %collective-permute-start.2 = (f32[232,256]{1,0:T(8,128)S(1)}, f32[232,256]{1,0:T(8,128)S(1)}, u32[]{:S(2)}, u32[]{:S(2)}) collective-permute-start(f32[232,256]{1,0:T(8,128)S(1)} %get-tuple-element.32), channel_id=1, source_target_pairs={{120,128},{128,120},{121,129},{129,121},{122,130},{130,122},{123,1... | collective-permute-start | bytes 712712 | tf_op jit(solution)/shard_map/ppermute | solution.py:45
  13.5 0.7 %copy-start.5 = (s32[32]{0:T(128)S(1)}, s32[32]{0:T(128)}, u32[]{:S(2)}) copy-start(s32[32]{0:T(128)} %param.11) | copy-start | bytes 388
  14.3 3.3 %copy-start.3 = (f32[2,16,128]{2,1,0:T(8,128)S(1)}, f32[2,16,128]{2,1,0:T(8,128)}, u32[]{:S(2)}) copy-start(f32[2,16,128]{2,1,0:T(8,128)} %cperm.5) | copy-start | bytes 49156
  17.6 3.9 %collective-permute-start.3 = (f32[72,256]{1,0:T(8,128)S(1)}, f32[72,256]{1,0:T(8,128)S(1)}, u32[]{:S(2)}, u32[]{:S(2)}) collective-permute-start(f32[72,256]{1,0:T(8,128)S(1)} %get-tuple-element.37), channel_id=1, source_target_pairs={{0,1},{1,2},{2,3},{3,4},{4,5},{5,6},{6,7},{7,0},{8,9},{9,10},{10,1... | collective-permute-start | bytes 221192 | tf_op jit(solution)/shard_map/ppermute | solution.py:72
  20.1 5.0 %collective-permute-start.4 = (f32[72,256]{1,0:T(8,128)S(1)}, f32[72,256]{1,0:T(8,128)S(1)}, u32[]{:S(2)}, u32[]{:S(2)}) collective-permute-start(f32[72,256]{1,0:T(8,128)S(1)} %get-tuple-element.38), channel_id=1, source_target_pairs={{0,7},{1,0},{2,1},{3,2},{4,3},{5,4},{6,5},{7,6},{8,15},{9,8},{10,9... | collective-permute-start | bytes 221192 | tf_op jit(solution)/shard_map/ppermute | solution.py:72
  20.4 4.7 %copy-start.4 = (f32[2,16,128]{2,1,0:T(8,128)S(1)}, f32[2,16,128]{2,1,0:T(8,128)}, u32[]{:S(2)}) copy-start(f32[2,16,128]{2,1,0:T(8,128)} %cacc.1) | copy-start | bytes 49156
  26.8 2.8 %collective-permute-start.5 = (f32[4,16,128]{2,1,0:T(8,128)S(1)}, f32[4,16,128]{2,1,0:T(8,128)S(1)}, u32[]{:S(2)}, u32[]{:S(2)}) collective-permute-start(f32[4,16,128]{2,1,0:T(8,128)S(1)} %get-tuple-element.40.ab), channel_id=1, source_target_pairs={{0,8},{1,0},{2,10},{3,2},{4,12},{5,4},{6,14},{7,6},{8,16},{9,1},{1... | collective-permute-start | bytes 98312 | tf_op jit(solution)/shard_map/ppermute | solution.py:34
  26.8 2.8 %collective-permute-start.6 = (f32[4,16,128]{2,1,0:T(8,128)S(1)}, f32[4,16,128]{2,1,0:T(8,128)S(1)}, u32[]{:S(2)}, u32[]{:S(2)}) collective-permute-start(f32[4,16,128]{2,1,0:T(8,128)S(1)} %get-tuple-element.40.ab), channel_id=1, source_target_pairs={{0,1},{1,9},{2,3},{3,11},{4,5},{5,13},{6,7},{7,15},{8,0},{9,17},{1... | collective-permute-start | bytes 98312 | tf_op jit(solution)/shard_map/ppermute | solution.py:34
  29.6 7.6 %collective-permute-start.8 = (f32[8,16,128]{2,1,0:T(8,128)S(1)}, f32[8,16,128]{2,1,0:T(8,128)S(1)}, u32[]{:S(2)}, u32[]{:S(2)}) collective-permute-start(f32[8,16,128]{2,1,0:T(8,128)S(1)} %pad_maximum_fusion), channel_id=1, source_target_pairs={{0,8},{1,0},{2,10},{3,2},{4,12},{5,4},{6,14},{7,6},{8,16},{9,1},{1... | collective-permute-start | bytes 196616 | tf_op jit(solution)/shard_map/ppermute | solution.py:34
  29.6 9.9 %collective-permute-start.9 = (f32[8,16,128]{2,1,0:T(8,128)S(1)}, f32[8,16,128]{2,1,0:T(8,128)S(1)}, u32[]{:S(2)}, u32[]{:S(2)}) collective-permute-start(f32[8,16,128]{2,1,0:T(8,128)S(1)} %pad_maximum_fusion.1), channel_id=1, source_target_pairs={{0,1},{1,9},{2,3},{3,11},{4,5},{5,13},{6,7},{7,15},{8,0},{9,17},{1... | collective-permute-start | bytes 196616 | tf_op jit(solution)/shard_map/ppermute | solution.py:34
  31.1 8.4 %collective-permute-start.7 = (f32[8,16,128]{2,1,0:T(8,128)S(1)}, f32[8,16,128]{2,1,0:T(8,128)S(1)}, u32[]{:S(2)}, u32[]{:S(2)}) collective-permute-start(f32[8,16,128]{2,1,0:T(8,128)S(1)} %get-tuple-element.41), channel_id=1, source_target_pairs={{120,128},{128,120},{121,129},{129,121},{122,130},{130,122},{123,1... | collective-permute-start | bytes 196616 | tf_op jit(solution)/shard_map/ppermute | solution.py:45
  35.2 8.9 %collective-permute-start.12 = (f32[7,16,128]{2,1,0:T(8,128)S(1)}, f32[7,16,128]{2,1,0:T(8,128)S(1)}, u32[]{:S(2)}, u32[]{:S(2)}) collective-permute-start(f32[7,16,128]{2,1,0:T(8,128)S(1)} %shard_map.68), channel_id=1, source_target_pairs={{104,128},{128,104},{105,129},{129,105},{106,130},{130,106},{107,1... | collective-permute-start | bytes 172040 | tf_op jit(solution)/shard_map/ppermute | solution.py:45
  37.2 6.9 %collective-permute-start.10 = (f32[4,16,128]{2,1,0:T(8,128)S(1)}, f32[4,16,128]{2,1,0:T(8,128)S(1)}, u32[]{:S(2)}, u32[]{:S(2)}) collective-permute-start(f32[4,16,128]{2,1,0:T(8,128)S(1)} %slice.8), channel_id=1, source_target_pairs={{0,8},{1,0},{2,10},{3,2},{4,12},{5,4},{6,14},{7,6},{8,16},{9,1},{1... | collective-permute-start | bytes 98312 | tf_op jit(solution)/shard_map/ppermute | solution.py:34
  39.5 4.6 %collective-permute-start.11 = (f32[4,16,128]{2,1,0:T(8,128)S(1)}, f32[4,16,128]{2,1,0:T(8,128)S(1)}, u32[]{:S(2)}, u32[]{:S(2)}) collective-permute-start(f32[4,16,128]{2,1,0:T(8,128)S(1)} %slice.9), channel_id=1, source_target_pairs={{0,1},{1,9},{2,3},{3,11},{4,5},{5,13},{6,7},{7,15},{8,0},{9,17},{1... | collective-permute-start | bytes 98312 | tf_op jit(solution)/shard_map/ppermute | solution.py:34
  44.2 6.1 %collective-permute-start.13 = (f32[200,128]{1,0:T(8,128)S(1)}, f32[200,128]{1,0:T(8,128)S(1)}, u32[]{:S(2)}, u32[]{:S(2)}) collective-permute-start(f32[200,128]{1,0:T(8,128)S(1)} %get-tuple-element.52), channel_id=1, source_target_pairs={{0,1},{1,2},{2,3},{3,4},{4,5},{5,6},{6,7},{7,0},{8,9},{9,10},{10,1... | collective-permute-start | bytes 307208 | tf_op jit(solution)/shard_map/ppermute | solution.py:72
  48.6 5.3 %collective-permute-start.14 = (f32[200,128]{1,0:T(8,128)S(1)}, f32[200,128]{1,0:T(8,128)S(1)}, u32[]{:S(2)}, u32[]{:S(2)}) collective-permute-start(f32[200,128]{1,0:T(8,128)S(1)} %get-tuple-element.53), channel_id=1, source_target_pairs={{0,7},{1,0},{2,1},{3,2},{4,3},{5,4},{6,5},{7,6},{8,15},{9,8},{10,9... | collective-permute-start | bytes 307208 | tf_op jit(solution)/shard_map/ppermute | solution.py:72

commit v14 on v12

--- a/solution.py
+++ b/solution.py
@@ -72,13 +72,21 @@
     return lax.ppermute(x, axis, [(i, (i + by) % devices) for i in range(devices)])
 
 
-def smooth_xy(v):
-    rows, cols = v.shape
+def smooth_x(v):
+    cols = v.shape[1]
     col = lax.broadcasted_iota(jnp.int32, v.shape, 1)
     left = jnp.where(col == 0, 0.0, pltpu.roll(v, 1, 1))
     right = jnp.where(col == cols - 1, 0.0, pltpu.roll(v, cols - 1, 1))
-    h = v + 0.5 * (left + right)
+    return v + 0.5 * (left + right)
+
+
+def smooth_y(h):
+    rows = h.shape[0]
     return h + 0.5 * (pltpu.roll(h, 1, 0) + pltpu.roll(h, rows - 1, 0))
+
+
+def smooth_xy(v):
+    return smooth_y(smooth_x(v))
 
 
 def to_wide(x):
@@ -164,12 +172,13 @@
             out[at : at + 1, lane : lane + CCOLS] = plane[rc : rc + 1, :]
 
 
-def frame_kernel(rhs, perm, acc, cperm, plus, minus, across, ts, rs, cs, ct):
+def frame_kernel(rhs, perm, acc, cperm, plus, minus, across, ts, rs, cs, ct, hs):
     lo, hi = below_above(plus, minus, across)
     zeros = jnp.zeros((FR, COLS), jnp.float32)
     for k in range(10):
         ts[k] = zeros
         ts[k, 4:36, :] = jnp.sqrt(fine_rows(perm, lo, hi, 0, 3, k - 3, 0, ROWS))
+        hs[k] = smooth_x(ts[k])
     for k in range(8):
         for ref, own, base in ((rs, rhs, Z1_RHS), (cs, acc, Z1_ACC)):
             ref[k] = zeros
@@ -180,11 +189,11 @@
 
 
 def pre_kernel(
-    masks, ts_in, rs_in, cs_in, ct_in, cacc, ylo, yhi,
-    ts, rs, cs, ct_out, a_out, b_out, u_out, ab_out, plus_out, minus_out, across_out,
+    masks, ts_in, rs_in, cs_in, ct_in, hs_in, cacc, ylo, yhi,
+    ts, rs, cs, ct_out, hs, a_out, b_out, u_out, ab_out, plus_out, minus_out, across_out,
     xs, us, ds, fs,
 ):
-    del ts_in, rs_in, cs_in, ct_in
+    del ts_in, rs_in, cs_in, ct_in, hs_in
     first, place_z = place()
     mlo = masks[0]
     mhi = masks[1]
@@ -196,7 +205,9 @@
             ref[k, 2:4, :] = ylo[ybase + 2 * k : ybase + 2 * k + 2, :] * mlo
             ref[k, 36:38, :] = yhi[ybase + 2 * k : ybase + 2 * k + 2, :] * mhi
     for k in range(10):
-        xs[k] = smooth_xy(ts[k])
+        for tile in (0, 32):
+            hs[k, tile : tile + 8, :] = smooth_x(ts[k, tile : tile + 8, :])
+        xs[k] = smooth_y(hs[k])
     for k in range(8):
         t = ts[k + 1]
         w = 2.0 * (xs[k + 1] + 0.5 * (xs[k] + xs[k + 2]) - t)
@@ -445,21 +456,24 @@
     return call(
         frame_kernel,
         [VM] * 7,
-        (f32(10, FR, COLS), f32(8, FR, COLS), f32(8, FR, COLS), f32(4, CR, CCOLS)),
+        (
+            f32(10, FR, COLS), f32(8, FR, COLS), f32(8, FR, COLS), f32(4, CR, CCOLS),
+            f32(10, FR, COLS),
+        ),
     )(*operands)
 
 
 def pre_call(*operands):
     return call(
         pre_kernel,
-        [SM] + [VM] * 7,
+        [SM] + [VM] * 8,
         (
             f32(10, FR, COLS), f32(8, FR, COLS), f32(8, FR, COLS), f32(4, CR, CCOLS),
-            f32(6, FR, COLS), f32(6, FR, COLS), f32(6, FR, COLS), f32(4, CROWS, CCOLS),
+            f32(10, FR, COLS), f32(6, FR, COLS), f32(6, FR, COLS), f32(6, FR, COLS), f32(4, CROWS, CCOLS),
             f32(4, CROWS, CCOLS), f32(4, CROWS, CCOLS), f32(8, CROWS, CCOLS),
         ),
         ((10, FR, COLS), (8, FR, COLS), (4, FR, COLS), (4, FR, CCOLS)),
-        in_place=4,
+        in_place=5,
     )(*operands)
 
 
@@ -523,7 +537,7 @@
     frames = frame_call(
         pressure_rhs, permeability, accumulation, coarse_perm, plus, minus, across
     )
-    t, _, _, ct, a, b, u, ab, plus, minus, across = pre_call(
+    t, _, _, ct, _, a, b, u, ab, plus, minus, across = pre_call(
         masks, *frames, coarse_accum, ylo, yhi
     )
     across = between_lines(across, 1)

time: 53.5 us -> 53.4 us (level)
  no operation moved by 1% of the time
where the time goes in v14:
time: 53.4 us; the launch traced here: 53.3 us
  starting transfers between devices  29 us (54%)
  waiting for transfers between devices  16.6 us (31%)
  Pallas kernels  6.11 us (11%)
  local copies, waits for them, and re-layouts  0.76 us (1%)
    ppermute x8, starting transfers between devices, along_lines(): return lax.ppermute(x, ('slab', 'pen'), pairs)  18.1 us
    ppermute x4, waiting for transfers between devices, rotated(): lax.ppermute(x, axis, [(i, (i + by) % devices) for i in range(devices)])  9.57 us
    ppermute x4, starting transfers between devices, rotated(): lax.ppermute(x, axis, [(i, (i + by) % devices) for i in range(devices)])  5.83 us
    ppermute x3, starting transfers between devices, between_lines(): return lax.ppermute(x, ('slab', 'pen'), pairs)  5.08 us
    ppermute x8, waiting for transfers between devices, along_lines(): return lax.ppermute(x, ('slab', 'pen'), pairs)  3.53 us
    ppermute x3, waiting for transfers between devices, between_lines(): return lax.ppermute(x, ('slab', 'pen'), pairs)  3.53 us
    pallas_call x1, Pallas kernels, post_call(): call(post_kernel, [SM] + [VM] * 8, (f32(26, CR, CCOLS), f32(8, FR, COLS),...  2.64 us
    pallas_call x1, Pallas kernels, pre_call(): call(pre_kernel, [SM] + [VM] * 8, (f32(10, FR, COLS), f32(8, FR, COLS), f...  1.61 us
  transfers between devices with their start and end apart: 15, of which 8 were waited for; matrix products, arithmetic and copies ran while one was open for 1% of the time, Pallas kernels for 1%

profile of v14, /device:TPU:63, one launch (start us, length us, event | category | flops | bytes accessed | tf_op | source)
XLA Modules:
  0.0 53.3 jit_solution(4344830270783291334)
XLA Ops:
  0.0 0.0 copy-start
  0.0 0.0 copy-start.1
  0.0 0.0 copy-start.2
  0.0 1.3 %shard_map.64 = (f32[232,256]{1,0:T(8,128)S(1)}, f32[232,256]{1,0:T(8,128)S(1)}, f32[232,256]{1,0:T(8,128)S(1)}) custom-call(f32[128,256]{1,0:T(8,128)} %bitcast.6, f32[128,256]{1,0:T(8,128)} %bitcast.7, f32[128,256]{1,0:T(8,128)} %bitcast.8, f32[2,16,128]{2,1,0:T(8,128)} %cperm.5), custom_call_target="tpu_custom_call" | custom-call | tf_op jit(solution)/shard_map/pallas_call | solution.py:498
  1.3 0.0 collective-permute-start
  1.3 1.7 %collective-permute-start.1 = (f32[232,256]{1,0:T(8,128)S(1)}, f32[232,256]{1,0:T(8,128)S(1)}, u32[]{:S(2)}, u32[]{:S(2)}) collective-permute-start(f32[232,256]{1,0:T(8,128)S(1)} %get-tuple-element.34), channel_id=1, source_target_pairs={{0,1},{1,9},{2,3},{3,11},{4,5},{5,13},{6,7},{7,15},{8,0},{9,17},{1... | collective-permute-start | bytes 712712 | tf_op jit(solution)/shard_map/ppermute | solution.py:34
  3.0 0.7 %collective-permute-start.2 = (f32[232,256]{1,0:T(8,128)S(1)}, f32[232,256]{1,0:T(8,128)S(1)}, u32[]{:S(2)}, u32[]{:S(2)}) collective-permute-start(f32[232,256]{1,0:T(8,128)S(1)} %get-tuple-element.35), channel_id=1, source_target_pairs={{120,128},{128,120},{121,129},{129,121},{122,130},{130,122},{123,1... | collective-permute-start | bytes 712712 | tf_op jit(solution)/shard_map/ppermute | solution.py:45
  3.7 0.0 copy-start.5
  3.7 0.6 %copy-done.5 = s32[32]{0:T(128)S(1)} copy-done((s32[32]{0:T(128)S(1)}, s32[32]{0:T(128)}, u32[]{:S(2)}) %copy-start.5) | copy-done | bytes 152
  4.3 0.1 copy.16
  4.4 0.1 reduce-window.9
  4.5 0.0 copy-start.3
  4.5 0.1 reduce
  4.6 0.2 compare_reduce_fusion
  4.8 0.1 add_convert_fusion
  4.9 1.9 %collective-permute-done.plus = f32[232,256]{1,0:T(8,128)S(1)} collective-permute-done((f32[232,256]{1,0:T(8,128)S(1)}, f32[232,256]{1,0:T(8,128)S(1)}, u32[]{:S(2)}, u32[]{:S(2)}) %collective-permute-start) | collective-permute-done | bytes 237600 | tf_op jit(solution)/shard_map/ppermute | solution.py:34
  6.8 1.3 %collective-permute-done.1.minus = f32[232,256]{1,0:T(8,128)S(1)} collective-permute-done((f32[232,256]{1,0:T(8,128)S(1)}, f32[232,256]{1,0:T(8,128)S(1)}, u32[]{:S(2)}, u32[]{:S(2)}) %collective-permute-start.1) | collective-permute-done | bytes 237600 | tf_op jit(solution)/shard_map/ppermute | solution.py:34
  8.0 0.0 collective-permute-done.2.across
  8.0 0.0 copy-done
  8.0 0.0 copy-done.1
  8.0 0.0 copy-done.2
  8.1 0.0 copy-done.3
  8.1 0.1 shard_map.66
  8.1 1.8 %collective-permute-start.3 = (f32[72,256]{1,0:T(8,128)S(1)}, f32[72,256]{1,0:T(8,128)S(1)}, u32[]{:S(2)}, u32[]{:S(2)}) collective-permute-start(f32[72,256]{1,0:T(8,128)S(1)} %get-tuple-element.41), channel_id=1, source_target_pairs={{0,1},{1,2},{2,3},{3,4},{4,5},{5,6},{6,7},{7,0},{8,9},{9,10},{10,1... | collective-permute-start | bytes 221192 | tf_op jit(solution)/shard_map/ppermute | solution.py:72
  10.0 0.2 collective-permute-start.4
  10.2 0.1 pad_maximum_fusion.2.masks
  10.2 0.0 copy-start.4
  10.2 0.4 shard_map.65
  10.6 0.8 %collective-permute-done.3.ylo = f32[72,256]{1,0:T(8,128)S(1)} collective-permute-done((f32[72,256]{1,0:T(8,128)S(1)}, f32[72,256]{1,0:T(8,128)S(1)}, u32[]{:S(2)}, u32[]{:S(2)}) %collective-permute-start.3) | collective-permute-done | bytes 73760 | tf_op jit(solution)/shard_map/ppermute | solution.py:72
  11.4 3.6 %collective-permute-done.4.yhi = f32[72,256]{1,0:T(8,128)S(1)} collective-permute-done((f32[72,256]{1,0:T(8,128)S(1)}, f32[72,256]{1,0:T(8,128)S(1)}, u32[]{:S(2)}, u32[]{:S(2)}) %collective-permute-start.4) | collective-permute-done | bytes 73760 | tf_op jit(solution)/shard_map/ppermute | solution.py:72
  14.9 0.0 copy-done.4
  15.0 1.6 %shard_map.67 = (f32[10,40,256]{2,1,0:T(8,128)S(1)}, f32[8,40,256]{2,1,0:T(8,128)S(1)}, f32[8,40,256]{2,1,0:T(8,128)S(1)}, f32[4,32,128]{2,1,0:T(8,128)S(1)}, f3...) custom-call(f32[8]{0:T(128)S(1)} %pad_maximum_fusion.2.masks, ...), custom_call_target="tpu_custom_call", output_to_operand_aliasing={{0}: (1, {}), {1}: (2, {}), {2}: (3, {}), {3}: (4, {}), {4}... | custom-call | tf_op jit(solution)/shard_map/pallas_call | solution.py:467
  16.6 10.0 %collective-permute-start.5 = (f32[4,16,128]{2,1,0:T(8,128)S(1)}, f32[4,16,128]{2,1,0:T(8,128)S(1)}, u32[]{:S(2)}, u32[]{:S(2)}) collective-permute-start(f32[4,16,128]{2,1,0:T(8,128)S(1)} %get-tuple-element.44.ab), channel_id=1, source_target_pairs={{0,8},{1,0},{2,10},{3,2},{4,12},{5,4},{6,14},{7,6},{8,16},{9,1},{1... | collective-permute-start | bytes 98312 | tf_op jit(solution)/shard_map/ppermute | solution.py:34
  26.5 0.0 collective-permute-start.6
  26.5 0.7 %collective-permute-start.7 = (f32[8,16,128]{2,1,0:T(8,128)S(1)}, f32[8,16,128]{2,1,0:T(8,128)S(1)}, u32[]{:S(2)}, u32[]{:S(2)}) collective-permute-start(f32[8,16,128]{2,1,0:T(8,128)S(1)} %get-tuple-element.45), channel_id=1, source_target_pairs={{120,128},{128,120},{121,129},{129,121},{122,130},{130,122},{123,1... | collective-permute-start | bytes 196616 | tf_op jit(solution)/shard_map/ppermute | solution.py:45
  27.2 0.4 collective-permute-done.5.plus1
  27.6 5.0 %collective-permute-start.8 = (f32[8,16,128]{2,1,0:T(8,128)S(1)}, f32[8,16,128]{2,1,0:T(8,128)S(1)}, u32[]{:S(2)}, u32[]{:S(2)}) collective-permute-start(f32[8,16,128]{2,1,0:T(8,128)S(1)} %pad_maximum_fusion), channel_id=1, source_target_pairs={{0,8},{1,0},{2,10},{3,2},{4,12},{5,4},{6,14},{7,6},{8,16},{9,1},{1... | collective-permute-start | bytes 196616 | tf_op jit(solution)/shard_map/ppermute | solution.py:34
  32.5 0.0 collective-permute-done.6.minus1
  32.6 0.0 collective-permute-start.9
  32.6 3.8 %collective-permute-start.12 = (f32[7,16,128]{2,1,0:T(8,128)S(1)}, f32[7,16,128]{2,1,0:T(8,128)S(1)}, u32[]{:S(2)}, u32[]{:S(2)}) collective-permute-start(f32[7,16,128]{2,1,0:T(8,128)S(1)} %shard_map.69), channel_id=1, source_target_pairs={{104,128},{128,104},{105,129},{129,105},{106,130},{130,106},{107,1... | collective-permute-start | bytes 172040 | tf_op jit(solution)/shard_map/ppermute | solution.py:45
  36.4 0.0 collective-permute-done.7.across
  36.4 0.0 collective-permute-done.8.plus2
  36.4 0.0 collective-permute-done.9.minus2
  36.4 0.0 collective-permute-start.10
  36.5 1.5 %collective-permute-start.11 = (f32[4,16,128]{2,1,0:T(8,128)S(1)}, f32[4,16,128]{2,1,0:T(8,128)S(1)}, u32[]{:S(2)}, u32[]{:S(2)}) collective-permute-start(f32[4,16,128]{2,1,0:T(8,128)S(1)} %get-tuple-element.49), channel_id=1, source_target_pairs={{0,1},{1,9},{2,3},{3,11},{4,5},{5,13},{6,7},{7,15},{8,0},{9,17},{1... | collective-permute-start | bytes 98312 | tf_op jit(solution)/shard_map/ppermute | solution.py:34
  37.9 3.5 %collective-permute-done.12.far = f32[7,16,128]{2,1,0:T(8,128)S(1)} collective-permute-done((f32[7,16,128]{2,1,0:T(8,128)S(1)}, f32[7,16,128]{2,1,0:T(8,128)S(1)}, u32[]{:S(2)}, u32[]{:S(2)}) %collective-permute-start.12) | collective-permute-done | bytes 57376 | tf_op jit(solution)/shard_map/ppermute | solution.py:45
  41.5 0.0 collective-permute-done.10.plus3
  41.5 0.0 collective-permute-done.11.minus3
  41.5 0.1 shard_map.70
  41.5 3.8 %collective-permute-start.13 = (f32[200,128]{1,0:T(8,128)S(1)}, f32[200,128]{1,0:T(8,128)S(1)}, u32[]{:S(2)}, u32[]{:S(2)}) collective-permute-start(f32[200,128]{1,0:T(8,128)S(1)} %get-tuple-element.58), channel_id=1, source_target_pairs={{0,1},{1,2},{2,3},{3,4},{4,5},{5,6},{6,7},{7,0},{8,9},{9,10},{10,1... | collective-permute-start | bytes 307208 | tf_op jit(solution)/shard_map/ppermute | solution.py:72
  45.3 0.0 collective-permute-start.14
  45.3 0.1 shard_map.71
  45.4 1.6 %collective-permute-done.13.ylo = f32[200,128]{1,0:T(8,128)S(1)} collective-permute-done((f32[200,128]{1,0:T(8,128)S(1)}, f32[200,128]{1,0:T(8,128)S(1)}, u32[]{:S(2)}, u32[]{:S(2)}) %collective-permute-start.13) | collective-permute-done | bytes 102432 | tf_op jit(solution)/shard_map/ppermute | solution.py:72
  47.0 3.6 %collective-permute-done.14.yhi = f32[200,128]{1,0:T(8,128)S(1)} collective-permute-done((f32[200,128]{1,0:T(8,128)S(1)}, f32[200,128]{1,0:T(8,128)S(1)}, u32[]{:S(2)}, u32[]{:S(2)}) %collective-permute-start.14) | collective-permute-done | bytes 102432 | tf_op jit(solution)/shard_map/ppermute | solution.py:72
  50.6 2.6 %shard_map.72 = (f32[26,32,128]{2,1,0:T(8,128)S(1)}, f32[8,40,256]{2,1,0:T(8,128)S(1)}, f32[4,32,256]{2,1,0:T(8,128)}) custom-call(f32[8]{0:T(128)S(1)} %pad_maximum_fusion.2.masks, f32[26,32,128]{2,1,0:T(8,128)S(1)} %get-tuple-element.52.ff_in, f32[8,40,256]{2,1,0:T(8,128)S(1)} %get-tuple-element.53.uf_in, ...), custom_call_target="tpu_custom_call", output_to_operand_aliasing={{0}: (1, {}), {1}: (2, {})} | custom-call | tf_op jit(solution)/shard_map/pallas_call | solution.py:487
  (7 shorter events, 0.1 us)
Async XLA Ops:
  0.0 8.0 %copy-start = (f32[4,32,256]{2,1,0:T(8,128)S(1)}, f32[4,32,256]{2,1,0:T(8,128)}, u32[]{:S(2)}) copy-start(f32[4,32,256]{2,1,0:T(8,128)} %rhs.4) | copy-start | bytes 393220
  0.0 8.0 %copy-start.1 = (f32[4,32,256]{2,1,0:T(8,128)S(1)}, f32[4,32,256]{2,1,0:T(8,128)}, u32[]{:S(2)}) copy-start(f32[4,32,256]{2,1,0:T(8,128)} %perm.3) | copy-start | bytes 393220
  0.0 8.0 %copy-start.2 = (f32[4,32,256]{2,1,0:T(8,128)S(1)}, f32[4,32,256]{2,1,0:T(8,128)}, u32[]{:S(2)}) copy-start(f32[4,32,256]{2,1,0:T(8,128)} %acc.3) | copy-start | bytes 393220
  1.3 5.4 %collective-permute-start = (f32[232,256]{1,0:T(8,128)S(1)}, f32[232,256]{1,0:T(8,128)S(1)}, u32[]{:S(2)}, u32[]{:S(2)}) collective-permute-start(f32[232,256]{1,0:T(8,128)S(1)} %get-tuple-element.33), channel_id=1, source_target_pairs={{0,8},{1,0},{2,10},{3,2},{4,12},{5,4},{6,14},{7,6},{8,16},{9,1},{1... | collective-permute-start | bytes 712712 | tf_op jit(solution)/shard_map/ppermute | solution.py:34
  1.3 6.7 %collective-permute-start.1 = (f32[232,256]{1,0:T(8,128)S(1)}, f32[232,256]{1,0:T(8,128)S(1)}, u32[]{:S(2)}, u32[]{:S(2)}) collective-permute-start(f32[232,256]{1,0:T(8,128)S(1)} %get-tuple-element.34), channel_id=1, source_target_pairs={{0,1},{1,9},{2,3},{3,11},{4,5},{5,13},{6,7},{7,15},{8,0},{9,17},{1... | collective-permute-start | bytes 712712 | tf_op jit(solution)/shard_map/ppermute | solution.py:34
  3.0 5.0 %collective-permute-start.2 = (f32[232,256]{1,0:T(8,128)S(1)}, f32[232,256]{1,0:T(8,128)S(1)}, u32[]{:S(2)}, u32[]{:S(2)}) collective-permute-start(f32[232,256]{1,0:T(8,128)S(1)} %get-tuple-element.35), channel_id=1, source_target_pairs={{120,128},{128,120},{121,129},{129,121},{122,130},{130,122},{123,1... | collective-permute-start | bytes 712712 | tf_op jit(solution)/shard_map/ppermute | solution.py:45
  3.7 0.7 %copy-start.5 = (s32[32]{0:T(128)S(1)}, s32[32]{0:T(128)}, u32[]{:S(2)}) copy-start(s32[32]{0:T(128)} %param.11) | copy-start | bytes 388
  4.5 3.6 %copy-start.3 = (f32[2,16,128]{2,1,0:T(8,128)S(1)}, f32[2,16,128]{2,1,0:T(8,128)}, u32[]{:S(2)}) copy-start(f32[2,16,128]{2,1,0:T(8,128)} %cperm.5) | copy-start | bytes 49156
  8.1 3.2 %collective-permute-start.3 = (f32[72,256]{1,0:T(8,128)S(1)}, f32[72,256]{1,0:T(8,128)S(1)}, u32[]{:S(2)}, u32[]{:S(2)}) collective-permute-start(f32[72,256]{1,0:T(8,128)S(1)} %get-tuple-element.41), channel_id=1, source_target_pairs={{0,1},{1,2},{2,3},{3,4},{4,5},{5,6},{6,7},{7,0},{8,9},{9,10},{10,1... | collective-permute-start | bytes 221192 | tf_op jit(solution)/shard_map/ppermute | solution.py:72
  10.0 5.0 %collective-permute-start.4 = (f32[72,256]{1,0:T(8,128)S(1)}, f32[72,256]{1,0:T(8,128)S(1)}, u32[]{:S(2)}, u32[]{:S(2)}) collective-permute-start(f32[72,256]{1,0:T(8,128)S(1)} %get-tuple-element.42), channel_id=1, source_target_pairs={{0,7},{1,0},{2,1},{3,2},{4,3},{5,4},{6,5},{7,6},{8,15},{9,8},{10,9... | collective-permute-start | bytes 221192 | tf_op jit(solution)/shard_map/ppermute | solution.py:72
  10.2 4.7 %copy-start.4 = (f32[2,16,128]{2,1,0:T(8,128)S(1)}, f32[2,16,128]{2,1,0:T(8,128)}, u32[]{:S(2)}) copy-start(f32[2,16,128]{2,1,0:T(8,128)} %cacc.1) | copy-start | bytes 49156
  16.6 11.0 %collective-permute-start.5 = (f32[4,16,128]{2,1,0:T(8,128)S(1)}, f32[4,16,128]{2,1,0:T(8,128)S(1)}, u32[]{:S(2)}, u32[]{:S(2)}) collective-permute-start(f32[4,16,128]{2,1,0:T(8,128)S(1)} %get-tuple-element.44.ab), channel_id=1, source_target_pairs={{0,8},{1,0},{2,10},{3,2},{4,12},{5,4},{6,14},{7,6},{8,16},{9,1},{1... | collective-permute-start | bytes 98312 | tf_op jit(solution)/shard_map/ppermute | solution.py:34
  26.5 6.0 %collective-permute-start.6 = (f32[4,16,128]{2,1,0:T(8,128)S(1)}, f32[4,16,128]{2,1,0:T(8,128)S(1)}, u32[]{:S(2)}, u32[]{:S(2)}) collective-permute-start(f32[4,16,128]{2,1,0:T(8,128)S(1)} %get-tuple-element.44.ab), channel_id=1, source_target_pairs={{0,1},{1,9},{2,3},{3,11},{4,5},{5,13},{6,7},{7,15},{8,0},{9,17},{1... | collective-permute-start | bytes 98312 | tf_op jit(solution)/shard_map/ppermute | solution.py:34
  26.5 9.9 %collective-permute-start.7 = (f32[8,16,128]{2,1,0:T(8,128)S(1)}, f32[8,16,128]{2,1,0:T(8,128)S(1)}, u32[]{:S(2)}, u32[]{:S(2)}) collective-permute-start(f32[8,16,128]{2,1,0:T(8,128)S(1)} %get-tuple-element.45), channel_id=1, source_target_pairs={{120,128},{128,120},{121,129},{129,121},{122,130},{130,122},{123,1... | collective-permute-start | bytes 196616 | tf_op jit(solution)/shard_map/ppermute | solution.py:45
  27.6 8.9 %collective-permute-start.8 = (f32[8,16,128]{2,1,0:T(8,128)S(1)}, f32[8,16,128]{2,1,0:T(8,128)S(1)}, u32[]{:S(2)}, u32[]{:S(2)}) collective-permute-start(f32[8,16,128]{2,1,0:T(8,128)S(1)} %pad_maximum_fusion), channel_id=1, source_target_pairs={{0,8},{1,0},{2,10},{3,2},{4,12},{5,4},{6,14},{7,6},{8,16},{9,1},{1... | collective-permute-start | bytes 196616 | tf_op jit(solution)/shard_map/ppermute | solution.py:34
  32.6 3.9 %collective-permute-start.9 = (f32[8,16,128]{2,1,0:T(8,128)S(1)}, f32[8,16,128]{2,1,0:T(8,128)S(1)}, u32[]{:S(2)}, u32[]{:S(2)}) collective-permute-start(f32[8,16,128]{2,1,0:T(8,128)S(1)} %pad_maximum_fusion.1), channel_id=1, source_target_pairs={{0,1},{1,9},{2,3},{3,11},{4,5},{5,13},{6,7},{7,15},{8,0},{9,17},{1... | collective-permute-start | bytes 196616 | tf_op jit(solution)/shard_map/ppermute | solution.py:34
  32.6 8.8 %collective-permute-start.12 = (f32[7,16,128]{2,1,0:T(8,128)S(1)}, f32[7,16,128]{2,1,0:T(8,128)S(1)}, u32[]{:S(2)}, u32[]{:S(2)}) collective-permute-start(f32[7,16,128]{2,1,0:T(8,128)S(1)} %shard_map.69), channel_id=1, source_target_pairs={{104,128},{128,104},{105,129},{129,105},{106,130},{130,106},{107,1... | collective-permute-start | bytes 172040 | tf_op jit(solution)/shard_map/ppermute | solution.py:45
  36.4 5.0 %collective-permute-start.10 = (f32[4,16,128]{2,1,0:T(8,128)S(1)}, f32[4,16,128]{2,1,0:T(8,128)S(1)}, u32[]{:S(2)}, u32[]{:S(2)}) collective-permute-start(f32[4,16,128]{2,1,0:T(8,128)S(1)} %get-tuple-element.48), channel_id=1, source_target_pairs={{0,8},{1,0},{2,10},{3,2},{4,12},{5,4},{6,14},{7,6},{8,16},{9,1},{1... | collective-permute-start | bytes 98312 | tf_op jit(solution)/shard_map/ppermute | solution.py:34
  36.5 5.0 %collective-permute-start.11 = (f32[4,16,128]{2,1,0:T(8,128)S(1)}, f32[4,16,128]{2,1,0:T(8,128)S(1)}, u32[]{:S(2)}, u32[]{:S(2)}) collective-permute-start(f32[4,16,128]{2,1,0:T(8,128)S(1)} %get-tuple-element.49), channel_id=1, source_target_pairs={{0,1},{1,9},{2,3},{3,11},{4,5},{5,13},{6,7},{7,15},{8,0},{9,17},{1... | collective-permute-start | bytes 98312 | tf_op jit(solution)/shard_map/ppermute | solution.py:34
  41.5 5.5 %collective-permute-start.13 = (f32[200,128]{1,0:T(8,128)S(1)}, f32[200,128]{1,0:T(8,128)S(1)}, u32[]{:S(2)}, u32[]{:S(2)}) collective-permute-start(f32[200,128]{1,0:T(8,128)S(1)} %get-tuple-element.58), channel_id=1, source_target_pairs={{0,1},{1,2},{2,3},{3,4},{4,5},{5,6},{6,7},{7,0},{8,9},{9,10},{10,1... | collective-permute-start | bytes 307208 | tf_op jit(solution)/shard_map/ppermute | solution.py:72
  45.3 5.3 %collective-permute-start.14 = (f32[200,128]{1,0:T(8,128)S(1)}, f32[200,128]{1,0:T(8,128)S(1)}, u32[]{:S(2)}, u32[]{:S(2)}) collective-permute-start(f32[200,128]{1,0:T(8,128)S(1)} %get-tuple-element.59), channel_id=1, source_target_pairs={{0,7},{1,0},{2,1},{3,2},{4,3},{5,4},{6,5},{7,6},{8,15},{9,8},{10,9... | collective-permute-start | bytes 307208 | tf_op jit(solution)/shard_map/ppermute | solution.py:72

commit v15 on v14

--- a/solution.py
+++ b/solution.py
@@ -282,10 +282,12 @@
             out[at + k] = u_out[plane, row : row + 16, lane : lane + CCOLS]
 
 
-def pass_on(plus2, minus2, across, plus_out, minus_out):
+def pass_on(plus2, minus2, plus, minus, across, plus_out, minus_out):
     del across
-    plus_out[...] = plus2[0:4]
-    minus_out[...] = minus2[0:4]
+    plus_out[0:4] = plus2[...]
+    plus_out[4:8] = plus[...]
+    minus_out[0:4] = minus2[...]
+    minus_out[4:8] = minus[...]
 
 
 def pack_far(ab, plus1, minus1, out):
@@ -319,8 +321,8 @@
         dom[8 + k if a else 19 + k] = above(plus1, minus1, k, 1, across[k])
         dom[2 + k if a else 13 + k] = below(plus2, minus2, k, 2, far[3 + k])
         dom[10 + k if a else 21 + k] = above(plus2, minus2, k, 2, far[3 + k])
-        edge[k] = below(plus2, minus2, 4 + k, 1, across[4 + k])
-        edge[4 + k] = above(plus2, minus2, 4 + k, 1, across[4 + k])
+        edge[k] = below(plus3, minus3, 4 + k, 1, across[4 + k])
+        edge[4 + k] = above(plus3, minus3, 4 + k, 1, across[4 + k])
     for k in range(3):
         low = 3 if k == 2 else k
         dom[14 if k == 2 else k] = below(plus3, minus3, low, 3, far[k])
@@ -546,10 +548,10 @@
     far = between_lines(
         call(pack_far, [VM] * 3, f32(7, CROWS, CCOLS))(ab, plus1, minus1), 3
     )
-    plus2 = along_lines(jnp.concatenate([plus1, plus], axis=0), 1)
-    minus2 = along_lines(jnp.concatenate([minus1, minus], axis=0), -1)
-    block = f32(4, CROWS, CCOLS)
-    plus, minus = call(pass_on, [VM] * 3, (block, block))(plus2, minus2, across)
+    plus2 = along_lines(plus1, 1)
+    minus2 = along_lines(minus1, -1)
+    block = f32(8, CROWS, CCOLS)
+    plus, minus = call(pass_on, [VM] * 5, (block, block))(plus2, minus2, plus, minus, across)
     plus3 = along_lines(plus, 1)
     minus3 = along_lines(minus, -1)
 

time: 53.4 us -> 57.5 us (1.077)
  the two profiles are of different devices: /device:TPU:63 before, /device:TPU:39 now
where the time goes in v15:
time: 57.5 us; the launch traced here: 57.3 us
  starting transfers between devices  33.8 us (59%)
  waiting for transfers between devices  16 us (28%)
  Pallas kernels  6.11 us (11%)
  local copies, waits for them, and re-layouts  0.76 us (1%)
    ppermute x8, starting transfers between devices, along_lines(): return lax.ppermute(x, ('slab', 'pen'), pairs)  19.1 us
    ppermute x4, starting transfers between devices, rotated(): lax.ppermute(x, axis, [(i, (i + by) % devices) for i in range(devices)])  8.16 us
    ppermute x4, waiting for transfers between devices, rotated(): lax.ppermute(x, axis, [(i, (i + by) % devices) for i in range(devices)])  7.35 us
    ppermute x3, starting transfers between devices, between_lines(): return lax.ppermute(x, ('slab', 'pen'), pairs)  6.56 us
    ppermute x8, waiting for transfers between devices, along_lines(): return lax.ppermute(x, ('slab', 'pen'), pairs)  5.04 us
    ppermute x3, waiting for transfers between devices, between_lines(): return lax.ppermute(x, ('slab', 'pen'), pairs)  3.59 us
    pallas_call x1, Pallas kernels, post_call(): call(post_kernel, [SM] + [VM] * 8, (f32(26, CR, CCOLS), f32(8, FR, COLS),...  2.64 us
    pallas_call x1, Pallas kernels, pre_call(): call(pre_kernel, [SM] + [VM] * 8, (f32(10, FR, COLS), f32(8, FR, COLS), f...  1.62 us
  transfers between devices with their start and end apart: 15, of which 9 were waited for; matrix products, arithmetic and copies ran while one was open for 1% of the time, Pallas kernels for 1%

profile of v15, /device:TPU:39, one launch (start us, length us, event | category | flops | bytes accessed | tf_op | source)
XLA Modules:
  0.0 57.3 jit_solution(4513823795354709368)
XLA Ops:
  0.0 0.0 copy-start
  0.0 0.0 copy-start.1
  0.0 0.0 copy-start.2
  0.0 1.3 %shard_map.64 = (f32[232,256]{1,0:T(8,128)S(1)}, f32[232,256]{1,0:T(8,128)S(1)}, f32[232,256]{1,0:T(8,128)S(1)}) custom-call(f32[128,256]{1,0:T(8,128)} %bitcast.6, f32[128,256]{1,0:T(8,128)} %bitcast.7, f32[128,256]{1,0:T(8,128)} %bitcast.8, f32[2,16,128]{2,1,0:T(8,128)} %cperm.5), custom_call_target="tpu_custom_call" | custom-call | tf_op jit(solution)/shard_map/pallas_call | solution.py:500
  1.3 0.0 collective-permute-start
  1.3 1.7 %collective-permute-start.1 = (f32[232,256]{1,0:T(8,128)S(1)}, f32[232,256]{1,0:T(8,128)S(1)}, u32[]{:S(2)}, u32[]{:S(2)}) collective-permute-start(f32[232,256]{1,0:T(8,128)S(1)} %get-tuple-element.34), channel_id=1, source_target_pairs={{0,1},{1,9},{2,3},{3,11},{4,5},{5,13},{6,7},{7,15},{8,0},{9,17},{1... | collective-permute-start | bytes 712712 | tf_op jit(solution)/shard_map/ppermute | solution.py:34
  3.0 0.7 %collective-permute-start.2 = (f32[232,256]{1,0:T(8,128)S(1)}, f32[232,256]{1,0:T(8,128)S(1)}, u32[]{:S(2)}, u32[]{:S(2)}) collective-permute-start(f32[232,256]{1,0:T(8,128)S(1)} %get-tuple-element.35), channel_id=1, source_target_pairs={{120,128},{128,120},{121,129},{129,121},{122,130},{130,122},{123,1... | collective-permute-start | bytes 712712 | tf_op jit(solution)/shard_map/ppermute | solution.py:45
  3.7 0.0 copy-start.5
  3.7 0.6 %copy-done.5 = s32[32]{0:T(128)S(1)} copy-done((s32[32]{0:T(128)S(1)}, s32[32]{0:T(128)}, u32[]{:S(2)}) %copy-start.5) | copy-done | bytes 152
  4.3 0.1 copy.16
  4.4 0.1 reduce-window.9
  4.5 0.0 copy-start.3
  4.5 0.1 reduce
  4.6 0.2 compare_reduce_fusion
  4.8 0.1 add_convert_fusion
  4.9 1.9 %collective-permute-done.plus = f32[232,256]{1,0:T(8,128)S(1)} collective-permute-done((f32[232,256]{1,0:T(8,128)S(1)}, f32[232,256]{1,0:T(8,128)S(1)}, u32[]{:S(2)}, u32[]{:S(2)}) %collective-permute-start) | collective-permute-done | bytes 237600 | tf_op jit(solution)/shard_map/ppermute | solution.py:34
  6.8 1.3 %collective-permute-done.1.minus = f32[232,256]{1,0:T(8,128)S(1)} collective-permute-done((f32[232,256]{1,0:T(8,128)S(1)}, f32[232,256]{1,0:T(8,128)S(1)}, u32[]{:S(2)}, u32[]{:S(2)}) %collective-permute-start.1) | collective-permute-done | bytes 237600 | tf_op jit(solution)/shard_map/ppermute | solution.py:34
  8.0 0.0 collective-permute-done.2.across
  8.0 0.0 copy-done
  8.0 0.0 copy-done.1
  8.0 0.0 copy-done.2
  8.1 0.0 copy-done.3
  8.1 0.1 shard_map.66
  8.1 3.2 %collective-permute-start.3 = (f32[72,256]{1,0:T(8,128)S(1)}, f32[72,256]{1,0:T(8,128)S(1)}, u32[]{:S(2)}, u32[]{:S(2)}) collective-permute-start(f32[72,256]{1,0:T(8,128)S(1)} %get-tuple-element.41), channel_id=1, source_target_pairs={{0,1},{1,2},{2,3},{3,4},{4,5},{5,6},{6,7},{7,0},{8,9},{9,10},{10,1... | collective-permute-start | bytes 221192 | tf_op jit(solution)/shard_map/ppermute | solution.py:72
  11.3 0.0 collective-permute-start.4
  11.3 0.1 pad_maximum_fusion.masks
  11.4 0.0 copy-start.4
  11.4 0.4 shard_map.65
  11.8 1.0 %collective-permute-done.3.ylo = f32[72,256]{1,0:T(8,128)S(1)} collective-permute-done((f32[72,256]{1,0:T(8,128)S(1)}, f32[72,256]{1,0:T(8,128)S(1)}, u32[]{:S(2)}, u32[]{:S(2)}) %collective-permute-start.3) | collective-permute-done | bytes 73760 | tf_op jit(solution)/shard_map/ppermute | solution.py:72
  12.7 2.4 %collective-permute-done.4.yhi = f32[72,256]{1,0:T(8,128)S(1)} collective-permute-done((f32[72,256]{1,0:T(8,128)S(1)}, f32[72,256]{1,0:T(8,128)S(1)}, u32[]{:S(2)}, u32[]{:S(2)}) %collective-permute-start.4) | collective-permute-done | bytes 73760 | tf_op jit(solution)/shard_map/ppermute | solution.py:72
  15.1 0.0 copy-done.4
  15.1 1.6 %shard_map.67 = (f32[10,40,256]{2,1,0:T(8,128)S(1)}, f32[8,40,256]{2,1,0:T(8,128)S(1)}, f32[8,40,256]{2,1,0:T(8,128)S(1)}, f32[4,32,128]{2,1,0:T(8,128)S(1)}, f3...) custom-call(f32[8]{0:T(128)S(1)} %pad_maximum_fusion.masks, ...), custom_call_target="tpu_custom_call", output_to_operand_aliasing={{0}: (1, {}), {1}: (2, {}), {2}: (3, {}), {3}: (4, {}), {4}... | custom-call | tf_op jit(solution)/shard_map/pallas_call | solution.py:469
  16.7 2.8 %collective-permute-start.6 = (f32[4,16,128]{2,1,0:T(8,128)S(1)}, f32[4,16,128]{2,1,0:T(8,128)S(1)}, u32[]{:S(2)}, u32[]{:S(2)}) collective-permute-start(f32[4,16,128]{2,1,0:T(8,128)S(1)} %get-tuple-element.44.ab), channel_id=1, source_target_pairs={{0,1},{1,9},{2,3},{3,11},{4,5},{5,13},{6,7},{7,15},{8,0},{9,17},{1... | collective-permute-start | bytes 98312 | tf_op jit(solution)/shard_map/ppermute | solution.py:34
  19.5 7.2 %collective-permute-start.5 = (f32[4,16,128]{2,1,0:T(8,128)S(1)}, f32[4,16,128]{2,1,0:T(8,128)S(1)}, u32[]{:S(2)}, u32[]{:S(2)}) collective-permute-start(f32[4,16,128]{2,1,0:T(8,128)S(1)} %get-tuple-element.44.ab), channel_id=1, source_target_pairs={{0,8},{1,0},{2,10},{3,2},{4,12},{5,4},{6,14},{7,6},{8,16},{9,1},{1... | collective-permute-start | bytes 98312 | tf_op jit(solution)/shard_map/ppermute | solution.py:34
  26.7 0.7 %collective-permute-start.7 = (f32[8,16,128]{2,1,0:T(8,128)S(1)}, f32[8,16,128]{2,1,0:T(8,128)S(1)}, u32[]{:S(2)}, u32[]{:S(2)}) collective-permute-start(f32[8,16,128]{2,1,0:T(8,128)S(1)} %get-tuple-element.45), channel_id=1, source_target_pairs={{120,128},{128,120},{121,129},{129,121},{122,130},{130,122},{123,1... | collective-permute-start | bytes 196616 | tf_op jit(solution)/shard_map/ppermute | solution.py:45
  27.4 0.6 %collective-permute-done.6.minus1 = f32[4,16,128]{2,1,0:T(8,128)S(1)} collective-permute-done((f32[4,16,128]{2,1,0:T(8,128)S(1)}, f32[4,16,128]{2,1,0:T(8,128)S(1)}, u32[]{:S(2)}, u32[]{:S(2)}) %collective-permute-start.6) | collective-permute-done | bytes 32800 | tf_op jit(solution)/shard_map/ppermute | solution.py:34
  28.0 0.0 collective-permute-start.9
  28.0 0.0 collective-permute-done.5.plus1
  28.0 5.7 %collective-permute-start.8 = (f32[4,16,128]{2,1,0:T(8,128)S(1)}, f32[4,16,128]{2,1,0:T(8,128)S(1)}, u32[]{:S(2)}, u32[]{:S(2)}) collective-permute-start(f32[4,16,128]{2,1,0:T(8,128)S(1)} %collective-permute-done.5.plus1), channel_id=1, source_target_pairs={{0,8},{1,0},{2,10},{3,2},{4,12},{5,4},{6,14},{7,6},{8,16},{9,1},{1... | collective-permute-start | bytes 98312 | tf_op jit(solution)/shard_map/ppermute | solution.py:34
  33.7 1.3 %collective-permute-done.9.minus2 = f32[4,16,128]{2,1,0:T(8,128)S(1)} collective-permute-done((f32[4,16,128]{2,1,0:T(8,128)S(1)}, f32[4,16,128]{2,1,0:T(8,128)S(1)}, u32[]{:S(2)}, u32[]{:S(2)}) %collective-permute-start.9) | collective-permute-done | bytes 32800 | tf_op jit(solution)/shard_map/ppermute | solution.py:34
  35.0 0.0 collective-permute-done.8.plus2
  35.0 0.0 collective-permute-done.7.across
  35.0 1.7 %collective-permute-start.10 = (f32[8,16,128]{2,1,0:T(8,128)S(1)}, f32[8,16,128]{2,1,0:T(8,128)S(1)}, u32[]{:S(2)}, u32[]{:S(2)}) collective-permute-start(f32[8,16,128]{2,1,0:T(8,128)S(1)} %get-tuple-element.48), channel_id=1, source_target_pairs={{0,8},{1,0},{2,10},{3,2},{4,12},{5,4},{6,14},{7,6},{8,16},{9,1},{1... | collective-permute-start | bytes 196616 | tf_op jit(solution)/shard_map/ppermute | solution.py:34
  36.7 0.0 collective-permute-start.11
  36.7 5.2 %collective-permute-start.12 = (f32[7,16,128]{2,1,0:T(8,128)S(1)}, f32[7,16,128]{2,1,0:T(8,128)S(1)}, u32[]{:S(2)}, u32[]{:S(2)}) collective-permute-start(f32[7,16,128]{2,1,0:T(8,128)S(1)} %shard_map.69), channel_id=1, source_target_pairs={{104,128},{128,104},{105,129},{129,105},{106,130},{130,106},{107,1... | collective-permute-start | bytes 172040 | tf_op jit(solution)/shard_map/ppermute | solution.py:45
  42.0 3.6 %collective-permute-done.12.far = f32[7,16,128]{2,1,0:T(8,128)S(1)} collective-permute-done((f32[7,16,128]{2,1,0:T(8,128)S(1)}, f32[7,16,128]{2,1,0:T(8,128)S(1)}, u32[]{:S(2)}, u32[]{:S(2)}) %collective-permute-start.12) | collective-permute-done | bytes 57376 | tf_op jit(solution)/shard_map/ppermute | solution.py:45
  45.5 0.0 collective-permute-done.10.plus3
  45.5 0.0 collective-permute-done.11.minus3
  45.5 0.1 shard_map.70
  45.6 5.0 %collective-permute-start.13 = (f32[200,128]{1,0:T(8,128)S(1)}, f32[200,128]{1,0:T(8,128)S(1)}, u32[]{:S(2)}, u32[]{:S(2)}) collective-permute-start(f32[200,128]{1,0:T(8,128)S(1)} %get-tuple-element.58), channel_id=1, source_target_pairs={{0,1},{1,2},{2,3},{3,4},{4,5},{5,6},{6,7},{7,0},{8,9},{9,10},{10,1... | collective-permute-start | bytes 307208 | tf_op jit(solution)/shard_map/ppermute | solution.py:72
  50.6 0.0 collective-permute-start.14
  50.6 0.1 shard_map.71
  50.6 1.6 %collective-permute-done.13.ylo = f32[200,128]{1,0:T(8,128)S(1)} collective-permute-done((f32[200,128]{1,0:T(8,128)S(1)}, f32[200,128]{1,0:T(8,128)S(1)}, u32[]{:S(2)}, u32[]{:S(2)}) %collective-permute-start.13) | collective-permute-done | bytes 102432 | tf_op jit(solution)/shard_map/ppermute | solution.py:72
  52.3 2.4 %collective-permute-done.14.yhi = f32[200,128]{1,0:T(8,128)S(1)} collective-permute-done((f32[200,128]{1,0:T(8,128)S(1)}, f32[200,128]{1,0:T(8,128)S(1)}, u32[]{:S(2)}, u32[]{:S(2)}) %collective-permute-start.14) | collective-permute-done | bytes 102432 | tf_op jit(solution)/shard_map/ppermute | solution.py:72
  54.7 2.6 %shard_map.72 = (f32[26,32,128]{2,1,0:T(8,128)S(1)}, f32[8,40,256]{2,1,0:T(8,128)S(1)}, f32[4,32,256]{2,1,0:T(8,128)}) custom-call(f32[8]{0:T(128)S(1)} %pad_maximum_fusion.masks, f32[26,32,128]{2,1,0:T(8,128)S(1)} %get-tuple-element.52.ff_in, f32[8,40,256]{2,1,0:T(8,128)S(1)} %get-tuple-element.53.uf_in, ...), custom_call_target="tpu_custom_call", output_to_operand_aliasing={{0}: (1, {}), {1}: (2, {})} | custom-call | tf_op jit(solution)/shard_map/pallas_call | solution.py:489
  (5 shorter events, 0.0 us)
Async XLA Ops:
  0.0 8.0 %copy-start = (f32[4,32,256]{2,1,0:T(8,128)S(1)}, f32[4,32,256]{2,1,0:T(8,128)}, u32[]{:S(2)}) copy-start(f32[4,32,256]{2,1,0:T(8,128)} %rhs.4) | copy-start | bytes 393220
  0.0 8.0 %copy-start.1 = (f32[4,32,256]{2,1,0:T(8,128)S(1)}, f32[4,32,256]{2,1,0:T(8,128)}, u32[]{:S(2)}) copy-start(f32[4,32,256]{2,1,0:T(8,128)} %perm.3) | copy-start | bytes 393220
  0.0 8.0 %copy-start.2 = (f32[4,32,256]{2,1,0:T(8,128)S(1)}, f32[4,32,256]{2,1,0:T(8,128)}, u32[]{:S(2)}) copy-start(f32[4,32,256]{2,1,0:T(8,128)} %acc.3) | copy-start | bytes 393220
  1.3 5.4 %collective-permute-start = (f32[232,256]{1,0:T(8,128)S(1)}, f32[232,256]{1,0:T(8,128)S(1)}, u32[]{:S(2)}, u32[]{:S(2)}) collective-permute-start(f32[232,256]{1,0:T(8,128)S(1)} %get-tuple-element.33), channel_id=1, source_target_pairs={{0,8},{1,0},{2,10},{3,2},{4,12},{5,4},{6,14},{7,6},{8,16},{9,1},{1... | collective-permute-start | bytes 712712 | tf_op jit(solution)/shard_map/ppermute | solution.py:34
  1.3 6.7 %collective-permute-start.1 = (f32[232,256]{1,0:T(8,128)S(1)}, f32[232,256]{1,0:T(8,128)S(1)}, u32[]{:S(2)}, u32[]{:S(2)}) collective-permute-start(f32[232,256]{1,0:T(8,128)S(1)} %get-tuple-element.34), channel_id=1, source_target_pairs={{0,1},{1,9},{2,3},{3,11},{4,5},{5,13},{6,7},{7,15},{8,0},{9,17},{1... | collective-permute-start | bytes 712712 | tf_op jit(solution)/shard_map/ppermute | solution.py:34
  3.0 5.0 %collective-permute-start.2 = (f32[232,256]{1,0:T(8,128)S(1)}, f32[232,256]{1,0:T(8,128)S(1)}, u32[]{:S(2)}, u32[]{:S(2)}) collective-permute-start(f32[232,256]{1,0:T(8,128)S(1)} %get-tuple-element.35), channel_id=1, source_target_pairs={{120,128},{128,120},{121,129},{129,121},{122,130},{130,122},{123,1... | collective-permute-start | bytes 712712 | tf_op jit(solution)/shard_map/ppermute | solution.py:45
  3.7 0.7 %copy-start.5 = (s32[32]{0:T(128)S(1)}, s32[32]{0:T(128)}, u32[]{:S(2)}) copy-start(s32[32]{0:T(128)} %param.11) | copy-start | bytes 388
  4.5 3.6 %copy-start.3 = (f32[2,16,128]{2,1,0:T(8,128)S(1)}, f32[2,16,128]{2,1,0:T(8,128)}, u32[]{:S(2)}) copy-start(f32[2,16,128]{2,1,0:T(8,128)} %cperm.5) | copy-start | bytes 49156
  8.1 4.6 %collective-permute-start.3 = (f32[72,256]{1,0:T(8,128)S(1)}, f32[72,256]{1,0:T(8,128)S(1)}, u32[]{:S(2)}, u32[]{:S(2)}) collective-permute-start(f32[72,256]{1,0:T(8,128)S(1)} %get-tuple-element.41), channel_id=1, source_target_pairs={{0,1},{1,2},{2,3},{3,4},{4,5},{5,6},{6,7},{7,0},{8,9},{9,10},{10,1... | collective-permute-start | bytes 221192 | tf_op jit(solution)/shard_map/ppermute | solution.py:72
  11.3 3.8 %collective-permute-start.4 = (f32[72,256]{1,0:T(8,128)S(1)}, f32[72,256]{1,0:T(8,128)S(1)}, u32[]{:S(2)}, u32[]{:S(2)}) collective-permute-start(f32[72,256]{1,0:T(8,128)S(1)} %get-tuple-element.42), channel_id=1, source_target_pairs={{0,7},{1,0},{2,1},{3,2},{4,3},{5,4},{6,5},{7,6},{8,15},{9,8},{10,9... | collective-permute-start | bytes 221192 | tf_op jit(solution)/shard_map/ppermute | solution.py:72
  11.4 3.7 %copy-start.4 = (f32[2,16,128]{2,1,0:T(8,128)S(1)}, f32[2,16,128]{2,1,0:T(8,128)}, u32[]{:S(2)}) copy-start(f32[2,16,128]{2,1,0:T(8,128)} %cacc.1) | copy-start | bytes 49156
  16.7 11.3 %collective-permute-start.6 = (f32[4,16,128]{2,1,0:T(8,128)S(1)}, f32[4,16,128]{2,1,0:T(8,128)S(1)}, u32[]{:S(2)}, u32[]{:S(2)}) collective-permute-start(f32[4,16,128]{2,1,0:T(8,128)S(1)} %get-tuple-element.44.ab), channel_id=1, source_target_pairs={{0,1},{1,9},{2,3},{3,11},{4,5},{5,13},{6,7},{7,15},{8,0},{9,17},{1... | collective-permute-start | bytes 98312 | tf_op jit(solution)/shard_map/ppermute | solution.py:34
  19.5 8.5 %collective-permute-start.5 = (f32[4,16,128]{2,1,0:T(8,128)S(1)}, f32[4,16,128]{2,1,0:T(8,128)S(1)}, u32[]{:S(2)}, u32[]{:S(2)}) collective-permute-start(f32[4,16,128]{2,1,0:T(8,128)S(1)} %get-tuple-element.44.ab), channel_id=1, source_target_pairs={{0,8},{1,0},{2,10},{3,2},{4,12},{5,4},{6,14},{7,6},{8,16},{9,1},{1... | collective-permute-start | bytes 98312 | tf_op jit(solution)/shard_map/ppermute | solution.py:34
  26.7 8.2 %collective-permute-start.7 = (f32[8,16,128]{2,1,0:T(8,128)S(1)}, f32[8,16,128]{2,1,0:T(8,128)S(1)}, u32[]{:S(2)}, u32[]{:S(2)}) collective-permute-start(f32[8,16,128]{2,1,0:T(8,128)S(1)} %get-tuple-element.45), channel_id=1, source_target_pairs={{120,128},{128,120},{121,129},{129,121},{122,130},{130,122},{123,1... | collective-permute-start | bytes 196616 | tf_op jit(solution)/shard_map/ppermute | solution.py:45
  28.0 7.0 %collective-permute-start.9 = (f32[4,16,128]{2,1,0:T(8,128)S(1)}, f32[4,16,128]{2,1,0:T(8,128)S(1)}, u32[]{:S(2)}, u32[]{:S(2)}) collective-permute-start(f32[4,16,128]{2,1,0:T(8,128)S(1)} %collective-permute-done.6.minus1), channel_id=1, source_target_pairs={{0,1},{1,9},{2,3},{3,11},{4,5},{5,13},{6,7},{7,15},{8,0},{9,17},{1... | collective-permute-start | bytes 98312 | tf_op jit(solution)/shard_map/ppermute | solution.py:34
  28.0 7.0 %collective-permute-start.8 = (f32[4,16,128]{2,1,0:T(8,128)S(1)}, f32[4,16,128]{2,1,0:T(8,128)S(1)}, u32[]{:S(2)}, u32[]{:S(2)}) collective-permute-start(f32[4,16,128]{2,1,0:T(8,128)S(1)} %collective-permute-done.5.plus1), channel_id=1, source_target_pairs={{0,8},{1,0},{2,10},{3,2},{4,12},{5,4},{6,14},{7,6},{8,16},{9,1},{1... | collective-permute-start | bytes 98312 | tf_op jit(solution)/shard_map/ppermute | solution.py:34
  35.0 10.6 %collective-permute-start.10 = (f32[8,16,128]{2,1,0:T(8,128)S(1)}, f32[8,16,128]{2,1,0:T(8,128)S(1)}, u32[]{:S(2)}, u32[]{:S(2)}) collective-permute-start(f32[8,16,128]{2,1,0:T(8,128)S(1)} %get-tuple-element.48), channel_id=1, source_target_pairs={{0,8},{1,0},{2,10},{3,2},{4,12},{5,4},{6,14},{7,6},{8,16},{9,1},{1... | collective-permute-start | bytes 196616 | tf_op jit(solution)/shard_map/ppermute | solution.py:34
  36.7 8.9 %collective-permute-start.11 = (f32[8,16,128]{2,1,0:T(8,128)S(1)}, f32[8,16,128]{2,1,0:T(8,128)S(1)}, u32[]{:S(2)}, u32[]{:S(2)}) collective-permute-start(f32[8,16,128]{2,1,0:T(8,128)S(1)} %get-tuple-element.49), channel_id=1, source_target_pairs={{0,1},{1,9},{2,3},{3,11},{4,5},{5,13},{6,7},{7,15},{8,0},{9,17},{1... | collective-permute-start | bytes 196616 | tf_op jit(solution)/shard_map/ppermute | solution.py:34
  36.7 8.8 %collective-permute-start.12 = (f32[7,16,128]{2,1,0:T(8,128)S(1)}, f32[7,16,128]{2,1,0:T(8,128)S(1)}, u32[]{:S(2)}, u32[]{:S(2)}) collective-permute-start(f32[7,16,128]{2,1,0:T(8,128)S(1)} %shard_map.69), channel_id=1, source_target_pairs={{104,128},{128,104},{105,129},{129,105},{106,130},{130,106},{107,1... | collective-permute-start | bytes 172040 | tf_op jit(solution)/shard_map/ppermute | solution.py:45
  45.6 6.6 %collective-permute-start.13 = (f32[200,128]{1,0:T(8,128)S(1)}, f32[200,128]{1,0:T(8,128)S(1)}, u32[]{:S(2)}, u32[]{:S(2)}) collective-permute-start(f32[200,128]{1,0:T(8,128)S(1)} %get-tuple-element.58), channel_id=1, source_target_pairs={{0,1},{1,2},{2,3},{3,4},{4,5},{5,6},{6,7},{7,0},{8,9},{9,10},{10,1... | collective-permute-start | bytes 307208 | tf_op jit(solution)/shard_map/ppermute | solution.py:72
  50.6 4.1 %collective-permute-start.14 = (f32[200,128]{1,0:T(8,128)S(1)}, f32[200,128]{1,0:T(8,128)S(1)}, u32[]{:S(2)}, u32[]{:S(2)}) collective-permute-start(f32[200,128]{1,0:T(8,128)S(1)} %get-tuple-element.59), channel_id=1, source_target_pairs={{0,7},{1,0},{2,1},{3,2},{4,3},{5,4},{6,5},{7,6},{8,15},{9,8},{10,9... | collective-permute-start | bytes 307208 | tf_op jit(solution)/shard_map/ppermute | solution.py:72
